TPU v7x, 32 devices: a whole 2x2x4 slice. The times are simulated.
32 devices in a mesh: fsdp: 8 (over z, core), sp: 4 (over y, x).
Axes of the slice: x: 2, y: 2, z: 4, core: 2. Of those that a mesh axis runs over, the one named last changes fastest.
Arguments:
- tokens: bfloat16 [8192, 2048], P(('fsdp', 'sp')), may hold values from -6 to 6
- w_attn: bfloat16 [2048, 8192], P(('fsdp', 'sp'))
- norm_gains: bfloat16 [2048, 4], P(('fsdp', 'sp')), may hold values from 0.25 to 1.75
- w_expert: bfloat16 [2048, 16, 3072], P('fsdp', 'sp')
- gate_weights: float32 [8192, 8], P(('fsdp', 'sp')), may hold values from 0.06 to 0.25
- routes: int32 [8192, 8], P(('fsdp', 'sp')), may hold values from 0 to 15, all different within a row; in each aligned block of 256 rows (0 to 255, 256 to 511, ...) at most 136 rows name the same one
- segment: int32 [8192], P('fsdp'), may hold values from 0 to 2, as said below
- valid_mask: int32 [8192], P(('fsdp', 'sp')), may hold values from 0 to 1, as said below
- teacher: bfloat16 [8192, 2048], P(('fsdp', 'sp')), may hold values from -6 to 6
- cotangent: bfloat16 [8192, 2048], P(('fsdp', 'sp')), may hold values from -6 to 6
Outputs:
- output: bfloat16 [8192, 2048], P(('fsdp', 'sp'))
- loss: float32 [], replicated
- grad_tokens: float32 [8192, 2048], P(('fsdp', 'sp'))
- grad_attn: float32 [2048, 8192], P(('fsdp', 'sp'))
- grad_gains: float32 [2048, 4], P(('fsdp', 'sp'))
- grad_expert: float32 [2048, 16, 3072], P('fsdp', 'sp')
Inputs may be any that keep to these rules, and one draw needn't show every extreme that they name: `routes`: each row names 8 different experts; among the 256 tokens of one device no expert is named more than 136 times. `segment`: ids never fall within a sequence of 1024 tokens. `valid_mask`: at least one token is valid.
All inputs are finite; a program needn't handle non-finite values.
Results may differ from a plain program's by a relative error of at most 0.017.
Values may be sent and summed in bfloat16 or wider, within the bound.
No kernel may reach another device: no remote copies, remote signals or barrier semaphores. Data moves between devices by JAX's collectives and lax.ppermute only.
A program may use at most 448 MiB of HBM per device.

v0:
```python
import jax
import jax.numpy as jnp
from jax import lax
from jax.sharding import PartitionSpec as P

H = 16
HD = 128
FF = 1024
TOP = 8
EXP_DEV = 4


epsilon = 1e-05
masked = -1e30


def rms_norm(values, gain_vec):
    factor = lax.rsqrt(jnp.mean(values * values, axis=-1, keepdims=True) + epsilon)
    return values * factor * gain_vec


def norm_back(values, gain_vec, grad_in):
    factor = lax.rsqrt(jnp.mean(values * values, axis=-1, keepdims=True) + epsilon)
    normed = values * factor
    gain_grad = jnp.sum(grad_in * normed, axis=0)
    inner_term = grad_in * gain_vec
    input_grad = factor * (
        inner_term - normed * jnp.mean(inner_term * normed, axis=-1, keepdims=True)
    )
    return (input_grad, gain_grad)


def rope_tables(positions, head_size):
    inverse = 10000.0 ** (-(jnp.arange(head_size // 2).astype(jnp.float32) * 2.0 / head_size))
    angles = positions.astype(jnp.float32)[:, None] * inverse[None, :]
    cosine = jnp.concatenate([jnp.cos(angles), jnp.cos(angles)], axis=-1)
    sine_table = jnp.concatenate([jnp.sin(angles), jnp.sin(angles)], axis=-1)
    return (cosine[:, None, :], sine_table[:, None, :])


def rotate_half(values):
    half_size = values.shape[-1] // 2
    return jnp.concatenate([-values[..., half_size:], values[..., :half_size]], axis=-1)


def rotate_back(values):
    half_size = values.shape[-1] // 2
    return jnp.concatenate([values[..., half_size:], -values[..., :half_size]], axis=-1)


def block_scores(query, keyed, segment, block_index, block_rows, score_scale):
    row_start = block_index * block_rows
    q_block = lax.dynamic_slice_in_dim(query, row_start, block_rows, 0)
    q_segment = lax.dynamic_slice_in_dim(segment, row_start, block_rows, 0)
    q_places = row_start + jnp.arange(block_rows)
    k_places = jnp.arange(keyed.shape[0])
    allowed = (q_segment[:, None] == segment[None, :]) & (q_places[:, None] >= k_places[None, :])
    scores = (
        jnp.einsum("qhd,khd->hqk", q_block, keyed, preferred_element_type=jnp.float32) * score_scale
    )
    return (q_block, jnp.where(allowed[None], scores, masked))


def attend_forward(query, keyed, valued, segment, block_rows, score_scale):
    blocks = keyed.shape[0] // block_rows

    def one_block(block_index):
        q_block, scores = block_scores(query, keyed, segment, block_index, block_rows, score_scale)
        row_top = jnp.max(scores, axis=-1, keepdims=True)
        exp_scores = jnp.exp(scores - row_top)
        row_total = jnp.sum(exp_scores, axis=-1, keepdims=True)
        weights = (exp_scores / row_total).astype(jnp.bfloat16)
        block_out = jnp.einsum("hqk,khd->qhd", weights, valued, preferred_element_type=jnp.float32)
        return (block_out.astype(jnp.bfloat16), (row_top + jnp.log(row_total))[..., 0])

    outputs, log_total = lax.map(one_block, jnp.arange(blocks))
    return (outputs.reshape(keyed.shape[0], -1), log_total)


def attend_backward(query, keyed, valued, segment, log_total, grad_heads, block_rows, score_scale):
    blocks = keyed.shape[0] // block_rows

    def one_block(carry_in, pieces):
        grad_k, grad_v = carry_in
        block_index, block_total = pieces
        q_block, scores = block_scores(query, keyed, segment, block_index, block_rows, score_scale)
        probs = jnp.exp(scores - block_total[:, :, None])
        grad_block = lax.dynamic_slice_in_dim(grad_heads, block_index * block_rows, block_rows, 0)
        grad_v = grad_v + jnp.einsum(
            "hqk,qhd->khd",
            probs.astype(jnp.bfloat16),
            grad_block,
            preferred_element_type=jnp.float32,
        )
        grad_probs = jnp.einsum(
            "qhd,khd->hqk", grad_block, valued, preferred_element_type=jnp.float32
        )
        inner_term = jnp.sum(probs * grad_probs, axis=-1, keepdims=True)
        grad_scores = (probs * (grad_probs - inner_term)).astype(jnp.bfloat16)
        grad_q = (
            jnp.einsum("hqk,khd->qhd", grad_scores, keyed, preferred_element_type=jnp.float32)
            * score_scale
        )
        grad_k = (
            grad_k
            + jnp.einsum("hqk,qhd->khd", grad_scores, q_block, preferred_element_type=jnp.float32)
            * score_scale
        )
        return ((grad_k, grad_v), grad_q)

    initial = jnp.zeros(keyed.shape, jnp.float32)
    (grad_k, grad_v), grad_q = lax.scan(
        one_block, (initial, initial), (jnp.arange(blocks), log_total)
    )
    return (grad_q.reshape(keyed.shape), grad_k, grad_v)


def shards(
    tokens,
    w_attn,
    norm_gains,
    w_expert,
    gate_weights,
    routes,
    segment,
    valid_mask,
    teacher,
    cotangent,
):
    sp_size = lax.axis_size("sp")
    sp_rank = lax.axis_index("sp")
    tok_rows, model_width = tokens.shape
    seq_len = tok_rows * sp_size
    head_local = H // sp_size
    experts_all = EXP_DEV * sp_size
    capacity = tok_rows * TOP * 17 // (16 * experts_all)
    block_rows = min(512, seq_len)
    score_scale = HD ** (-0.5)
    head_shape = (seq_len, head_local, HD)
    inputs = tokens.astype(jnp.float32)
    full_attn, full_gains = (
        lax.all_gather(w_attn, ("fsdp", "sp"), axis=0, tiled=True),
        lax.all_gather(norm_gains, ("fsdp", "sp"), axis=0, tiled=True),
    )
    experts_full = lax.all_gather(w_expert, "fsdp", axis=0, tiled=True)
    gain_rows = full_gains.astype(jnp.float32)
    normed_in = rms_norm(inputs, gain_rows[:, 0]).astype(jnp.bfloat16)
    projected = jnp.dot(
        normed_in, full_attn[:, : 3 * model_width], preferred_element_type=jnp.float32
    )
    query_raw = projected[:, :model_width]
    key_raw = projected[:, model_width : 2 * model_width]
    value_low = projected[:, 2 * model_width :].astype(jnp.bfloat16)
    positions = sp_rank * tok_rows + jnp.arange(tok_rows)
    cosine, sine_table = rope_tables(positions, HD)
    query_norm = rms_norm(query_raw, gain_rows[:, 2]).reshape(tok_rows, H, HD)
    key_norm = rms_norm(key_raw, gain_rows[:, 3]).reshape(tok_rows, H, HD)
    query_rot = (
        (query_norm * cosine + rotate_half(query_norm) * sine_table)
        .reshape(tok_rows, model_width)
        .astype(jnp.bfloat16)
    )
    key_rot = (
        (key_norm * cosine + rotate_half(key_norm) * sine_table)
        .reshape(tok_rows, model_width)
        .astype(jnp.bfloat16)
    )
    query_heads, key_heads, value_heads = (
        lax.all_to_all(query_rot, "sp", split_axis=1, concat_axis=0, tiled=True),
        lax.all_to_all(key_rot, "sp", split_axis=1, concat_axis=0, tiled=True),
        lax.all_to_all(value_low, "sp", split_axis=1, concat_axis=0, tiled=True),
    )
    query_heads = query_heads.reshape(head_shape)
    key_heads = key_heads.reshape(head_shape)
    value_heads = value_heads.reshape(head_shape)
    attn_heads, log_total = attend_forward(
        query_heads, key_heads, value_heads, segment, block_rows, score_scale
    )
    attn_tokens = lax.all_to_all(attn_heads, "sp", split_axis=0, concat_axis=1, tiled=True)
    attn_out = jnp.einsum(
        "tc,dc->td",
        attn_tokens,
        full_attn[:, 3 * model_width :],
        preferred_element_type=jnp.float32,
    )
    residual = inputs + attn_out
    normed_mid = rms_norm(residual, gain_rows[:, 1]).astype(jnp.bfloat16)
    route_flat = routes.reshape(-1)
    onehot = (route_flat[:, None] == jnp.arange(experts_all)[None, :]).astype(jnp.int32)
    slot_place = jnp.sum(jnp.cumsum(onehot, axis=0) * onehot, axis=-1) - 1
    slot_index = route_flat * capacity + slot_place
    token_of = jnp.arange(tok_rows * TOP) // TOP

    def dispatch(rows_in):
        buffer = (
            jnp.zeros((experts_all * capacity, model_width), jnp.bfloat16)
            .at[slot_index]
            .set(rows_in)
        )
        return buffer.reshape(sp_size, EXP_DEV, capacity, model_width)

    def collect(returned):
        picked = returned.reshape(experts_all * capacity, model_width)[slot_index]
        return picked.reshape(tok_rows, TOP, model_width).astype(jnp.float32)

    received = lax.all_to_all(
        dispatch(normed_mid[token_of]), "sp", split_axis=0, concat_axis=2, tiled=True
    )[0]
    gate_up = jnp.einsum(
        "erd,def->erf", received, experts_full[:, :, : 2 * FF], preferred_element_type=jnp.float32
    )
    activated = (jax.nn.silu(gate_up[..., :FF]) * gate_up[..., FF:]).astype(jnp.bfloat16)
    expert_out = jnp.einsum(
        "erf,def->erd", activated, experts_full[:, :, 2 * FF :], preferred_element_type=jnp.float32
    ).astype(jnp.bfloat16)
    returned = lax.all_to_all(expert_out[None], "sp", split_axis=2, concat_axis=0, tiled=True)
    expert_sum = jnp.sum(gate_weights[:, :, None] * collect(returned), axis=1)
    final_out = residual + expert_sum
    valid_f = valid_mask.astype(jnp.float32)
    difference = final_out - teacher.astype(jnp.float32)
    total_sq, total_count = lax.psum(
        (jnp.sum(valid_f[:, None] * difference * difference), jnp.sum(valid_f)), ("fsdp", "sp")
    )
    loss_value = total_sq / (total_count * model_width)
    grad_out = (
        cotangent.astype(jnp.float32)
        + 2.0 / (total_count * model_width) * valid_f[:, None] * difference
    )
    back_attn, back_gains = (
        lax.all_gather(w_attn, ("fsdp", "sp"), axis=0, tiled=True),
        lax.all_gather(norm_gains, ("fsdp", "sp"), axis=0, tiled=True),
    )
    back_experts = lax.all_gather(w_expert, "fsdp", axis=0, tiled=True)
    moe_low = grad_out.astype(jnp.bfloat16)
    slot_grad = (
        (gate_weights[:, :, None] * moe_low[:, None, :])
        .astype(jnp.bfloat16)
        .reshape(tok_rows * TOP, model_width)
    )
    grad_received = lax.all_to_all(
        dispatch(slot_grad), "sp", split_axis=0, concat_axis=2, tiled=True
    )[0]
    grad_act = jnp.einsum(
        "erd,def->erf",
        grad_received,
        back_experts[:, :, 2 * FF :],
        preferred_element_type=jnp.float32,
    )
    gate_pre = gate_up[..., :FF]
    up_pre = gate_up[..., FF:]
    sigmoid_val = jax.nn.sigmoid(gate_pre)
    grad_gate = grad_act * up_pre * sigmoid_val * (1.0 + gate_pre * (1.0 - sigmoid_val))
    grad_up = grad_act * gate_pre * sigmoid_val
    grad_gate_up = jnp.concatenate([grad_gate, grad_up], axis=-1).astype(jnp.bfloat16)
    upper = jnp.einsum("erd,erf->def", received, grad_gate_up, preferred_element_type=jnp.float32)
    lower = jnp.einsum("erd,erf->def", grad_received, activated, preferred_element_type=jnp.float32)
    grad_expert = lax.psum_scatter(
        jnp.concatenate([upper, lower], axis=-1).astype(jnp.bfloat16),
        "fsdp",
        scatter_dimension=0,
        tiled=True,
    ).astype(jnp.float32)
    grad_rows = jnp.einsum(
        "erf,def->erd",
        grad_gate_up,
        back_experts[:, :, : 2 * FF],
        preferred_element_type=jnp.float32,
    ).astype(jnp.bfloat16)
    grad_back = lax.all_to_all(grad_rows[None], "sp", split_axis=2, concat_axis=0, tiled=True)
    grad_mid = jnp.sum(collect(grad_back), axis=1)
    grad_resid_norm, gain_ffn_grad = norm_back(residual, gain_rows[:, 1], grad_mid)
    grad_resid = grad_out + grad_resid_norm
    attn_grad_low = grad_resid.astype(jnp.bfloat16)
    out_weight_grad = jnp.einsum(
        "td,tc->dc", attn_grad_low, attn_tokens, preferred_element_type=jnp.float32
    )
    grad_attn_tok = jnp.einsum(
        "td,dc->tc",
        attn_grad_low,
        back_attn[:, 3 * model_width :],
        preferred_element_type=jnp.float32,
    ).astype(jnp.bfloat16)
    grad_heads = lax.all_to_all(
        grad_attn_tok, "sp", split_axis=1, concat_axis=0, tiled=True
    ).reshape(head_shape)
    grad_q, grad_k, grad_v = attend_backward(
        query_heads, key_heads, value_heads, segment, log_total, grad_heads, block_rows, score_scale
    )
    grad_q_tok, grad_k_tok, grad_v_tok = (
        lax.all_to_all(
            grad_q.reshape(seq_len, -1).astype(jnp.bfloat16),
            "sp",
            split_axis=0,
            concat_axis=1,
            tiled=True,
        ),
        lax.all_to_all(
            grad_k.reshape(seq_len, -1).astype(jnp.bfloat16),
            "sp",
            split_axis=0,
            concat_axis=1,
            tiled=True,
        ),
        lax.all_to_all(
            grad_v.reshape(seq_len, -1).astype(jnp.bfloat16),
            "sp",
            split_axis=0,
            concat_axis=1,
            tiled=True,
        ),
    )

    def unrotate(grad_low):
        grad_cube = grad_low.astype(jnp.float32).reshape(tok_rows, H, HD)
        return (grad_cube * cosine + rotate_back(grad_cube * sine_table)).reshape(
            tok_rows, model_width
        )

    grad_q_raw, gain_q_grad = norm_back(query_raw, gain_rows[:, 2], unrotate(grad_q_tok))
    grad_k_raw, gain_k_grad = norm_back(key_raw, gain_rows[:, 3], unrotate(grad_k_tok))
    grad_proj = jnp.concatenate(
        [grad_q_raw.astype(jnp.bfloat16), grad_k_raw.astype(jnp.bfloat16), grad_v_tok], axis=1
    )
    proj_weight_grad = jnp.einsum(
        "td,tc->dc", normed_in, grad_proj, preferred_element_type=jnp.float32
    )
    grad_normed = jnp.einsum(
        "tc,dc->td", grad_proj, back_attn[:, : 3 * model_width], preferred_element_type=jnp.float32
    )
    grad_in_norm, gain_attn_grad = norm_back(
        inputs, back_gains[:, 0].astype(jnp.float32), grad_normed
    )
    grad_tokens = grad_resid + grad_in_norm
    weight_term = jnp.concatenate([proj_weight_grad, out_weight_grad], axis=1)
    gain_term = jnp.stack([gain_attn_grad, gain_ffn_grad, gain_q_grad, gain_k_grad], axis=1)
    grad_attn, grad_gains = (
        lax.psum_scatter(weight_term, ("fsdp", "sp"), scatter_dimension=0, tiled=True),
        lax.psum_scatter(gain_term, ("fsdp", "sp"), scatter_dimension=0, tiled=True),
    )
    return (
        final_out.astype(jnp.bfloat16),
        loss_value,
        grad_tokens,
        grad_attn,
        grad_gains,
        grad_expert,
    )


def solution(mesh):
    return jax.shard_map(
        shards,
        mesh=mesh,
        in_specs=(
            P(("fsdp", "sp"), None),
            P(("fsdp", "sp"), None),
            P(("fsdp", "sp"), None),
            P("fsdp", "sp", None),
            P(("fsdp", "sp"), None),
            P(("fsdp", "sp"), None),
            P("fsdp"),
            P(("fsdp", "sp")),
            P(("fsdp", "sp"), None),
            P(("fsdp", "sp"), None),
        ),
        out_specs=(
            P(("fsdp", "sp"), None),
            P(),
            P(("fsdp", "sp"), None),
            P(("fsdp", "sp"), None),
            P(("fsdp", "sp"), None),
            P("fsdp", "sp", None),
        ),
        check_vma=False,
    )
```

profile of v0, /device:TPU:0, one launch (start us, length us, event | category | flops | bytes accessed | tf_op | source)
XLA Modules:
  0.0 3494.7 jit_solution(6095966174428246448)
XLA Ops:
  16.1 70.9 %all-gather = bf16[32,64,4]{1,2,0:T(4,128)(2,1)S(1)} all-gather(bf16[1,64,4]{1,2,0:T(4,128)(2,1)S(1)} %bitcast.259), channel_id=1, replica_groups=mesh['fsdp'=8,'sp'=4] {'fsdp','sp'}, dimensions={0}, use_global_device_ids=true | all-gather | bytes 16896 | tf_op jit(solution)/shard_map/all_gather | solution.py:143
  87.9 120.8 %all-gather.4.cloned.1.call-done = bf16[2048,8192]{1,0:T(8,128)(2,1)} async-done(((bf16[64,8192]{1,0:T(8,128)(2,1)}), bf16[2048,8192]{1,0:T(8,128)(2,1)}) %all-gather.4.cloned.1.call-update) | async-done | bytes 33554448 | tf_op jit(solution)/shard_map/all_gather | solution.py:142
  208.7 13.2 fusion.39
  299.3 21.4 while.27
  328.0 13.0 all-to-all-done.3
  351.7 44.6 %scatter_custom_fusion = bf16[2176,2048]{1,0:T(8,128)(2,1)} fusion(s32[2048]{0:T(1024)S(1)} %bitcast.252, bf16[256,2048]{1,0:T(8,128)(2,1)S(1)} %multiply_convert_fusion.6, s32[2048]{0:T(1024)S(1)} %broadcast_clamp_fusion.1, bf16[]{:T(256)} %constant.76.clone.1), kind=kCustom, calls=%fused_computation.81 | custom fusion | bytes 8912898 | tf_op jit(solution)/shard_map/scatter | solution.py:198
  396.3 105.8 %all_to_all.179 = bf16[4,4,136,2048]{3,2,1,0:T(8,128)(2,1)} all-to-all(bf16[4,4,136,2048]{3,2,1,0:T(8,128)(2,1)} %bitcast.208), channel_id=1, replica_groups=mesh['fsdp'=8,'sp'=4] {'sp'}, dimensions={0} | all-to-all | bytes 17825792 | tf_op jit(solution)/shard_map/all_to_all | solution.py:206
  511.0 123.9 %all-gather.6.cloned.1.call-done = bf16[2048,4,3072]{2,0,1:T(8,128)(2,1)} async-done(((bf16[256,4,3072]{2,0,1:T(8,128)(2,1)}), bf16[2048,4,3072]{2,0,1:T(8,128)(2,1)}) %all-gather.6.cloned.1.call-update) | async-done | bytes 50331664 | tf_op jit(solution)/shard_map/all_gather | solution.py:145
  634.9 27.5 fusion.35
  671.5 16.5 convert_bitcast_fusion.3
  688.0 29.8 copy.125
  724.3 130.3 %psum.15 = f32[]{:T(128)} all-reduce(f32[]{:T(128)} %convert_reduce_fusion.1), channel_id=1, replica_groups=mesh['fsdp'=8,'sp'=4] {'fsdp','sp'}, use_global_device_ids=true, to_apply=%region_16.17 | all-reduce | flops 1 | bytes 8 | tf_op jit(solution)/shard_map/psum | solution.py:221
  867.5 21.1 gather_fusion
  888.7 12.6 fusion.41
  905.2 18.6 scatter_custom_fusion.1
  923.9 106.1 %all_to_all.180 = bf16[4,4,136,2048]{3,2,1,0:T(8,128)(2,1)} all-to-all(bf16[4,4,136,2048]{3,2,1,0:T(8,128)(2,1)} %bitcast.207), channel_id=1, replica_groups=mesh['fsdp'=8,'sp'=4] {'sp'}, dimensions={0} | all-to-all | bytes 17825792 | tf_op jit(solution)/shard_map/all_to_all | solution.py:240
  1038.9 22.1 multiply_convert_fusion.2
  1060.9 26.2 convert_bitcast_fusion.2
  1087.2 29.5 copy.129
  1122.9 96.0 %all-to-all-done.7 = bf16[1,4,544,2048]{3,1,0,2:T(4,128)(2,1)} async-done(((bf16[1,4,544,2048]{3,1,0,2:T(4,128)(2,1)}), bf16[1,4,544,2048]{3,1,0,2:T(4,128)(2,1)}, u32[]{:S(2)}, u32[]{:S(2)}) %all-to-all-start.7) | async-done | bytes 8912928 | tf_op jit(solution)/shard_map/all_to_all | solution.py:269
  1230.9 21.2 gather_fusion.1
  1282.0 13.1 all-to-all-done.8
  1297.4 34.1 while.28
  1354.7 33.3 convert_bitcast_fusion
  1395.6 21.1 convert_bitcast_fusion.1
  1448.0 14.2 fusion.77
  1463.6 43.6 %pad_maximum_fusion.1 = bf16[2048,4,3072]{0,2,1:T(8,128)(2,1)} fusion(bf16[2048,4,1024]{0,2,1:T(8,128)(2,1)} %convert_bitcast_fusion.1, bf16[2048,4,2048]{0,2,1:T(8,128)(2,1)} %convert_bitcast_fusion), kind=kLoop, calls=%fused_computation.53 | loop fusion | flops 100663296 | bytes 100663296 | tf_op jit(solution)/shard_map/concatenate | solution.py:258
  1518.2 21.4 fusion.88
  1539.7 43.5 %pad_maximum_fusion = f32[2048,8192]{1,0:T(8,128)} fusion(f32[2048,2048]{1,0:T(8,128)} %fusion.89, f32[2048,6144]{1,0:T(8,128)} %fusion.88), kind=kLoop, calls=%fused_computation.52 | loop fusion | flops 16777216 | bytes 134217728 | tf_op jit(solution)/shard_map/concatenate | solution.py:334
  1583.2 40.9 %psum.14 = f32[]{:T(128)} all-reduce(f32[]{:T(128)} %get-tuple-element.242), channel_id=1, replica_groups=mesh['fsdp'=8,'sp'=4] {'fsdp','sp'}, use_global_device_ids=true, to_apply=%region_14.15 | all-reduce | flops 1 | bytes 8 | tf_op jit(solution)/shard_map/psum | solution.py:221
  1629.6 451.7 %reduce-scatter.8.cloned.1.call-done = bf16[256,4,3072]{0,2,1:T(8,128)(2,1)} async-done(((bf16[2048,4,3072]{0,2,1:T(8,128)(2,1)}), bf16[256,4,3072]{0,2,1:T(8,128)(2,1)}) %reduce-scatter.8.cloned.1.call-update) | async-done | bytes 6291472 | tf_op jit(solution)/shard_map/reduce_scatter | solution.py:257
  2093.4 1393.4 %reduce-scatter.6.cloned.1.call-done = f32[64,8192]{1,0:T(8,128)} async-done(((f32[2048,8192]{1,0:T(8,128)}), f32[64,8192]{1,0:T(8,128)}) %reduce-scatter.6.cloned.1.call-update) | async-done | bytes 2097168 | tf_op jit(solution)/shard_map/reduce_scatter | solution.py:337
  (313 shorter events, 348.2 us)
Async XLA Ops:
  7.2 201.5 %all-gather.4.cloned.1.call-start = ((), (), s32[]{:S(2)}) async-start(), calls=%async_computation.15 | async-start | bytes 34603008 | tf_op jit(solution)/shard_map/all_gather | solution.py:142
  7.9 627.0 %all-gather.6.cloned.1.call-start = ((), (), s32[]{:S(2)}) async-start(), calls=%async_computation.16 | async-start | bytes 56623104 | tf_op jit(solution)/shard_map/all_gather | solution.py:145
  15.4 72.1 %copy-start.14 = (bf16[256,2048]{1,0:T(8,128)(2,1)S(1)}, bf16[256,2048]{1,0:T(8,128)(2,1)}, u32[]{:S(2)}) copy-start(bf16[256,2048]{1,0:T(8,128)(2,1)} %param.14) | copy-start | bytes 3145732
  87.0 134.9 %copy-start.31 = (bf16[2048,4]{0,1:T(4,128)(2,1)}, bf16[2048,4]{0,1:T(4,128)(2,1)S(1)}, u32[]{:S(2)}) copy-start(bf16[2048,4]{0,1:T(4,128)(2,1)S(1)} %reshape.487) | copy-start | bytes 49156
  87.4 157.8 %copy-start.21 = (f32[256,128]{0,1:T(8,128)}, f32[256,128]{0,1:T(8,128)S(1)}, u32[]{:S(2)}) copy-start(f32[256,128]{0,1:T(8,128)S(1)} %get-tuple-element.325) | copy-start | bytes 393220
  87.8 134.1 %copy-start.41 = (f32[256]{0:T(256)}, f32[256]{0:T(256)S(1)}, u32[]{:S(2)}) copy-start(f32[256]{0:T(256)S(1)} %add_rsqrt_fusion.3) | copy-start | bytes 3076
  87.9 134.1 %copy-start.29 = (f32[2048,1]{0,1:T(1,128)}, f32[2048,1]{0,1:T(1,128)S(1)}, u32[]{:S(2)}) copy-start(f32[2048,1]{0,1:T(1,128)S(1)} %get-tuple-element.316) | copy-start | bytes 24580
  87.9 146.1 %copy-start.33 = (f32[2048,1]{0,1:T(1,128)}, f32[2048,1]{0,1:T(1,128)S(1)}, u32[]{:S(2)}) copy-start(f32[2048,1]{0,1:T(1,128)S(1)} %get-tuple-element.314) | copy-start | bytes 24580
  87.9 146.1 %copy-start.35 = (f32[2048,1]{0,1:T(1,128)}, f32[2048,1]{0,1:T(1,128)S(1)}, u32[]{:S(2)}) copy-start(f32[2048,1]{0,1:T(1,128)S(1)} %get-tuple-element.315) | copy-start | bytes 24580
  87.9 262.3 %copy-start.37 = (f32[2048,1]{0,1:T(1,128)}, f32[2048,1]{0,1:T(1,128)S(1)}, u32[]{:S(2)}) copy-start(f32[2048,1]{0,1:T(1,128)S(1)} %get-tuple-element.313) | copy-start | bytes 24580
  226.7 33.1 all-to-all-start.2
  259.8 17.8 all-to-all-start
  277.6 18.0 all-to-all-start.1
  320.6 29.4 copy-start
  320.6 29.4 copy-start.2
  320.6 29.4 copy-start.5
  320.7 29.4 copy-start.39
  323.6 17.4 all-to-all-start.3
  350.1 46.2 %copy-start.45 = (f32[256]{0:T(256)}, f32[256]{0:T(256)S(1)}, u32[]{:S(2)}) copy-start(f32[256]{0:T(256)S(1)} %add_rsqrt_fusion) | copy-start | bytes 3076
  717.9 136.7 %copy-start.51 = (f32[256,8]{0,1:T(8,128)S(1)}, f32[256,8]{0,1:T(8,128)}, u32[]{:S(2)}) copy-start(f32[256,8]{0,1:T(8,128)} %param.18) | copy-start | bytes 24580
  717.9 137.7 %all-to-all-start.5 = ((bf16[1,4,544,2048]{3,1,0,2:T(4,128)(2,1)}), bf16[1,4,544,2048]{3,1,0,2:T(4,128)(2,1)}, u32[]{:S(2)}, u32[]{:S(2)}) async-start(bf16[1,4,544,2048]{3,1,0,2:T(4,128)(2,1)} %copy.125), calls=%async_computation.5 | async-start | bytes 17825792 | tf_op jit(solution)/shard_map/all_to_all | solution.py:216
  1116.6 102.3 %all-to-all-start.7 = ((bf16[1,4,544,2048]{3,1,0,2:T(4,128)(2,1)}), bf16[1,4,544,2048]{3,1,0,2:T(4,128)(2,1)}, u32[]{:S(2)}, u32[]{:S(2)}) async-start(bf16[1,4,544,2048]{3,1,0,2:T(4,128)(2,1)} %copy.129), calls=%async_computation.7 | async-start | bytes 17825792 | tf_op jit(solution)/shard_map/all_to_all | solution.py:269
  1276.4 20.9 copy-start.1
  1276.4 20.9 copy-start.28
  1276.4 20.9 copy-start.40
  1277.5 17.6 all-to-all-start.8
  1334.2 16.6 all-to-all-start.10
  1350.8 40.5 %all-to-all-start.11 = ((bf16[4,256,512]{2,1,0:T(8,128)(2,1)}), bf16[4,256,512]{2,1,0:T(8,128)(2,1)S(1)}, u32[]{:S(2)}, u32[]{:S(2)}) async-start(bf16[4,256,512]{2,1,0:T(8,128)(2,1)} %copy.156), calls=%async_computation.11 | async-start | bytes 2097152 | tf_op jit(solution)/shard_map/all_to_all | solution.py:304
  1391.3 30.1 all-to-all-start.9
  1395.5 232.7 %reduce-scatter.10.cloned.1.call-start = ((), (), s32[]{:S(2)}) async-start(), calls=%async_computation.19 | async-start | bytes 1081344
  1463.6 617.7 %reduce-scatter.8.cloned.1.call-start = ((), (), s32[]{:S(2)}) async-start(), calls=%async_computation.18 | async-start | bytes 56623104 | tf_op jit(solution)/shard_map/reduce_scatter | solution.py:257
  1507.3 1979.5 %reduce-scatter.6.cloned.1.call-start = ((), (), s32[]{:S(2)}) async-start(), calls=%async_computation.17 | async-start | bytes 69206016 | tf_op jit(solution)/shard_map/reduce_scatter | solution.py:337
  (47 other events, 226.3 us)
Sparse Core Ops, SparseCore 0:
  10.9 197.7 all-gather.3
  210.3 424.5 all-gather.5
  1463.7 135.3 reduce-scatter.9
  1601.4 479.8 reduce-scatter.7
  2084.1 1402.6 reduce-scatter.5
where the time goes:
time: 3510 us; the launch traced here: 3490 us
  waiting for transfers between devices  2240 us (64%)
  blocking collectives  454 us (13%)
  local copies, waits for them, and re-layouts  278 us (8%)
  matrix products  251 us (7%)
  other arithmetic  208 us (6%)
  starting transfers between devices  45.9 us (1%)
    reduce_scatter x1, waiting for transfers between devices, shards(): lax.psum_scatter(weight_term, ('fsdp', 'sp'), scatter_dimension=0, tiled=...  1390 us
    reduce_scatter x1, waiting for transfers between devices, shards(): lax.psum_scatter(jnp.concatenate([upper, lower], axis=-1).astype(jnp.bflo...  452 us
    psum x2, blocking collectives, shards(): lax.psum((jnp.sum(valid_f[:, None] * difference * difference), jnp.sum(va...  171 us
    all_gather x1, waiting for transfers between devices, shards(): experts_full = lax.all_gather(w_expert, 'fsdp', axis=0, tiled=True)  124 us
    all_gather x1, waiting for transfers between devices, shards(): lax.all_gather(w_attn, ('fsdp', 'sp'), axis=0, tiled=True)  121 us
    all_to_all x1, blocking collectives, shards(): lax.all_to_all(dispatch(slot_grad), 'sp', split_axis=0, concat_axis=2, ti...  106 us
    all_to_all x1, blocking collectives, shards(): lax.all_to_all(dispatch(normed_mid[token_of]), 'sp', split_axis=0, concat...  106 us
    all_to_all x1, waiting for transfers between devices, shards(): lax.all_to_all(grad_rows[None], 'sp', split_axis=2, concat_axis=0, tiled=...  96 us
  transfers between devices with their start and end apart: 15, of which 10 were waited for; matrix products, arithmetic and copies ran while one was open for 10% of the time, Pallas kernels for 0%

commit v1 on v0

v1 whole, which is shorter than its diff:
```python
import jax
import jax.numpy as jnp
from jax import lax
from jax.sharding import Mesh, PartitionSpec as P

H = 16
HD = 128
TOP = 8
CORES = 2
PAD = 128

epsilon = 1e-05
masked = -1e30
f32 = jnp.float32
bf16 = jnp.bfloat16


def swap(pieces, axis):
    if pieces.shape[0] == 1:
        return pieces
    return lax.all_to_all(pieces, axis, split_axis=0, concat_axis=0, tiled=True)


def collect(block, axis):
    size = lax.axis_size(axis)
    return swap(jnp.broadcast_to(block[None], (size,) + block.shape), axis)


def rms_factor(values):
    return lax.rsqrt(jnp.mean(values * values, axis=-1, keepdims=True) + epsilon)


def norm_back(values, gain_vec, grad_in):
    factor = rms_factor(values)
    normed = values * factor
    gain_grad = jnp.sum(grad_in * normed, axis=0)
    inner = grad_in * gain_vec
    grad = factor * (inner - normed * jnp.mean(inner * normed, axis=-1, keepdims=True))
    return grad, gain_grad


def rope_tables(rows):
    inverse = 10000.0 ** (-(jnp.arange(HD // 2).astype(f32) * 2.0 / HD))
    angles = jnp.arange(rows).astype(f32)[:, None] * inverse[None, :]
    cosine = jnp.concatenate([jnp.cos(angles), jnp.cos(angles)], axis=-1)
    sine = jnp.concatenate([jnp.sin(angles), jnp.sin(angles)], axis=-1)
    return cosine[:, None, :], sine[:, None, :]


def rotate_half(values):
    half = values.shape[-1] // 2
    return jnp.concatenate([-values[..., half:], values[..., :half]], axis=-1)


def rotate_back(values):
    half = values.shape[-1] // 2
    return jnp.concatenate([values[..., half:], -values[..., :half]], axis=-1)


def block_scores(query, keyed, segment, block_index, rows, scale):
    start = block_index * rows
    q_block = lax.dynamic_slice_in_dim(query, start, rows, 0)
    q_segment = lax.dynamic_slice_in_dim(segment, start, rows, 0)
    q_places = start + jnp.arange(rows)
    k_places = jnp.arange(keyed.shape[0])
    allowed = (q_segment[:, None] == segment[None, :]) & (q_places[:, None] >= k_places[None, :])
    scores = jnp.einsum("qhd,khd->hqk", q_block, keyed, preferred_element_type=f32) * scale
    return q_block, jnp.where(allowed[None], scores, masked)


def attend_forward(query, keyed, valued, segment, rows, scale):
    blocks = keyed.shape[0] // rows

    def one_block(block_index):
        q_block, scores = block_scores(query, keyed, segment, block_index, rows, scale)
        row_top = jnp.max(scores, axis=-1, keepdims=True)
        exp_scores = jnp.exp(scores - row_top)
        row_total = jnp.sum(exp_scores, axis=-1, keepdims=True)
        weights = (exp_scores / row_total).astype(bf16)
        out = jnp.einsum("hqk,khd->qhd", weights, valued, preferred_element_type=f32)
        return out.astype(bf16), (row_top + jnp.log(row_total))[..., 0]

    outputs, log_total = lax.map(one_block, jnp.arange(blocks))
    return outputs.reshape(keyed.shape[0], -1), log_total


def attend_backward(query, keyed, valued, segment, log_total, grad_heads, rows, scale):
    blocks = keyed.shape[0] // rows

    def one_block(carry, pieces):
        grad_k, grad_v = carry
        block_index, block_total = pieces
        q_block, scores = block_scores(query, keyed, segment, block_index, rows, scale)
        probs = jnp.exp(scores - block_total[:, :, None])
        grad_block = lax.dynamic_slice_in_dim(grad_heads, block_index * rows, rows, 0)
        grad_v = grad_v + jnp.einsum(
            "hqk,qhd->khd", probs.astype(bf16), grad_block, preferred_element_type=f32
        )
        grad_probs = jnp.einsum("qhd,khd->hqk", grad_block, valued, preferred_element_type=f32)
        inner = jnp.sum(probs * grad_probs, axis=-1, keepdims=True)
        grad_scores = (probs * (grad_probs - inner)).astype(bf16)
        grad_q = jnp.einsum("hqk,khd->qhd", grad_scores, keyed, preferred_element_type=f32) * scale
        grad_k = (
            grad_k
            + jnp.einsum("hqk,qhd->khd", grad_scores, q_block, preferred_element_type=f32) * scale
        )
        return (grad_k, grad_v), grad_q

    initial = jnp.zeros(keyed.shape, f32)
    (grad_k, grad_v), grad_q = lax.scan(
        one_block, (initial, initial), (jnp.arange(blocks), log_total)
    )
    return grad_q.reshape(keyed.shape), grad_k, grad_v


def dot(spec, left, right):
    return jnp.einsum(spec, left, right, preferred_element_type=f32)


def shards(
    tokens,
    w_attn,
    norm_gains,
    w_expert,
    gate_weights,
    routes,
    segment,
    valid_mask,
    teacher,
    cotangent,
):
    outer, planes, seqs = lax.axis_size("o"), lax.axis_size("z"), lax.axis_size("s")
    plane, rank = lax.axis_index("z"), lax.axis_index("s")
    own, width = tokens.shape
    rows_dev = w_attn.shape[0]
    seq = own * seqs
    heads = H // seqs
    cols = heads * HD
    hidden = w_expert.shape[2] // 3
    part = w_expert.shape[0]
    capacity = own * TOP * 17 // (16 * planes * seqs)
    scale = HD ** (-0.5)
    block_rows = min(512, seq)

    def to_inner(v):
        lead = v.shape[:-1]
        v = v.reshape(lead + (outer, planes, CORES, part))
        return jnp.swapaxes(v, -3, -2).reshape(lead + (width,))

    def to_outer(v):
        lead = v.shape[:-1]
        v = v.reshape(lead + (outer, CORES, planes, part))
        return jnp.swapaxes(v, -3, -2).reshape(lead + (width,))

    def gather_rows(block):
        return collect(collect(collect(block, "z"), "c"), "o").reshape((-1,) + block.shape[1:])

    count = jnp.sum(valid_mask).astype(jnp.int32)
    digits = jnp.stack([count // 128, count % 128]).astype(bf16)
    extra = jnp.concatenate(
        [
            norm_gains,
            jnp.broadcast_to(digits[None], (rows_dev, 2)),
            jnp.zeros((rows_dev, PAD - 6), bf16),
        ],
        axis=1,
    )
    packed = jnp.concatenate(
        [
            w_attn.reshape(rows_dev, 4, seqs, cols).transpose(2, 0, 1, 3).reshape(
                seqs, rows_dev, 4 * cols
            ),
            jnp.broadcast_to(extra[None], (seqs, rows_dev, PAD)),
        ],
        axis=2,
    )
    mine = swap(packed, "s").reshape(part, 4 * cols + PAD)
    weights = gather_rows(mine)
    w_qkv = weights[:, : 3 * cols]
    w_out = weights[:, 3 * cols : 4 * cols]
    side = weights[:, 4 * cols : 4 * cols + 6].astype(f32).T
    gain_in, gain_mid = side[0], side[1]
    gain_q = lax.dynamic_slice_in_dim(to_outer(side[2]), rank * cols, cols, 0)
    gain_k = lax.dynamic_slice_in_dim(to_outer(side[3]), rank * cols, cols, 0)
    total_count = jnp.sum(side[4, ::rows_dev]) * 128.0 + jnp.sum(side[5, ::rows_dev])

    expert_parts = []
    for i in range(3):
        chunk = w_expert[:, :, i * hidden : (i + 1) * hidden].transpose(1, 0, 2)
        chunk = swap(chunk, "z").reshape(planes * part, hidden)
        chunk = lax.all_gather(chunk, ("s", "o", "c"), axis=0, tiled=True)
        expert_parts.append(chunk.reshape(seqs, width, hidden))
    w_gate, w_up, w_down = expert_parts

    routed = collect(
        jnp.concatenate([routes.astype(f32), gate_weights.astype(f32)], axis=1), "z"
    )
    route_all, gate_all = routed[..., :TOP].astype(jnp.int32), routed[..., TOP:]
    expert_ids = jnp.arange(seqs) * planes + plane
    match = route_all[:, :, None, :] == expert_ids[None, None, :, None]
    used = jnp.any(match, axis=-1)
    gate_of = jnp.sum(jnp.where(match, gate_all[:, :, None, :], 0.0), axis=-1)
    before = (jnp.arange(own)[:, None] > jnp.arange(own)[None, :]).astype(bf16)
    place = dot("tu,buk->btk", before, used.astype(bf16)).astype(jnp.int32)
    place = jnp.where(used, place, -1)
    taken = place.transpose(0, 2, 1)[:, :, None, :] == jnp.arange(capacity)[None, None, :, None]
    choose = taken.astype(bf16)
    gate_slot = jnp.sum(jnp.where(taken, gate_of.transpose(0, 2, 1)[:, :, None, :], 0.0), axis=-1)
    gate_slot = gate_slot.transpose(1, 0, 2).reshape(seqs, planes * capacity, 1)

    def dispatch(rows_in):
        spread = dot("bkjt,btd->kbjd", choose, rows_in)
        return spread.reshape(seqs, planes * capacity, width)

    def combine(rows_out):
        rows_out = rows_out.reshape(seqs, planes, capacity, width)
        partial = dot("bkjt,kbjd->btd", choose, rows_out).astype(bf16)
        return jnp.sum(swap(partial, "z").astype(f32), axis=0)

    inputs = to_inner(tokens)
    seq_tokens = to_inner(collect(tokens, "s").reshape(seq, width)).astype(f32)
    normed_in = (seq_tokens * rms_factor(seq_tokens) * gain_in).astype(bf16)
    inputs = inputs.astype(f32)
    projected = jnp.dot(normed_in, w_qkv, preferred_element_type=f32)
    query_raw = projected[:, :cols]
    key_raw = projected[:, cols : 2 * cols]
    valued = projected[:, 2 * cols :].astype(bf16).reshape(seq, heads, HD)

    def over_heads(first, second):
        pair = jnp.stack([jnp.sum(first, axis=-1), jnp.sum(second, axis=-1)])
        pair = jnp.sum(collect(pair, "s"), axis=0) / width
        return pair[0][:, None], pair[1][:, None]

    q_mean, k_mean = over_heads(query_raw * query_raw, key_raw * key_raw)
    q_factor, k_factor = lax.rsqrt(q_mean + epsilon), lax.rsqrt(k_mean + epsilon)
    cosine, sine = rope_tables(seq)

    def rope(raw, factor, gain):
        cube = (raw * factor * gain).reshape(seq, heads, HD)
        return (cube * cosine + rotate_half(cube) * sine).astype(bf16)

    query, keyed = rope(query_raw, q_factor, gain_q), rope(key_raw, k_factor, gain_k)
    attended, log_total = attend_forward(query, keyed, valued, segment, block_rows, scale)
    attn_out = dot("tc,dc->td", attended, w_out).astype(bf16)
    attn_out = jnp.sum(swap(attn_out.reshape(seqs, own, width), "s").astype(f32), axis=0)
    residual = inputs + attn_out

    normed_mid = (residual * rms_factor(residual) * gain_mid).astype(bf16)
    rows_in = dispatch(collect(normed_mid, "z")).astype(bf16)
    gate_pre = dot("krd,kdf->krf", rows_in, w_gate)
    up_pre = dot("krd,kdf->krf", rows_in, w_up)
    activated = (jax.nn.silu(gate_pre) * up_pre).astype(bf16)
    expert_out = (dot("krf,kdf->krd", activated, w_down) * gate_slot).astype(bf16)
    final_out = residual + combine(expert_out)

    valid_f = valid_mask.astype(f32)[:, None]
    difference = final_out - to_inner(teacher).astype(f32)
    squared = jnp.sum(valid_f * difference * difference)
    for axis in ("z", "s", "c", "o"):
        squared = jnp.sum(collect(jnp.broadcast_to(squared, (1, PAD)), axis)[:, 0, 0])
    loss_value = squared / (total_count * width)
    grad_out = (
        to_inner(cotangent).astype(f32) + 2.0 / (total_count * width) * valid_f * difference
    )

    grad_rows = dispatch(collect(grad_out.astype(bf16), "z"))
    grad_rows = (grad_rows * gate_slot).astype(bf16)

    def scatter_expert(grad):
        grad = grad.astype(bf16).reshape(seqs * width, hidden)
        grad = lax.psum_scatter(grad, ("s", "o", "c"), scatter_dimension=0, tiled=True)
        return swap(grad.reshape(planes, part, hidden), "z").astype(f32).transpose(1, 0, 2)

    grad_down = scatter_expert(dot("krd,krf->kdf", grad_rows, activated))
    grad_act = dot("krd,kdf->krf", grad_rows, w_down)
    sigmoid = jax.nn.sigmoid(gate_pre)
    grad_gate = (grad_act * up_pre * sigmoid * (1.0 + gate_pre * (1.0 - sigmoid))).astype(bf16)
    grad_up = (grad_act * gate_pre * sigmoid).astype(bf16)
    back_rows = dot("krf,kdf->krd", grad_gate, w_gate) + dot("krf,kdf->krd", grad_up, w_up)
    grad_mid = combine(back_rows.astype(bf16))
    grad_w_gate = scatter_expert(dot("krd,krf->kdf", rows_in, grad_gate))
    grad_w_up = scatter_expert(dot("krd,krf->kdf", rows_in, grad_up))
    grad_expert = jnp.concatenate([grad_w_gate, grad_w_up, grad_down], axis=2)

    grad_resid_norm, gain_mid_grad = norm_back(residual, gain_mid, grad_mid)
    grad_resid = grad_out + grad_resid_norm

    grad_attn_out = collect(grad_resid.astype(bf16), "s").reshape(seq, width)
    grad_w_out = dot("td,tc->dc", grad_attn_out, attended)
    grad_heads = jnp.dot(grad_attn_out, w_out, preferred_element_type=f32).astype(bf16)
    grad_q, grad_k, grad_v = attend_backward(
        query,
        keyed,
        valued,
        segment,
        log_total,
        grad_heads.reshape(seq, heads, HD),
        block_rows,
        scale,
    )

    def unrotate(grad):
        grad = grad.astype(bf16).astype(f32)
        return (grad * cosine + rotate_back(grad * sine)).reshape(seq, cols)

    grad_q, grad_k = unrotate(grad_q), unrotate(grad_k)
    q_normed, k_normed = query_raw * q_factor, key_raw * k_factor
    gain_q_grad = jnp.sum(grad_q * q_normed, axis=0)
    gain_k_grad = jnp.sum(grad_k * k_normed, axis=0)
    grad_q, grad_k = grad_q * gain_q, grad_k * gain_k
    q_inner, k_inner = over_heads(grad_q * q_normed, grad_k * k_normed)
    grad_q = q_factor * (grad_q - q_normed * q_inner)
    grad_k = k_factor * (grad_k - k_normed * k_inner)
    grad_proj = jnp.concatenate(
        [grad_q.astype(bf16), grad_k.astype(bf16), grad_v.reshape(seq, cols).astype(bf16)], axis=1
    )
    grad_w_qkv = dot("td,tc->dc", normed_in, grad_proj)
    grad_normed = dot("tc,dc->td", grad_proj, w_qkv).astype(bf16)
    grad_normed = jnp.sum(swap(grad_normed.reshape(seqs, own, width), "s").astype(f32), axis=0)
    grad_in_norm, gain_in_grad = norm_back(inputs, gain_in, grad_normed)
    grad_tokens = to_outer(grad_resid + grad_in_norm)

    def widen(local):
        full = jnp.zeros((width,), f32)
        return to_inner(lax.dynamic_update_slice_in_dim(full, local, rank * cols, 0))

    gains = jnp.stack(
        [gain_in_grad, gain_mid_grad, widen(gain_q_grad), widen(gain_k_grad)], axis=1
    )
    high = gains.astype(bf16)
    low = (gains - high.astype(f32)).astype(bf16)
    term = jnp.concatenate(
        [
            grad_w_qkv.astype(bf16),
            grad_w_out.astype(bf16),
            high,
            low,
            jnp.zeros((width, PAD - 8), bf16),
        ],
        axis=1,
    )
    term = lax.psum_scatter(term, ("o", "c", "z"), scatter_dimension=0, tiled=True)
    term = swap(term.reshape(seqs, rows_dev, 4 * cols + PAD), "s").astype(f32)
    grad_attn = (
        term[:, :, : 4 * cols]
        .reshape(seqs, rows_dev, 4, cols)
        .transpose(1, 2, 0, 3)
        .reshape(rows_dev, 4 * width)
    )
    gain_term = jnp.sum(term[:, :, 4 * cols : 4 * cols + 8], axis=0)
    grad_gains = gain_term[:, :4] + gain_term[:, 4:]
    return (
        to_outer(final_out).astype(bf16),
        loss_value,
        grad_tokens,
        grad_attn,
        grad_gains,
        grad_expert,
    )


def solution(mesh):
    fsdp, seqs = mesh.shape["fsdp"], mesh.shape["sp"]

    def whole(*arrays):
        planes = arrays[3].shape[1] // seqs
        outer = fsdp // (planes * CORES)
        inner = Mesh(mesh.devices.reshape(outer, planes, CORES, seqs), ("o", "z", "c", "s"))
        every = ("o", "z", "c", "s")
        rows = P(every, None)
        experts = P(("o", "z", "c"), "s", None)
        return jax.shard_map(
            shards,
            mesh=inner,
            in_specs=(
                rows,
                rows,
                rows,
                experts,
                rows,
                rows,
                P(("o", "z", "c")),
                P(every),
                rows,
                rows,
            ),
            out_specs=(rows, P(), rows, rows, rows, experts),
            check_vma=False,
        )(*arrays)

    return whole
```

time: 3510 us -> 1840 us (0.52)
  waiting for transfers between devices: 2240 us -> 838 us
  blocking collectives: 454 us -> 266 us
  other arithmetic: 208 us -> 93.5 us
  matrix products: 251 us -> 298 us
  local copies, waits for them, and re-layouts: 278 us -> 242 us
    reduce_scatter x2 -> x4, waiting for transfers between devices: 1850 us -> 34.8 us  [the longest x1 34.7 us: shards(): lax.psum_scatter(term, ('o', 'c', 'z'), scatter_dimension=0, tiled=True)]
    all_to_all x10 -> x16, waiting for transfers between devices: 147 us -> 803 us  [swap(): return lax.all_to_all(pieces, axis, split_axis=0, concat_axis=0, tiled=True)]
    all_gather x2 -> x3, waiting for transfers between devices: 245 us -> 0.01 us  [shards(): chunk = lax.all_gather(chunk, ('s', 'o', 'c'), axis=0, tiled=True)]
    psum x2 -> x0, blocking collectives: 171 us -> none  [shards(): lax.psum((jnp.sum(valid_f[:, None] * difference * difference), jnp.sum(va...]
    concatenate x4, other arithmetic: 88.9 us -> 3.74 us  [the longest x1 3.62 us: shards(): grad_expert = jnp.concatenate([grad_w_gate, grad_w_up, grad_down], axis=2)]
    all_gather x1 -> x0, blocking collectives: 70.9 us -> none  [shards(): lax.all_gather(norm_gains, ('fsdp', 'sp'), axis=0, tiled=True)]
    all_to_all x2 -> x8, blocking collectives: 212 us -> 266 us  [swap(): return lax.all_to_all(pieces, axis, split_axis=0, concat_axis=0, tiled=True)]
    dot_general x26 -> x34, matrix products: 251 us -> 298 us  [the longest x18 240 us: dot(): return jnp.einsum(spec, left, right, preferred_element_type=f32)]
  transfers between devices with their start and end apart: 15 -> 23, of which waited for: 10 -> 14; matrix products, arithmetic and copies ran while one was open for 10% -> 28% of each run, Pallas kernels for 0% -> 0%
where the time goes in v1:
time: 1840 us; the launch traced here: 1830 us
  waiting for transfers between devices  838 us (46%)
  matrix products  298 us (16%)
  blocking collectives  266 us (14%)
  local copies, waits for them, and re-layouts  242 us (13%)
  other arithmetic  93.5 us (5%)
  starting transfers between devices  72 us (4%)
  between operations  21.7 us (1%)
    all_to_all x16, waiting for transfers between devices, swap(): return lax.all_to_all(pieces, axis, split_axis=0, concat_axis=0, tiled=True)  803 us
    all_to_all x8, blocking collectives, swap(): return lax.all_to_all(pieces, axis, split_axis=0, concat_axis=0, tiled=True)  266 us
    dot_general x18, matrix products, dot(): return jnp.einsum(spec, left, right, preferred_element_type=f32)  240 us
    all_to_all x16, starting transfers between devices, swap(): return lax.all_to_all(pieces, axis, split_axis=0, concat_axis=0, tiled=True)  71.2 us
    unnamed x176, local copies, waits for them, and re-layouts  44.9 us
    concatenate x1, local copies, waits for them, and re-layouts, shards(): jnp.concatenate([grad_w_qkv.astype(bf16), grad_w_out.astype(bf16), high,...  39.6 us
  transfers between devices with their start and end apart: 23, of which 14 were waited for; matrix products, arithmetic and copies ran while one was open for 28% of the time, Pallas kernels for 0%

profile of v1, /device:TPU:0, one launch (start us, length us, event | category | flops | bytes accessed | tf_op | source)
XLA Modules:
  0.0 1834.1 jit_solution(10550427459373330252)
XLA Ops:
  13.3 54.4 %all_to_all.120 = bf16[4,256,1024]{2,1,0:T(8,128)(2,1)} all-to-all(bf16[4,256,1024]{2,1,0:T(8,128)(2,1)S(1)} %bitcast.329), channel_id=1, replica_groups=mesh['o'=1,'z'=4,'c'=2,'s'=4] {'z'}, dimensions={0} | all-to-all | bytes 4194304 | tf_op jit(solution)/shard_map/all_to_all | solution.py:21
  70.0 50.6 %all_to_all.121 = bf16[4,256,1024]{2,1,0:T(8,128)(2,1)} all-to-all(bf16[4,256,1024]{2,1,0:T(8,128)(2,1)S(1)} %bitcast.330), channel_id=1, replica_groups=mesh['o'=1,'z'=4,'c'=2,'s'=4] {'z'}, dimensions={0} | all-to-all | bytes 4194304 | tf_op jit(solution)/shard_map/all_to_all | solution.py:21
  130.5 30.8 %all_to_all.122 = bf16[4,64,2176]{2,1,0:T(8,128)(2,1)S(1)} all-to-all(bf16[4,64,2176]{2,1,0:T(8,128)(2,1)S(1)} %pad_maximum_fusion.3), channel_id=1, replica_groups=mesh['o'=1,'z'=4,'c'=2,'s'=4] {'s'}, dimensions={0} | all-to-all | bytes 2228224 | tf_op jit(solution)/shard_map/all_to_all | solution.py:21
  170.7 65.6 %all-to-all-done = bf16[4,256,2048]{2,1,0:T(8,128)(2,1)} async-done(((bf16[4,256,2048]{2,1,0:T(8,128)(2,1)}), bf16[4,256,2048]{2,1,0:T(8,128)(2,1)}, u32[]{:S(2)}, u32[]{:S(2)}) %all-to-all-start) | async-done | bytes 4194336 | tf_op jit(solution)/shard_map/all_to_all | solution.py:21
  241.3 44.1 %all-to-all-done.10 = bf16[4,256,1024]{2,1,0:T(8,128)(2,1)S(1)} async-done(((bf16[4,256,1024]{2,1,0:T(8,128)(2,1)}), bf16[4,256,1024]{2,1,0:T(8,128)(2,1)S(1)}, u32[]{:S(2)}, u32[]{:S(2)}) %all-to-all-start.10) | async-done | bytes 2097184 | tf_op jit(solution)/shard_map/all_to_all | solution.py:21
  326.4 66.6 %all-to-all-done.2 = bf16[4,256,2176]{1,2,0:T(8,128)(2,1)} async-done(((bf16[4,256,2176]{1,2,0:T(8,128)(2,1)}), bf16[4,256,2176]{1,2,0:T(8,128)(2,1)}, u32[]{:S(2)}, u32[]{:S(2)}) %all-to-all-start.2) | async-done | bytes 4456480 | tf_op jit(solution)/shard_map/all_to_all | solution.py:21
  392.9 17.9 copy.403
  425.7 14.7 copy.404
  474.6 20.9 %while.27 = (s32[]{:T(128)}, bf16[2,512,4,128]{3,2,1,0:T(4,128)(2,1)}, f32[2,4,512]{2,1,0:T(4,128)S(1)}, s32[2]{0:T(128)S(1)}, s32[1024]{0:T(1024)S(1)}, /*index...) while((s32[]{:T(128)}, ...), condition=%wide.region_8.9_spmd, body=%wide.region_5.8_spmd.sunk | while | flops 1100741120 | bytes 31537856 | solution.py:83
  510.7 44.1 %all-to-all-done.5 = bf16[4,256,2048]{2,1,0:T(8,128)(2,1)} async-done(((bf16[4,256,2048]{2,1,0:T(8,128)(2,1)}), bf16[4,256,2048]{2,1,0:T(8,128)(2,1)}, u32[]{:S(2)}, u32[]{:S(2)}) %all-to-all-start.5) | async-done | bytes 4194336 | tf_op jit(solution)/shard_map/all_to_all | solution.py:21
  581.0 91.3 %all-to-all-done.7 = bf16[4,256,2048]{2,1,0:T(8,128)(2,1)} async-done(((bf16[4,256,2048]{2,1,0:T(8,128)(2,1)}), bf16[4,256,2048]{2,1,0:T(8,128)(2,1)}, u32[]{:S(2)}, u32[]{:S(2)}) %all-to-all-start.7) | async-done | bytes 4194336 | tf_op jit(solution)/shard_map/all_to_all | solution.py:21
  689.3 17.6 fusion.96
  706.9 21.7 %multiply_convert_fusion.4 = (bf16[4,544,1024]{2,1,0:T(8,128)(2,1)}, f32[4,544,1024]{2,1,0:T(8,128)}) fusion(f32[4,544,1024]{2,1,0:T(8,128)} %fusion.96, bf16[4,544,2048]{2,1,0:T(8,128)(2,1)} %bitcast.320, bf16[4,2048,1024]{2,1,0:T(8,128)(2,1)} %bitcast.373), kind=kOutput, calls=%fused_computation.61 | convolution fusion | flops 9140174848 | bytes 47972352 | tf_op jit(solution)/shard_map/krd,kdf->krf/dot_general | solution.py:117
  728.6 16.6 multiply_convert_fusion.1
  775.2 76.3 %all-to-all-done.11 = bf16[4,256,2048]{2,1,0:T(8,128)(2,1)} async-done(((bf16[4,256,2048]{2,1,0:T(8,128)(2,1)}), bf16[4,256,2048]{2,1,0:T(8,128)(2,1)}, u32[]{:S(2)}, u32[]{:S(2)}) %all-to-all-start.11) | async-done | bytes 4194336 | tf_op jit(solution)/shard_map/all_to_all | solution.py:21
  857.8 96.6 %all_to_all.124 = bf16[4,256,2048]{2,1,0:T(8,128)(2,1)} all-to-all(bf16[4,256,2048]{2,1,0:T(8,128)(2,1)S(1)} %broadcast_in_dim.125), channel_id=1, replica_groups=mesh['o'=1,'z'=4,'c'=2,'s'=4] {'z'}, dimensions={0} | all-to-all | bytes 8388608 | tf_op jit(solution)/shard_map/all_to_all | solution.py:21
  965.3 23.5 %multiply_convert_fusion.2 = (bf16[4,544,1024]{2,1,0:T(8,128)(2,1)}, bf16[4,544,1024]{2,1,0:T(8,128)(2,1)}) fusion(f32[4,544,1024]{2,1,0:T(8,128)} %fusion.96, f32[4,544,1024]{2,1,0:T(8,128)} %get-tuple-element.441, bf16[4,544,2048]{2,1,0:T(8,128)(2,1)} %fusion.35, bf16[4,2048,1024]{2,1,0:T(8,128)(2,1)} %bitcast.376), kind=kOutput, calls=%fused_computation.59 | convolution fusion | flops 9155772416 | bytes 52428800 | tf_op jit(solution)/shard_map/krd,kdf->krf/dot_general | solution.py:117
  988.8 20.4 %convolution_convert_fusion.2 = bf16[4,2048,1024]{2,1,0:T(8,128)(2,1)} fusion(bf16[4,544,2048]{2,1,0:T(8,128)(2,1)} %bitcast.321, bf16[4,544,1024]{2,1,0:T(8,128)(2,1)} %get-tuple-element.408), kind=kOutput, calls=%fused_computation.54 | convolution fusion | flops 9135194112 | bytes 30146560 | tf_op jit(solution)/shard_map/krd,krf->kdf/dot_general | solution.py:117
  1009.2 22.4 %convolution_convert_fusion.1 = bf16[4,2048,1024]{2,1,0:T(8,128)(2,1)} fusion(bf16[4,544,2048]{2,1,0:T(8,128)(2,1)} %bitcast.322, bf16[4,544,1024]{2,1,0:T(8,128)(2,1)} %get-tuple-element.407), kind=kOutput, calls=%fused_computation.53 | convolution fusion | flops 9135194112 | bytes 30146560 | tf_op jit(solution)/shard_map/krd,krf->kdf/dot_general | solution.py:117
  1031.7 18.4 %fusion.97 = f32[4,544,2048]{2,1,0:T(8,128)} fusion(bf16[4,544,1024]{2,1,0:T(8,128)(2,1)} %get-tuple-element.408, bf16[4,2048,1024]{2,1,0:T(8,128)(2,1)} %bitcast.372), kind=kOutput, calls=%fused_computation.220 | convolution fusion | flops 9126805504 | bytes 39059456 | tf_op jit(solution)/shard_map/krf,kdf->krd/dot_general | solution.py:117
  1050.1 17.3 add_convert_fusion
  1077.4 20.8 %convolution_convert_fusion = bf16[4,2048,1024]{2,1,0:T(8,128)(2,1)} fusion(bf16[4,544,2048]{2,1,0:T(8,128)(2,1)} %fusion.35, bf16[4,544,1024]{2,1,0:T(8,128)(2,1)} %get-tuple-element.440), kind=kOutput, calls=%fused_computation.52 | convolution fusion | flops 9135194112 | bytes 30146560 | tf_op jit(solution)/shard_map/krd,krf->kdf/dot_general | solution.py:117
  1100.9 68.7 %all-to-all-done.16 = bf16[4,256,2048]{2,1,0:T(8,128)(2,1)} async-done(((bf16[4,256,2048]{2,1,0:T(8,128)(2,1)}), bf16[4,256,2048]{2,1,0:T(8,128)(2,1)}, u32[]{:S(2)}, u32[]{:S(2)}) %all-to-all-start.16) | async-done | bytes 4194336 | tf_op jit(solution)/shard_map/all_to_all | solution.py:21
  1190.2 63.8 %all-to-all-done.17 = bf16[4,256,2048]{2,1,0:T(8,128)(2,1)} async-done(((bf16[4,256,2048]{2,1,0:T(8,128)(2,1)}), bf16[4,256,2048]{2,1,0:T(8,128)(2,1)}, u32[]{:S(2)}, u32[]{:S(2)}) %all-to-all-start.17) | async-done | bytes 4194336 | tf_op jit(solution)/shard_map/all_to_all | solution.py:21
  1260.3 50.9 %while.28 = (s32[]{:T(128)}, f32[1024,4,128]{0,2,1:T(8,128)S(1)}, f32[1024,4,128]{0,2,1:T(8,128)}, bf16[2,512,4,128]{3,1,0,2:T(8,128)(2,1)}, s32[2]{0:T(128)S(1)...) while((s32[]{:T(128)}, f32[1024,4,128]{0,2,1:T(8,128)S(1)}, ...), condition=%wide.region_26.27_spmd.clone, body=%wide.region_24.26_spmd.clone.sunk | while | flops 2720266752 | bytes 180427760 | solution.py:110
  1369.7 45.4 %all-to-all-done.19 = bf16[4,256,2048]{2,1,0:T(8,128)(2,1)} async-done(((bf16[4,256,2048]{2,1,0:T(8,128)(2,1)}), bf16[4,256,2048]{2,1,0:T(8,128)(2,1)}, u32[]{:S(2)}, u32[]{:S(2)}) %all-to-all-start.19) | async-done | bytes 4194336 | tf_op jit(solution)/shard_map/all_to_all | solution.py:21
  1423.4 39.6 %concatenate.57 = bf16[2048,2176]{0,1:T(8,128)(2,1)} concatenate(bf16[2048,1536]{0,1:T(8,128)(2,1)} %convolution_convert_fusion.3, bf16[2048,512]{0,1:T(8,128)(2,1)} %convolution_convert_fusion.5, bf16[2048,4]{0,1:T(4,128)(2,1)S(1)} %fusion.84, bf16[2048,4]{0,1:T(4,128)(2,1)S(1)} %subtract_convert_fusion, bf16[2048,120]{0,1:T(8,128)(2,1)} %broadcast_in_dim.130), dimensions={1} | concatenate | bytes 17825792 | tf_op jit(solution)/shard_map/concatenate | solution.py:332
  1490.7 104.6 %all-to-all-done.21 = bf16[4,256,1024]{2,1,0:T(8,128)(2,1)S(1)} async-done(((bf16[4,256,1024]{2,1,0:T(8,128)(2,1)}), bf16[4,256,1024]{2,1,0:T(8,128)(2,1)S(1)}, u32[]{:S(2)}, u32[]{:S(2)}) %all-to-all-start.21) | async-done | bytes 2097184 | tf_op jit(solution)/shard_map/all_to_all | solution.py:21
  1601.1 102.2 %all-to-all-done.22 = bf16[4,256,1024]{2,1,0:T(8,128)(2,1)} async-done(((bf16[4,256,1024]{2,1,0:T(8,128)(2,1)}), bf16[4,256,1024]{2,1,0:T(8,128)(2,1)}, u32[]{:S(2)}, u32[]{:S(2)}) %all-to-all-start.22) | async-done | bytes 2097184 | tf_op jit(solution)/shard_map/all_to_all | solution.py:21
  1709.1 34.7 %reduce-scatter.5.cloned.1.call-done = bf16[256,2176]{0,1:T(8,128)(2,1)} async-done(((bf16[2048,2176]{0,1:T(8,128)(2,1)}), bf16[256,2176]{0,1:T(8,128)(2,1)}) %reduce-scatter.5.cloned.1.call-update) | async-done | bytes 1114128 | tf_op jit(solution)/shard_map/reduce_scatter | solution.py:342
  1746.1 28.0 %all-to-all-done.23 = bf16[4,256,1024]{2,1,0:T(8,128)(2,1)} async-done(((bf16[4,256,1024]{2,1,0:T(8,128)(2,1)}), bf16[4,256,1024]{2,1,0:T(8,128)(2,1)}, u32[]{:S(2)}, u32[]{:S(2)}) %all-to-all-start.23) | async-done | bytes 2097184 | tf_op jit(solution)/shard_map/all_to_all | solution.py:21
  1792.6 19.3 %copy.466 = f32[256,4,3072]{2,1,0:T(4,128)} copy(f32[256,4,3072]{2,0,1:T(8,128)S(1)} %maximum_convert_fusion) | data formatting | bytes 25165824
  (455 shorter events, 471.4 us)
Async XLA Ops:
  7.2 682.1 %all-gather.4.cloned.1.call-start = ((), (), s32[]{:S(2)}) async-start(), calls=%async_computation.28 | async-start | bytes 18874368 | tf_op jit(solution)/shard_map/all_gather | solution.py:191
  67.7 639.2 %all-gather.6.cloned.1.call-start = ((), (), s32[]{:S(2)}) async-start(), calls=%async_computation.29 | async-start | bytes 18874368 | tf_op jit(solution)/shard_map/all_gather | solution.py:191
  163.8 72.4 %all-to-all-start = ((bf16[4,256,2048]{2,1,0:T(8,128)(2,1)}), bf16[4,256,2048]{2,1,0:T(8,128)(2,1)}, u32[]{:S(2)}, u32[]{:S(2)}) async-start(bf16[4,256,2048]{2,1,0:T(8,128)(2,1)} %broadcast_in_dim.102), calls=%async_computation | async-start | bytes 8388608 | tf_op jit(solution)/shard_map/all_to_all | solution.py:21
  236.3 49.1 %all-to-all-start.10 = ((bf16[4,256,1024]{2,1,0:T(8,128)(2,1)}), bf16[4,256,1024]{2,1,0:T(8,128)(2,1)S(1)}, u32[]{:S(2)}, u32[]{:S(2)}) async-start(bf16[4,256,1024]{2,1,0:T(8,128)(2,1)} %bitcast.328), calls=%async_computation.10 | async-start | bytes 4194304 | tf_op jit(solution)/shard_map/all_to_all | solution.py:21
  289.7 103.2 %all-to-all-start.2 = ((bf16[4,256,2176]{1,2,0:T(8,128)(2,1)}), bf16[4,256,2176]{1,2,0:T(8,128)(2,1)}, u32[]{:S(2)}, u32[]{:S(2)}) async-start(bf16[4,256,2176]{1,2,0:T(8,128)(2,1)} %broadcast_in_dim.107), calls=%async_computation.2 | async-start | bytes 8912896 | tf_op jit(solution)/shard_map/all_to_all | solution.py:21
  294.6 434.0 %all-gather.8.cloned.1.call-start = ((), (), s32[]{:S(2)}) async-start(), calls=%async_computation.30 | async-start | bytes 18874368 | tf_op jit(solution)/shard_map/all_gather | solution.py:191
  443.5 123.7 %copy-start.56 = (f32[2048]{0:T(1024)}, f32[2048]{0:T(1024)S(1)}, u32[]{:S(2)}) copy-start(f32[2048]{0:T(1024)S(1)} %get-tuple-element.356) | copy-start | bytes 24580
  460.1 8.2 all-to-all-start.4
  503.0 51.9 %all-to-all-start.5 = ((bf16[4,256,2048]{2,1,0:T(8,128)(2,1)}), bf16[4,256,2048]{2,1,0:T(8,128)(2,1)}, u32[]{:S(2)}, u32[]{:S(2)}) async-start(bf16[4,256,2048]{2,1,0:T(8,128)(2,1)} %bitcast.343), calls=%async_computation.5 | async-start | bytes 8388608 | tf_op jit(solution)/shard_map/all_to_all | solution.py:21
  508.5 260.7 %copy-start.11 = (bf16[256,2048]{0,1:T(8,128)(2,1)}, bf16[256,2048]{0,1:T(8,128)(2,1)S(1)}, u32[]{:S(2)}) copy-start(bf16[256,2048]{0,1:T(8,128)(2,1)S(1)} %copy.398) | copy-start | bytes 3145732
  555.5 15.1 all-to-all-start.6
  574.3 98.0 %all-to-all-start.7 = ((bf16[4,256,2048]{2,1,0:T(8,128)(2,1)}), bf16[4,256,2048]{2,1,0:T(8,128)(2,1)}, u32[]{:S(2)}, u32[]{:S(2)}) async-start(bf16[4,256,2048]{2,1,0:T(8,128)(2,1)} %broadcast_in_dim.112), calls=%async_computation.7 | async-start | bytes 8388608 | tf_op jit(solution)/shard_map/all_to_all | solution.py:21
  753.8 97.7 %all-to-all-start.11 = ((bf16[4,256,2048]{2,1,0:T(8,128)(2,1)}), bf16[4,256,2048]{2,1,0:T(8,128)(2,1)}, u32[]{:S(2)}, u32[]{:S(2)}) async-start(bf16[4,256,2048]{2,1,0:T(8,128)(2,1)} %bitcast_convert_fusion.1), calls=%async_computation.11 | async-start | bytes 8388608 | tf_op jit(solution)/shard_map/all_to_all | solution.py:21
  758.8 728.3 %reduce-scatter.7.cloned.1.call-start = ((), (), s32[]{:S(2)}) async-start(), calls=%async_computation.32 | async-start | bytes 18874368 | tf_op jit(solution)/shard_map/reduce_scatter | solution.py:271
  775.2 79.7 %copy-start.79 = (f32[256]{0:T(256)}, f32[256]{0:T(256)S(1)}, u32[]{:S(2)}) copy-start(f32[256]{0:T(256)S(1)} %get-tuple-element.447) | copy-start | bytes 3076
  775.2 79.7 %copy-start.18 = (f32[256,2048]{1,0:T(8,128)S(1)}, f32[256,2048]{1,0:T(8,128)}, u32[]{:S(2)}) copy-start(f32[256,2048]{1,0:T(8,128)} %get-tuple-element.402) | copy-start | bytes 6291460
  1009.2 481.5 %reduce-scatter.9.cloned.1.call-start = ((), (), s32[]{:S(2)}) async-start(), calls=%async_computation.33 | async-start | bytes 18874368 | tf_op jit(solution)/shard_map/reduce_scatter | solution.py:271
  1072.5 97.1 %all-to-all-start.16 = ((bf16[4,256,2048]{2,1,0:T(8,128)(2,1)}), bf16[4,256,2048]{2,1,0:T(8,128)(2,1)}, u32[]{:S(2)}, u32[]{:S(2)}) async-start(bf16[4,256,2048]{2,1,0:T(8,128)(2,1)} %bitcast_convert_fusion), calls=%async_computation.16 | async-start | bytes 8388608 | tf_op jit(solution)/shard_map/all_to_all | solution.py:21
  1077.4 523.7 %reduce-scatter.11.cloned.1.call-start = ((), (), s32[]{:S(2)}) async-start(), calls=%async_computation.34 | async-start | bytes 18874368 | tf_op jit(solution)/shard_map/reduce_scatter | solution.py:271
  1099.0 78.4 %copy-start.60 = (f32[2,4,256]{2,0,1:T(2,128)}, f32[2,4,256]{2,0,1:T(2,128)S(1)}, u32[]{:S(2)}) copy-start(f32[2,4,256]{2,0,1:T(2,128)S(1)} %copy.440) | copy-start | bytes 24580
  1100.9 76.5 %copy-start.14 = (f32[256,2048]{0,1:T(8,128)}, f32[256,2048]{0,1:T(8,128)S(1)}, u32[]{:S(2)}) copy-start(f32[256,2048]{0,1:T(8,128)S(1)} %copy.426) | copy-start | bytes 6291460
  1184.9 69.1 %all-to-all-start.17 = ((bf16[4,256,2048]{2,1,0:T(8,128)(2,1)}), bf16[4,256,2048]{2,1,0:T(8,128)(2,1)}, u32[]{:S(2)}, u32[]{:S(2)}) async-start(bf16[4,256,2048]{2,1,0:T(8,128)(2,1)} %broadcast_in_dim.128), calls=%async_computation.17 | async-start | bytes 8388608 | tf_op jit(solution)/shard_map/all_to_all | solution.py:21
  1323.1 8.3 all-to-all-start.18
  1348.3 66.8 %all-to-all-start.19 = ((bf16[4,256,2048]{2,1,0:T(8,128)(2,1)}), bf16[4,256,2048]{2,1,0:T(8,128)(2,1)}, u32[]{:S(2)}, u32[]{:S(2)}) async-start(bf16[4,256,2048]{2,1,0:T(8,128)(2,1)} %bitcast.342), calls=%async_computation.19 | async-start | bytes 8388608 | tf_op jit(solution)/shard_map/all_to_all | solution.py:21
  1353.3 390.5 %reduce-scatter.5.cloned.1.call-start = ((), (), s32[]{:S(2)}) async-start(), calls=%async_computation.31 | async-start | bytes 10027008 | tf_op jit(solution)/shard_map/reduce_scatter | solution.py:342
  1487.1 108.2 %all-to-all-start.21 = ((bf16[4,256,1024]{2,1,0:T(8,128)(2,1)}), bf16[4,256,1024]{2,1,0:T(8,128)(2,1)S(1)}, u32[]{:S(2)}, u32[]{:S(2)}) async-start(bf16[4,256,1024]{2,1,0:T(8,128)(2,1)} %bitcast.346), calls=%async_computation.23 | async-start | bytes 4194304 | tf_op jit(solution)/shard_map/all_to_all | solution.py:21
  1596.6 106.7 %all-to-all-start.22 = ((bf16[4,256,1024]{2,1,0:T(8,128)(2,1)}), bf16[4,256,1024]{2,1,0:T(8,128)(2,1)}, u32[]{:S(2)}, u32[]{:S(2)}) async-start(bf16[4,256,1024]{2,1,0:T(8,128)(2,1)} %bitcast.345), calls=%async_computation.25 | async-start | bytes 4194304 | tf_op jit(solution)/shard_map/all_to_all | solution.py:21
  1703.2 70.9 %all-to-all-start.23 = ((bf16[4,256,1024]{2,1,0:T(8,128)(2,1)}), bf16[4,256,1024]{2,1,0:T(8,128)(2,1)}, u32[]{:S(2)}, u32[]{:S(2)}) async-start(bf16[4,256,1024]{2,1,0:T(8,128)(2,1)} %bitcast.347), calls=%async_computation.27 | async-start | bytes 4194304 | tf_op jit(solution)/shard_map/all_to_all | solution.py:21
  1709.0 69.6 %copy-start.15 = (f32[256,2048]{0,1:T(8,128)S(1)}, f32[256,2048]{0,1:T(8,128)}, u32[]{:S(2)}) copy-start(f32[256,2048]{0,1:T(8,128)} %copy-done.14) | copy-start | bytes 6291460
  1709.0 69.6 %copy-start.61 = (f32[2,4,256]{2,0,1:T(2,128)S(1)}, f32[2,4,256]{2,0,1:T(2,128)}, u32[]{:S(2)}) copy-start(f32[2,4,256]{2,0,1:T(2,128)} %copy-done.60) | copy-start | bytes 24580
  1709.0 69.6 %copy-start.75 = (f32[256]{0:T(256)S(1)}, f32[256]{0:T(256)}, u32[]{:S(2)}) copy-start(f32[256]{0:T(256)} %copy-done.73) | copy-start | bytes 3076
  1774.1 37.8 %all-to-all-start.20 = ((bf16[4,64,2176]{2,1,0:T(8,128)(2,1)}), bf16[4,64,2176]{2,1,0:T(8,128)(2,1)}, u32[]{:S(2)}, u32[]{:S(2)}) async-start(bf16[4,64,2176]{2,1,0:T(8,128)(2,1)} %bitcast.338), calls=%async_computation.21 | async-start | bytes 2228224 | tf_op jit(solution)/shard_map/all_to_all | solution.py:21
  (88 other events, 550.0 us)
Sparse Core Ops, SparseCore 0:
  67.8 101.0 all-gather.3
  170.8 119.4 all-gather.5
  326.5 90.1 all-gather.7
  1009.3 113.0 reduce-scatter.6
  1125.8 157.1 reduce-scatter.8
  1286.5 152.3 reduce-scatter.10
  1463.2 280.5 reduce-scatter.4

commit v2 on v1

--- a/solution.py
+++ b/solution.py
@@ -15,15 +15,47 @@
 bf16 = jnp.bfloat16
 
 
-def swap(pieces, axis):
-    if pieces.shape[0] == 1:
-        return pieces
-    return lax.all_to_all(pieces, axis, split_axis=0, concat_axis=0, tiled=True)
+def send(block, axis, step):
+    size = lax.axis_size(axis)
+    return lax.ppermute(block, axis, [(i, i ^ step) for i in range(size)])
+
+
+def gather_near(block, axis):
+    return [block] + [send(block, axis, k) for k in range(1, lax.axis_size(axis))]
+
+
+def in_order(blocks, axis, start=0):
+    rank = lax.axis_index(axis)
+    if len(blocks) == 1:
+        return blocks[0][None]
+    stacked = jnp.zeros((len(blocks),) + blocks[0].shape, blocks[0].dtype)
+    for k, block in enumerate(blocks):
+        stacked = lax.dynamic_update_index_in_dim(stacked, block, (rank ^ k) + start, 0)
+    return stacked
 
 
 def collect(block, axis):
-    size = lax.axis_size(axis)
-    return swap(jnp.broadcast_to(block[None], (size,) + block.shape), axis)
+    return in_order(gather_near(block, axis), axis)
+
+
+def exchange(piece_for, axis, start=0):
+    rank, size = lax.axis_index(axis) + start, lax.axis_size(axis)
+    return [piece_for(rank)] + [send(piece_for(rank ^ k), axis, k) for k in range(1, size)]
+
+
+def exchange_sum(pieces, axis):
+    got = exchange(lambda i: lax.dynamic_index_in_dim(pieces, i, 0, keepdims=False), axis)
+    return sum(piece.astype(f32) for piece in got)
+
+
+def token(*values):
+    firsts = [value[(slice(0, 1),) * value.ndim].reshape(()).astype(f32) for value in values]
+    total = sum(firsts)
+    return (total != total).astype(jnp.int32)
+
+
+def after(value, *others):
+    return value + token(*others).astype(value.dtype)
 
 
 def rms_factor(values):
@@ -155,6 +187,27 @@
     def gather_rows(block):
         return collect(collect(collect(block, "z"), "c"), "o").reshape((-1,) + block.shape[1:])
 
+    def gather_sum(value):
+        for axis in ("z", "s", "c", "o"):
+            value = sum(gather_near(jnp.broadcast_to(value, (8, PAD)), axis))[0, 0]
+        return value
+
+    by_expert = w_expert.transpose(1, 0, 2)
+
+    def expert_chunk(i, start=0):
+        def piece_for(owner):
+            return lax.dynamic_slice(by_expert, (owner, 0, i * hidden), (1, part, hidden))[0]
+
+        return exchange(piece_for, "z", start)
+
+    def gather_plane(blocks, start=0):
+        chunk = in_order(blocks, "z", start).reshape(planes * part, hidden)
+        chunk = lax.all_gather(chunk, ("s", "o", "c"), axis=0, tiled=True)
+        return chunk.reshape(seqs, width, hidden)
+
+    gate_blocks = expert_chunk(0)
+    w_gate = gather_plane(gate_blocks)
+
     count = jnp.sum(valid_mask).astype(jnp.int32)
     digits = jnp.stack([count // 128, count % 128]).astype(bf16)
     extra = jnp.concatenate(
@@ -165,35 +218,27 @@
         ],
         axis=1,
     )
-    packed = jnp.concatenate(
-        [
-            w_attn.reshape(rows_dev, 4, seqs, cols).transpose(2, 0, 1, 3).reshape(
-                seqs, rows_dev, 4 * cols
-            ),
-            jnp.broadcast_to(extra[None], (seqs, rows_dev, PAD)),
-        ],
-        axis=2,
-    )
-    mine = swap(packed, "s").reshape(part, 4 * cols + PAD)
-    weights = gather_rows(mine)
-    w_qkv = weights[:, : 3 * cols]
-    w_out = weights[:, 3 * cols : 4 * cols]
-    side = weights[:, 4 * cols : 4 * cols + 6].astype(f32).T
+
+    def columns_of(owner):
+        picked = [
+            lax.dynamic_slice_in_dim(w_attn, i * width + owner * cols, cols, 1) for i in range(4)
+        ]
+        return jnp.concatenate(picked + [extra], axis=1)
+
+    mine = in_order(exchange(columns_of, "s"), "s", token(*gate_blocks))
+    mine = mine.reshape(part, 4 * cols + PAD)
+    w_in = gather_rows(jnp.concatenate([mine[:, : 3 * cols], mine[:, 4 * cols :]], axis=1))
+    w_out = gather_rows(after(mine[:, 3 * cols : 4 * cols], w_in))
+    side = w_in[:, 3 * cols : 3 * cols + 6].astype(f32).T
     gain_in, gain_mid = side[0], side[1]
     gain_q = lax.dynamic_slice_in_dim(to_outer(side[2]), rank * cols, cols, 0)
     gain_k = lax.dynamic_slice_in_dim(to_outer(side[3]), rank * cols, cols, 0)
     total_count = jnp.sum(side[4, ::rows_dev]) * 128.0 + jnp.sum(side[5, ::rows_dev])
 
-    expert_parts = []
-    for i in range(3):
-        chunk = w_expert[:, :, i * hidden : (i + 1) * hidden].transpose(1, 0, 2)
-        chunk = swap(chunk, "z").reshape(planes * part, hidden)
-        chunk = lax.all_gather(chunk, ("s", "o", "c"), axis=0, tiled=True)
-        expert_parts.append(chunk.reshape(seqs, width, hidden))
-    w_gate, w_up, w_down = expert_parts
-
-    routed = collect(
-        jnp.concatenate([routes.astype(f32), gate_weights.astype(f32)], axis=1), "z"
+    up_blocks = expert_chunk(1, token(w_in))
+
+    routed = jnp.stack(
+        gather_near(jnp.concatenate([routes.astype(f32), gate_weights], axis=1), "z")
     )
     route_all, gate_all = routed[..., :TOP].astype(jnp.int32), routed[..., TOP:]
     expert_ids = jnp.arange(seqs) * planes + plane
@@ -212,23 +257,26 @@
         spread = dot("bkjt,btd->kbjd", choose, rows_in)
         return spread.reshape(seqs, planes * capacity, width)
 
-    def combine(rows_out):
+    def combine(rows_out, *others):
         rows_out = rows_out.reshape(seqs, planes, capacity, width)
         partial = dot("bkjt,kbjd->btd", choose, rows_out).astype(bf16)
-        return jnp.sum(swap(partial, "z").astype(f32), axis=0)
+        got = [partial[0]] + [send(partial[k], "z", k) for k in range(1, planes)]
+        if others:
+            got[0] = after(got[0], *others)
+        return sum(piece.astype(f32) for piece in got)
 
     inputs = to_inner(tokens)
-    seq_tokens = to_inner(collect(tokens, "s").reshape(seq, width)).astype(f32)
+    seq_tokens = collect(inputs, "s").reshape(seq, width).astype(f32)
     normed_in = (seq_tokens * rms_factor(seq_tokens) * gain_in).astype(bf16)
     inputs = inputs.astype(f32)
-    projected = jnp.dot(normed_in, w_qkv, preferred_element_type=f32)
+    projected = jnp.dot(normed_in, w_in, preferred_element_type=f32)
     query_raw = projected[:, :cols]
     key_raw = projected[:, cols : 2 * cols]
-    valued = projected[:, 2 * cols :].astype(bf16).reshape(seq, heads, HD)
+    valued = projected[:, 2 * cols : 3 * cols].astype(bf16).reshape(seq, heads, HD)
 
     def over_heads(first, second):
         pair = jnp.stack([jnp.sum(first, axis=-1), jnp.sum(second, axis=-1)])
-        pair = jnp.sum(collect(pair, "s"), axis=0) / width
+        pair = sum(gather_near(pair, "s")) / width
         return pair[0][:, None], pair[1][:, None]
 
     q_mean, k_mean = over_heads(query_raw * query_raw, key_raw * key_raw)
@@ -240,13 +288,19 @@
         return (cube * cosine + rotate_half(cube) * sine).astype(bf16)
 
     query, keyed = rope(query_raw, q_factor, gain_q), rope(key_raw, k_factor, gain_k)
+    query = after(query, w_gate)
     attended, log_total = attend_forward(query, keyed, valued, segment, block_rows, scale)
+    attended = after(attended, *up_blocks)
+    w_up = gather_plane(up_blocks, token(attended))
+    down_blocks = expert_chunk(2, token(attended))
     attn_out = dot("tc,dc->td", attended, w_out).astype(bf16)
-    attn_out = jnp.sum(swap(attn_out.reshape(seqs, own, width), "s").astype(f32), axis=0)
-    residual = inputs + attn_out
+    residual = inputs + exchange_sum(attn_out.reshape(seqs, own, width), "s")
+
+    residual = after(residual, *down_blocks)
+    w_down = gather_plane(down_blocks, token(residual))
 
     normed_mid = (residual * rms_factor(residual) * gain_mid).astype(bf16)
-    rows_in = dispatch(collect(normed_mid, "z")).astype(bf16)
+    rows_in = dispatch(after(jnp.stack(gather_near(normed_mid, "z")), w_up)).astype(bf16)
     gate_pre = dot("krd,kdf->krf", rows_in, w_gate)
     up_pre = dot("krd,kdf->krf", rows_in, w_up)
     activated = (jax.nn.silu(gate_pre) * up_pre).astype(bf16)
@@ -256,37 +310,50 @@
     valid_f = valid_mask.astype(f32)[:, None]
     difference = final_out - to_inner(teacher).astype(f32)
     squared = jnp.sum(valid_f * difference * difference)
-    for axis in ("z", "s", "c", "o"):
-        squared = jnp.sum(collect(jnp.broadcast_to(squared, (1, PAD)), axis)[:, 0, 0])
+    squared = gather_sum(squared)
     loss_value = squared / (total_count * width)
     grad_out = (
         to_inner(cotangent).astype(f32) + 2.0 / (total_count * width) * valid_f * difference
     )
 
-    grad_rows = dispatch(collect(grad_out.astype(bf16), "z"))
+    grad_rows = dispatch(jnp.stack(gather_near(grad_out.astype(bf16), "z")))
     grad_rows = (grad_rows * gate_slot).astype(bf16)
 
     def scatter_expert(grad):
-        grad = grad.astype(bf16).reshape(seqs * width, hidden)
+        grad = grad.reshape(seqs * width, hidden)
         grad = lax.psum_scatter(grad, ("s", "o", "c"), scatter_dimension=0, tiled=True)
-        return swap(grad.reshape(planes, part, hidden), "z").astype(f32).transpose(1, 0, 2)
-
-    grad_down = scatter_expert(dot("krd,krf->kdf", grad_rows, activated))
+        return grad.reshape(planes, part, hidden)
+
+    def to_owners(grad, start=0):
+        def piece_for(owner):
+            return lax.dynamic_index_in_dim(grad, owner, 0, keepdims=False)
+
+        return exchange(piece_for, "z", start)
+
+    grad_w_down = scatter_expert(dot("krd,krf->kdf", grad_rows, activated).astype(bf16))
     grad_act = dot("krd,kdf->krf", grad_rows, w_down)
     sigmoid = jax.nn.sigmoid(gate_pre)
     grad_gate = (grad_act * up_pre * sigmoid * (1.0 + gate_pre * (1.0 - sigmoid))).astype(bf16)
     grad_up = (grad_act * gate_pre * sigmoid).astype(bf16)
     back_rows = dot("krf,kdf->krd", grad_gate, w_gate) + dot("krf,kdf->krd", grad_up, w_up)
-    grad_mid = combine(back_rows.astype(bf16))
-    grad_w_gate = scatter_expert(dot("krd,krf->kdf", rows_in, grad_gate))
-    grad_w_up = scatter_expert(dot("krd,krf->kdf", rows_in, grad_up))
-    grad_expert = jnp.concatenate([grad_w_gate, grad_w_up, grad_down], axis=2)
+    grad_w_gate = dot("krd,krf->kdf", rows_in, grad_gate).astype(bf16)
+    grad_w_up = dot("krd,krf->kdf", rows_in, grad_up).astype(bf16)
+    grad_mid = combine(back_rows.astype(bf16), grad_w_gate, grad_w_up)
+    grad_w_gate, grad_w_up = scatter_expert(grad_w_gate), scatter_expert(grad_w_up)
+    down_part = to_owners(grad_w_down, token(grad_mid))
+    gate_part = to_owners(grad_w_gate)
+    up_part = to_owners(grad_w_up)
 
     grad_resid_norm, gain_mid_grad = norm_back(residual, gain_mid, grad_mid)
     grad_resid = grad_out + grad_resid_norm
 
+    def scatter_rows(grad):
+        grad = grad.astype(bf16)
+        return lax.psum_scatter(grad, ("o", "c", "z"), scatter_dimension=0, tiled=True)
+
     grad_attn_out = collect(grad_resid.astype(bf16), "s").reshape(seq, width)
-    grad_w_out = dot("td,tc->dc", grad_attn_out, attended)
+    grad_w_out = scatter_rows(dot("td,tc->dc", grad_attn_out, attended))
+    grad_attn_out = after(grad_attn_out, *down_part)
     grad_heads = jnp.dot(grad_attn_out, w_out, preferred_element_type=f32).astype(bf16)
     grad_q, grad_k, grad_v = attend_backward(
         query,
@@ -303,6 +370,8 @@
         grad = grad.astype(bf16).astype(f32)
         return (grad * cosine + rotate_back(grad * sine)).reshape(seq, cols)
 
+    down_part = in_order(down_part, "z", token(grad_q))
+    grad_q = after(grad_q, *gate_part)
     grad_q, grad_k = unrotate(grad_q), unrotate(grad_k)
     q_normed, k_normed = query_raw * q_factor, key_raw * k_factor
     gain_q_grad = jnp.sum(grad_q * q_normed, axis=0)
@@ -314,9 +383,13 @@
     grad_proj = jnp.concatenate(
         [grad_q.astype(bf16), grad_k.astype(bf16), grad_v.reshape(seq, cols).astype(bf16)], axis=1
     )
-    grad_w_qkv = dot("td,tc->dc", normed_in, grad_proj)
-    grad_normed = dot("tc,dc->td", grad_proj, w_qkv).astype(bf16)
-    grad_normed = jnp.sum(swap(grad_normed.reshape(seqs, own, width), "s").astype(f32), axis=0)
+    gate_part = in_order(gate_part, "z", token(grad_proj))
+    grad_padded = jnp.concatenate([grad_proj, jnp.zeros((seq, PAD), bf16)], axis=1)
+    grad_normed = dot("tc,dc->td", grad_padded, w_in).astype(bf16)
+    grad_normed = exchange_sum(grad_normed.reshape(seqs, own, width), "s")
+    grad_w_qkv = scatter_rows(
+        dot("td,tc->dc", normed_in, grad_proj)
+    )
     grad_in_norm, gain_in_grad = norm_back(inputs, gain_in, grad_normed)
     grad_tokens = to_outer(grad_resid + grad_in_norm)
 
@@ -324,31 +397,26 @@
         full = jnp.zeros((width,), f32)
         return to_inner(lax.dynamic_update_slice_in_dim(full, local, rank * cols, 0))
 
-    gains = jnp.stack(
-        [gain_in_grad, gain_mid_grad, widen(gain_q_grad), widen(gain_k_grad)], axis=1
-    )
-    high = gains.astype(bf16)
-    low = (gains - high.astype(f32)).astype(bf16)
-    term = jnp.concatenate(
-        [
-            grad_w_qkv.astype(bf16),
-            grad_w_out.astype(bf16),
-            high,
-            low,
-            jnp.zeros((width, PAD - 8), bf16),
-        ],
+    gains = jnp.stack([gain_in_grad, gain_mid_grad, widen(gain_q_grad), widen(gain_k_grad)])
+    for axis in ("z", "c", "s", "o"):
+        gains = sum(gather_near(gains, axis))
+    row = (lax.axis_index(("o", "c", "z")) * seqs + rank) * rows_dev
+    grad_gains = lax.dynamic_slice_in_dim(gains, row, rows_dev, 1).T
+
+    def own_rows(grad):
+        grad = grad.reshape(seqs, rows_dev, grad.shape[1])
+        got = exchange(lambda i: lax.dynamic_index_in_dim(grad, i, 0, keepdims=False), "s")
+        return in_order(got, "s").astype(f32)
+
+    qkv_rows, out_rows = own_rows(grad_w_qkv), own_rows(grad_w_out)
+    grad_attn = jnp.concatenate(
+        [qkv_rows[s, :, i * cols : (i + 1) * cols] for i in range(3) for s in range(seqs)]
+        + [out_rows[s] for s in range(seqs)],
         axis=1,
     )
-    term = lax.psum_scatter(term, ("o", "c", "z"), scatter_dimension=0, tiled=True)
-    term = swap(term.reshape(seqs, rows_dev, 4 * cols + PAD), "s").astype(f32)
-    grad_attn = (
-        term[:, :, : 4 * cols]
-        .reshape(seqs, rows_dev, 4, cols)
-        .transpose(1, 2, 0, 3)
-        .reshape(rows_dev, 4 * width)
-    )
-    gain_term = jnp.sum(term[:, :, 4 * cols : 4 * cols + 8], axis=0)
-    grad_gains = gain_term[:, :4] + gain_term[:, 4:]
+    up_part = in_order(up_part, "z")
+    grad_expert = jnp.concatenate([gate_part, up_part, down_part], axis=2)
+    grad_expert = grad_expert.astype(f32).transpose(1, 0, 2)
     return (
         to_outer(final_out).astype(bf16),
         loss_value,

time: 1840 us -> 1730 us (0.940)
  blocking collectives: 266 us -> 0 us
  starting transfers between devices: 72 us -> 247 us
  waiting for transfers between devices: 838 us -> 759 us
  local copies, waits for them, and re-layouts: 242 us -> 276 us
  between operations: 21.7 us -> 47.5 us
    all_to_all x16 -> x0, waiting for transfers between devices: 803 us -> none  [swap(): return lax.all_to_all(pieces, axis, split_axis=0, concat_axis=0, tiled=True)]
    ppermute x0 -> x82, waiting for transfers between devices: none -> 750 us  [send(): return lax.ppermute(block, axis, [(i, i ^ step) for i in range(size)])]
    all_to_all x8 -> x0, blocking collectives: 266 us -> none  [swap(): return lax.all_to_all(pieces, axis, split_axis=0, concat_axis=0, tiled=True)]
    ppermute x0 -> x82, starting transfers between devices: none -> 246 us  [send(): return lax.ppermute(block, axis, [(i, i ^ step) for i in range(size)])]
    all_to_all x16 -> x0, starting transfers between devices: 71.2 us -> none  [swap(): return lax.all_to_all(pieces, axis, split_axis=0, concat_axis=0, tiled=True)]
    dynamic_update_slice x2 -> x50, local copies, waits for them, and re-layouts: 2.46 us -> 44.6 us  [in_order(): lax.dynamic_update_index_in_dim(stacked, block, (rank ^ k) + start, 0)]
    concatenate x2 -> x6, local copies, waits for them, and re-layouts: 39.7 us -> 0.42 us  [the longest x4 0.4 us: columns_of(): return jnp.concatenate(picked + [extra], axis=1)]
    reduce_scatter x1 -> x2, waiting for transfers between devices: 34.7 us -> 0.02 us  [scatter_rows(): lax.psum_scatter(grad, ('o', 'c', 'z'), scatter_dimension=0, tiled=True)]
  transfers between devices with their start and end apart: 23 -> 90, of which waited for: 14 -> 42; matrix products, arithmetic and copies ran while one was open for 28% -> 30% of each run, Pallas kernels for 0% -> 0%
where the time goes in v2:
time: 1730 us
  waiting for transfers between devices  759 us (44%)
  matrix products  284 us (16%)
  local copies, waits for them, and re-layouts  276 us (16%)
  starting transfers between devices  247 us (14%)
  other arithmetic  110 us (6%)
  between operations  47.5 us (3%)
    ppermute x82, waiting for transfers between devices, send(): return lax.ppermute(block, axis, [(i, i ^ step) for i in range(size)])  750 us
    ppermute x82, starting transfers between devices, send(): return lax.ppermute(block, axis, [(i, i ^ step) for i in range(size)])  246 us
    dot_general x18, matrix products, dot(): return jnp.einsum(spec, left, right, preferred_element_type=f32)  227 us
    unnamed x231, local copies, waits for them, and re-layouts  54.3 us
    dynamic_update_slice x50, local copies, waits for them, and re-layouts, in_order(): lax.dynamic_update_index_in_dim(stacked, block, (rank ^ k) + start, 0)  44.6 us
  transfers between devices with their start and end apart: 90, of which 42 were waited for; matrix products, arithmetic and copies ran while one was open for 30% of the time, Pallas kernels for 0%

profile of v2, /device:TPU:0, one launch (start us, length us, event | category | flops | bytes accessed | tf_op | source)
XLA Modules:
  0.0 1726.4 jit_solution(6580212039308333450)
XLA Ops:
  21.1 18.7 %collective-permute-done.3 = bf16[256,1024]{1,0:T(8,128)(2,1)S(1)} collective-permute-done((bf16[256,1024]{1,0:T(8,128)(2,1)S(1)}, bf16[256,1024]{1,0:T(8,128)(2,1)S(1)}, u32[]{:S(2)}, u32[]{:S(2)}) %collective-permute-start.3) | collective-permute-done | bytes 524320 | tf_op jit(solution)/shard_map/ppermute | solution.py:20
  78.5 20.9 %collective-permute-start.9 = (bf16[256,1664]{1,0:T(8,128)(2,1)}, bf16[256,1664]{1,0:T(8,128)(2,1)}, u32[]{:S(2)}, u32[]{:S(2)}) collective-permute-start(bf16[256,1664]{1,0:T(8,128)(2,1)} %pad_maximum_fusion), channel_id=1, source_target_pairs={{0,8},{8,0},{16,24},{24,16},{1,9},{9,1},{17,25},{25,17},{2,10},{10... | collective-permute-start | bytes 2555912 | tf_op jit(solution)/shard_map/ppermute | solution.py:20
  129.6 29.4 %collective-permute-done.10 = bf16[256,1664]{1,0:T(8,128)(2,1)} collective-permute-done((bf16[256,1664]{1,0:T(8,128)(2,1)}, bf16[256,1664]{1,0:T(8,128)(2,1)}, u32[]{:S(2)}, u32[]{:S(2)}) %collective-permute-start.10) | collective-permute-done | bytes 852000 | tf_op jit(solution)/shard_map/ppermute | solution.py:20
  175.4 38.7 %collective-permute-done.1 = bf16[256,2048]{1,0:T(8,128)(2,1)} collective-permute-done((bf16[256,2048]{1,0:T(8,128)(2,1)S(1)}, bf16[256,2048]{1,0:T(8,128)(2,1)}, u32[]{:S(2)}, u32[]{:S(2)}) %collective-permute-start.1) | collective-permute-done | bytes 1048608 | tf_op jit(solution)/shard_map/ppermute | solution.py:20
  348.5 19.4 %while.27 = (s32[]{:T(128)}, bf16[2,512,4,128]{3,1,2,0:T(8,128)(2,1)}, f32[2,4,512]{2,1,0:T(4,128)S(1)}, s32[2]{0:T(128)S(1)}, s32[1024]{0:T(1024)S(1)}, /*index...) while((s32[]{:T(128)}, ...), condition=%wide.region_7.8_spmd, body=%wide.region_4.7_spmd.sunk | while | flops 1100741120 | bytes 30489280 | solution.py:115
  443.5 23.0 %collective-permute-done.27 = bf16[256,1024]{1,0:T(8,128)(2,1)S(1)} collective-permute-done((bf16[256,1024]{1,0:T(8,128)(2,1)S(1)}, bf16[256,1024]{1,0:T(8,128)(2,1)S(1)}, u32[]{:S(2)}, u32[]{:S(2)}) %collective-permute-start.27) | collective-permute-done | bytes 524320 | tf_op jit(solution)/shard_map/ppermute | solution.py:20
  475.9 41.0 %collective-permute-done.25 = bf16[256,2048]{1,0:T(8,128)(2,1)S(1)} collective-permute-done((bf16[256,2048]{1,0:T(8,128)(2,1)S(1)}, bf16[256,2048]{1,0:T(8,128)(2,1)S(1)}, u32[]{:S(2)}, u32[]{:S(2)}) %collective-permute-start.25) | collective-permute-done | bytes 1048608 | tf_op jit(solution)/shard_map/ppermute | solution.py:20
  543.7 32.1 %collective-permute-done.32 = bf16[256,2048]{1,0:T(8,128)(2,1)} collective-permute-done((bf16[256,2048]{1,0:T(8,128)(2,1)S(1)}, bf16[256,2048]{1,0:T(8,128)(2,1)}, u32[]{:S(2)}, u32[]{:S(2)}) %collective-permute-start.32) | collective-permute-done | bytes 1048608 | tf_op jit(solution)/shard_map/ppermute | solution.py:20
  575.8 30.8 %collective-permute-done.33 = bf16[256,2048]{1,0:T(8,128)(2,1)} collective-permute-done((bf16[256,2048]{1,0:T(8,128)(2,1)S(1)}, bf16[256,2048]{1,0:T(8,128)(2,1)}, u32[]{:S(2)}, u32[]{:S(2)}) %collective-permute-start.33) | collective-permute-done | bytes 1048608 | tf_op jit(solution)/shard_map/ppermute | solution.py:20
  621.8 17.7 %fusion.152 = f32[4,544,1024]{2,1,0:T(8,128)} fusion(bf16[4,544,2048]{2,1,0:T(8,128)(2,1)} %bitcast.582, bf16[4,2048,1024]{2,1,0:T(8,128)(2,1)} %bitcast.675), kind=kOutput, calls=%fused_computation.416 | convolution fusion | flops 9126805504 | bytes 34603008 | tf_op jit(solution)/shard_map/krd,kdf->krf/dot_general | solution.py:149
  639.5 21.7 %multiply_convert_fusion.4 = (bf16[4,544,1024]{2,1,0:T(8,128)(2,1)}, f32[4,544,1024]{2,1,0:T(8,128)}) fusion(f32[4,544,1024]{2,1,0:T(8,128)} %fusion.152, bf16[4,544,2048]{2,1,0:T(8,128)(2,1)} %bitcast.583, bf16[4,2048,1024]{2,1,0:T(8,128)(2,1)} %bitcast.678), kind=kOutput, calls=%fused_computation.62 | convolution fusion | flops 9140174848 | bytes 47972352 | tf_op jit(solution)/shard_map/krd,kdf->krf/dot_general | solution.py:149
  688.4 18.5 %collective-permute-start.35 = (bf16[256,2048]{1,0:T(8,128)(2,1)}, bf16[256,2048]{1,0:T(8,128)(2,1)}, u32[]{:S(2)}, u32[]{:S(2)}) collective-permute-start(bf16[256,2048]{1,0:T(8,128)(2,1)} %get-tuple-element.411), channel_id=1, source_target_pairs={{0,8},{8,0},{16,24},{24,16},{1,9},{9,1},{17,25},{25,17},{2,10},{10... | collective-permute-start | bytes 3145736 | tf_op jit(solution)/shard_map/ppermute | solution.py:20
  746.4 32.8 %collective-permute-done.36 = bf16[256,2048]{1,0:T(8,128)(2,1)} collective-permute-done((bf16[256,2048]{1,0:T(8,128)(2,1)}, bf16[256,2048]{1,0:T(8,128)(2,1)}, u32[]{:S(2)}, u32[]{:S(2)}) %collective-permute-start.36) | collective-permute-done | bytes 1048608 | tf_op jit(solution)/shard_map/ppermute | solution.py:20
  785.8 17.6 %collective-permute-start.45 = (bf16[256,2048]{1,0:T(8,128)(2,1)S(1)}, bf16[256,2048]{1,0:T(8,128)(2,1)S(1)}, u32[]{:S(2)}, u32[]{:S(2)}) collective-permute-start(bf16[256,2048]{1,0:T(8,128)(2,1)S(1)} %get-tuple-element.376), channel_id=1, source_target_pairs={{0,8},{8,0},{16,24},{24,16},{1,9},{9,1},{17,25},{25,17},{2,10},{10... | collective-permute-start | bytes 3145736 | tf_op jit(solution)/shard_map/ppermute | solution.py:20
  806.7 35.5 %collective-permute-done.45 = bf16[256,2048]{1,0:T(8,128)(2,1)S(1)} collective-permute-done((bf16[256,2048]{1,0:T(8,128)(2,1)S(1)}, bf16[256,2048]{1,0:T(8,128)(2,1)S(1)}, u32[]{:S(2)}, u32[]{:S(2)}) %collective-permute-start.45) | collective-permute-done | bytes 1048608 | tf_op jit(solution)/shard_map/ppermute | solution.py:20
  842.3 33.0 %collective-permute-done.46 = bf16[256,2048]{1,0:T(8,128)(2,1)S(1)} collective-permute-done((bf16[256,2048]{1,0:T(8,128)(2,1)S(1)}, bf16[256,2048]{1,0:T(8,128)(2,1)S(1)}, u32[]{:S(2)}, u32[]{:S(2)}) %collective-permute-start.46) | collective-permute-done | bytes 1048608 | tf_op jit(solution)/shard_map/ppermute | solution.py:20
  886.6 23.6 %multiply_convert_fusion.2 = (bf16[4,544,1024]{2,1,0:T(8,128)(2,1)}, bf16[4,544,1024]{2,1,0:T(8,128)(2,1)}) fusion(f32[4,544,1024]{2,1,0:T(8,128)} %fusion.152, f32[4,544,1024]{2,1,0:T(8,128)} %get-tuple-element.482, bf16[4,544,2048]{2,1,0:T(8,128)(2,1)} %fusion.36, bf16[4,2048,1024]{2,1,0:T(8,128)(2,1)} %bitcast.681), kind=kOutput, calls=%fused_computation.60 | convolution fusion | flops 9155772416 | bytes 52428800 | tf_op jit(solution)/shard_map/krd,kdf->krf/dot_general | solution.py:149
  910.1 20.5 %convolution_convert_fusion.2 = bf16[4,2048,1024]{2,1,0:T(8,128)(2,1)} fusion(bf16[4,544,2048]{2,1,0:T(8,128)(2,1)} %bitcast.584, bf16[4,544,1024]{2,1,0:T(8,128)(2,1)} %get-tuple-element.388), kind=kOutput, calls=%fused_computation.54 | convolution fusion | flops 9135194112 | bytes 30146560 | tf_op jit(solution)/shard_map/krd,krf->kdf/dot_general | solution.py:149
  930.7 20.6 %convolution_convert_fusion = bf16[4,2048,1024]{2,1,0:T(8,128)(2,1)} fusion(bf16[4,544,2048]{2,1,0:T(8,128)(2,1)} %fusion.36, bf16[4,544,1024]{2,1,0:T(8,128)(2,1)} %get-tuple-element.481), kind=kOutput, calls=%fused_computation.52 | convolution fusion | flops 9135194112 | bytes 30146560 | tf_op jit(solution)/shard_map/krd,krf->kdf/dot_general | solution.py:149
  952.6 21.2 %fusion.153 = f32[4,544,2048]{2,1,0:T(8,128)} fusion(bf16[4,544,1024]{2,1,0:T(8,128)(2,1)} %get-tuple-element.388, bf16[4,2048,1024]{2,1,0:T(8,128)(2,1)} %bitcast.676), kind=kOutput, calls=%fused_computation.417 | convolution fusion | flops 9126805504 | bytes 39059456 | tf_op jit(solution)/shard_map/krf,kdf->krd/dot_general | solution.py:149
  1017.7 21.0 %convolution_convert_fusion.1 = bf16[4,2048,1024]{2,1,0:T(8,128)(2,1)} fusion(bf16[4,544,2048]{2,1,0:T(8,128)(2,1)} %bitcast.585, bf16[4,544,1024]{2,1,0:T(8,128)(2,1)} %get-tuple-element.387), kind=kOutput, calls=%fused_computation.53 | convolution fusion | flops 9135194112 | bytes 30146560 | tf_op jit(solution)/shard_map/krd,krf->kdf/dot_general | solution.py:149
  1052.4 34.5 %collective-permute-done.49 = bf16[256,2048]{1,0:T(8,128)(2,1)} collective-permute-done((bf16[256,2048]{1,0:T(8,128)(2,1)}, bf16[256,2048]{1,0:T(8,128)(2,1)}, u32[]{:S(2)}, u32[]{:S(2)}) %collective-permute-start.49) | collective-permute-done | bytes 1048608 | tf_op jit(solution)/shard_map/ppermute | solution.py:20
  1100.6 41.1 %collective-permute-done.51 = bf16[256,2048]{1,0:T(8,128)(2,1)S(1)} collective-permute-done((bf16[256,2048]{1,0:T(8,128)(2,1)S(1)}, bf16[256,2048]{1,0:T(8,128)(2,1)S(1)}, u32[]{:S(2)}, u32[]{:S(2)}) %collective-permute-start.51) | collective-permute-done | bytes 1048608 | tf_op jit(solution)/shard_map/ppermute | solution.py:20
  1145.0 31.4 %collective-permute-done.53 = bf16[256,2048]{1,0:T(8,128)(2,1)S(1)} collective-permute-done((bf16[256,2048]{1,0:T(8,128)(2,1)S(1)}, bf16[256,2048]{1,0:T(8,128)(2,1)S(1)}, u32[]{:S(2)}, u32[]{:S(2)}) %collective-permute-start.53) | collective-permute-done | bytes 1048608 | tf_op jit(solution)/shard_map/ppermute | solution.py:20
  1186.0 21.3 %collective-permute-start.57 = (bf16[256,1024]{1,0:T(8,128)(2,1)S(1)}, bf16[256,1024]{1,0:T(8,128)(2,1)S(1)}, u32[]{:S(2)}, u32[]{:S(2)}) collective-permute-start(bf16[256,1024]{1,0:T(8,128)(2,1)S(1)} %get-tuple-element.425), channel_id=1, source_target_pairs={{0,8},{8,0},{16,24},{24,16},{1,9},{9,1},{17,25},{25,17},{2,10},{10... | collective-permute-start | bytes 1572872 | tf_op jit(solution)/shard_map/ppermute | solution.py:20
  1232.1 28.8 %collective-permute-done.58 = bf16[256,1024]{1,0:T(8,128)(2,1)S(1)} collective-permute-done((bf16[256,1024]{1,0:T(8,128)(2,1)}, bf16[256,1024]{1,0:T(8,128)(2,1)S(1)}, u32[]{:S(2)}, u32[]{:S(2)}) %collective-permute-start.58) | collective-permute-done | bytes 524320 | tf_op jit(solution)/shard_map/ppermute | solution.py:20
  1276.9 55.8 %collective-permute-done.55 = bf16[256,1024]{1,0:T(8,128)(2,1)} collective-permute-done((bf16[256,1024]{1,0:T(8,128)(2,1)}, bf16[256,1024]{1,0:T(8,128)(2,1)}, u32[]{:S(2)}, u32[]{:S(2)}) %collective-permute-start.55) | collective-permute-done | bytes 524320 | tf_op jit(solution)/shard_map/ppermute | solution.py:20
  1343.9 49.1 %while.28 = (s32[]{:T(128)}, f32[1024,4,128]{0,2,1:T(8,128)S(1)}, f32[1024,4,128]{0,2,1:T(8,128)}, f32[2,512,4,128]{3,1,2,0:T(8,128)}, s32[2]{0:T(128)S(1)}, /*i...) while((s32[]{:T(128)}, f32[1024,4,128]{0,2,1:T(8,128)S(1)}, ...), condition=%wide.region_20.21_spmd.clone, body=%wide.region_18.20_spmd.clone.sunk | while | flops 2720266752 | bytes 180427760 | solution.py:142
  1490.5 35.4 %collective-permute-done.79 = bf16[256,1024]{1,0:T(8,128)(2,1)S(1)} collective-permute-done((bf16[256,1024]{1,0:T(8,128)(2,1)}, bf16[256,1024]{1,0:T(8,128)(2,1)S(1)}, u32[]{:S(2)}, u32[]{:S(2)}) %collective-permute-start.79) | collective-permute-done | bytes 524320 | tf_op jit(solution)/shard_map/ppermute | solution.py:20
  1593.2 21.2 %collective-permute-done.64 = bf16[256,2048]{1,0:T(8,128)(2,1)} collective-permute-done((bf16[256,2048]{1,0:T(8,128)(2,1)}, bf16[256,2048]{1,0:T(8,128)(2,1)}, u32[]{:S(2)}, u32[]{:S(2)}) %collective-permute-start.64) | collective-permute-done | bytes 1048608 | tf_op jit(solution)/shard_map/ppermute | solution.py:20
  1618.8 35.0 %collective-permute-start.72 = (f32[4,2048]{1,0:T(4,128)S(1)}, f32[4,2048]{1,0:T(4,128)S(1)}, u32[]{:S(2)}, u32[]{:S(2)}) collective-permute-start(f32[4,2048]{1,0:T(4,128)S(1)} %pad_maximum_fusion.4), channel_id=1, source_target_pairs={{0,8},{8,0},{16,24},{24,16},{1,9},{9,1},{17,25},{25,17},{2,10},{10... | collective-permute-start | bytes 98312 | tf_op jit(solution)/shard_map/ppermute | solution.py:20
  1659.4 19.5 %copy.375 = f32[256,4,3072]{2,1,0:T(4,128)} copy(f32[256,4,3072]{2,0,1:T(8,128)S(1)} %convert_bitcast_fusion) | data formatting | bytes 25165824
  (733 shorter events, 833.1 us)
Async XLA Ops:
  7.2 334.9 %all-gather.4.cloned.1.call-start = ((), (), s32[]{:S(2)}) async-start(), calls=%async_computation.5 | async-start | bytes 18874368 | tf_op jit(solution)/shard_map/all_gather | solution.py:205
  58.4 482.8 %all-gather.6.cloned.1.call-start = ((), (), s32[]{:S(2)}) async-start(), calls=%async_computation.6 | async-start | bytes 18874368 | tf_op jit(solution)/shard_map/all_gather | solution.py:205
  99.4 59.6 %collective-permute-start.10 = (bf16[256,1664]{1,0:T(8,128)(2,1)}, bf16[256,1664]{1,0:T(8,128)(2,1)}, u32[]{:S(2)}, u32[]{:S(2)}) collective-permute-start(bf16[256,1664]{1,0:T(8,128)(2,1)} %pad_maximum_fusion), channel_id=1, source_target_pairs={{0,16},{8,24},{16,0},{24,8},{1,17},{9,25},{17,1},{25,9},{2,18},{10... | collective-permute-start | bytes 2555912 | tf_op jit(solution)/shard_map/ppermute | solution.py:20
  104.2 68.5 %collective-permute-start = (bf16[256,2048]{1,0:T(8,128)(2,1)S(1)}, bf16[256,2048]{1,0:T(8,128)(2,1)}, u32[]{:S(2)}, u32[]{:S(2)}) collective-permute-start(bf16[256,2048]{1,0:T(8,128)(2,1)S(1)} %reshape.551), channel_id=1, source_target_pairs={{0,1},{1,0},{2,3},{3,2},{4,5},{5,4},{6,7},{7,6},{8,9},{9,8},{10,11... | collective-permute-start | bytes 3145736 | tf_op jit(solution)/shard_map/ppermute | solution.py:20
  106.7 54.4 %collective-permute-start.11 = (bf16[256,1664]{1,0:T(8,128)(2,1)}, bf16[256,1664]{1,0:T(8,128)(2,1)S(1)}, u32[]{:S(2)}, u32[]{:S(2)}) collective-permute-start(bf16[256,1664]{1,0:T(8,128)(2,1)} %pad_maximum_fusion), channel_id=1, source_target_pairs={{0,24},{8,16},{16,8},{24,0},{1,25},{9,17},{17,9},{25,1},{2,26},{10... | collective-permute-start | bytes 2555912 | tf_op jit(solution)/shard_map/ppermute | solution.py:20
  162.1 74.1 %collective-permute-start.12 = (bf16[4,256,1664]{2,1,0:T(8,128)(2,1)}, bf16[4,256,1664]{2,1,0:T(8,128)(2,1)}, u32[]{:S(2)}, u32[]{:S(2)}) collective-permute-start(bf16[4,256,1664]{2,1,0:T(8,128)(2,1)} %bitcast_dynamic-update-slice_fusion.10), channel_id=1, source_target_pairs={{0,4},{4,0},{1,5},{5,1},{2,6},{6,2},{3,7},{7,3},{8,12},{12,8},{9,1... | collective-permute-start | bytes 10223624 | tf_op jit(solution)/shard_map/ppermute | solution.py:20
  162.1 52.0 %collective-permute-start.1 = (bf16[256,2048]{1,0:T(8,128)(2,1)S(1)}, bf16[256,2048]{1,0:T(8,128)(2,1)}, u32[]{:S(2)}, u32[]{:S(2)}) collective-permute-start(bf16[256,2048]{1,0:T(8,128)(2,1)S(1)} %reshape.551), channel_id=1, source_target_pairs={{0,2},{1,3},{2,0},{3,1},{4,6},{5,7},{6,4},{7,5},{8,10},{9,11},{10,... | collective-permute-start | bytes 3145736 | tf_op jit(solution)/shard_map/ppermute | solution.py:20
  162.6 53.8 %collective-permute-start.2 = (bf16[256,2048]{1,0:T(8,128)(2,1)S(1)}, bf16[256,2048]{1,0:T(8,128)(2,1)}, u32[]{:S(2)}, u32[]{:S(2)}) collective-permute-start(bf16[256,2048]{1,0:T(8,128)(2,1)S(1)} %reshape.551), channel_id=1, source_target_pairs={{0,3},{1,2},{2,1},{3,0},{4,7},{5,6},{6,5},{7,4},{8,11},{9,10},{10,... | collective-permute-start | bytes 3145736 | tf_op jit(solution)/shard_map/ppermute | solution.py:20
  378.0 283.2 %all-gather.8.cloned.1.call-start = ((), (), s32[]{:S(2)}) async-start(), calls=%async_computation.7 | async-start | bytes 18874368 | tf_op jit(solution)/shard_map/all_gather | solution.py:205
  426.5 90.4 %collective-permute-start.25 = (bf16[256,2048]{1,0:T(8,128)(2,1)S(1)}, bf16[256,2048]{1,0:T(8,128)(2,1)S(1)}, u32[]{:S(2)}, u32[]{:S(2)}) collective-permute-start(bf16[256,2048]{1,0:T(8,128)(2,1)S(1)} %get-tuple-element.415), channel_id=1, source_target_pairs={{0,3},{1,2},{2,1},{3,0},{4,7},{5,6},{6,5},{7,4},{8,11},{9,10},{10,... | collective-permute-start | bytes 3145736 | tf_op jit(solution)/shard_map/ppermute | solution.py:20
  524.9 658.3 %reduce-scatter.8.cloned.1.call-start = ((), (), s32[]{:S(2)}) async-start(), calls=%async_computation.9 | async-start | bytes 18874368 | tf_op jit(solution)/shard_map/reduce_scatter | solution.py:324
  534.4 72.1 %collective-permute-start.33 = (bf16[256,2048]{1,0:T(8,128)(2,1)S(1)}, bf16[256,2048]{1,0:T(8,128)(2,1)}, u32[]{:S(2)}, u32[]{:S(2)}) collective-permute-start(bf16[256,2048]{1,0:T(8,128)(2,1)S(1)} %multiply_convert_fusion.8), channel_id=1, source_target_pairs={{0,16},{8,24},{16,0},{24,8},{1,17},{9,25},{17,1},{25,9},{2,18},{10... | collective-permute-start | bytes 3145736 | tf_op jit(solution)/shard_map/ppermute | solution.py:20
  536.3 70.3 %collective-permute-start.34 = (bf16[256,2048]{1,0:T(8,128)(2,1)S(1)}, bf16[256,2048]{1,0:T(8,128)(2,1)}, u32[]{:S(2)}, u32[]{:S(2)}) collective-permute-start(bf16[256,2048]{1,0:T(8,128)(2,1)S(1)} %multiply_convert_fusion.8), channel_id=1, source_target_pairs={{0,24},{8,16},{16,8},{24,0},{1,25},{9,17},{17,9},{25,1},{2,26},{10... | collective-permute-start | bytes 3145736 | tf_op jit(solution)/shard_map/ppermute | solution.py:20
  688.4 58.0 %collective-permute-start.35 = (bf16[256,2048]{1,0:T(8,128)(2,1)}, bf16[256,2048]{1,0:T(8,128)(2,1)}, u32[]{:S(2)}, u32[]{:S(2)}) collective-permute-start(bf16[256,2048]{1,0:T(8,128)(2,1)} %get-tuple-element.411), channel_id=1, source_target_pairs={{0,8},{8,0},{16,24},{24,16},{1,9},{9,1},{17,25},{25,17},{2,10},{10... | collective-permute-start | bytes 3145736 | tf_op jit(solution)/shard_map/ppermute | solution.py:20
  706.9 72.3 %collective-permute-start.36 = (bf16[256,2048]{1,0:T(8,128)(2,1)}, bf16[256,2048]{1,0:T(8,128)(2,1)}, u32[]{:S(2)}, u32[]{:S(2)}) collective-permute-start(bf16[256,2048]{1,0:T(8,128)(2,1)} %get-tuple-element.413), channel_id=1, source_target_pairs={{0,16},{8,24},{16,0},{24,8},{1,17},{9,25},{17,1},{25,9},{2,18},{10... | collective-permute-start | bytes 3145736 | tf_op jit(solution)/shard_map/ppermute | solution.py:20
  707.9 71.3 %collective-permute-start.37 = (bf16[256,2048]{1,0:T(8,128)(2,1)}, bf16[256,2048]{1,0:T(8,128)(2,1)}, u32[]{:S(2)}, u32[]{:S(2)}) collective-permute-start(bf16[256,2048]{1,0:T(8,128)(2,1)} %get-tuple-element.412), channel_id=1, source_target_pairs={{0,24},{8,16},{16,8},{24,0},{1,25},{9,17},{17,9},{25,1},{2,26},{10... | collective-permute-start | bytes 3145736 | tf_op jit(solution)/shard_map/ppermute | solution.py:20
  785.8 56.5 %collective-permute-start.45 = (bf16[256,2048]{1,0:T(8,128)(2,1)S(1)}, bf16[256,2048]{1,0:T(8,128)(2,1)S(1)}, u32[]{:S(2)}, u32[]{:S(2)}) collective-permute-start(bf16[256,2048]{1,0:T(8,128)(2,1)S(1)} %get-tuple-element.376), channel_id=1, source_target_pairs={{0,8},{8,0},{16,24},{24,16},{1,9},{9,1},{17,25},{25,17},{2,10},{10... | collective-permute-start | bytes 3145736 | tf_op jit(solution)/shard_map/ppermute | solution.py:20
  803.4 71.9 %collective-permute-start.46 = (bf16[256,2048]{1,0:T(8,128)(2,1)S(1)}, bf16[256,2048]{1,0:T(8,128)(2,1)S(1)}, u32[]{:S(2)}, u32[]{:S(2)}) collective-permute-start(bf16[256,2048]{1,0:T(8,128)(2,1)S(1)} %get-tuple-element.376), channel_id=1, source_target_pairs={{0,16},{8,24},{16,0},{24,8},{1,17},{9,25},{17,1},{25,9},{2,18},{10... | collective-permute-start | bytes 3145736 | tf_op jit(solution)/shard_map/ppermute | solution.py:20
  805.3 70.0 %collective-permute-start.47 = (bf16[256,2048]{1,0:T(8,128)(2,1)S(1)}, bf16[256,2048]{1,0:T(8,128)(2,1)S(1)}, u32[]{:S(2)}, u32[]{:S(2)}) collective-permute-start(bf16[256,2048]{1,0:T(8,128)(2,1)S(1)} %get-tuple-element.376), channel_id=1, source_target_pairs={{0,24},{8,16},{16,8},{24,0},{1,25},{9,17},{17,9},{25,1},{2,26},{10... | collective-permute-start | bytes 3145736 | tf_op jit(solution)/shard_map/ppermute | solution.py:20
  930.7 289.8 %reduce-scatter.6.cloned.1.call-start = ((), (), s32[]{:S(2)}) async-start(), calls=%async_computation.8 | async-start | bytes 18874368 | tf_op jit(solution)/shard_map/reduce_scatter | solution.py:324
  951.4 518.0 %reduce-scatter.12.cloned.1.call-start = ((), (), s32[]{:S(2)}) async-start(), calls=%async_computation.11 | async-start | bytes 2359296 | tf_op jit(solution)/shard_map/reduce_scatter | solution.py:352
  997.6 54.9 %collective-permute-start.48 = (bf16[256,2048]{1,0:T(8,128)(2,1)}, bf16[256,2048]{1,0:T(8,128)(2,1)S(1)}, u32[]{:S(2)}, u32[]{:S(2)}) collective-permute-start(bf16[256,2048]{1,0:T(8,128)(2,1)} %get-tuple-element.408), channel_id=1, source_target_pairs={{0,8},{8,0},{16,24},{24,16},{1,9},{9,1},{17,25},{25,17},{2,10},{10... | collective-permute-start | bytes 3145736 | tf_op jit(solution)/shard_map/ppermute | solution.py:20
  1014.7 72.3 %collective-permute-start.49 = (bf16[256,2048]{1,0:T(8,128)(2,1)}, bf16[256,2048]{1,0:T(8,128)(2,1)}, u32[]{:S(2)}, u32[]{:S(2)}) collective-permute-start(bf16[256,2048]{1,0:T(8,128)(2,1)} %get-tuple-element.410), channel_id=1, source_target_pairs={{0,16},{8,24},{16,0},{24,8},{1,17},{9,25},{17,1},{25,9},{2,18},{10... | collective-permute-start | bytes 3145736 | tf_op jit(solution)/shard_map/ppermute | solution.py:20
  1016.2 70.8 %collective-permute-start.50 = (bf16[256,2048]{1,0:T(8,128)(2,1)}, bf16[256,2048]{1,0:T(8,128)(2,1)}, u32[]{:S(2)}, u32[]{:S(2)}) collective-permute-start(bf16[256,2048]{1,0:T(8,128)(2,1)} %get-tuple-element.409), channel_id=1, source_target_pairs={{0,24},{8,16},{16,8},{24,0},{1,25},{9,17},{17,9},{25,1},{2,26},{10... | collective-permute-start | bytes 3145736 | tf_op jit(solution)/shard_map/ppermute | solution.py:20
  1099.7 76.7 %collective-permute-start.53 = (bf16[256,2048]{1,0:T(8,128)(2,1)S(1)}, bf16[256,2048]{1,0:T(8,128)(2,1)S(1)}, u32[]{:S(2)}, u32[]{:S(2)}) collective-permute-start(bf16[256,2048]{1,0:T(8,128)(2,1)S(1)} %get-tuple-element.373), channel_id=1, source_target_pairs={{0,3},{1,2},{2,1},{3,0},{4,7},{5,6},{6,5},{7,4},{8,11},{9,10},{10,... | collective-permute-start | bytes 3145736 | tf_op jit(solution)/shard_map/ppermute | solution.py:20
  1182.4 293.5 %reduce-scatter.14.cloned.1.call-start = ((), (), s32[]{:S(2)}) async-start(), calls=%async_computation.12 | async-start | bytes 18874368 | tf_op jit(solution)/shard_map/reduce_scatter | solution.py:324
  1183.1 501.3 %reduce-scatter.10.cloned.1.call-start = ((), (), s32[]{:S(2)}) async-start(), calls=%async_computation.10 | async-start | bytes 7077888 | tf_op jit(solution)/shard_map/reduce_scatter | solution.py:352
  1224.9 107.8 %collective-permute-start.55 = (bf16[256,1024]{1,0:T(8,128)(2,1)}, bf16[256,1024]{1,0:T(8,128)(2,1)}, u32[]{:S(2)}, u32[]{:S(2)}) collective-permute-start(bf16[256,1024]{1,0:T(8,128)(2,1)} %get-tuple-element.430), channel_id=1, source_target_pairs={{0,16},{8,24},{16,0},{24,8},{1,17},{9,25},{17,1},{25,9},{2,18},{10... | collective-permute-start | bytes 1572872 | tf_op jit(solution)/shard_map/ppermute | solution.py:20
  1227.3 107.3 %collective-permute-start.56 = (bf16[256,1024]{1,0:T(8,128)(2,1)}, bf16[256,1024]{1,0:T(8,128)(2,1)}, u32[]{:S(2)}, u32[]{:S(2)}) collective-permute-start(bf16[256,1024]{1,0:T(8,128)(2,1)} %get-tuple-element.429), channel_id=1, source_target_pairs={{0,24},{8,16},{16,8},{24,0},{1,25},{9,17},{17,9},{25,1},{2,26},{10... | collective-permute-start | bytes 1572872 | tf_op jit(solution)/shard_map/ppermute | solution.py:20
  1478.8 55.2 %collective-permute-start.80 = (bf16[256,1024]{1,0:T(8,128)(2,1)}, bf16[256,1024]{1,0:T(8,128)(2,1)}, u32[]{:S(2)}, u32[]{:S(2)}) collective-permute-start(bf16[256,1024]{1,0:T(8,128)(2,1)} %get-tuple-element.418), channel_id=1, source_target_pairs={{0,16},{8,24},{16,0},{24,8},{1,17},{9,25},{17,1},{25,9},{2,18},{10... | collective-permute-start | bytes 1572872 | tf_op jit(solution)/shard_map/ppermute | solution.py:20
  1481.5 67.5 %collective-permute-start.81 = (bf16[256,1024]{1,0:T(8,128)(2,1)}, bf16[256,1024]{1,0:T(8,128)(2,1)}, u32[]{:S(2)}, u32[]{:S(2)}) collective-permute-start(bf16[256,1024]{1,0:T(8,128)(2,1)} %get-tuple-element.417), channel_id=1, source_target_pairs={{0,24},{8,16},{16,8},{24,0},{1,25},{9,17},{17,9},{25,1},{2,26},{10... | collective-permute-start | bytes 1572872 | tf_op jit(solution)/shard_map/ppermute | solution.py:20
  1618.8 60.1 %collective-permute-start.72 = (f32[4,2048]{1,0:T(4,128)S(1)}, f32[4,2048]{1,0:T(4,128)S(1)}, u32[]{:S(2)}, u32[]{:S(2)}) collective-permute-start(f32[4,2048]{1,0:T(4,128)S(1)} %pad_maximum_fusion.4), channel_id=1, source_target_pairs={{0,8},{8,0},{16,24},{24,16},{1,9},{9,1},{17,25},{25,17},{2,10},{10... | collective-permute-start | bytes 98312 | tf_op jit(solution)/shard_map/ppermute | solution.py:20
  (173 other events, 3549.4 us)
Sparse Core Ops, SparseCore 0:
  58.5 139.5 all-gather.3
  378.1 139.6 all-gather.5
  525.0 89.0 all-gather.7
  930.8 132.8 reduce-scatter.7
  1067.2 153.3 reduce-scatter.5
  1222.7 99.2 reduce-scatter.11
  1325.6 115.1 reduce-scatter.13
  1443.1 168.9 reduce-scatter.9

commit v3 on v2

--- a/solution.py
+++ b/solution.py
@@ -176,16 +176,34 @@
 
     def to_inner(v):
         lead = v.shape[:-1]
-        v = v.reshape(lead + (outer, planes, CORES, part))
+        v = v.reshape(lead + (outer * planes, CORES, part))
         return jnp.swapaxes(v, -3, -2).reshape(lead + (width,))
 
     def to_outer(v):
         lead = v.shape[:-1]
-        v = v.reshape(lead + (outer, CORES, planes, part))
+        v = v.reshape(lead + (CORES, outer * planes, part))
         return jnp.swapaxes(v, -3, -2).reshape(lead + (width,))
 
-    def gather_rows(block):
-        return collect(collect(collect(block, "z"), "c"), "o").reshape((-1,) + block.shape[1:])
+    first_core = lax.axis_index("c") == 0
+
+    def halves(v):
+        low, high = v[..., : width // 2], v[..., width // 2 :]
+        return jnp.where(first_core, low, high), jnp.where(first_core, high, low)
+
+    def whole_of(mine, other, axis):
+        low, high = jnp.where(first_core, mine, other), jnp.where(first_core, other, mine)
+        return jnp.concatenate([low, high], axis=axis)
+
+    def stack_rows(blocks, start=0):
+        rows = in_order(blocks, "z", start)
+        return collect(rows, "o").reshape((width // 2,) + rows.shape[2:])
+
+    def sum_rows(grad):
+        count = grad.shape[1]
+        grad = exchange_sum(grad.reshape(CORES, width // 2, count), "c").astype(bf16)
+        if outer > 1:
+            grad = exchange_sum(grad.reshape(outer, planes * part, count), "o").astype(bf16)
+        return exchange_sum(grad.reshape(planes, part, count), "z")
 
     def gather_sum(value):
         for axis in ("z", "s", "c", "o"):
@@ -200,13 +218,10 @@
 
         return exchange(piece_for, "z", start)
 
-    def gather_plane(blocks, start=0):
-        chunk = in_order(blocks, "z", start).reshape(planes * part, hidden)
-        chunk = lax.all_gather(chunk, ("s", "o", "c"), axis=0, tiled=True)
+    def gather_plane(ready):
+        chunk = ready.reshape(planes * part, hidden)
+        chunk = lax.all_gather(chunk, ("s", "c", "o"), axis=0, tiled=True)
         return chunk.reshape(seqs, width, hidden)
-
-    gate_blocks = expert_chunk(0)
-    w_gate = gather_plane(gate_blocks)
 
     count = jnp.sum(valid_mask).astype(jnp.int32)
     digits = jnp.stack([count // 128, count % 128]).astype(bf16)
@@ -223,19 +238,29 @@
         picked = [
             lax.dynamic_slice_in_dim(w_attn, i * width + owner * cols, cols, 1) for i in range(4)
         ]
-        return jnp.concatenate(picked + [extra], axis=1)
-
-    mine = in_order(exchange(columns_of, "s"), "s", token(*gate_blocks))
-    mine = mine.reshape(part, 4 * cols + PAD)
-    w_in = gather_rows(jnp.concatenate([mine[:, : 3 * cols], mine[:, 4 * cols :]], axis=1))
-    w_out = gather_rows(after(mine[:, 3 * cols : 4 * cols], w_in))
-    side = w_in[:, 3 * cols : 3 * cols + 6].astype(f32).T
+        return jnp.concatenate(picked[:3] + [extra] + picked[3:], axis=1)
+
+    mine_blocks = exchange(columns_of, "s")
+    gate_blocks = expert_chunk(0)
+    inputs = to_inner(tokens)
+    token_blocks = gather_near(inputs, "s")
+    inputs = inputs.astype(f32)
+
+    mine = in_order(mine_blocks, "s").reshape(part, 4 * cols + PAD)
+    in_blocks = gather_near(mine[:, : 3 * cols + PAD], "z")
+    gate_ready = in_order(gate_blocks, "z", token(mine))
+    w_gate = gather_plane(gate_ready)
+    seq_tokens = in_order(token_blocks, "s", token(gate_ready)).reshape(seq, width).astype(f32)
+    seq_factor = rms_factor(seq_tokens)
+    w_in = stack_rows(in_blocks, token(seq_factor))
+    w_in_other = send(w_in, "c", 1)
+    up_blocks = expert_chunk(1, token(w_in))
+
+    side = whole_of(w_in[:, 3 * cols :], w_in_other[:, 3 * cols :], 0)[:, :6].astype(f32).T
     gain_in, gain_mid = side[0], side[1]
     gain_q = lax.dynamic_slice_in_dim(to_outer(side[2]), rank * cols, cols, 0)
     gain_k = lax.dynamic_slice_in_dim(to_outer(side[3]), rank * cols, cols, 0)
     total_count = jnp.sum(side[4, ::rows_dev]) * 128.0 + jnp.sum(side[5, ::rows_dev])
-
-    up_blocks = expert_chunk(1, token(w_in))
 
     routed = jnp.stack(
         gather_near(jnp.concatenate([routes.astype(f32), gate_weights], axis=1), "z")
@@ -257,19 +282,21 @@
         spread = dot("bkjt,btd->kbjd", choose, rows_in)
         return spread.reshape(seqs, planes * capacity, width)
 
-    def combine(rows_out, *others):
+    def combine_rows(rows_out):
         rows_out = rows_out.reshape(seqs, planes, capacity, width)
-        partial = dot("bkjt,kbjd->btd", choose, rows_out).astype(bf16)
+        return dot("bkjt,kbjd->btd", choose, rows_out).astype(bf16)
+
+    def send_back(partial, *others):
         got = [partial[0]] + [send(partial[k], "z", k) for k in range(1, planes)]
         if others:
             got[0] = after(got[0], *others)
         return sum(piece.astype(f32) for piece in got)
 
-    inputs = to_inner(tokens)
-    seq_tokens = collect(inputs, "s").reshape(seq, width).astype(f32)
-    normed_in = (seq_tokens * rms_factor(seq_tokens) * gain_in).astype(bf16)
-    inputs = inputs.astype(f32)
-    projected = jnp.dot(normed_in, w_in, preferred_element_type=f32)
+    normed_in = (seq_tokens * seq_factor * gain_in).astype(bf16)
+    normed_mine, normed_other = halves(normed_in)
+    projected = jnp.dot(normed_mine, w_in, preferred_element_type=f32) + jnp.dot(
+        normed_other, w_in_other, preferred_element_type=f32
+    )
     query_raw = projected[:, :cols]
     key_raw = projected[:, cols : 2 * cols]
     valued = projected[:, 2 * cols : 3 * cols].astype(bf16).reshape(seq, heads, HD)
@@ -289,15 +316,18 @@
 
     query, keyed = rope(query_raw, q_factor, gain_q), rope(key_raw, k_factor, gain_k)
     query = after(query, w_gate)
+    up_ready = in_order(up_blocks, "z", token(keyed))
+    keyed = after(keyed, up_ready)
+    w_up = gather_plane(up_ready)
+    out_blocks = gather_near(after(mine[:, 3 * cols + PAD :], up_ready), "z")
     attended, log_total = attend_forward(query, keyed, valued, segment, block_rows, scale)
-    attended = after(attended, *up_blocks)
-    w_up = gather_plane(up_blocks, token(attended))
+    w_out = collect(stack_rows(out_blocks, token(attended)), "c").reshape(width, cols)
     down_blocks = expert_chunk(2, token(attended))
     attn_out = dot("tc,dc->td", attended, w_out).astype(bf16)
     residual = inputs + exchange_sum(attn_out.reshape(seqs, own, width), "s")
-
-    residual = after(residual, *down_blocks)
-    w_down = gather_plane(down_blocks, token(residual))
+    down_ready = in_order(down_blocks, "z", token(residual))
+    residual = after(residual, down_ready)
+    w_down = gather_plane(down_ready)
 
     normed_mid = (residual * rms_factor(residual) * gain_mid).astype(bf16)
     rows_in = dispatch(after(jnp.stack(gather_near(normed_mid, "z")), w_up)).astype(bf16)
@@ -305,7 +335,7 @@
     up_pre = dot("krd,kdf->krf", rows_in, w_up)
     activated = (jax.nn.silu(gate_pre) * up_pre).astype(bf16)
     expert_out = (dot("krf,kdf->krd", activated, w_down) * gate_slot).astype(bf16)
-    final_out = residual + combine(expert_out)
+    final_out = residual + send_back(combine_rows(expert_out))
 
     valid_f = valid_mask.astype(f32)[:, None]
     difference = final_out - to_inner(teacher).astype(f32)
@@ -321,7 +351,7 @@
 
     def scatter_expert(grad):
         grad = grad.reshape(seqs * width, hidden)
-        grad = lax.psum_scatter(grad, ("s", "o", "c"), scatter_dimension=0, tiled=True)
+        grad = lax.psum_scatter(grad, ("s", "c", "o"), scatter_dimension=0, tiled=True)
         return grad.reshape(planes, part, hidden)
 
     def to_owners(grad, start=0):
@@ -336,24 +366,19 @@
     grad_gate = (grad_act * up_pre * sigmoid * (1.0 + gate_pre * (1.0 - sigmoid))).astype(bf16)
     grad_up = (grad_act * gate_pre * sigmoid).astype(bf16)
     back_rows = dot("krf,kdf->krd", grad_gate, w_gate) + dot("krf,kdf->krd", grad_up, w_up)
+    back_rows = combine_rows(back_rows.astype(bf16))
+    grad_gate, grad_up = after(grad_gate, back_rows), after(grad_up, back_rows)
     grad_w_gate = dot("krd,krf->kdf", rows_in, grad_gate).astype(bf16)
     grad_w_up = dot("krd,krf->kdf", rows_in, grad_up).astype(bf16)
-    grad_mid = combine(back_rows.astype(bf16), grad_w_gate, grad_w_up)
+    grad_mid = send_back(back_rows, grad_w_gate, grad_w_up)
     grad_w_gate, grad_w_up = scatter_expert(grad_w_gate), scatter_expert(grad_w_up)
-    down_part = to_owners(grad_w_down, token(grad_mid))
-    gate_part = to_owners(grad_w_gate)
-    up_part = to_owners(grad_w_up)
-
+    down_blocks = to_owners(grad_w_down, token(grad_mid))
+    gate_blocks = to_owners(grad_w_gate)
     grad_resid_norm, gain_mid_grad = norm_back(residual, gain_mid, grad_mid)
     grad_resid = grad_out + grad_resid_norm
 
-    def scatter_rows(grad):
-        grad = grad.astype(bf16)
-        return lax.psum_scatter(grad, ("o", "c", "z"), scatter_dimension=0, tiled=True)
-
     grad_attn_out = collect(grad_resid.astype(bf16), "s").reshape(seq, width)
-    grad_w_out = scatter_rows(dot("td,tc->dc", grad_attn_out, attended))
-    grad_attn_out = after(grad_attn_out, *down_part)
+    grad_w_out = sum_rows(dot("td,tc->dc", grad_attn_out, attended).astype(bf16))
     grad_heads = jnp.dot(grad_attn_out, w_out, preferred_element_type=f32).astype(bf16)
     grad_q, grad_k, grad_v = attend_backward(
         query,
@@ -370,8 +395,8 @@
         grad = grad.astype(bf16).astype(f32)
         return (grad * cosine + rotate_back(grad * sine)).reshape(seq, cols)
 
-    down_part = in_order(down_part, "z", token(grad_q))
-    grad_q = after(grad_q, *gate_part)
+    down_ready = in_order(down_blocks, "z", token(grad_q))
+    grad_q = after(grad_q, down_ready)
     grad_q, grad_k = unrotate(grad_q), unrotate(grad_k)
     q_normed, k_normed = query_raw * q_factor, key_raw * k_factor
     gain_q_grad = jnp.sum(grad_q * q_normed, axis=0)
@@ -383,13 +408,17 @@
     grad_proj = jnp.concatenate(
         [grad_q.astype(bf16), grad_k.astype(bf16), grad_v.reshape(seq, cols).astype(bf16)], axis=1
     )
-    gate_part = in_order(gate_part, "z", token(grad_proj))
     grad_padded = jnp.concatenate([grad_proj, jnp.zeros((seq, PAD), bf16)], axis=1)
-    grad_normed = dot("tc,dc->td", grad_padded, w_in).astype(bf16)
-    grad_normed = exchange_sum(grad_normed.reshape(seqs, own, width), "s")
-    grad_w_qkv = scatter_rows(
-        dot("td,tc->dc", normed_in, grad_proj)
-    )
+
+    def back_half(weight):
+        grad = dot("tc,dc->td", grad_padded, weight).astype(bf16)
+        return exchange_sum(grad.reshape(seqs, own, width // 2), "s")
+
+    grad_normed = whole_of(back_half(w_in), back_half(w_in_other), 1)
+    grad_w_qkv = dot("td,tc->dc", normed_in, grad_proj).astype(bf16)
+    gate_ready = in_order(gate_blocks, "z", token(grad_w_qkv))
+    grad_w_qkv = sum_rows(grad_w_qkv)
+    up_blocks = to_owners(grad_w_up, token(grad_w_qkv))
     grad_in_norm, gain_in_grad = norm_back(inputs, gain_in, grad_normed)
     grad_tokens = to_outer(grad_resid + grad_in_norm)
 
@@ -400,11 +429,11 @@
     gains = jnp.stack([gain_in_grad, gain_mid_grad, widen(gain_q_grad), widen(gain_k_grad)])
     for axis in ("z", "c", "s", "o"):
         gains = sum(gather_near(gains, axis))
-    row = (lax.axis_index(("o", "c", "z")) * seqs + rank) * rows_dev
+    row = (lax.axis_index(("c", "o", "z")) * seqs + rank) * rows_dev
     grad_gains = lax.dynamic_slice_in_dim(gains, row, rows_dev, 1).T
 
     def own_rows(grad):
-        grad = grad.reshape(seqs, rows_dev, grad.shape[1])
+        grad = grad.astype(bf16).reshape(seqs, rows_dev, grad.shape[1])
         got = exchange(lambda i: lax.dynamic_index_in_dim(grad, i, 0, keepdims=False), "s")
         return in_order(got, "s").astype(f32)
 
@@ -414,8 +443,8 @@
         + [out_rows[s] for s in range(seqs)],
         axis=1,
     )
-    up_part = in_order(up_part, "z")
-    grad_expert = jnp.concatenate([gate_part, up_part, down_part], axis=2)
+    up_ready = in_order(up_blocks, "z")
+    grad_expert = jnp.concatenate([gate_ready, up_ready, down_ready], axis=2)
     grad_expert = grad_expert.astype(f32).transpose(1, 0, 2)
     return (
         to_outer(final_out).astype(bf16),

time: 1730 us -> 1510 us (0.87)
  waiting for transfers between devices: 759 us -> 552 us
  local copies, waits for them, and re-layouts: 276 us -> 257 us
    ppermute x82 -> x93, waiting for transfers between devices: 750 us -> 552 us  [send(): return lax.ppermute(block, axis, [(i, i ^ step) for i in range(size)])]
    ppermute x82 -> x93, starting transfers between devices: 246 us -> 236 us  [send(): return lax.ppermute(block, axis, [(i, i ^ step) for i in range(size)])]
    dynamic_update_slice x50 -> x47, local copies, waits for them, and re-layouts: 44.6 us -> 49.6 us  [in_order(): lax.dynamic_update_index_in_dim(stacked, block, (rank ^ k) + start, 0)]
    dot_general x18 -> x19, matrix products: 227 us -> 231 us  [dot(): return jnp.einsum(spec, left, right, preferred_element_type=f32)]
    unnamed x231 -> x217, local copies, waits for them, and re-layouts: 54.3 us -> 52.9 us
  transfers between devices with their start and end apart: 90 -> 99, of which waited for: 42 -> 41; matrix products, arithmetic and copies ran while one was open for 30% -> 36% of each run, Pallas kernels for 0% -> 0%
where the time goes in v3:
time: 1510 us; the launch traced here: 1490 us
  waiting for transfers between devices  552 us (37%)
  matrix products  294 us (19%)
  local copies, waits for them, and re-layouts  257 us (17%)
  starting transfers between devices  236 us (16%)
  other arithmetic  103 us (7%)
  between operations  46.2 us (3%)
    ppermute x93, waiting for transfers between devices, send(): return lax.ppermute(block, axis, [(i, i ^ step) for i in range(size)])  552 us
    ppermute x93, starting transfers between devices, send(): return lax.ppermute(block, axis, [(i, i ^ step) for i in range(size)])  236 us
    dot_general x19, matrix products, dot(): return jnp.einsum(spec, left, right, preferred_element_type=f32)  231 us
    unnamed x217, local copies, waits for them, and re-layouts  52.9 us
    dynamic_update_slice x47, local copies, waits for them, and re-layouts, in_order(): lax.dynamic_update_index_in_dim(stacked, block, (rank ^ k) + start, 0)  49.6 us
  transfers between devices with their start and end apart: 99, of which 41 were waited for; matrix products, arithmetic and copies ran while one was open for 36% of the time, Pallas kernels for 0%

profile of v3, /device:TPU:0, one launch (start us, length us, event | category | flops | bytes accessed | tf_op | source)
XLA Modules:
  0.0 1492.2 jit_solution(9435074793400410942)
XLA Ops:
  53.4 17.5 %collective-permute-done.4 = bf16[256,1024]{1,0:T(8,128)(2,1)} collective-permute-done((bf16[256,1024]{1,0:T(8,128)(2,1)}, bf16[256,1024]{1,0:T(8,128)(2,1)}, u32[]{:S(2)}, u32[]{:S(2)}) %collective-permute-start.4) | collective-permute-done | bytes 524320 | tf_op jit(solution)/shard_map/ppermute | solution.py:20
  123.5 18.9 %collective-permute-done.8 = bf16[256,2048]{1,0:T(8,128)(2,1)} collective-permute-done((bf16[256,2048]{1,0:T(8,128)(2,1)S(1)}, bf16[256,2048]{1,0:T(8,128)(2,1)}, u32[]{:S(2)}, u32[]{:S(2)}) %collective-permute-start.8) | collective-permute-done | bytes 1048608 | tf_op jit(solution)/shard_map/ppermute | solution.py:20
  229.4 17.0 %collective-permute-done.17 = bf16[256,1024]{1,0:T(8,128)(2,1)} collective-permute-done((bf16[256,1024]{1,0:T(8,128)(2,1)}, bf16[256,1024]{1,0:T(8,128)(2,1)}, u32[]{:S(2)}, u32[]{:S(2)}) %collective-permute-start.17) | collective-permute-done | bytes 524320 | tf_op jit(solution)/shard_map/ppermute | solution.py:20
  263.7 21.1 %while.27 = (s32[]{:T(128)}, bf16[2,512,4,128]{3,2,1,0:T(4,128)(2,1)}, f32[2,4,512]{2,1,0:T(4,128)S(1)}, s32[2]{0:T(128)S(1)}, s32[1024]{0:T(1024)S(1)}, /*index...) while((s32[]{:T(128)}, ...), condition=%wide.region_7.8_spmd, body=%wide.region_4.7_spmd.sunk | while | flops 1100741120 | bytes 31537856 | solution.py:115
  352.0 14.9 collective-permute-done.23
  370.2 19.8 %collective-permute-done.25 = bf16[256,2048]{1,0:T(8,128)(2,1)} collective-permute-done((bf16[256,2048]{1,0:T(8,128)(2,1)S(1)}, bf16[256,2048]{1,0:T(8,128)(2,1)}, u32[]{:S(2)}, u32[]{:S(2)}) %collective-permute-start.25) | collective-permute-done | bytes 1048608 | tf_op jit(solution)/shard_map/ppermute | solution.py:20
  425.1 35.4 %collective-permute-done.32 = bf16[256,2048]{1,0:T(8,128)(2,1)} collective-permute-done((bf16[256,2048]{1,0:T(8,128)(2,1)S(1)}, bf16[256,2048]{1,0:T(8,128)(2,1)}, u32[]{:S(2)}, u32[]{:S(2)}) %collective-permute-start.32) | collective-permute-done | bytes 1048608 | tf_op jit(solution)/shard_map/ppermute | solution.py:20
  460.5 27.5 %collective-permute-done.33 = bf16[256,2048]{1,0:T(8,128)(2,1)} collective-permute-done((bf16[256,2048]{1,0:T(8,128)(2,1)S(1)}, bf16[256,2048]{1,0:T(8,128)(2,1)}, u32[]{:S(2)}, u32[]{:S(2)}) %collective-permute-start.33) | collective-permute-done | bytes 1048608 | tf_op jit(solution)/shard_map/ppermute | solution.py:20
  503.2 17.6 %fusion.170 = f32[4,544,1024]{2,1,0:T(8,128)} fusion(bf16[4,544,2048]{2,1,0:T(8,128)(2,1)} %bitcast.621, bf16[4,2048,1024]{2,1,0:T(8,128)(2,1)} %bitcast.703), kind=kOutput, calls=%fused_computation.456 | convolution fusion | flops 9126805504 | bytes 34603008 | tf_op jit(solution)/shard_map/krd,kdf->krf/dot_general | solution.py:149
  520.7 21.7 %multiply_convert_fusion.4 = (bf16[4,544,1024]{2,1,0:T(8,128)(2,1)}, f32[4,544,1024]{2,1,0:T(8,128)}) fusion(f32[4,544,1024]{2,1,0:T(8,128)} %fusion.170, bf16[4,544,2048]{2,1,0:T(8,128)(2,1)} %bitcast.622, bf16[4,2048,1024]{2,1,0:T(8,128)(2,1)} %bitcast.706), kind=kOutput, calls=%fused_computation.62 | convolution fusion | flops 9140174848 | bytes 47972352 | tf_op jit(solution)/shard_map/krd,kdf->krf/dot_general | solution.py:149
  542.4 16.9 %multiply_convert_fusion.1 = bf16[4,544,2048]{2,1,0:T(8,128)(2,1)} fusion(f32[4,544]{1,0:T(4,128)S(1)} %mul.514, bf16[4,544,1024]{2,1,0:T(8,128)(2,1)} %get-tuple-element.493, bf16[4,2048,1024]{2,1,0:T(8,128)(2,1)} %bitcast.708), kind=kOutput, calls=%fused_computation.51 | convolution fusion | flops 9135718400 | bytes 30155264 | tf_op jit(solution)/shard_map/krf,kdf->krd/dot_general | solution.py:149
  569.4 20.2 %collective-permute-start.35 = (bf16[256,2048]{1,0:T(8,128)(2,1)}, bf16[256,2048]{1,0:T(8,128)(2,1)}, u32[]{:S(2)}, u32[]{:S(2)}) collective-permute-start(bf16[256,2048]{1,0:T(8,128)(2,1)} %get-tuple-element.413), channel_id=1, source_target_pairs={{0,8},{8,0},{16,24},{24,16},{1,9},{9,1},{17,25},{25,17},{2,10},{10... | collective-permute-start | bytes 3145736 | tf_op jit(solution)/shard_map/ppermute | solution.py:20
  630.5 31.4 %collective-permute-done.36 = bf16[256,2048]{1,0:T(8,128)(2,1)} collective-permute-done((bf16[256,2048]{1,0:T(8,128)(2,1)}, bf16[256,2048]{1,0:T(8,128)(2,1)}, u32[]{:S(2)}, u32[]{:S(2)}) %collective-permute-start.36) | collective-permute-done | bytes 1048608 | tf_op jit(solution)/shard_map/ppermute | solution.py:20
  668.6 19.1 %collective-permute-start.45 = (bf16[256,2048]{1,0:T(8,128)(2,1)S(1)}, bf16[256,2048]{1,0:T(8,128)(2,1)S(1)}, u32[]{:S(2)}, u32[]{:S(2)}) collective-permute-start(bf16[256,2048]{1,0:T(8,128)(2,1)S(1)} %get-tuple-element.379), channel_id=1, source_target_pairs={{0,8},{8,0},{16,24},{24,16},{1,9},{9,1},{17,25},{25,17},{2,10},{10... | collective-permute-start | bytes 3145736 | tf_op jit(solution)/shard_map/ppermute | solution.py:20
  690.0 36.9 %collective-permute-done.45 = bf16[256,2048]{1,0:T(8,128)(2,1)S(1)} collective-permute-done((bf16[256,2048]{1,0:T(8,128)(2,1)S(1)}, bf16[256,2048]{1,0:T(8,128)(2,1)S(1)}, u32[]{:S(2)}, u32[]{:S(2)}) %collective-permute-start.45) | collective-permute-done | bytes 1048608 | tf_op jit(solution)/shard_map/ppermute | solution.py:20
  727.0 32.6 %collective-permute-done.46 = bf16[256,2048]{1,0:T(8,128)(2,1)S(1)} collective-permute-done((bf16[256,2048]{1,0:T(8,128)(2,1)S(1)}, bf16[256,2048]{1,0:T(8,128)(2,1)S(1)}, u32[]{:S(2)}, u32[]{:S(2)}) %collective-permute-start.46) | collective-permute-done | bytes 1048608 | tf_op jit(solution)/shard_map/ppermute | solution.py:20
  771.0 20.3 %convolution_convert_fusion = bf16[4,2048,1024]{2,1,0:T(8,128)(2,1)} fusion(bf16[4,544,2048]{2,1,0:T(8,128)(2,1)} %fusion.35, bf16[4,544,1024]{2,1,0:T(8,128)(2,1)} %get-tuple-element.493), kind=kOutput, calls=%fused_computation.52 | convolution fusion | flops 9135194112 | bytes 30146560 | tf_op jit(solution)/shard_map/krd,krf->kdf/dot_general | solution.py:149
  791.4 24.3 %multiply_convert_fusion.2 = (bf16[4,544,1024]{2,1,0:T(8,128)(2,1)}, bf16[4,544,1024]{2,1,0:T(8,128)(2,1)}) fusion(f32[4,544,1024]{2,1,0:T(8,128)} %fusion.170, f32[4,544,1024]{2,1,0:T(8,128)} %get-tuple-element.494, bf16[4,544,2048]{2,1,0:T(8,128)(2,1)} %fusion.35, bf16[4,2048,1024]{2,1,0:T(8,128)(2,1)} %bitcast.709), kind=kOutput, calls=%fused_computation.60 | convolution fusion | flops 9155772416 | bytes 52428800 | tf_op jit(solution)/shard_map/krd,kdf->krf/dot_general | solution.py:149
  815.6 20.2 %fusion.171 = f32[4,544,2048]{2,1,0:T(8,128)} fusion(bf16[4,544,1024]{2,1,0:T(8,128)(2,1)} %get-tuple-element.389, bf16[4,2048,1024]{2,1,0:T(8,128)(2,1)} %bitcast.704), kind=kOutput, calls=%fused_computation.457 | convolution fusion | flops 9126805504 | bytes 39059456 | tf_op jit(solution)/shard_map/krf,kdf->krd/dot_general | solution.py:149
  835.8 16.9 %add_convert_fusion = bf16[4,544,2048]{2,1,0:T(8,128)(2,1)S(1)} fusion(f32[4,544,2048]{2,1,0:T(8,128)} %fusion.171, bf16[4,544,1024]{2,1,0:T(8,128)(2,1)} %get-tuple-element.388, bf16[4,2048,1024]{2,1,0:T(8,128)(2,1)} %bitcast.707), kind=kOutput, calls=%fused_computation.50 | convolution fusion | flops 9135718400 | bytes 47972352 | tf_op jit(solution)/shard_map/krf,kdf->krd/dot_general | solution.py:149
  860.7 20.6 %convolution_convert_fusion.2 = bf16[4,2048,1024]{2,1,0:T(8,128)(2,1)} fusion(bf16[4,544,2048]{2,1,0:T(8,128)(2,1)} %bitcast.623, bf16[4,544,1024]{2,1,0:T(8,128)(2,1)} %get-tuple-element.389, bf16[]{:T(256)} %bitcast.119), kind=kOutput, calls=%fused_computation.54 | convolution fusion | flops 9137422336 | bytes 30146562 | tf_op jit(solution)/shard_map/krd,krf->kdf/dot_general | solution.py:149
  886.3 19.1 %collective-permute-start.48 = (bf16[256,2048]{1,0:T(8,128)(2,1)}, bf16[256,2048]{1,0:T(8,128)(2,1)S(1)}, u32[]{:S(2)}, u32[]{:S(2)}) collective-permute-start(bf16[256,2048]{1,0:T(8,128)(2,1)} %get-tuple-element.410), channel_id=1, source_target_pairs={{0,8},{8,0},{16,24},{24,16},{1,9},{9,1},{17,25},{25,17},{2,10},{10... | collective-permute-start | bytes 3145736 | tf_op jit(solution)/shard_map/ppermute | solution.py:20
  907.7 20.8 %convolution_convert_fusion.1 = bf16[4,2048,1024]{2,1,0:T(8,128)(2,1)} fusion(bf16[4,544,2048]{2,1,0:T(8,128)(2,1)} %bitcast.624, bf16[4,544,1024]{2,1,0:T(8,128)(2,1)} %get-tuple-element.388, bf16[]{:T(256)} %bitcast.119), kind=kOutput, calls=%fused_computation.53 | convolution fusion | flops 9137422336 | bytes 30146562 | tf_op jit(solution)/shard_map/krd,krf->kdf/dot_general | solution.py:149
  942.9 34.7 %collective-permute-done.49 = bf16[256,2048]{1,0:T(8,128)(2,1)} collective-permute-done((bf16[256,2048]{1,0:T(8,128)(2,1)}, bf16[256,2048]{1,0:T(8,128)(2,1)}, u32[]{:S(2)}, u32[]{:S(2)}) %collective-permute-start.49) | collective-permute-done | bytes 1048608 | tf_op jit(solution)/shard_map/ppermute | solution.py:20
  990.0 15.8 %collective-permute-start.38 = (f32[8,128]{1,0:T(8,128)S(1)}, f32[8,128]{1,0:T(8,128)S(1)}, u32[]{:S(2)}, u32[]{:S(2)}) collective-permute-start(f32[8,128]{1,0:T(8,128)S(1)} %broadcast_in_dim.341), channel_id=1, source_target_pairs={{0,8},{8,0},{16,24},{24,16},{1,9},{9,1},{17,25},{25,17},{2,10},{10... | collective-permute-start | bytes 12296 | tf_op jit(solution)/shard_map/ppermute | solution.py:20
  1032.9 34.9 %collective-permute-done.42 = f32[8,128]{1,0:T(8,128)S(1)} collective-permute-done((f32[8,128]{1,0:T(8,128)S(1)}, f32[8,128]{1,0:T(8,128)S(1)}, u32[]{:S(2)}, u32[]{:S(2)}) %collective-permute-start.42) | collective-permute-done | bytes 4128 | tf_op jit(solution)/shard_map/ppermute | solution.py:20
  1089.5 52.1 %while.28 = (s32[]{:T(128)}, f32[1024,4,128]{0,2,1:T(8,128)S(1)}, f32[1024,4,128]{0,2,1:T(8,128)}, f32[2,512,4,128]{3,1,2,0:T(8,128)}, s32[2]{0:T(128)S(1)}, /*i...) while((s32[]{:T(128)}, f32[1024,4,128]{0,2,1:T(8,128)S(1)}, ...), condition=%wide.region_19.20_spmd.clone, body=%wide.region_17.19_spmd.clone.sunk | while | flops 2720266752 | bytes 180427760 | solution.py:142
  1187.8 23.4 %collective-permute-done.55 = bf16[256,1024]{1,0:T(8,128)(2,1)S(1)} collective-permute-done((bf16[256,1024]{1,0:T(8,128)(2,1)}, bf16[256,1024]{1,0:T(8,128)(2,1)S(1)}, u32[]{:S(2)}, u32[]{:S(2)}) %collective-permute-start.55) | collective-permute-done | bytes 524320 | tf_op jit(solution)/shard_map/ppermute | solution.py:20
  1371.7 28.7 %collective-permute-done.68 = bf16[256,1536]{1,0:T(8,128)(2,1)} collective-permute-done((bf16[256,1536]{1,0:T(8,128)(2,1)}, bf16[256,1536]{1,0:T(8,128)(2,1)}, u32[]{:S(2)}, u32[]{:S(2)}) %collective-permute-start.68) | collective-permute-done | bytes 786464 | tf_op jit(solution)/shard_map/ppermute | solution.py:20
  1407.9 14.6 collective-permute-start.90
  1441.9 18.8 %collective-permute-done.91 = bf16[256,1024]{1,0:T(8,128)(2,1)S(1)} collective-permute-done((bf16[256,1024]{1,0:T(8,128)(2,1)S(1)}, bf16[256,1024]{1,0:T(8,128)(2,1)S(1)}, u32[]{:S(2)}, u32[]{:S(2)}) %collective-permute-start.91) | collective-permute-done | bytes 524320 | tf_op jit(solution)/shard_map/ppermute | solution.py:20
  1464.5 19.3 %copy.378 = f32[256,4,3072]{2,1,0:T(4,128)} copy(f32[256,4,3072]{2,0,1:T(8,128)S(1)} %convert_bitcast_fusion) | data formatting | bytes 25165824
  (732 shorter events, 762.7 us)
Async XLA Ops:
  7.2 250.1 %all-gather.4.cloned.1.call-start = ((), (), s32[]{:S(2)}) async-start(), calls=%async_computation.3 | async-start | bytes 18874368 | tf_op jit(solution)/shard_map/all_gather | solution.py:223
  74.3 348.3 %all-gather.6.cloned.1.call-start = ((), (), s32[]{:S(2)}) async-start(), calls=%async_computation.4 | async-start | bytes 18874368 | tf_op jit(solution)/shard_map/all_gather | solution.py:223
  80.7 61.7 %collective-permute-start.8 = (bf16[256,2048]{1,0:T(8,128)(2,1)S(1)}, bf16[256,2048]{1,0:T(8,128)(2,1)}, u32[]{:S(2)}, u32[]{:S(2)}) collective-permute-start(bf16[256,2048]{1,0:T(8,128)(2,1)S(1)} %reshape.588), channel_id=1, source_target_pairs={{0,3},{1,2},{2,1},{3,0},{4,7},{5,6},{6,5},{7,4},{8,11},{9,10},{10,... | collective-permute-start | bytes 3145736 | tf_op jit(solution)/shard_map/ppermute | solution.py:20
  84.3 68.3 %collective-permute-start.9 = (bf16[256,1664]{1,0:T(8,128)(2,1)}, bf16[256,1664]{1,0:T(8,128)(2,1)}, u32[]{:S(2)}, u32[]{:S(2)}) collective-permute-start(bf16[256,1664]{1,0:T(8,128)(2,1)} %slice.311), channel_id=1, source_target_pairs={{0,8},{8,0},{16,24},{24,16},{1,9},{9,1},{17,25},{25,17},{2,10},{10... | collective-permute-start | bytes 2555912 | tf_op jit(solution)/shard_map/ppermute | solution.py:20
  92.9 61.8 %collective-permute-start.10 = (bf16[256,1664]{1,0:T(8,128)(2,1)}, bf16[256,1664]{1,0:T(8,128)(2,1)S(1)}, u32[]{:S(2)}, u32[]{:S(2)}) collective-permute-start(bf16[256,1664]{1,0:T(8,128)(2,1)} %slice.311), channel_id=1, source_target_pairs={{0,16},{8,24},{16,0},{24,8},{1,17},{9,25},{17,1},{25,9},{2,18},{10... | collective-permute-start | bytes 2555912 | tf_op jit(solution)/shard_map/ppermute | solution.py:20
  250.0 292.4 %all-gather.8.cloned.1.call-start = ((), (), s32[]{:S(2)}) async-start(), calls=%async_computation.5 | async-start | bytes 18874368 | tf_op jit(solution)/shard_map/all_gather | solution.py:223
  337.0 53.0 %collective-permute-start.25 = (bf16[256,2048]{1,0:T(8,128)(2,1)S(1)}, bf16[256,2048]{1,0:T(8,128)(2,1)}, u32[]{:S(2)}, u32[]{:S(2)}) collective-permute-start(bf16[256,2048]{1,0:T(8,128)(2,1)S(1)} %get-tuple-element.417), channel_id=1, source_target_pairs={{0,3},{1,2},{2,1},{3,0},{4,7},{5,6},{6,5},{7,4},{8,11},{9,10},{10,... | collective-permute-start | bytes 3145736 | tf_op jit(solution)/shard_map/ppermute | solution.py:20
  403.1 751.6 %reduce-scatter.4.cloned.1.call-start = ((), (), s32[]{:S(2)}) async-start(), calls=%async_computation.6 | async-start | bytes 18874368 | tf_op jit(solution)/shard_map/reduce_scatter | solution.py:354
  415.9 72.1 %collective-permute-start.33 = (bf16[256,2048]{1,0:T(8,128)(2,1)S(1)}, bf16[256,2048]{1,0:T(8,128)(2,1)}, u32[]{:S(2)}, u32[]{:S(2)}) collective-permute-start(bf16[256,2048]{1,0:T(8,128)(2,1)S(1)} %multiply_convert_fusion.7), channel_id=1, source_target_pairs={{0,16},{8,24},{16,0},{24,8},{1,17},{9,25},{17,1},{25,9},{2,18},{10... | collective-permute-start | bytes 3145736 | tf_op jit(solution)/shard_map/ppermute | solution.py:20
  416.9 71.1 %collective-permute-start.34 = (bf16[256,2048]{1,0:T(8,128)(2,1)S(1)}, bf16[256,2048]{1,0:T(8,128)(2,1)}, u32[]{:S(2)}, u32[]{:S(2)}) collective-permute-start(bf16[256,2048]{1,0:T(8,128)(2,1)S(1)} %multiply_convert_fusion.7), channel_id=1, source_target_pairs={{0,24},{8,16},{16,8},{24,0},{1,25},{9,17},{17,9},{25,1},{2,26},{10... | collective-permute-start | bytes 3145736 | tf_op jit(solution)/shard_map/ppermute | solution.py:20
  569.4 61.1 %collective-permute-start.35 = (bf16[256,2048]{1,0:T(8,128)(2,1)}, bf16[256,2048]{1,0:T(8,128)(2,1)}, u32[]{:S(2)}, u32[]{:S(2)}) collective-permute-start(bf16[256,2048]{1,0:T(8,128)(2,1)} %get-tuple-element.413), channel_id=1, source_target_pairs={{0,8},{8,0},{16,24},{24,16},{1,9},{9,1},{17,25},{25,17},{2,10},{10... | collective-permute-start | bytes 3145736 | tf_op jit(solution)/shard_map/ppermute | solution.py:20
  589.7 72.3 %collective-permute-start.36 = (bf16[256,2048]{1,0:T(8,128)(2,1)}, bf16[256,2048]{1,0:T(8,128)(2,1)}, u32[]{:S(2)}, u32[]{:S(2)}) collective-permute-start(bf16[256,2048]{1,0:T(8,128)(2,1)} %get-tuple-element.415), channel_id=1, source_target_pairs={{0,16},{8,24},{16,0},{24,8},{1,17},{9,25},{17,1},{25,9},{2,18},{10... | collective-permute-start | bytes 3145736 | tf_op jit(solution)/shard_map/ppermute | solution.py:20
  589.7 72.3 %collective-permute-start.37 = (bf16[256,2048]{1,0:T(8,128)(2,1)}, bf16[256,2048]{1,0:T(8,128)(2,1)}, u32[]{:S(2)}, u32[]{:S(2)}) collective-permute-start(bf16[256,2048]{1,0:T(8,128)(2,1)} %get-tuple-element.414), channel_id=1, source_target_pairs={{0,24},{8,16},{16,8},{24,0},{1,25},{9,17},{17,9},{25,1},{2,26},{10... | collective-permute-start | bytes 3145736 | tf_op jit(solution)/shard_map/ppermute | solution.py:20
  668.6 58.4 %collective-permute-start.45 = (bf16[256,2048]{1,0:T(8,128)(2,1)S(1)}, bf16[256,2048]{1,0:T(8,128)(2,1)S(1)}, u32[]{:S(2)}, u32[]{:S(2)}) collective-permute-start(bf16[256,2048]{1,0:T(8,128)(2,1)S(1)} %get-tuple-element.379), channel_id=1, source_target_pairs={{0,8},{8,0},{16,24},{24,16},{1,9},{9,1},{17,25},{25,17},{2,10},{10... | collective-permute-start | bytes 3145736 | tf_op jit(solution)/shard_map/ppermute | solution.py:20
  687.7 71.9 %collective-permute-start.46 = (bf16[256,2048]{1,0:T(8,128)(2,1)S(1)}, bf16[256,2048]{1,0:T(8,128)(2,1)S(1)}, u32[]{:S(2)}, u32[]{:S(2)}) collective-permute-start(bf16[256,2048]{1,0:T(8,128)(2,1)S(1)} %get-tuple-element.379), channel_id=1, source_target_pairs={{0,16},{8,24},{16,0},{24,8},{1,17},{9,25},{17,1},{25,9},{2,18},{10... | collective-permute-start | bytes 3145736 | tf_op jit(solution)/shard_map/ppermute | solution.py:20
  687.7 71.9 %collective-permute-start.47 = (bf16[256,2048]{1,0:T(8,128)(2,1)S(1)}, bf16[256,2048]{1,0:T(8,128)(2,1)S(1)}, u32[]{:S(2)}, u32[]{:S(2)}) collective-permute-start(bf16[256,2048]{1,0:T(8,128)(2,1)S(1)} %get-tuple-element.379), channel_id=1, source_target_pairs={{0,24},{8,16},{16,8},{24,0},{1,25},{9,17},{17,9},{25,1},{2,26},{10... | collective-permute-start | bytes 3145736 | tf_op jit(solution)/shard_map/ppermute | solution.py:20
  791.3 491.8 %reduce-scatter.6.cloned.1.call-start = ((), (), s32[]{:S(2)}) async-start(), calls=%async_computation.7 | async-start | bytes 18874368 | tf_op jit(solution)/shard_map/reduce_scatter | solution.py:354
  881.3 524.8 %reduce-scatter.8.cloned.1.call-start = ((), (), s32[]{:S(2)}) async-start(), calls=%async_computation.8 | async-start | bytes 18874368 | tf_op jit(solution)/shard_map/reduce_scatter | solution.py:354
  886.3 56.6 %collective-permute-start.48 = (bf16[256,2048]{1,0:T(8,128)(2,1)}, bf16[256,2048]{1,0:T(8,128)(2,1)S(1)}, u32[]{:S(2)}, u32[]{:S(2)}) collective-permute-start(bf16[256,2048]{1,0:T(8,128)(2,1)} %get-tuple-element.410), channel_id=1, source_target_pairs={{0,8},{8,0},{16,24},{24,16},{1,9},{9,1},{17,25},{25,17},{2,10},{10... | collective-permute-start | bytes 3145736 | tf_op jit(solution)/shard_map/ppermute | solution.py:20
  905.4 72.3 %collective-permute-start.49 = (bf16[256,2048]{1,0:T(8,128)(2,1)}, bf16[256,2048]{1,0:T(8,128)(2,1)}, u32[]{:S(2)}, u32[]{:S(2)}) collective-permute-start(bf16[256,2048]{1,0:T(8,128)(2,1)} %get-tuple-element.412), channel_id=1, source_target_pairs={{0,16},{8,24},{16,0},{24,8},{1,17},{9,25},{17,1},{25,9},{2,18},{10... | collective-permute-start | bytes 3145736 | tf_op jit(solution)/shard_map/ppermute | solution.py:20
  905.4 72.2 %collective-permute-start.50 = (bf16[256,2048]{1,0:T(8,128)(2,1)}, bf16[256,2048]{1,0:T(8,128)(2,1)}, u32[]{:S(2)}, u32[]{:S(2)}) collective-permute-start(bf16[256,2048]{1,0:T(8,128)(2,1)} %get-tuple-element.411), channel_id=1, source_target_pairs={{0,24},{8,16},{16,8},{24,0},{1,25},{9,17},{17,9},{25,1},{2,26},{10... | collective-permute-start | bytes 3145736 | tf_op jit(solution)/shard_map/ppermute | solution.py:20
  986.1 86.3 %collective-permute-start.51 = (bf16[256,2048]{1,0:T(8,128)(2,1)}, bf16[256,2048]{1,0:T(8,128)(2,1)}, u32[]{:S(2)}, u32[]{:S(2)}) collective-permute-start(bf16[256,2048]{1,0:T(8,128)(2,1)} %get-tuple-element.376), channel_id=1, source_target_pairs={{0,1},{1,0},{2,3},{3,2},{4,5},{5,4},{6,7},{7,6},{8,9},{9,8},{10,11... | collective-permute-start | bytes 3145736 | tf_op jit(solution)/shard_map/ppermute | solution.py:20
  1009.4 65.4 %collective-permute-start.52 = (bf16[256,2048]{1,0:T(8,128)(2,1)}, bf16[256,2048]{1,0:T(8,128)(2,1)}, u32[]{:S(2)}, u32[]{:S(2)}) collective-permute-start(bf16[256,2048]{1,0:T(8,128)(2,1)} %get-tuple-element.376), channel_id=1, source_target_pairs={{0,2},{1,3},{2,0},{3,1},{4,6},{5,7},{6,4},{7,5},{8,10},{9,11},{10,... | collective-permute-start | bytes 3145736 | tf_op jit(solution)/shard_map/ppermute | solution.py:20
  1014.3 53.5 %collective-permute-start.42 = (f32[8,128]{1,0:T(8,128)S(1)}, f32[8,128]{1,0:T(8,128)S(1)}, u32[]{:S(2)}, u32[]{:S(2)}) collective-permute-start(f32[8,128]{1,0:T(8,128)S(1)} %broadcast_in_dim.342), channel_id=1, source_target_pairs={{0,2},{1,3},{2,0},{3,1},{4,6},{5,7},{6,4},{7,5},{8,10},{9,11},{10,... | collective-permute-start | bytes 12296 | tf_op jit(solution)/shard_map/ppermute | solution.py:20
  1014.6 53.2 %collective-permute-start.43 = (f32[8,128]{1,0:T(8,128)S(1)}, f32[8,128]{1,0:T(8,128)S(1)}, u32[]{:S(2)}, u32[]{:S(2)}) collective-permute-start(f32[8,128]{1,0:T(8,128)S(1)} %broadcast_in_dim.342), channel_id=1, source_target_pairs={{0,3},{1,2},{2,1},{3,0},{4,7},{5,6},{6,5},{7,4},{8,11},{9,10},{10,... | collective-permute-start | bytes 12296 | tf_op jit(solution)/shard_map/ppermute | solution.py:20
  1069.6 88.8 %collective-permute-start.44 = (f32[8,128]{1,0:T(8,128)S(1)}, f32[8,128]{1,0:T(8,128)S(1)}, u32[]{:S(2)}, u32[]{:S(2)}) collective-permute-start(f32[8,128]{1,0:T(8,128)S(1)} %broadcast_in_dim.343), channel_id=1, source_target_pairs={{0,4},{4,0},{1,5},{5,1},{2,6},{6,2},{3,7},{7,3},{8,12},{12,8},{9,1... | collective-permute-start | bytes 12296 | tf_op jit(solution)/shard_map/ppermute | solution.py:20
  1085.6 60.9 %collective-permute-start.73 = (bf16[1024,512]{1,0:T(8,128)(2,1)}, bf16[1024,512]{1,0:T(8,128)(2,1)}, u32[]{:S(2)}, u32[]{:S(2)}) collective-permute-start(bf16[1024,512]{1,0:T(8,128)(2,1)} %dynamic-slice_bitcast_fusion.2), channel_id=1, source_target_pairs={{0,4},{4,0},{1,5},{5,1},{2,6},{6,2},{3,7},{7,3},{8,12},{12,8},{9,1... | collective-permute-start | bytes 3145736 | tf_op jit(solution)/shard_map/ppermute | solution.py:20
  1176.4 83.1 %collective-permute-start.78 = (bf16[64,512]{1,0:T(8,128)(2,1)S(1)}, bf16[64,512]{1,0:T(8,128)(2,1)S(1)}, u32[]{:S(2)}, u32[]{:S(2)}) collective-permute-start(bf16[64,512]{1,0:T(8,128)(2,1)S(1)} %get-tuple-element.476), channel_id=1, source_target_pairs={{0,2},{1,3},{2,0},{3,1},{4,6},{5,7},{6,4},{7,5},{8,10},{9,11},{10,... | collective-permute-start | bytes 196616 | tf_op jit(solution)/shard_map/ppermute | solution.py:20
  1185.9 73.7 %collective-permute-start.79 = (bf16[64,512]{1,0:T(8,128)(2,1)S(1)}, bf16[64,512]{1,0:T(8,128)(2,1)S(1)}, u32[]{:S(2)}, u32[]{:S(2)}) collective-permute-start(bf16[64,512]{1,0:T(8,128)(2,1)S(1)} %get-tuple-element.475), channel_id=1, source_target_pairs={{0,3},{1,2},{2,1},{3,0},{4,7},{5,6},{6,5},{7,4},{8,11},{9,10},{10,... | collective-permute-start | bytes 196616 | tf_op jit(solution)/shard_map/ppermute | solution.py:20
  1243.1 83.9 %collective-permute-start.66 = (bf16[1024,1536]{1,0:T(8,128)(2,1)}, bf16[1024,1536]{1,0:T(8,128)(2,1)}, u32[]{:S(2)}, u32[]{:S(2)}) collective-permute-start(bf16[1024,1536]{1,0:T(8,128)(2,1)} %dynamic-slice_bitcast_fusion.1), channel_id=1, source_target_pairs={{0,4},{4,0},{1,5},{5,1},{2,6},{6,2},{3,7},{7,3},{8,12},{12,8},{9,1... | collective-permute-start | bytes 9437192 | tf_op jit(solution)/shard_map/ppermute | solution.py:20
  1298.2 56.3 %collective-permute-start.89 = (bf16[256,1024]{1,0:T(8,128)(2,1)}, bf16[256,1024]{1,0:T(8,128)(2,1)}, u32[]{:S(2)}, u32[]{:S(2)}) collective-permute-start(bf16[256,1024]{1,0:T(8,128)(2,1)} %get-tuple-element.422), channel_id=1, source_target_pairs={{0,24},{8,16},{16,8},{24,0},{1,25},{9,17},{17,9},{25,1},{2,26},{10... | collective-permute-start | bytes 1572872 | tf_op jit(solution)/shard_map/ppermute | solution.py:20
  1337.2 63.2 %collective-permute-start.68 = (bf16[256,1536]{1,0:T(8,128)(2,1)}, bf16[256,1536]{1,0:T(8,128)(2,1)}, u32[]{:S(2)}, u32[]{:S(2)}) collective-permute-start(bf16[256,1536]{1,0:T(8,128)(2,1)} %get-tuple-element.421), channel_id=1, source_target_pairs={{0,16},{8,24},{16,0},{24,8},{1,17},{9,25},{17,1},{25,9},{2,18},{10... | collective-permute-start | bytes 2359304 | tf_op jit(solution)/shard_map/ppermute | solution.py:20
  (176 other events, 3376.0 us)
Sparse Core Ops, SparseCore 0:
  74.5 133.9 all-gather.3
  250.1 101.9 all-gather.5
  403.2 88.9 all-gather.7
  791.4 129.3 reduce-scatter.3
  924.2 158.3 reduce-scatter.5
  1086.1 116.8 reduce-scatter.7

commit v4 on v3

--- a/solution.py
+++ b/solution.py
@@ -1,6 +1,10 @@
+import functools
+
 import jax
 import jax.numpy as jnp
 from jax import lax
+from jax.experimental import pallas as pl
+from jax.experimental.pallas import tpu as pltpu
 from jax.sharding import Mesh, PartitionSpec as P
 
 H = 16
@@ -75,74 +79,190 @@
     inverse = 10000.0 ** (-(jnp.arange(HD // 2).astype(f32) * 2.0 / HD))
     angles = jnp.arange(rows).astype(f32)[:, None] * inverse[None, :]
     cosine = jnp.concatenate([jnp.cos(angles), jnp.cos(angles)], axis=-1)
-    sine = jnp.concatenate([jnp.sin(angles), jnp.sin(angles)], axis=-1)
-    return cosine[:, None, :], sine[:, None, :]
-
-
-def rotate_half(values):
-    half = values.shape[-1] // 2
-    return jnp.concatenate([-values[..., half:], values[..., :half]], axis=-1)
-
-
-def rotate_back(values):
-    half = values.shape[-1] // 2
-    return jnp.concatenate([values[..., half:], -values[..., :half]], axis=-1)
-
-
-def block_scores(query, keyed, segment, block_index, rows, scale):
-    start = block_index * rows
-    q_block = lax.dynamic_slice_in_dim(query, start, rows, 0)
-    q_segment = lax.dynamic_slice_in_dim(segment, start, rows, 0)
-    q_places = start + jnp.arange(rows)
-    k_places = jnp.arange(keyed.shape[0])
-    allowed = (q_segment[:, None] == segment[None, :]) & (q_places[:, None] >= k_places[None, :])
-    scores = jnp.einsum("qhd,khd->hqk", q_block, keyed, preferred_element_type=f32) * scale
-    return q_block, jnp.where(allowed[None], scores, masked)
-
-
-def attend_forward(query, keyed, valued, segment, rows, scale):
-    blocks = keyed.shape[0] // rows
-
-    def one_block(block_index):
-        q_block, scores = block_scores(query, keyed, segment, block_index, rows, scale)
-        row_top = jnp.max(scores, axis=-1, keepdims=True)
-        exp_scores = jnp.exp(scores - row_top)
-        row_total = jnp.sum(exp_scores, axis=-1, keepdims=True)
-        weights = (exp_scores / row_total).astype(bf16)
-        out = jnp.einsum("hqk,khd->qhd", weights, valued, preferred_element_type=f32)
-        return out.astype(bf16), (row_top + jnp.log(row_total))[..., 0]
-
-    outputs, log_total = lax.map(one_block, jnp.arange(blocks))
-    return outputs.reshape(keyed.shape[0], -1), log_total
-
-
-def attend_backward(query, keyed, valued, segment, log_total, grad_heads, rows, scale):
-    blocks = keyed.shape[0] // rows
-
-    def one_block(carry, pieces):
-        grad_k, grad_v = carry
-        block_index, block_total = pieces
-        q_block, scores = block_scores(query, keyed, segment, block_index, rows, scale)
-        probs = jnp.exp(scores - block_total[:, :, None])
-        grad_block = lax.dynamic_slice_in_dim(grad_heads, block_index * rows, rows, 0)
-        grad_v = grad_v + jnp.einsum(
-            "hqk,qhd->khd", probs.astype(bf16), grad_block, preferred_element_type=f32
+    sine = jnp.concatenate([-jnp.sin(angles), jnp.sin(angles)], axis=-1)
+    return cosine, sine
+
+
+def mm(left, right, dims):
+    return lax.dot_general(left, right, (dims, ((), ())), preferred_element_type=f32)
+
+
+def masked_scores(query, keyed, seg_col, seg_row, first, scale):
+    scores = mm(query, keyed, ((1,), (1,))) * scale
+    rows = first + lax.broadcasted_iota(jnp.int32, scores.shape, 0)
+    allowed = (rows >= lax.broadcasted_iota(jnp.int32, scores.shape, 1)) & (seg_col == seg_row)
+    return jnp.where(allowed, scores, masked)
+
+
+def attend_kernel(
+    block,
+    q_raw,
+    k_raw,
+    v_raw,
+    q_mean,
+    k_mean,
+    gain_q,
+    gain_k,
+    cosine,
+    sine,
+    seg_col,
+    seg_row,
+    out,
+    q_out,
+    k_out,
+    v_out,
+    log_total,
+):
+    def rope(raw, mean, gain):
+        values = raw[...] * lax.rsqrt(mean[...] + epsilon) * gain[...]
+        turned = pltpu.roll(values, HD // 2, 1)
+        return (values * cosine[...] + turned * sine[...]).astype(bf16)
+
+    q_out[...] = rope(q_raw, q_mean, gain_q)
+    k_out[...] = rope(k_raw, k_mean, gain_k)
+    v_out[...] = v_raw[...].astype(bf16)
+    for first in range(0, out.shape[0], block):
+        last = first + block
+        scores = masked_scores(
+            q_out[first:last],
+            k_out[:last],
+            seg_col[first:last],
+            seg_row[:, :last],
+            first,
+            HD**-0.5,
         )
-        grad_probs = jnp.einsum("qhd,khd->hqk", grad_block, valued, preferred_element_type=f32)
+        top = jnp.max(scores, axis=-1, keepdims=True)
+        exps = jnp.exp(scores - top)
+        total = jnp.sum(exps, axis=-1, keepdims=True)
+        weights = (exps * (1.0 / total)).astype(bf16)
+        out[first:last] = mm(weights, v_out[:last], ((1,), (0,))).astype(bf16)
+        log_total[0, first:last] = top + jnp.log(total)
+
+
+def attend_back_kernel(
+    block,
+    q_raw,
+    k_raw,
+    q_mean,
+    k_mean,
+    gain_q,
+    gain_k,
+    cosine,
+    sine,
+    seg_col,
+    seg_row,
+    query,
+    keyed,
+    valued,
+    grad,
+    log_total,
+    grad_q,
+    grad_k,
+    grad_v,
+    q_inner,
+    k_inner,
+    gain_q_grad,
+    gain_k_grad,
+    sum_q,
+    sum_k,
+    sum_v,
+):
+    scale = HD**-0.5
+    sum_k[...] = jnp.zeros_like(sum_k)
+    sum_v[...] = jnp.zeros_like(sum_v)
+    for first in range(0, query.shape[0], block):
+        last = first + block
+        q_block, g_block = query[first:last], grad[first:last]
+        scores = masked_scores(
+            q_block, keyed[:last], seg_col[first:last], seg_row[:, :last], first, scale
+        )
+        probs = jnp.exp(scores - log_total[0, first:last])
+        sum_v[:last] += mm(probs.astype(bf16), g_block, ((0,), (0,)))
+        grad_probs = mm(g_block, valued[:last], ((1,), (1,)))
         inner = jnp.sum(probs * grad_probs, axis=-1, keepdims=True)
         grad_scores = (probs * (grad_probs - inner)).astype(bf16)
-        grad_q = jnp.einsum("hqk,khd->qhd", grad_scores, keyed, preferred_element_type=f32) * scale
-        grad_k = (
-            grad_k
-            + jnp.einsum("hqk,qhd->khd", grad_scores, q_block, preferred_element_type=f32) * scale
-        )
-        return (grad_k, grad_v), grad_q
-
-    initial = jnp.zeros(keyed.shape, f32)
-    (grad_k, grad_v), grad_q = lax.scan(
-        one_block, (initial, initial), (jnp.arange(blocks), log_total)
-    )
-    return grad_q.reshape(keyed.shape), grad_k, grad_v
+        sum_q[first:last] = mm(grad_scores, keyed[:last], ((1,), (0,))) * scale
+        sum_k[:last] += mm(grad_scores, q_block, ((0,), (0,))) * scale
+    grad_v[...] = sum_v[...].astype(bf16)
+
+    def undo(total, raw, mean, gain, inner_out, gain_out, grad_out):
+        low = total[...].astype(bf16).astype(f32)
+        back = low * cosine[...] + pltpu.roll(low * sine[...], HD // 2, 1)
+        normed = raw[...] * lax.rsqrt(mean[...] + epsilon)
+        gain_out[...] = jnp.sum(back * normed, axis=0, keepdims=True)
+        back = back * gain[...]
+        grad_out[...] = back
+        inner = jnp.sum(back * normed, axis=-1, keepdims=True)
+
+        @pl.when(pl.program_id(0) == 0)
+        def _():
+            inner_out[...] = inner
+
+        @pl.when(pl.program_id(0) > 0)
+        def _():
+            inner_out[...] += inner
+
+    undo(sum_q, q_raw, q_mean, gain_q, q_inner, gain_q_grad, grad_q)
+    undo(sum_k, k_raw, k_mean, gain_k, k_inner, gain_k_grad, grad_k)
+
+
+def head_specs(seq, heads):
+    column = pl.BlockSpec((seq, 1), lambda h: (0, 0))
+    gain = pl.BlockSpec((1, HD), lambda h: (0, h))
+    table = pl.BlockSpec((seq, HD), lambda h: (0, 0))
+    return [column, column, gain, gain, table, table, column, pl.BlockSpec((1, seq), lambda h: (0, 0))]
+
+
+def raw_spec(seq, heads, which):
+    return pl.BlockSpec((seq, HD), lambda h: (0, which * heads + h))
+
+
+def attend(projected, shared, heads):
+    seq = projected.shape[0]
+    block = min(256, seq)
+    head = pl.BlockSpec((seq, HD), lambda h: (0, h))
+    low = jax.ShapeDtypeStruct((seq, heads * HD), bf16)
+    return pl.pallas_call(
+        functools.partial(attend_kernel, block),
+        grid=(heads,),
+        in_specs=[raw_spec(seq, heads, i) for i in range(3)] + head_specs(seq, heads),
+        out_specs=[head] * 4 + [pl.BlockSpec((1, seq, 1), lambda h: (h, 0, 0))],
+        out_shape=[low] * 4 + [jax.ShapeDtypeStruct((heads, seq, 1), f32)],
+        compiler_params=pltpu.CompilerParams(vmem_limit_bytes=48 * 2**20),
+        cost_estimate=pl.CostEstimate(
+            flops=heads * seq * seq * HD * 4,
+            bytes_accessed=heads * seq * HD * 24,
+            transcendentals=heads * seq * seq,
+        ),
+    )(projected, projected, projected, *shared)
+
+
+def attend_back(projected, shared, query, keyed, valued, grad, log_total, heads):
+    seq = projected.shape[0]
+    block = min(256, seq)
+    head = pl.BlockSpec((seq, HD), lambda h: (0, h))
+    column = pl.BlockSpec((seq, 1), lambda h: (0, 0))
+    gain = pl.BlockSpec((1, HD), lambda h: (0, h))
+    wide = jax.ShapeDtypeStruct((seq, heads * HD), f32)
+    return pl.pallas_call(
+        functools.partial(attend_back_kernel, block),
+        grid=(heads,),
+        in_specs=[raw_spec(seq, heads, i) for i in range(2)]
+        + head_specs(seq, heads)
+        + [head] * 4
+        + [pl.BlockSpec((1, seq, 1), lambda h: (h, 0, 0))],
+        out_specs=[head] * 3 + [column] * 2 + [gain] * 2,
+        out_shape=[wide, wide, jax.ShapeDtypeStruct((seq, heads * HD), bf16)]
+        + [jax.ShapeDtypeStruct((seq, 1), f32)] * 2
+        + [jax.ShapeDtypeStruct((1, heads * HD), f32)] * 2,
+        scratch_shapes=[pltpu.VMEM((seq, HD), f32)] * 3,
+        compiler_params=pltpu.CompilerParams(vmem_limit_bytes=48 * 2**20),
+        cost_estimate=pl.CostEstimate(
+            flops=heads * seq * seq * HD * 10,
+            bytes_accessed=heads * seq * HD * 36,
+            transcendentals=heads * seq * seq,
+        ),
+    )(projected, projected, *shared, query, keyed, valued, grad, log_total)
 
 
 def dot(spec, left, right):
@@ -172,7 +292,6 @@
     part = w_expert.shape[0]
     capacity = own * TOP * 17 // (16 * planes * seqs)
     scale = HD ** (-0.5)
-    block_rows = min(512, seq)
 
     def to_inner(v):
         lead = v.shape[:-1]
@@ -276,21 +395,41 @@
     taken = place.transpose(0, 2, 1)[:, :, None, :] == jnp.arange(capacity)[None, None, :, None]
     choose = taken.astype(bf16)
     gate_slot = jnp.sum(jnp.where(taken, gate_of.transpose(0, 2, 1)[:, :, None, :], 0.0), axis=-1)
-    gate_slot = gate_slot.transpose(1, 0, 2).reshape(seqs, planes * capacity, 1)
-
-    def dispatch(rows_in):
-        spread = dot("bkjt,btd->kbjd", choose, rows_in)
-        return spread.reshape(seqs, planes * capacity, width)
-
-    def combine_rows(rows_out):
-        rows_out = rows_out.reshape(seqs, planes, capacity, width)
-        return dot("bkjt,kbjd->btd", choose, rows_out).astype(bf16)
-
-    def send_back(partial, *others):
-        got = [partial[0]] + [send(partial[k], "z", k) for k in range(1, planes)]
-        if others:
-            got[0] = after(got[0], *others)
-        return sum(piece.astype(f32) for piece in got)
+    gate_slot = gate_slot.transpose(1, 0, 2)
+
+    groups = [[k for k in range(planes) if k % 2 == odd] for odd in range(2)]
+    slots = capacity * planes // 2
+
+    def pick(table, group, axis):
+        return jnp.concatenate([lax.slice_in_dim(table, k, k + 1, axis=axis) for k in group], axis)
+
+    chosen = [pick(choose, group, 0) for group in groups]
+    weight_of = [pick(gate_slot, group, 1).reshape(seqs, slots, 1) for group in groups]
+
+    def dispatch(i, blocks):
+        spread = dot("bkjt,btd->kbjd", chosen[i], blocks)
+        return spread.reshape(seqs, slots, width)
+
+    def combine(i, rows_out):
+        rows_out = rows_out.reshape(seqs, planes // 2, capacity, width)
+        return dot("bkjt,kbjd->btd", chosen[i], rows_out).astype(bf16)
+
+    def through_planes(block, work):
+        near = [block] + [None] * (planes - 1)
+        for k in groups[0][1:]:
+            near[k] = send(block, "z", k)
+        later = after(block, *[near[k] for k in groups[0][1:]])
+        for k in groups[1]:
+            near[k] = send(later, "z", k)
+        first = work(0, jnp.stack([near[k] for k in groups[0]]))[0]
+        got = [first[0]] + [send(first[i], "z", k) for i, k in enumerate(groups[0]) if k]
+        second, halfway = work(1, after(jnp.stack([near[k] for k in groups[1]]), first[0]))
+        base = after(total(got), halfway)
+        second = after(second, base)
+        return second, [base] + [send(second[i], "z", k) for i, k in enumerate(groups[1])]
+
+    def total(pieces):
+        return sum(piece.astype(f32) for piece in pieces)
 
     normed_in = (seq_tokens * seq_factor * gain_in).astype(bf16)
     normed_mine, normed_other = halves(normed_in)
@@ -299,28 +438,29 @@
     )
     query_raw = projected[:, :cols]
     key_raw = projected[:, cols : 2 * cols]
-    valued = projected[:, 2 * cols : 3 * cols].astype(bf16).reshape(seq, heads, HD)
 
     def over_heads(first, second):
-        pair = jnp.stack([jnp.sum(first, axis=-1), jnp.sum(second, axis=-1)])
-        pair = sum(gather_near(pair, "s")) / width
+        pair = sum(gather_near(jnp.stack([first, second]), "s")) / width
         return pair[0][:, None], pair[1][:, None]
 
-    q_mean, k_mean = over_heads(query_raw * query_raw, key_raw * key_raw)
-    q_factor, k_factor = lax.rsqrt(q_mean + epsilon), lax.rsqrt(k_mean + epsilon)
-    cosine, sine = rope_tables(seq)
-
-    def rope(raw, factor, gain):
-        cube = (raw * factor * gain).reshape(seq, heads, HD)
-        return (cube * cosine + rotate_half(cube) * sine).astype(bf16)
-
-    query, keyed = rope(query_raw, q_factor, gain_q), rope(key_raw, k_factor, gain_k)
-    query = after(query, w_gate)
-    up_ready = in_order(up_blocks, "z", token(keyed))
-    keyed = after(keyed, up_ready)
+    q_mean, k_mean = over_heads(
+        jnp.sum(query_raw * query_raw, axis=-1), jnp.sum(key_raw * key_raw, axis=-1)
+    )
+    up_ready = in_order(up_blocks, "z", token(projected))
     w_up = gather_plane(up_ready)
     out_blocks = gather_near(after(mine[:, 3 * cols + PAD :], up_ready), "z")
-    attended, log_total = attend_forward(query, keyed, valued, segment, block_rows, scale)
+    cosine, sine = rope_tables(seq)
+    shared = [
+        after(q_mean, up_ready, w_gate),
+        k_mean,
+        gain_q[None],
+        gain_k[None],
+        cosine,
+        sine,
+        segment[:, None],
+        segment[None],
+    ]
+    attended, query, keyed, valued, log_total = attend(projected, shared, heads)
     w_out = collect(stack_rows(out_blocks, token(attended)), "c").reshape(width, cols)
     down_blocks = expert_chunk(2, token(attended))
     attn_out = dot("tc,dc->td", attended, w_out).astype(bf16)
@@ -330,13 +470,20 @@
     w_down = gather_plane(down_ready)
 
     normed_mid = (residual * rms_factor(residual) * gain_mid).astype(bf16)
-    rows_in = dispatch(after(jnp.stack(gather_near(normed_mid, "z")), w_up)).astype(bf16)
-    gate_pre = dot("krd,kdf->krf", rows_in, w_gate)
-    up_pre = dot("krd,kdf->krf", rows_in, w_up)
-    activated = (jax.nn.silu(gate_pre) * up_pre).astype(bf16)
-    expert_out = (dot("krf,kdf->krd", activated, w_down) * gate_slot).astype(bf16)
-    final_out = residual + send_back(combine_rows(expert_out))
-
+    kept = [None, None]
+
+    def forward(i, blocks):
+        rows_in = dispatch(i, blocks).astype(bf16)
+        gate_pre = dot("krd,kdf->krf", rows_in, w_gate)
+        up_pre = dot("krd,kdf->krf", rows_in, w_up)
+        activated = (jax.nn.silu(gate_pre) * up_pre).astype(bf16)
+        kept[i] = (rows_in, gate_pre, up_pre, activated)
+        out = dot("krf,kdf->krd", activated, w_down) * weight_of[i]
+        return combine(i, out.astype(bf16)), activated
+
+    final_out = residual + total(through_planes(normed_mid, forward)[1])
+
+    w_out_near = gather_near(after(w_out, kept[1][3]), "s")
     valid_f = valid_mask.astype(f32)[:, None]
     difference = final_out - to_inner(teacher).astype(f32)
     squared = jnp.sum(valid_f * difference * difference)
@@ -346,9 +493,6 @@
         to_inner(cotangent).astype(f32) + 2.0 / (total_count * width) * valid_f * difference
     )
 
-    grad_rows = dispatch(jnp.stack(gather_near(grad_out.astype(bf16), "z")))
-    grad_rows = (grad_rows * gate_slot).astype(bf16)
-
     def scatter_expert(grad):
         grad = grad.reshape(seqs * width, hidden)
         grad = lax.psum_scatter(grad, ("s", "c", "o"), scatter_dimension=0, tiled=True)
@@ -360,53 +504,69 @@
 
         return exchange(piece_for, "z", start)
 
-    grad_w_down = scatter_expert(dot("krd,krf->kdf", grad_rows, activated).astype(bf16))
-    grad_act = dot("krd,kdf->krf", grad_rows, w_down)
-    sigmoid = jax.nn.sigmoid(gate_pre)
-    grad_gate = (grad_act * up_pre * sigmoid * (1.0 + gate_pre * (1.0 - sigmoid))).astype(bf16)
-    grad_up = (grad_act * gate_pre * sigmoid).astype(bf16)
-    back_rows = dot("krf,kdf->krd", grad_gate, w_gate) + dot("krf,kdf->krd", grad_up, w_up)
-    back_rows = combine_rows(back_rows.astype(bf16))
-    grad_gate, grad_up = after(grad_gate, back_rows), after(grad_up, back_rows)
-    grad_w_gate = dot("krd,krf->kdf", rows_in, grad_gate).astype(bf16)
-    grad_w_up = dot("krd,krf->kdf", rows_in, grad_up).astype(bf16)
-    grad_mid = send_back(back_rows, grad_w_gate, grad_w_up)
-    grad_w_gate, grad_w_up = scatter_expert(grad_w_gate), scatter_expert(grad_w_up)
+    grads = [None, None]
+
+    def backward(i, blocks):
+        gate_pre, up_pre = kept[i][1:3]
+        grad_rows = (dispatch(i, blocks) * weight_of[i]).astype(bf16)
+        grad_act = dot("krd,kdf->krf", grad_rows, w_down)
+        sigmoid = jax.nn.sigmoid(gate_pre)
+        grad_gate = grad_act * up_pre * sigmoid * (1.0 + gate_pre * (1.0 - sigmoid))
+        grad_gate, grad_up = grad_gate.astype(bf16), (grad_act * gate_pre * sigmoid).astype(bf16)
+        back = dot("krf,kdf->krd", grad_gate, w_gate) + dot("krf,kdf->krd", grad_up, w_up)
+        grads[i] = (grad_rows, grad_gate, grad_up)
+        return combine(i, back.astype(bf16)), grad_gate
+
+    back_last, back_pieces = through_planes(grad_out.astype(bf16), backward)
+
+    def both(table, which):
+        return jnp.concatenate([table[0][which], table[1][which]], axis=1)
+
+    rows_in, activated = both(kept, 0), both(kept, 3)
+    grad_w_down = dot("krd,krf->kdf", both(grads, 0), activated).astype(bf16)
+    grad_w_gate = dot("krd,krf->kdf", rows_in, after(both(grads, 1), back_last)).astype(bf16)
+    grad_w_up = dot("krd,krf->kdf", rows_in, after(both(grads, 2), back_last)).astype(bf16)
+    back_pieces[0] = after(back_pieces[0], grad_w_down, grad_w_gate)
+    grad_mid = total(back_pieces)
+    up_done = grad_w_up
+    grad_w_down, grad_w_gate, grad_w_up = [
+        scatter_expert(grad) for grad in (grad_w_down, grad_w_gate, grad_w_up)
+    ]
     down_blocks = to_owners(grad_w_down, token(grad_mid))
     gate_blocks = to_owners(grad_w_gate)
     grad_resid_norm, gain_mid_grad = norm_back(residual, gain_mid, grad_mid)
     grad_resid = grad_out + grad_resid_norm
 
-    grad_attn_out = collect(grad_resid.astype(bf16), "s").reshape(seq, width)
-    grad_w_out = sum_rows(dot("td,tc->dc", grad_attn_out, attended).astype(bf16))
-    grad_heads = jnp.dot(grad_attn_out, w_out, preferred_element_type=f32).astype(bf16)
-    grad_q, grad_k, grad_v = attend_backward(
-        query,
-        keyed,
-        valued,
-        segment,
-        log_total,
-        grad_heads.reshape(seq, heads, HD),
-        block_rows,
-        scale,
-    )
-
-    def unrotate(grad):
-        grad = grad.astype(bf16).astype(f32)
-        return (grad * cosine + rotate_back(grad * sine)).reshape(seq, cols)
-
+    grad_low = grad_resid.astype(bf16)
+    head_blocks = [
+        send(jnp.dot(grad_low, w_out_near[k], preferred_element_type=f32).astype(bf16), "s", k)
+        if k
+        else jnp.dot(grad_low, w_out, preferred_element_type=f32).astype(bf16)
+        for k in range(seqs)
+    ]
+    grad_heads = in_order(head_blocks, "s", token(up_done)).reshape(seq, cols)
+    low_blocks = gather_near(after(grad_low, head_blocks[-1]), "s")
+    grad_q, grad_k, grad_v, q_inner, k_inner, gain_q_grad, gain_k_grad = attend_back(
+        projected, shared, query, keyed, valued, grad_heads, log_total, heads
+    )
     down_ready = in_order(down_blocks, "z", token(grad_q))
-    grad_q = after(grad_q, down_ready)
-    grad_q, grad_k = unrotate(grad_q), unrotate(grad_k)
-    q_normed, k_normed = query_raw * q_factor, key_raw * k_factor
-    gain_q_grad = jnp.sum(grad_q * q_normed, axis=0)
-    gain_k_grad = jnp.sum(grad_k * k_normed, axis=0)
-    grad_q, grad_k = grad_q * gain_q, grad_k * gain_k
-    q_inner, k_inner = over_heads(grad_q * q_normed, grad_k * k_normed)
-    grad_q = q_factor * (grad_q - q_normed * q_inner)
-    grad_k = k_factor * (grad_k - k_normed * k_inner)
+    grad_attn_out = in_order(low_blocks, "s", token(grad_q)).reshape(seq, width)
+    grad_w_out = dot("td,tc->dc", grad_attn_out, attended).astype(bf16)
+    q_inner = after(q_inner, down_ready, grad_w_out)
+    grad_w_out = sum_rows(grad_w_out)
+    q_inner, k_inner = over_heads(q_inner[:, 0], k_inner[:, 0])
+
+    def norm_grad(grad, raw, mean, inner):
+        factor = lax.rsqrt(mean + epsilon)
+        return (factor * (grad - raw * factor * inner)).astype(bf16)
+
     grad_proj = jnp.concatenate(
-        [grad_q.astype(bf16), grad_k.astype(bf16), grad_v.reshape(seq, cols).astype(bf16)], axis=1
+        [
+            norm_grad(grad_q, query_raw, q_mean, q_inner),
+            norm_grad(grad_k, key_raw, k_mean, k_inner),
+            grad_v,
+        ],
+        axis=1,
     )
     grad_padded = jnp.concatenate([grad_proj, jnp.zeros((seq, PAD), bf16)], axis=1)
 
@@ -426,7 +586,7 @@
         full = jnp.zeros((width,), f32)
         return to_inner(lax.dynamic_update_slice_in_dim(full, local, rank * cols, 0))
 
-    gains = jnp.stack([gain_in_grad, gain_mid_grad, widen(gain_q_grad), widen(gain_k_grad)])
+    gains = jnp.stack([gain_in_grad, gain_mid_grad, widen(gain_q_grad[0]), widen(gain_k_grad[0])])
     for axis in ("z", "c", "s", "o"):
         gains = sum(gather_near(gains, axis))
     row = (lax.axis_index(("c", "o", "z")) * seqs + rank) * rows_dev

time: 1510 us -> 1510 us (level)
  Pallas kernels: 0 us -> 37.6 us
  starting transfers between devices: 236 us -> 210 us
  other arithmetic: 103 us -> 84.2 us
    dot_general x15 -> x4, matrix products: 48.3 us -> 7.69 us  [the longest x3 6.96 us: shards(): jnp.dot(grad_low, w_out_near[k], preferred_element_type=f32).astype(bf16)]
    dot_general x19 -> x29, matrix products: 231 us -> 271 us  [dot(): return jnp.einsum(spec, left, right, preferred_element_type=f32)]
    pallas_call x0 -> x2, Pallas kernels: none -> 37.6 us  [the longest x1 19.3 us: attend_back(): pl.pallas_call(functools.partial(attend_back_kernel, block), grid=(heads,...]
    ppermute x93 -> x99, starting transfers between devices: 236 us -> 209 us  [send(): return lax.ppermute(block, axis, [(i, i ^ step) for i in range(size)])]
    ppermute x93 -> x99, waiting for transfers between devices: 552 us -> 565 us  [send(): return lax.ppermute(block, axis, [(i, i ^ step) for i in range(size)])]
    another operation x13 -> x15, local copies, waits for them, and re-layouts: 28 us -> 33.9 us  [whole(): jax.shard_map(shards, mesh=inner, in_specs=(rows, rows, rows, experts, ro...]
    dynamic_update_slice x47 -> x50, local copies, waits for them, and re-layouts: 49.6 us -> 52.1 us  [in_order(): lax.dynamic_update_index_in_dim(stacked, block, (rank ^ k) + start, 0)]
    unnamed x217 -> x222, local copies, waits for them, and re-layouts: 52.9 us -> 55 us
  transfers between devices with their start and end apart: 99 -> 105, of which waited for: 41 -> 41; matrix products, arithmetic and copies ran while one was open for 36% -> 33% of each run, Pallas kernels for 0% -> 3%
where the time goes in v4:
time: 1510 us; the launch traced here: 1500 us
  waiting for transfers between devices  565 us (37%)
  matrix products  293 us (19%)
  local copies, waits for them, and re-layouts  249 us (16%)
  starting transfers between devices  210 us (14%)
  other arithmetic  84.2 us (6%)
  between operations  57.9 us (4%)
  Pallas kernels  37.6 us (2%)
    ppermute x99, waiting for transfers between devices, send(): return lax.ppermute(block, axis, [(i, i ^ step) for i in range(size)])  565 us
    dot_general x29, matrix products, dot(): return jnp.einsum(spec, left, right, preferred_element_type=f32)  271 us
    ppermute x99, starting transfers between devices, send(): return lax.ppermute(block, axis, [(i, i ^ step) for i in range(size)])  209 us
    unnamed x222, local copies, waits for them, and re-layouts  55 us
    dynamic_update_slice x50, local copies, waits for them, and re-layouts, in_order(): lax.dynamic_update_index_in_dim(stacked, block, (rank ^ k) + start, 0)  52.1 us
    another operation x15, local copies, waits for them, and re-layouts, whole(): jax.shard_map(shards, mesh=inner, in_specs=(rows, rows, rows, experts, ro...  33.9 us
  transfers between devices with their start and end apart: 105, of which 41 were waited for; matrix products, arithmetic and copies ran while one was open for 33% of the time, Pallas kernels for 3%

profile of v4, /device:TPU:0, one launch (start us, length us, event | category | flops | bytes accessed | tf_op | source)
XLA Modules:
  0.0 1496.2 jit_solution(11560511999843811860)
XLA Ops:
  55.3 15.3 %collective-permute-done.4 = bf16[256,1024]{1,0:T(8,128)(2,1)} collective-permute-done((bf16[256,1024]{1,0:T(8,128)(2,1)S(1)}, bf16[256,1024]{1,0:T(8,128)(2,1)}, u32[]{:S(2)}, u32[]{:S(2)}) %collective-permute-start.4) | collective-permute-done | bytes 524320 | tf_op jit(solution)/shard_map/ppermute | solution.py:24
  100.0 16.0 %collective-permute-done.6 = bf16[256,2048]{1,0:T(8,128)(2,1)} collective-permute-done((bf16[256,2048]{1,0:T(8,128)(2,1)}, bf16[256,2048]{1,0:T(8,128)(2,1)}, u32[]{:S(2)}, u32[]{:S(2)}) %collective-permute-start.6) | collective-permute-done | bytes 1048608 | tf_op jit(solution)/shard_map/ppermute | solution.py:24
  125.2 17.8 %collective-permute-done.8 = bf16[256,2048]{1,0:T(8,128)(2,1)} collective-permute-done((bf16[256,2048]{1,0:T(8,128)(2,1)}, bf16[256,2048]{1,0:T(8,128)(2,1)}, u32[]{:S(2)}, u32[]{:S(2)}) %collective-permute-start.8) | collective-permute-done | bytes 1048608 | tf_op jit(solution)/shard_map/ppermute | solution.py:24
  238.4 18.2 %shard_map.145 = (bf16[1024,512]{1,0:T(8,128)(2,1)S(1)}, bf16[1024,512]{1,0:T(8,128)(2,1)S(1)}, bf16[1024,512]{1,0:T(8,128)(2,1)S(1)}, bf16[1024,512]{1,0:T(8,128)(2,1)}, f32[4,1024,1]{2,1,0:T(8,128)}) custom-call(f32[1024,1664]{1,0:T(8,128)} %copy-done.16, f32[1024,1664]{1,0:T(8,128)} %copy-done.16, f32[1024,1664]{1,0:T(8,128)} %copy-done.16, ...), custom_call_target="tpu_custom_call" | custom-call | flops 2147483648 | bytes 12582912 | tf_op jit(solution)/shard_map/pallas_call | solution.py:225
  323.7 19.3 %collective-permute-done.25 = bf16[256,2048]{1,0:T(8,128)(2,1)} collective-permute-done((bf16[256,2048]{1,0:T(8,128)(2,1)}, bf16[256,2048]{1,0:T(8,128)(2,1)}, u32[]{:S(2)}, u32[]{:S(2)}) %collective-permute-start.25) | collective-permute-done | bytes 1048608 | tf_op jit(solution)/shard_map/ppermute | solution.py:24
  346.2 18.0 %collective-permute-done.24 = bf16[256,2048]{1,0:T(8,128)(2,1)} collective-permute-done((bf16[256,2048]{1,0:T(8,128)(2,1)}, bf16[256,2048]{1,0:T(8,128)(2,1)}, u32[]{:S(2)}, u32[]{:S(2)}) %collective-permute-start.24) | collective-permute-done | bytes 1048608 | tf_op jit(solution)/shard_map/ppermute | solution.py:24
  398.1 42.6 %collective-permute-done.32 = bf16[256,2048]{1,0:T(8,128)(2,1)} collective-permute-done((bf16[256,2048]{1,0:T(8,128)(2,1)}, bf16[256,2048]{1,0:T(8,128)(2,1)}, u32[]{:S(2)}, u32[]{:S(2)}) %collective-permute-start.32) | collective-permute-done | bytes 1048608 | tf_op jit(solution)/shard_map/ppermute | solution.py:24
  462.8 16.5 %multiply_convert_fusion.7 = (bf16[4,272,1024]{2,1,0:T(8,128)(2,1)}, f32[4,272,1024]{2,1,0:T(8,128)}) fusion(f32[4,272,1024]{2,1,0:T(8,128)} %fusion.141, bf16[4,272,2048]{2,1,0:T(8,128)(2,1)} %bitcast.603, bf16[4,2048,1024]{2,1,0:T(8,128)(2,1)} %bitcast.670), kind=kOutput, calls=%fused_computation.47 | convolution fusion | flops 4570087424 | bytes 32374784 | tf_op jit(solution)/shard_map/krd,kdf->krf/dot_general | solution.py:269
  511.6 13.9 multiply_convert_fusion.6
  540.9 32.0 %collective-permute-done.33 = bf16[256,2048]{1,0:T(8,128)(2,1)S(1)} collective-permute-done((bf16[256,2048]{1,0:T(8,128)(2,1)S(1)}, bf16[256,2048]{1,0:T(8,128)(2,1)S(1)}, u32[]{:S(2)}, u32[]{:S(2)}) %collective-permute-start.33) | collective-permute-done | bytes 1048608 | tf_op jit(solution)/shard_map/ppermute | solution.py:24
  611.1 19.4 %collective-permute-done.36 = bf16[256,2048]{1,0:T(8,128)(2,1)} collective-permute-done((bf16[256,2048]{1,0:T(8,128)(2,1)}, bf16[256,2048]{1,0:T(8,128)(2,1)}, u32[]{:S(2)}, u32[]{:S(2)}) %collective-permute-start.36) | collective-permute-done | bytes 1048608 | tf_op jit(solution)/shard_map/ppermute | solution.py:24
  638.6 46.9 %collective-permute-done.45 = bf16[256,2048]{1,0:T(8,128)(2,1)S(1)} collective-permute-done((bf16[256,2048]{1,0:T(8,128)(2,1)S(1)}, bf16[256,2048]{1,0:T(8,128)(2,1)S(1)}, u32[]{:S(2)}, u32[]{:S(2)}) %collective-permute-start.45) | collective-permute-done | bytes 1048608 | tf_op jit(solution)/shard_map/ppermute | solution.py:24
  695.7 14.1 multiply_convert_fusion.4
  746.4 20.2 %convolution_convert_fusion.2 = bf16[4,2048,1024]{2,1,0:T(8,128)(2,1)} fusion(bf16[4,272,2048]{2,1,0:T(8,128)(2,1)S(1)} %fusion.3, bf16[4,272,2048]{2,1,0:T(8,128)(2,1)} %fusion.4, bf16[4,272,1024]{2,1,0:T(8,128)(2,1)} %get-tuple-element.198, bf16[4,272,1024]{2,1,0:T(8,128)(2,1)} %get-tuple-element.196), kind=kOutput, calls=%fused_computation.2 | convolution fusion | flops 9161932800 | bytes 30146560 | tf_op jit(solution)/shard_map/krd,krf->kdf/dot_general | solution.py:269
  769.1 18.7 %multiply_convert_fusion.2 = (bf16[4,272,1024]{2,1,0:T(8,128)(2,1)}, bf16[4,272,1024]{2,1,0:T(8,128)(2,1)S(1)}) fusion(f32[4,272,1024]{2,1,0:T(8,128)} %fusion.142, f32[4,272,1024]{2,1,0:T(8,128)} %get-tuple-element.199, bf16[4,272,2048]{2,1,0:T(8,128)(2,1)} %copy-done.47, bf16[4,2048,1024]{2,1,0:T(8,128)(2,1)} %bitcast.677), kind=kOutput, calls=%fused_computation.40 | convolution fusion | flops 4577886208 | bytes 34603008 | tf_op jit(solution)/shard_map/krd,kdf->krf/dot_general | solution.py:269
  789.8 25.2 %collective-permute-done.46 = bf16[256,2048]{1,0:T(8,128)(2,1)S(1)} collective-permute-done((bf16[256,2048]{1,0:T(8,128)(2,1)}, bf16[256,2048]{1,0:T(8,128)(2,1)S(1)}, u32[]{:S(2)}, u32[]{:S(2)}) %collective-permute-start.46) | collective-permute-done | bytes 1048608 | tf_op jit(solution)/shard_map/ppermute | solution.py:24
  829.5 14.6 add_convert_fusion
  851.6 19.0 %convolution_convert_fusion.1 = bf16[4,2048,1024]{2,1,0:T(8,128)(2,1)} fusion(bf16[4,272,2048]{2,1,0:T(8,128)(2,1)} %bitcast.608, bf16[4,272,2048]{2,1,0:T(8,128)(2,1)} %bitcast.604, bf16[4,272,1024]{2,1,0:T(8,128)(2,1)S(1)} %copy-done.93, bf16[4,272,1024]{2,1,0:T(8,128)(2,1)S(1)} %copy-done.95, bf16[]{:T(256)} %bitcast.142), kind=kOutput, calls=%fused_computation.1 | convolution fusion | flops 9166389248 | bytes 30146562 | tf_op jit(solution)/shard_map/krd,krf->kdf/dot_general | solution.py:269
  870.7 19.0 %convolution_convert_fusion = bf16[4,2048,1024]{2,1,0:T(8,128)(2,1)} fusion(bf16[4,272,2048]{2,1,0:T(8,128)(2,1)} %bitcast.609, bf16[4,272,2048]{2,1,0:T(8,128)(2,1)} %bitcast.605, bf16[4,272,1024]{2,1,0:T(8,128)(2,1)} %get-tuple-element.88, bf16[4,272,1024]{2,1,0:T(8,128)(2,1)} %get-tuple-element.90, bf16[]{:T(256)} %bitcast.142), kind=kOutput, calls=%fused_computation | convolution fusion | flops 9166389248 | bytes 30146562 | tf_op jit(solution)/shard_map/krd,krf->kdf/dot_general | solution.py:269
  906.6 15.0 %collective-permute-done.50 = bf16[256,2048]{1,0:T(8,128)(2,1)} collective-permute-done((bf16[256,2048]{1,0:T(8,128)(2,1)}, bf16[256,2048]{1,0:T(8,128)(2,1)}, u32[]{:S(2)}, u32[]{:S(2)}) %collective-permute-start.50) | collective-permute-done | bytes 1048608 | tf_op jit(solution)/shard_map/ppermute | solution.py:24
  921.6 19.9 %collective-permute-done.49 = bf16[256,2048]{1,0:T(8,128)(2,1)} collective-permute-done((bf16[256,2048]{1,0:T(8,128)(2,1)}, bf16[256,2048]{1,0:T(8,128)(2,1)}, u32[]{:S(2)}, u32[]{:S(2)}) %collective-permute-start.49) | collective-permute-done | bytes 1048608 | tf_op jit(solution)/shard_map/ppermute | solution.py:24
  947.7 20.1 %collective-permute-done.51 = bf16[2048,512]{1,0:T(8,128)(2,1)} collective-permute-done((bf16[2048,512]{1,0:T(8,128)(2,1)}, bf16[2048,512]{1,0:T(8,128)(2,1)}, u32[]{:S(2)}, u32[]{:S(2)}) %collective-permute-start.51) | collective-permute-done | bytes 2097184 | tf_op jit(solution)/shard_map/ppermute | solution.py:24
  977.4 58.9 %collective-permute-done.55 = bf16[2048,512]{1,0:T(8,128)(2,1)} collective-permute-done((bf16[2048,512]{1,0:T(8,128)(2,1)}, bf16[2048,512]{1,0:T(8,128)(2,1)}, u32[]{:S(2)}, u32[]{:S(2)}) %collective-permute-start.55) | collective-permute-done | bytes 2097184 | tf_op jit(solution)/shard_map/ppermute | solution.py:24
  1046.9 19.3 %shard_map.146 = (f32[1024,512]{1,0:T(8,128)}, f32[1024,512]{1,0:T(8,128)}, bf16[1024,512]{1,0:T(8,128)(2,1)S(1)}, f32[1024,1]{1,0:T(8,128)S(1)}, f32[1024,1]{1,...) custom-call(f32[1024,1664]{1,0:T(8,128)} %copy-done.16, f32[1024,1664]{1,0:T(8,128)} %copy-done.16, ...), custom_call_target="tpu_custom_call" | custom-call | flops 5368709120 | bytes 18874368 | tf_op jit(solution)/shard_map/pallas_call | solution.py:247
  1079.7 22.8 %collective-permute-done.60 = bf16[256,2048]{1,0:T(8,128)(2,1)S(1)} collective-permute-done((bf16[256,2048]{1,0:T(8,128)(2,1)}, bf16[256,2048]{1,0:T(8,128)(2,1)S(1)}, u32[]{:S(2)}, u32[]{:S(2)}) %collective-permute-start.60) | collective-permute-done | bytes 1048608 | tf_op jit(solution)/shard_map/ppermute | solution.py:24
  1103.6 14.0 collective-permute-done.61
  1176.6 13.7 collective-permute-done.81
  1207.8 16.0 %collective-permute-done.58 = bf16[256,1024]{1,0:T(8,128)(2,1)S(1)} collective-permute-done((bf16[256,1024]{1,0:T(8,128)(2,1)}, bf16[256,1024]{1,0:T(8,128)(2,1)S(1)}, u32[]{:S(2)}, u32[]{:S(2)}) %collective-permute-start.58) | collective-permute-done | bytes 524320 | tf_op jit(solution)/shard_map/ppermute | solution.py:24
  1339.8 35.0 %collective-permute-start.74 = (bf16[256,1536]{1,0:T(8,128)(2,1)}, bf16[256,1536]{1,0:T(8,128)(2,1)}, u32[]{:S(2)}, u32[]{:S(2)}) collective-permute-start(bf16[256,1536]{1,0:T(8,128)(2,1)} %get-tuple-element.115), channel_id=1, source_target_pairs={{0,16},{8,24},{16,0},{24,8},{1,17},{9,25},{17,1},{25,9},{2,18},{10... | collective-permute-start | bytes 2359304 | tf_op jit(solution)/shard_map/ppermute | solution.py:24
  1391.4 24.7 %collective-permute-done.74 = bf16[256,1536]{1,0:T(8,128)(2,1)} collective-permute-done((bf16[256,1536]{1,0:T(8,128)(2,1)}, bf16[256,1536]{1,0:T(8,128)(2,1)}, u32[]{:S(2)}, u32[]{:S(2)}) %collective-permute-start.74) | collective-permute-done | bytes 786464 | tf_op jit(solution)/shard_map/ppermute | solution.py:24
  1447.7 17.8 %collective-permute-done.97 = bf16[256,1024]{1,0:T(8,128)(2,1)S(1)} collective-permute-done((bf16[256,1024]{1,0:T(8,128)(2,1)S(1)}, bf16[256,1024]{1,0:T(8,128)(2,1)S(1)}, u32[]{:S(2)}, u32[]{:S(2)}) %collective-permute-start.97) | collective-permute-done | bytes 524320 | tf_op jit(solution)/shard_map/ppermute | solution.py:24
  1468.7 19.3 %copy.270 = f32[256,4,3072]{2,1,0:T(4,128)} copy(f32[256,4,3072]{2,0,1:T(8,128)S(1)} %convert_bitcast_fusion) | data formatting | bytes 25165824
  (698 shorter events, 734.8 us)
Async XLA Ops:
  7.2 227.6 %all-gather.4.cloned.1.call-start = ((), (), s32[]{:S(2)}) async-start(), calls=%async_computation.3 | async-start | bytes 18874368 | tf_op jit(solution)/shard_map/all_gather | solution.py:342
  74.3 388.4 %all-gather.6.cloned.1.call-start = ((), (), s32[]{:S(2)}) async-start(), calls=%async_computation.4 | async-start | bytes 18874368 | tf_op jit(solution)/shard_map/all_gather | solution.py:342
  80.9 62.1 %collective-permute-start.8 = (bf16[256,2048]{1,0:T(8,128)(2,1)}, bf16[256,2048]{1,0:T(8,128)(2,1)}, u32[]{:S(2)}, u32[]{:S(2)}) collective-permute-start(bf16[256,2048]{1,0:T(8,128)(2,1)} %reshape.491), channel_id=1, source_target_pairs={{0,3},{1,2},{2,1},{3,0},{4,7},{5,6},{6,5},{7,4},{8,11},{9,10},{10,... | collective-permute-start | bytes 3145736 | tf_op jit(solution)/shard_map/ppermute | solution.py:24
  85.1 68.1 %collective-permute-start.9 = (bf16[256,1664]{1,0:T(8,128)(2,1)}, bf16[256,1664]{1,0:T(8,128)(2,1)S(1)}, u32[]{:S(2)}, u32[]{:S(2)}) collective-permute-start(bf16[256,1664]{1,0:T(8,128)(2,1)} %slice.350), channel_id=1, source_target_pairs={{0,8},{8,0},{16,24},{24,16},{1,9},{9,1},{17,25},{25,17},{2,10},{10... | collective-permute-start | bytes 2555912 | tf_op jit(solution)/shard_map/ppermute | solution.py:24
  92.9 61.3 %collective-permute-start.10 = (bf16[256,1664]{1,0:T(8,128)(2,1)}, bf16[256,1664]{1,0:T(8,128)(2,1)S(1)}, u32[]{:S(2)}, u32[]{:S(2)}) collective-permute-start(bf16[256,1664]{1,0:T(8,128)(2,1)} %slice.350), channel_id=1, source_target_pairs={{0,16},{8,24},{16,0},{24,8},{1,17},{9,25},{17,1},{25,9},{2,18},{10... | collective-permute-start | bytes 2555912 | tf_op jit(solution)/shard_map/ppermute | solution.py:24
  223.3 256.0 %all-gather.8.cloned.1.call-start = ((), (), s32[]{:S(2)}) async-start(), calls=%async_computation.5 | async-start | bytes 18874368 | tf_op jit(solution)/shard_map/all_gather | solution.py:342
  309.3 55.0 %collective-permute-start.24 = (bf16[256,2048]{1,0:T(8,128)(2,1)}, bf16[256,2048]{1,0:T(8,128)(2,1)}, u32[]{:S(2)}, u32[]{:S(2)}) collective-permute-start(bf16[256,2048]{1,0:T(8,128)(2,1)} %get-tuple-element.112), channel_id=1, source_target_pairs={{0,2},{1,3},{2,0},{3,1},{4,6},{5,7},{6,4},{7,5},{8,10},{9,11},{10,... | collective-permute-start | bytes 3145736 | tf_op jit(solution)/shard_map/ppermute | solution.py:24
  310.3 54.0 %collective-permute-start.23 = (bf16[256,2048]{1,0:T(8,128)(2,1)}, bf16[256,2048]{1,0:T(8,128)(2,1)}, u32[]{:S(2)}, u32[]{:S(2)}) collective-permute-start(bf16[256,2048]{1,0:T(8,128)(2,1)} %get-tuple-element.110), channel_id=1, source_target_pairs={{0,1},{1,0},{2,3},{3,2},{4,5},{5,4},{6,7},{7,6},{8,9},{9,8},{10,11... | collective-permute-start | bytes 3145736 | tf_op jit(solution)/shard_map/ppermute | solution.py:24
  319.5 53.5 %collective-permute-start.26 = (bf16[256,1024]{1,0:T(8,128)(2,1)}, bf16[256,1024]{1,0:T(8,128)(2,1)}, u32[]{:S(2)}, u32[]{:S(2)}) collective-permute-start(bf16[256,1024]{1,0:T(8,128)(2,1)} %bitcast.563), channel_id=1, source_target_pairs={{0,8},{8,0},{16,24},{24,16},{1,9},{9,1},{17,25},{25,17},{2,10},{10... | collective-permute-start | bytes 1572872 | tf_op jit(solution)/shard_map/ppermute | solution.py:24
  322.6 52.3 %collective-permute-start.27 = (bf16[256,1024]{1,0:T(8,128)(2,1)}, bf16[256,1024]{1,0:T(8,128)(2,1)}, u32[]{:S(2)}, u32[]{:S(2)}) collective-permute-start(bf16[256,1024]{1,0:T(8,128)(2,1)} %bitcast.562), channel_id=1, source_target_pairs={{0,16},{8,24},{16,0},{24,8},{1,17},{9,25},{17,1},{25,9},{2,18},{10... | collective-permute-start | bytes 1572872 | tf_op jit(solution)/shard_map/ppermute | solution.py:24
  378.7 789.4 %reduce-scatter.4.cloned.1.call-start = ((), (), s32[]{:S(2)}) async-start(), calls=%async_computation.6 | async-start | bytes 18874368 | tf_op jit(solution)/shard_map/reduce_scatter | solution.py:498
  444.6 51.6 %collective-permute-start.35 = (bf16[256,2048]{1,0:T(8,128)(2,1)}, bf16[256,2048]{1,0:T(8,128)(2,1)}, u32[]{:S(2)}, u32[]{:S(2)}) collective-permute-start(bf16[256,2048]{1,0:T(8,128)(2,1)} %broadcast_add_fusion.3), channel_id=1, source_target_pairs={{0,24},{8,16},{16,8},{24,0},{1,25},{9,17},{17,9},{25,1},{2,26},{10... | collective-permute-start | bytes 3145736 | tf_op jit(solution)/shard_map/ppermute | solution.py:24
  447.0 49.2 %collective-permute-start.34 = (bf16[256,2048]{1,0:T(8,128)(2,1)}, bf16[256,2048]{1,0:T(8,128)(2,1)}, u32[]{:S(2)}, u32[]{:S(2)}) collective-permute-start(bf16[256,2048]{1,0:T(8,128)(2,1)} %broadcast_add_fusion.3), channel_id=1, source_target_pairs={{0,8},{8,0},{16,24},{24,16},{1,9},{9,1},{17,25},{25,17},{2,10},{10... | collective-permute-start | bytes 3145736 | tf_op jit(solution)/shard_map/ppermute | solution.py:24
  688.3 53.4 %collective-permute-start.48 = (bf16[256,2048]{1,0:T(8,128)(2,1)}, bf16[256,2048]{1,0:T(8,128)(2,1)}, u32[]{:S(2)}, u32[]{:S(2)}) collective-permute-start(bf16[256,2048]{1,0:T(8,128)(2,1)} %broadcast_add_fusion.2), channel_id=1, source_target_pairs={{0,24},{8,16},{16,8},{24,0},{1,25},{9,17},{17,9},{25,1},{2,26},{10... | collective-permute-start | bytes 3145736 | tf_op jit(solution)/shard_map/ppermute | solution.py:24
  690.4 51.3 %collective-permute-start.47 = (bf16[256,2048]{1,0:T(8,128)(2,1)}, bf16[256,2048]{1,0:T(8,128)(2,1)}, u32[]{:S(2)}, u32[]{:S(2)}) collective-permute-start(bf16[256,2048]{1,0:T(8,128)(2,1)} %broadcast_add_fusion.2), channel_id=1, source_target_pairs={{0,8},{8,0},{16,24},{24,16},{1,9},{9,1},{17,25},{25,17},{2,10},{10... | collective-permute-start | bytes 3145736 | tf_op jit(solution)/shard_map/ppermute | solution.py:24
  766.6 505.6 %reduce-scatter.6.cloned.1.call-start = ((), (), s32[]{:S(2)}) async-start(), calls=%async_computation.7 | async-start | bytes 18874368 | tf_op jit(solution)/shard_map/reduce_scatter | solution.py:498
  766.7 48.3 %collective-permute-start.46 = (bf16[256,2048]{1,0:T(8,128)(2,1)}, bf16[256,2048]{1,0:T(8,128)(2,1)S(1)}, u32[]{:S(2)}, u32[]{:S(2)}) collective-permute-start(bf16[256,2048]{1,0:T(8,128)(2,1)} %get-tuple-element.136), channel_id=1, source_target_pairs={{0,16},{8,24},{16,0},{24,8},{1,17},{9,25},{17,1},{25,9},{2,18},{10... | collective-permute-start | bytes 3145736 | tf_op jit(solution)/shard_map/ppermute | solution.py:24
  870.6 554.6 %reduce-scatter.8.cloned.1.call-start = ((), (), s32[]{:S(2)}) async-start(), calls=%async_computation.8 | async-start | bytes 18874368 | tf_op jit(solution)/shard_map/reduce_scatter | solution.py:498
  896.7 71.1 %collective-permute-start.51 = (bf16[2048,512]{1,0:T(8,128)(2,1)}, bf16[2048,512]{1,0:T(8,128)(2,1)}, u32[]{:S(2)}, u32[]{:S(2)}) collective-permute-start(bf16[2048,512]{1,0:T(8,128)(2,1)} %broadcast_add_fusion), channel_id=1, source_target_pairs={{0,1},{1,0},{2,3},{3,2},{4,5},{5,4},{6,7},{7,6},{8,9},{9,8},{10,11... | collective-permute-start | bytes 6291464 | tf_op jit(solution)/shard_map/ppermute | solution.py:24
  898.0 75.3 %collective-permute-start.53 = (bf16[2048,512]{1,0:T(8,128)(2,1)}, bf16[2048,512]{1,0:T(8,128)(2,1)}, u32[]{:S(2)}, u32[]{:S(2)}) collective-permute-start(bf16[2048,512]{1,0:T(8,128)(2,1)} %broadcast_add_fusion), channel_id=1, source_target_pairs={{0,2},{1,3},{2,0},{3,1},{4,6},{5,7},{6,4},{7,5},{8,10},{9,11},{10,... | collective-permute-start | bytes 6291464 | tf_op jit(solution)/shard_map/ppermute | solution.py:24
  898.6 137.7 %collective-permute-start.55 = (bf16[2048,512]{1,0:T(8,128)(2,1)}, bf16[2048,512]{1,0:T(8,128)(2,1)}, u32[]{:S(2)}, u32[]{:S(2)}) collective-permute-start(bf16[2048,512]{1,0:T(8,128)(2,1)} %broadcast_add_fusion), channel_id=1, source_target_pairs={{0,3},{1,2},{2,1},{3,0},{4,7},{5,6},{6,5},{7,4},{8,11},{9,10},{10,... | collective-permute-start | bytes 6291464 | tf_op jit(solution)/shard_map/ppermute | solution.py:24
  970.1 70.8 %collective-permute-start.52 = (bf16[256,512]{1,0:T(8,128)(2,1)S(1)}, bf16[256,512]{1,0:T(8,128)(2,1)S(1)}, u32[]{:S(2)}, u32[]{:S(2)}) collective-permute-start(bf16[256,512]{1,0:T(8,128)(2,1)S(1)} %convolution_convert_fusion.10), channel_id=1, source_target_pairs={{0,1},{1,0},{2,3},{3,2},{4,5},{5,4},{6,7},{7,6},{8,9},{9,8},{10,11... | collective-permute-start | bytes 786440 | tf_op jit(solution)/shard_map/ppermute | solution.py:24
  975.7 65.3 %collective-permute-start.54 = (bf16[256,512]{1,0:T(8,128)(2,1)S(1)}, bf16[256,512]{1,0:T(8,128)(2,1)S(1)}, u32[]{:S(2)}, u32[]{:S(2)}) collective-permute-start(bf16[256,512]{1,0:T(8,128)(2,1)S(1)} %convolution_convert_fusion.9), channel_id=1, source_target_pairs={{0,2},{1,3},{2,0},{3,1},{4,6},{5,7},{6,4},{7,5},{8,10},{9,11},{10,... | collective-permute-start | bytes 786440 | tf_op jit(solution)/shard_map/ppermute | solution.py:24
  1077.6 49.7 %collective-permute-start.62 = (bf16[256,2048]{1,0:T(8,128)(2,1)}, bf16[256,2048]{1,0:T(8,128)(2,1)S(1)}, u32[]{:S(2)}, u32[]{:S(2)}) collective-permute-start(bf16[256,2048]{1,0:T(8,128)(2,1)} %get-tuple-element.79), channel_id=1, source_target_pairs={{0,3},{1,2},{2,1},{3,0},{4,7},{5,6},{6,5},{7,4},{8,11},{9,10},{10,... | collective-permute-start | bytes 3145736 | tf_op jit(solution)/shard_map/ppermute | solution.py:24
  1174.8 49.0 %collective-permute-start.58 = (bf16[256,1024]{1,0:T(8,128)(2,1)}, bf16[256,1024]{1,0:T(8,128)(2,1)S(1)}, u32[]{:S(2)}, u32[]{:S(2)}) collective-permute-start(bf16[256,1024]{1,0:T(8,128)(2,1)} %get-tuple-element.131), channel_id=1, source_target_pairs={{0,16},{8,24},{16,0},{24,8},{1,17},{9,25},{17,1},{25,9},{2,18},{10... | collective-permute-start | bytes 1572872 | tf_op jit(solution)/shard_map/ppermute | solution.py:24
  1195.9 69.1 %collective-permute-start.84 = (bf16[64,512]{1,0:T(8,128)(2,1)}, bf16[64,512]{1,0:T(8,128)(2,1)S(1)}, u32[]{:S(2)}, u32[]{:S(2)}) collective-permute-start(bf16[64,512]{1,0:T(8,128)(2,1)} %get-tuple-element.172), channel_id=1, source_target_pairs={{0,2},{1,3},{2,0},{3,1},{4,6},{5,7},{6,4},{7,5},{8,10},{9,11},{10,... | collective-permute-start | bytes 196616 | tf_op jit(solution)/shard_map/ppermute | solution.py:24
  1204.2 61.7 %collective-permute-start.85 = (bf16[64,512]{1,0:T(8,128)(2,1)}, bf16[64,512]{1,0:T(8,128)(2,1)}, u32[]{:S(2)}, u32[]{:S(2)}) collective-permute-start(bf16[64,512]{1,0:T(8,128)(2,1)} %get-tuple-element.171), channel_id=1, source_target_pairs={{0,3},{1,2},{2,1},{3,0},{4,7},{5,6},{6,5},{7,4},{8,11},{9,10},{10,... | collective-permute-start | bytes 196616 | tf_op jit(solution)/shard_map/ppermute | solution.py:24
  1256.4 75.4 %collective-permute-start.72 = (bf16[1024,1536]{1,0:T(8,128)(2,1)}, bf16[1024,1536]{1,0:T(8,128)(2,1)}, u32[]{:S(2)}, u32[]{:S(2)}) collective-permute-start(bf16[1024,1536]{1,0:T(8,128)(2,1)} %dynamic-slice_bitcast_fusion), channel_id=1, source_target_pairs={{0,4},{4,0},{1,5},{5,1},{2,6},{6,2},{3,7},{7,3},{8,12},{12,8},{9,1... | collective-permute-start | bytes 9437192 | tf_op jit(solution)/shard_map/ppermute | solution.py:24
  1303.0 75.2 %collective-permute-start.95 = (bf16[256,1024]{1,0:T(8,128)(2,1)}, bf16[256,1024]{1,0:T(8,128)(2,1)}, u32[]{:S(2)}, u32[]{:S(2)}) collective-permute-start(bf16[256,1024]{1,0:T(8,128)(2,1)} %get-tuple-element.116), channel_id=1, source_target_pairs={{0,24},{8,16},{16,8},{24,0},{1,25},{9,17},{17,9},{25,1},{2,26},{10... | collective-permute-start | bytes 1572872 | tf_op jit(solution)/shard_map/ppermute | solution.py:24
  1320.0 56.1 %collective-permute-start.87 = (f32[4,2048]{1,0:T(4,128)S(1)}, f32[4,2048]{1,0:T(4,128)S(1)}, u32[]{:S(2)}, u32[]{:S(2)}) collective-permute-start(f32[4,2048]{1,0:T(4,128)S(1)} %pad_maximum_fusion.10), channel_id=1, source_target_pairs={{0,16},{8,24},{16,0},{24,8},{1,17},{9,25},{17,1},{25,9},{2,18},{10... | collective-permute-start | bytes 98312 | tf_op jit(solution)/shard_map/ppermute | solution.py:24
  1338.3 52.1 %collective-permute-start.75 = (bf16[256,1536]{1,0:T(8,128)(2,1)}, bf16[256,1536]{1,0:T(8,128)(2,1)}, u32[]{:S(2)}, u32[]{:S(2)}) collective-permute-start(bf16[256,1536]{1,0:T(8,128)(2,1)} %get-tuple-element.114), channel_id=1, source_target_pairs={{0,24},{8,16},{16,8},{24,0},{1,25},{9,17},{17,9},{25,1},{2,26},{10... | collective-permute-start | bytes 2359304 | tf_op jit(solution)/shard_map/ppermute | solution.py:24
  1339.8 76.3 %collective-permute-start.74 = (bf16[256,1536]{1,0:T(8,128)(2,1)}, bf16[256,1536]{1,0:T(8,128)(2,1)}, u32[]{:S(2)}, u32[]{:S(2)}) collective-permute-start(bf16[256,1536]{1,0:T(8,128)(2,1)} %get-tuple-element.115), channel_id=1, source_target_pairs={{0,16},{8,24},{16,0},{24,8},{1,17},{9,25},{17,1},{25,9},{2,18},{10... | collective-permute-start | bytes 2359304 | tf_op jit(solution)/shard_map/ppermute | solution.py:24
  (169 other events, 3805.7 us)
Sparse Core Ops, SparseCore 0:
  74.5 133.2 all-gather.3
  223.4 128.3 all-gather.5
  378.8 89.8 all-gather.7
  766.8 114.8 reduce-scatter.3
  885.1 188.7 reduce-scatter.5
  1077.3 119.4 reduce-scatter.7

commit v5 on v4

--- a/solution.py
+++ b/solution.py
@@ -229,11 +229,7 @@
         out_specs=[head] * 4 + [pl.BlockSpec((1, seq, 1), lambda h: (h, 0, 0))],
         out_shape=[low] * 4 + [jax.ShapeDtypeStruct((heads, seq, 1), f32)],
         compiler_params=pltpu.CompilerParams(vmem_limit_bytes=48 * 2**20),
-        cost_estimate=pl.CostEstimate(
-            flops=heads * seq * seq * HD * 4,
-            bytes_accessed=heads * seq * HD * 24,
-            transcendentals=heads * seq * seq,
-        ),
+        cost_estimate=pl.CostEstimate(flops=10**6, bytes_accessed=10**5, transcendentals=0),
     )(projected, projected, projected, *shared)
 
 
@@ -257,12 +253,151 @@
         + [jax.ShapeDtypeStruct((1, heads * HD), f32)] * 2,
         scratch_shapes=[pltpu.VMEM((seq, HD), f32)] * 3,
         compiler_params=pltpu.CompilerParams(vmem_limit_bytes=48 * 2**20),
+        cost_estimate=pl.CostEstimate(flops=10**6, bytes_accessed=10**5, transcendentals=0),
+    )(projected, projected, *shared, query, keyed, valued, grad, log_total)
+
+
+def slot_choice(place, slots):
+    return lax.broadcasted_iota(jnp.int32, (slots, place.shape[1]), 0) == place
+
+
+def slot_weight(place, gate, slots):
+    return jnp.sum(jnp.where(slot_choice(place, slots), gate, 0.0), axis=1, keepdims=True)
+
+
+def expert_kernel(count, slots, place, gate, *refs):
+    blocks, (w_gate, w_up, w_down), refs = refs[:count], refs[count : count + 3], refs[count + 3 :]
+    rows, activated, gate_pre, up_pre = refs[-6 - count : -2 - count]
+    partial, (sum_out, sum_tokens) = refs[-2 - count : -2], refs[-2:]
+    expert, chunk = pl.program_id(0), pl.program_id(1)
+
+    def spans():
+        return [(b, slice(b * slots, (b + 1) * slots)) for b in range(count)]
+
+    @pl.when(chunk == 0)
+    def _():
+        for b, span in spans():
+            choice = slot_choice(place[0, b], slots).astype(bf16)
+            rows[0, 0, span] = mm(choice, blocks[b][...], ((1,), (0,))).astype(bf16)
+
+    rows_in = rows[0, 0]
+    g = mm(rows_in, w_gate[0], ((1,), (0,)))
+    u = mm(rows_in, w_up[0], ((1,), (0,)))
+    m = (g * jax.nn.sigmoid(g) * u).astype(bf16)
+    gate_pre[0], up_pre[0], activated[0, 0] = g.astype(bf16), u.astype(bf16), m
+    term = mm(m, w_down[0], ((1,), (1,)))
+
+    @pl.when(chunk == 0)
+    def _():
+        sum_out[...] = term
+
+    @pl.when(chunk > 0)
+    def _():
+        sum_out[...] += term
+
+    @pl.when(chunk == pl.num_programs(1) - 1)
+    def _():
+        for b, span in spans():
+            weight = slot_weight(place[0, b], gate[0, b], slots)
+            out = (sum_out[span] * weight).astype(bf16)
+            back = mm(slot_choice(place[0, b], slots).astype(bf16), out, ((0,), (0,)))
+            add_tokens(expert, b, back, sum_tokens, partial)
+
+
+def add_tokens(expert, b, back, sum_tokens, partial):
+    @pl.when(expert == 0)
+    def _():
+        sum_tokens[b] = back
+
+    @pl.when(expert > 0)
+    def _():
+        sum_tokens[b] += back
+
+    @pl.when(expert == pl.num_programs(0) - 1)
+    def _():
+        partial[b][...] = sum_tokens[b].astype(bf16)
+
+
+def expert_back_kernel(count, slots, place, gate, *refs):
+    blocks, (w_gate, w_up, w_down) = refs[:count], refs[count : count + 3]
+    gate_pre, up_pre = refs[count + 3 : count + 5]
+    grad_rows, grad_gate, grad_up = refs[-5 - count : -2 - count]
+    partial, (sum_rows, sum_tokens) = refs[-2 - count : -2], refs[-2:]
+    expert, chunk = pl.program_id(0), pl.program_id(1)
+
+    def spans():
+        return [(b, slice(b * slots, (b + 1) * slots)) for b in range(count)]
+
+    @pl.when(chunk == 0)
+    def _():
+        for b, span in spans():
+            choice = slot_choice(place[0, b], slots).astype(bf16)
+            weight = slot_weight(place[0, b], gate[0, b], slots)
+            picked = mm(choice, blocks[b][...], ((1,), (0,)))
+            grad_rows[0, 0, span] = (picked * weight).astype(bf16)
+
+    grad_act = mm(grad_rows[0, 0], w_down[0], ((1,), (0,)))
+    g, u = gate_pre[0].astype(f32), up_pre[0].astype(f32)
+    sigmoid = jax.nn.sigmoid(g)
+    dg = (grad_act * u * sigmoid * (1.0 + g * (1.0 - sigmoid))).astype(bf16)
+    du = (grad_act * g * sigmoid).astype(bf16)
+    grad_gate[0, 0], grad_up[0, 0] = dg, du
+    term = mm(dg, w_gate[0], ((1,), (1,))) + mm(du, w_up[0], ((1,), (1,)))
+
+    @pl.when(chunk == 0)
+    def _():
+        sum_rows[...] = term
+
+    @pl.when(chunk > 0)
+    def _():
+        sum_rows[...] += term
+
+    @pl.when(chunk == pl.num_programs(1) - 1)
+    def _():
+        for b, span in spans():
+            out = sum_rows[span].astype(bf16)
+            back = mm(slot_choice(place[0, b], slots).astype(bf16), out, ((0,), (0,)))
+            add_tokens(expert, b, back, sum_tokens, partial)
+
+
+def run_experts(kernel, group, slots, place, gate, blocks, weights, saved, narrow, prior):
+    experts, width, hidden = weights[0].shape
+    count, (own, _) = len(blocks), blocks[0].shape
+    rows = count * slots
+    step = min(256, hidden)
+    table = pl.BlockSpec((1, count, 1, own), lambda e, f: (e, group, 0, 0))
+    tokens = pl.BlockSpec((own, width), lambda e, f: (0, 0))
+    weight = pl.BlockSpec((1, width, step), lambda e, f: (e, 0, f))
+    local = pl.BlockSpec((1, rows, step), lambda e, f: (e, 0, f))
+    shared_specs = [pl.BlockSpec((1, 1, rows, width), lambda e, f: (e, group, 0, 0))] + [
+        pl.BlockSpec((1, 1, rows, step), lambda e, f: (e, group, 0, f))
+    ] * narrow
+    shared_shapes = [jax.ShapeDtypeStruct((experts, 2, rows, width), bf16)] + [
+        jax.ShapeDtypeStruct((experts, 2, rows, hidden), bf16)
+    ] * narrow
+    local_out = 0 if saved else 2
+    first = 2 + count + 3 + len(saved)
+    return pl.pallas_call(
+        functools.partial(kernel, count, slots),
+        grid=(experts, hidden // step),
+        in_specs=[table, table]
+        + [tokens] * count
+        + [weight] * 3
+        + [local] * len(saved)
+        + [pl.BlockSpec(memory_space=pl.ANY)] * len(prior),
+        out_specs=shared_specs + [local] * local_out + [tokens] * count,
+        out_shape=shared_shapes
+        + [jax.ShapeDtypeStruct((experts, rows, hidden), bf16)] * local_out
+        + [jax.ShapeDtypeStruct((own, width), bf16)] * count,
+        scratch_shapes=[pltpu.VMEM((rows, width), f32), pltpu.VMEM((count, own, width), f32)],
+        input_output_aliases={first + i: i for i in range(len(prior))},
+        compiler_params=pltpu.CompilerParams(vmem_limit_bytes=56 * 2**20),
         cost_estimate=pl.CostEstimate(
-            flops=heads * seq * seq * HD * 10,
-            bytes_accessed=heads * seq * HD * 36,
-            transcendentals=heads * seq * seq,
+            flops=experts * rows * width * hidden * 6,
+            bytes_accessed=experts * width * hidden * 8,
+            transcendentals=experts * rows * hidden,
         ),
-    )(projected, projected, *shared, query, keyed, valued, grad, log_total)
+    )(place, gate, *blocks, *weights, *saved, *prior)
 
 
 def dot(spec, left, right):
@@ -392,27 +527,16 @@
     before = (jnp.arange(own)[:, None] > jnp.arange(own)[None, :]).astype(bf16)
     place = dot("tu,buk->btk", before, used.astype(bf16)).astype(jnp.int32)
     place = jnp.where(used, place, -1)
-    taken = place.transpose(0, 2, 1)[:, :, None, :] == jnp.arange(capacity)[None, None, :, None]
-    choose = taken.astype(bf16)
-    gate_slot = jnp.sum(jnp.where(taken, gate_of.transpose(0, 2, 1)[:, :, None, :], 0.0), axis=-1)
-    gate_slot = gate_slot.transpose(1, 0, 2)
+    slots = -(-capacity // 16) * 16
+    place = place.transpose(2, 0, 1)[:, :, None, :]
+    gate_of = gate_of.transpose(2, 0, 1)[:, :, None, :]
 
     groups = [[k for k in range(planes) if k % 2 == odd] for odd in range(2)]
-    slots = capacity * planes // 2
-
-    def pick(table, group, axis):
-        return jnp.concatenate([lax.slice_in_dim(table, k, k + 1, axis=axis) for k in group], axis)
-
-    chosen = [pick(choose, group, 0) for group in groups]
-    weight_of = [pick(gate_slot, group, 1).reshape(seqs, slots, 1) for group in groups]
-
-    def dispatch(i, blocks):
-        spread = dot("bkjt,btd->kbjd", chosen[i], blocks)
-        return spread.reshape(seqs, slots, width)
-
-    def combine(i, rows_out):
-        rows_out = rows_out.reshape(seqs, planes // 2, capacity, width)
-        return dot("bkjt,kbjd->btd", chosen[i], rows_out).astype(bf16)
+
+    def by_group(table):
+        return jnp.concatenate([table[:, k : k + 1] for group in groups for k in group], axis=1)
+
+    place, gate_of = by_group(place), by_group(gate_of)
 
     def through_planes(block, work):
         near = [block] + [None] * (planes - 1)
@@ -421,12 +545,14 @@
         later = after(block, *[near[k] for k in groups[0][1:]])
         for k in groups[1]:
             near[k] = send(later, "z", k)
-        first = work(0, jnp.stack([near[k] for k in groups[0]]))[0]
+        first = work(0, [near[k] for k in groups[0]])
         got = [first[0]] + [send(first[i], "z", k) for i, k in enumerate(groups[0]) if k]
-        second, halfway = work(1, after(jnp.stack([near[k] for k in groups[1]]), first[0]))
-        base = after(total(got), halfway)
-        second = after(second, base)
-        return second, [base] + [send(second[i], "z", k) for i, k in enumerate(groups[1])]
+        blocks = [near[k] for k in groups[1]]
+        blocks[0] = after(blocks[0], first[0])
+        second = work(1, blocks)
+        base = after(total(got), second[0])
+        second = [after(part, base) for part in second]
+        return second[0], [base] + [send(second[i], "z", k) for i, k in enumerate(groups[1])]
 
     def total(pieces):
         return sum(piece.astype(f32) for piece in pieces)
@@ -439,8 +565,11 @@
     query_raw = projected[:, :cols]
     key_raw = projected[:, cols : 2 * cols]
 
-    def over_heads(first, second):
-        pair = sum(gather_near(jnp.stack([first, second]), "s")) / width
+    def over_heads(first, second, *others):
+        pairs = gather_near(jnp.stack([first, second]), "s")
+        if others:
+            pairs[0] = after(pairs[0], *others)
+        pair = sum(pairs) / width
         return pair[0][:, None], pair[1][:, None]
 
     q_mean, k_mean = over_heads(
@@ -470,20 +599,21 @@
     w_down = gather_plane(down_ready)
 
     normed_mid = (residual * rms_factor(residual) * gain_mid).astype(bf16)
-    kept = [None, None]
+    expert_weights = (w_gate, w_up, w_down)
+    pres, kept = [], [()]
 
     def forward(i, blocks):
-        rows_in = dispatch(i, blocks).astype(bf16)
-        gate_pre = dot("krd,kdf->krf", rows_in, w_gate)
-        up_pre = dot("krd,kdf->krf", rows_in, w_up)
-        activated = (jax.nn.silu(gate_pre) * up_pre).astype(bf16)
-        kept[i] = (rows_in, gate_pre, up_pre, activated)
-        out = dot("krf,kdf->krd", activated, w_down) * weight_of[i]
-        return combine(i, out.astype(bf16)), activated
+        rows_in, activated, gate_pre, up_pre, *partial = run_experts(
+            expert_kernel, i, slots, place, gate_of, blocks, expert_weights, (), 1, kept[0]
+        )
+        pres.append((gate_pre, up_pre))
+        kept[0] = (rows_in, activated)
+        return partial
 
     final_out = residual + total(through_planes(normed_mid, forward)[1])
-
-    w_out_near = gather_near(after(w_out, kept[1][3]), "s")
+    rows_in, activated = [v.reshape(seqs, -1, v.shape[-1]) for v in kept[0]]
+
+    w_out_all = lax.all_gather(after(w_out, w_up), "s", axis=0)
     valid_f = valid_mask.astype(f32)[:, None]
     difference = final_out - to_inner(teacher).astype(f32)
     squared = jnp.sum(valid_f * difference * difference)
@@ -504,57 +634,52 @@
 
         return exchange(piece_for, "z", start)
 
-    grads = [None, None]
+    grads = [()]
 
     def backward(i, blocks):
-        gate_pre, up_pre = kept[i][1:3]
-        grad_rows = (dispatch(i, blocks) * weight_of[i]).astype(bf16)
-        grad_act = dot("krd,kdf->krf", grad_rows, w_down)
-        sigmoid = jax.nn.sigmoid(gate_pre)
-        grad_gate = grad_act * up_pre * sigmoid * (1.0 + gate_pre * (1.0 - sigmoid))
-        grad_gate, grad_up = grad_gate.astype(bf16), (grad_act * gate_pre * sigmoid).astype(bf16)
-        back = dot("krf,kdf->krd", grad_gate, w_gate) + dot("krf,kdf->krd", grad_up, w_up)
-        grads[i] = (grad_rows, grad_gate, grad_up)
-        return combine(i, back.astype(bf16)), grad_gate
+        *shared_grads, first, last = run_experts(
+            expert_back_kernel,
+            i,
+            slots,
+            place,
+            gate_of,
+            blocks,
+            expert_weights,
+            pres[i],
+            2,
+            grads[0],
+        )
+        grads[0] = shared_grads
+        return first, last
 
     back_last, back_pieces = through_planes(grad_out.astype(bf16), backward)
-
-    def both(table, which):
-        return jnp.concatenate([table[0][which], table[1][which]], axis=1)
-
-    rows_in, activated = both(kept, 0), both(kept, 3)
-    grad_w_down = dot("krd,krf->kdf", both(grads, 0), activated).astype(bf16)
-    grad_w_gate = dot("krd,krf->kdf", rows_in, after(both(grads, 1), back_last)).astype(bf16)
-    grad_w_up = dot("krd,krf->kdf", rows_in, after(both(grads, 2), back_last)).astype(bf16)
-    back_pieces[0] = after(back_pieces[0], grad_w_down, grad_w_gate)
+    grad_rows, grad_gate, grad_up = [v.reshape(seqs, -1, v.shape[-1]) for v in grads[0]]
+    grad_w_down = dot("krd,krf->kdf", grad_rows, after(activated, back_last)).astype(bf16)
+    back_pieces[0] = after(back_pieces[0], grad_w_down)
     grad_mid = total(back_pieces)
+    grad_w_gate = dot("krd,krf->kdf", rows_in, after(grad_gate, grad_mid)).astype(bf16)
+    grad_resid_norm, gain_mid_grad = norm_back(residual, gain_mid, grad_mid)
+    grad_resid = grad_out + grad_resid_norm
+
+    grad_low = grad_resid.astype(bf16)
+    grad_heads = dot("td,sdc->stc", grad_low, w_out_all).astype(bf16)
+    head_blocks = exchange(
+        lambda i: lax.dynamic_index_in_dim(grad_heads, i, 0, keepdims=False), "s"
+    )
+    grad_heads = in_order(head_blocks, "s", token(grad_w_gate)).reshape(seq, cols)
+    grad_w_up = dot("krd,krf->kdf", rows_in, after(grad_up, grad_heads)).astype(bf16)
     up_done = grad_w_up
     grad_w_down, grad_w_gate, grad_w_up = [
         scatter_expert(grad) for grad in (grad_w_down, grad_w_gate, grad_w_up)
     ]
-    down_blocks = to_owners(grad_w_down, token(grad_mid))
-    gate_blocks = to_owners(grad_w_gate)
-    grad_resid_norm, gain_mid_grad = norm_back(residual, gain_mid, grad_mid)
-    grad_resid = grad_out + grad_resid_norm
-
-    grad_low = grad_resid.astype(bf16)
-    head_blocks = [
-        send(jnp.dot(grad_low, w_out_near[k], preferred_element_type=f32).astype(bf16), "s", k)
-        if k
-        else jnp.dot(grad_low, w_out, preferred_element_type=f32).astype(bf16)
-        for k in range(seqs)
-    ]
-    grad_heads = in_order(head_blocks, "s", token(up_done)).reshape(seq, cols)
-    low_blocks = gather_near(after(grad_low, head_blocks[-1]), "s")
+    down_blocks, gate_blocks = to_owners(grad_w_down), to_owners(grad_w_gate)
+    low_blocks = gather_near(grad_low, "s")
     grad_q, grad_k, grad_v, q_inner, k_inner, gain_q_grad, gain_k_grad = attend_back(
         projected, shared, query, keyed, valued, grad_heads, log_total, heads
     )
-    down_ready = in_order(down_blocks, "z", token(grad_q))
     grad_attn_out = in_order(low_blocks, "s", token(grad_q)).reshape(seq, width)
-    grad_w_out = dot("td,tc->dc", grad_attn_out, attended).astype(bf16)
-    q_inner = after(q_inner, down_ready, grad_w_out)
-    grad_w_out = sum_rows(grad_w_out)
-    q_inner, k_inner = over_heads(q_inner[:, 0], k_inner[:, 0])
+    grad_w_out = sum_rows(dot("td,tc->dc", grad_attn_out, attended).astype(bf16))
+    q_inner, k_inner = over_heads(q_inner[:, 0], k_inner[:, 0], up_done)
 
     def norm_grad(grad, raw, mean, inner):
         factor = lax.rsqrt(mean + epsilon)
@@ -576,9 +701,10 @@
 
     grad_normed = whole_of(back_half(w_in), back_half(w_in_other), 1)
     grad_w_qkv = dot("td,tc->dc", normed_in, grad_proj).astype(bf16)
+    down_ready = in_order(down_blocks, "z", token(grad_w_qkv))
+    grad_w_qkv = sum_rows(grad_w_qkv)
     gate_ready = in_order(gate_blocks, "z", token(grad_w_qkv))
-    grad_w_qkv = sum_rows(grad_w_qkv)
-    up_blocks = to_owners(grad_w_up, token(grad_w_qkv))
+    up_blocks = to_owners(grad_w_up, token(down_ready, gate_ready))
     grad_in_norm, gain_in_grad = norm_back(inputs, gain_in, grad_normed)
     grad_tokens = to_outer(grad_resid + grad_in_norm)
 

time: 1510 us -> 1490 us (0.987)
  matrix products: 293 us -> 112 us
  Pallas kernels: 37.6 us -> 215 us
  starting transfers between devices: 210 us -> 182 us
  other arithmetic: 84.2 us -> 101 us
    dot_general x29 -> x10, matrix products: 271 us -> 98.4 us  [dot(): return jnp.einsum(spec, left, right, preferred_element_type=f32)]
    pallas_call x0 -> x4, Pallas kernels: none -> 170 us  [run_experts(): pl.pallas_call(functools.partial(kernel, count, slots), grid=(experts, hi...]
    ppermute x99 -> x96, waiting for transfers between devices: 565 us -> 533 us  [send(): return lax.ppermute(block, axis, [(i, i ^ step) for i in range(size)])]
    ppermute x99 -> x96, starting transfers between devices: 209 us -> 181 us  [send(): return lax.ppermute(block, axis, [(i, i ^ step) for i in range(size)])]
    add x6 -> x14, other arithmetic: 4.96 us -> 27.3 us  [after(): return value + token(*others).astype(value.dtype)]
    all_gather x3, waiting for transfers between devices: 0.02 us -> 18.2 us  [gather_plane(): chunk = lax.all_gather(chunk, ('s', 'c', 'o'), axis=0, tiled=True)]
    unnamed x222 -> x182, local copies, waits for them, and re-layouts: 55 us -> 67.5 us
    dynamic_update_slice x50 -> x52, local copies, waits for them, and re-layouts: 52.1 us -> 52.7 us  [in_order(): lax.dynamic_update_index_in_dim(stacked, block, (rank ^ k) + start, 0)]
  transfers between devices with their start and end apart: 105 -> 103, of which waited for: 41 -> 46; matrix products, arithmetic and copies ran while one was open for 33% -> 28% of each run, Pallas kernels for 3% -> 15%
where the time goes in v5:
time: 1490 us; the launch traced here: 1470 us
  waiting for transfers between devices  551 us (37%)
  local copies, waits for them, and re-layouts  250 us (17%)
  Pallas kernels  215 us (14%)
  starting transfers between devices  182 us (12%)
  matrix products  112 us (8%)
  other arithmetic  101 us (7%)
  between operations  61 us (4%)
    ppermute x96, waiting for transfers between devices, send(): return lax.ppermute(block, axis, [(i, i ^ step) for i in range(size)])  533 us
    ppermute x96, starting transfers between devices, send(): return lax.ppermute(block, axis, [(i, i ^ step) for i in range(size)])  181 us
    pallas_call x4, Pallas kernels, run_experts(): pl.pallas_call(functools.partial(kernel, count, slots), grid=(experts, hi...  170 us
    dot_general x10, matrix products, dot(): return jnp.einsum(spec, left, right, preferred_element_type=f32)  98.4 us
    unnamed x182, local copies, waits for them, and re-layouts  67.5 us
    dynamic_update_slice x52, local copies, waits for them, and re-layouts, in_order(): lax.dynamic_update_index_in_dim(stacked, block, (rank ^ k) + start, 0)  52.7 us
    another operation x15, local copies, waits for them, and re-layouts, whole(): jax.shard_map(shards, mesh=inner, in_specs=(rows, rows, rows, experts, ro...  32.9 us
  transfers between devices with their start and end apart: 103, of which 46 were waited for; matrix products, arithmetic and copies ran while one was open for 28% of the time, Pallas kernels for 15%

profile of v5, /device:TPU:0, one launch (start us, length us, event | category | flops | bytes accessed | tf_op | source)
XLA Modules:
  0.0 1473.1 jit_solution(2011761627323872234)
XLA Ops:
  39.6 12.5 collective-permute-done.3
  53.2 17.5 %collective-permute-done.4 = bf16[256,1024]{1,0:T(8,128)(2,1)} collective-permute-done((bf16[256,1024]{1,0:T(8,128)(2,1)}, bf16[256,1024]{1,0:T(8,128)(2,1)}, u32[]{:S(2)}, u32[]{:S(2)}) %collective-permute-start.4) | collective-permute-done | bytes 524320 | tf_op jit(solution)/shard_map/ppermute | solution.py:24
  99.8 14.7 collective-permute-done.6
  123.7 18.8 %collective-permute-done.8 = bf16[256,2048]{1,0:T(8,128)(2,1)} collective-permute-done((bf16[256,2048]{1,0:T(8,128)(2,1)S(1)}, bf16[256,2048]{1,0:T(8,128)(2,1)}, u32[]{:S(2)}, u32[]{:S(2)}) %collective-permute-start.8) | collective-permute-done | bytes 1048608 | tf_op jit(solution)/shard_map/ppermute | solution.py:24
  168.7 12.8 collective-permute-start.16
  239.6 26.7 %shard_map.145 = (bf16[1024,512]{1,0:T(8,128)(2,1)S(1)}, bf16[1024,512]{1,0:T(8,128)(2,1)S(1)}, bf16[1024,512]{1,0:T(8,128)(2,1)S(1)}, bf16[1024,512]{1,0:T(8,128)(2,1)}, f32[4,1024,1]{2,1,0:T(8,128)}) custom-call(f32[1024,1664]{1,0:T(8,128)} %copy-done.15, f32[1024,1664]{1,0:T(8,128)} %copy-done.15, f32[1024,1664]{1,0:T(8,128)} %copy-done.15, ...), custom_call_target="tpu_custom_call" | custom-call | flops 1000000 | bytes 100000 | tf_op jit(solution)/shard_map/pallas_call | solution.py:225
  346.8 18.9 %collective-permute-done.24 = bf16[256,2048]{1,0:T(8,128)(2,1)} collective-permute-done((bf16[256,2048]{1,0:T(8,128)(2,1)}, bf16[256,2048]{1,0:T(8,128)(2,1)}, u32[]{:S(2)}, u32[]{:S(2)}) %collective-permute-start.24) | collective-permute-done | bytes 1048608 | tf_op jit(solution)/shard_map/ppermute | solution.py:24
  397.2 43.9 %collective-permute-done.32.refs_1_ = bf16[256,2048]{1,0:T(8,128)(2,1)S(1)} collective-permute-done((bf16[256,2048]{1,0:T(8,128)(2,1)S(1)}, bf16[256,2048]{1,0:T(8,128)(2,1)S(1)}, u32[]{:S(2)}, u32[]{:S(2)}) %collective-permute-start.32) | collective-permute-done | bytes 1048608 | tf_op jit(solution)/shard_map/ppermute | solution.py:24
  453.4 18.2 %all-gather.9.cloned.1.call-done = bf16[8192,1024]{1,0:T(8,128)(2,1)} async-done(((bf16[1024,1024]{1,0:T(8,128)(2,1)}), bf16[8192,1024]{1,0:T(8,128)(2,1)}) %all-gather.9.cloned.1.call-update) | async-done | bytes 16777232 | tf_op jit(solution)/shard_map/all_gather | solution.py:477
  471.6 40.1 %shard_map.146 = (bf16[4,2,288,2048]{3,2,1,0:T(8,128)(2,1)}, bf16[4,2,288,1024]{3,2,1,0:T(8,128)(2,1)}, bf16[4,288,1024]{2,1,0:T(8,128)(2,1)}, bf16[4,288,1024]{...) custom-call(s32[4,4,1,256]{3,2,1,0:T(1,128)} %pad_add_fusion.place, ...), custom_call_target="tpu_custom_call" | custom-call | flops 14495514624 | bytes 67108864 | tf_op jit(solution)/shard_map/pallas_call | solution.py:380
  518.8 39.5 %shard_map.147 = (bf16[4,2,288,2048]{3,2,1,0:T(8,128)(2,1)}, bf16[4,2,288,1024]{3,2,1,0:T(8,128)(2,1)}, bf16[4,288,1024]{2,1,0:T(8,128)(2,1)}, bf16[4,288,1024]{...) custom-call(s32[4,4,1,256]{3,2,1,0:T(1,128)} %pad_add_fusion.place, ...), custom_call_target="tpu_custom_call", output_to_operand_aliasing={{0}: (7, {}), {1}: (8, {})} | custom-call | flops 14495514624 | bytes 67108864 | tf_op jit(solution)/shard_map/pallas_call | solution.py:380
  598.5 19.0 %collective-permute-done.36 = bf16[256,2048]{1,0:T(8,128)(2,1)} collective-permute-done((bf16[256,2048]{1,0:T(8,128)(2,1)}, bf16[256,2048]{1,0:T(8,128)(2,1)}, u32[]{:S(2)}, u32[]{:S(2)}) %collective-permute-start.36) | collective-permute-done | bytes 1048608 | tf_op jit(solution)/shard_map/ppermute | solution.py:24
  625.7 47.9 %collective-permute-done.45.refs_1_ = bf16[256,2048]{1,0:T(8,128)(2,1)S(1)} collective-permute-done((bf16[256,2048]{1,0:T(8,128)(2,1)S(1)}, bf16[256,2048]{1,0:T(8,128)(2,1)S(1)}, u32[]{:S(2)}, u32[]{:S(2)}) %collective-permute-start.45) | collective-permute-done | bytes 1048608 | tf_op jit(solution)/shard_map/ppermute | solution.py:24
  676.6 45.2 %shard_map.148 = (bf16[4,2,288,2048]{3,2,1,0:T(8,128)(2,1)}, bf16[4,2,288,1024]{3,2,1,0:T(8,128)(2,1)}, bf16[4,2,288,1024]{3,2,1,0:T(8,128)(2,1)}, bf16[256,2048]{1,0:T(8,128)(2,1)}, bf16[256,2048]{1,0:T(8,128)(2,1)}) custom-call(s32[4,4,1,256]{3,2,1,0:T(1,128)} %pad_add_fusion.place, f32[4,4,1,256]{3,2,1,0:T(1,128)} %pad_maximum_fusion.7.gate, ...), custom_call_target="tpu_custom_call" | custom-call | flops 14495514624 | bytes 67108864 | tf_op jit(solution)/shard_map/pallas_call | solution.py:380
  730.0 45.3 %shard_map.149 = (bf16[4,2,288,2048]{3,2,1,0:T(8,128)(2,1)}, bf16[4,2,288,1024]{3,2,1,0:T(8,128)(2,1)}, bf16[4,2,288,1024]{3,2,1,0:T(8,128)(2,1)}, bf16[256,2048]{1,0:T(8,128)(2,1)}, bf16[256,2048]{1,0:T(8,128)(2,1)}) custom-call(s32[4,4,1,256]{3,2,1,0:T(1,128)} %pad_add_fusion.place, ...), custom_call_target="tpu_custom_call", output_to_operand_aliasing={{0}: (9, {}), {1}: (10, {}), {2}: (11, {})} | custom-call | flops 14495514624 | bytes 67108864 | tf_op jit(solution)/shard_map/pallas_call | solution.py:380
  788.4 20.7 %convolution_convert_fusion.2 = bf16[4,2048,1024]{2,1,0:T(8,128)(2,1)} fusion(bf16[4,576,2048]{2,1,0:T(8,128)(2,1)} %bitcast.511, bf16[4,576,1024]{2,1,0:T(8,128)(2,1)} %bitcast.529), kind=kOutput, calls=%fused_computation.2 | convolution fusion | flops 9672065024 | bytes 30932992 | tf_op jit(solution)/shard_map/krd,krf->kdf/dot_general | solution.py:404
  814.2 24.3 %collective-permute-done.50 = bf16[256,2048]{1,0:T(8,128)(2,1)S(1)} collective-permute-done((bf16[256,2048]{1,0:T(8,128)(2,1)S(1)}, bf16[256,2048]{1,0:T(8,128)(2,1)S(1)}, u32[]{:S(2)}, u32[]{:S(2)}) %collective-permute-start.50) | collective-permute-done | bytes 1048608 | tf_op jit(solution)/shard_map/ppermute | solution.py:24
  838.5 19.6 %collective-permute-done.49 = bf16[256,2048]{1,0:T(8,128)(2,1)S(1)} collective-permute-done((bf16[256,2048]{1,0:T(8,128)(2,1)}, bf16[256,2048]{1,0:T(8,128)(2,1)S(1)}, u32[]{:S(2)}, u32[]{:S(2)}) %collective-permute-start.49) | collective-permute-done | bytes 1048608 | tf_op jit(solution)/shard_map/ppermute | solution.py:24
  868.6 21.0 %convolution_convert_fusion.1 = bf16[4,2048,1024]{2,1,0:T(8,128)(2,1)} fusion(bf16[4,576,2048]{2,1,0:T(8,128)(2,1)} %bitcast.514, bf16[4,576,1024]{2,1,0:T(8,128)(2,1)} %bitcast.530), kind=kOutput, calls=%fused_computation.1 | convolution fusion | flops 9672065024 | bytes 30932992 | tf_op jit(solution)/shard_map/krd,krf->kdf/dot_general | solution.py:404
  937.4 22.1 %convolution_convert_fusion = bf16[4,2048,1024]{2,1,0:T(8,128)(2,1)} fusion(bf16[4,576,2048]{2,1,0:T(8,128)(2,1)} %bitcast.515, bf16[4,576,1024]{2,1,0:T(8,128)(2,1)} %bitcast.531), kind=kOutput, calls=%fused_computation | convolution fusion | flops 9672065024 | bytes 30932992 | tf_op jit(solution)/shard_map/krd,krf->kdf/dot_general | solution.py:404
  995.6 18.5 %shard_map.150 = (f32[1024,512]{1,0:T(8,128)}, f32[1024,512]{1,0:T(8,128)}, bf16[1024,512]{1,0:T(8,128)(2,1)S(1)}, f32[1024,1]{1,0:T(8,128)S(1)}, f32[1024,1]{1,...) custom-call(f32[1024,1664]{1,0:T(8,128)} %copy-done.15, f32[1024,1664]{1,0:T(8,128)} %copy-done.15, ...), custom_call_target="tpu_custom_call" | custom-call | flops 1000000 | bytes 100000 | tf_op jit(solution)/shard_map/pallas_call | solution.py:243
  1074.9 12.5 collective-permute-start.70
  1130.2 36.5 %collective-permute-done.72 = bf16[256,2048]{1,0:T(8,128)(2,1)} collective-permute-done((bf16[256,2048]{1,0:T(8,128)(2,1)}, bf16[256,2048]{1,0:T(8,128)(2,1)}, u32[]{:S(2)}, u32[]{:S(2)}) %collective-permute-start.72) | collective-permute-done | bytes 1048608 | tf_op jit(solution)/shard_map/ppermute | solution.py:24
  1206.6 28.9 %collective-permute-done.75 = bf16[256,512]{1,0:T(8,128)(2,1)S(1)} collective-permute-done((bf16[256,512]{1,0:T(8,128)(2,1)S(1)}, bf16[256,512]{1,0:T(8,128)(2,1)S(1)}, u32[]{:S(2)}, u32[]{:S(2)}) %collective-permute-start.75) | collective-permute-done | bytes 262176 | tf_op jit(solution)/shard_map/ppermute | solution.py:24
  1235.5 17.8 %collective-permute-start.64 = (bf16[256,1536]{1,0:T(8,128)(2,1)S(1)}, bf16[256,1536]{1,0:T(8,128)(2,1)S(1)}, u32[]{:S(2)}, u32[]{:S(2)}) collective-permute-start(bf16[256,1536]{1,0:T(8,128)(2,1)S(1)} %get-tuple-element.145), channel_id=1, source_target_pairs={{0,8},{8,0},{16,24},{24,16},{1,9},{9,1},{17,25},{25,17},{2,10},{10... | collective-permute-start | bytes 2359304 | tf_op jit(solution)/shard_map/ppermute | solution.py:24
  1262.4 22.6 %collective-permute-done.65 = bf16[256,1536]{1,0:T(8,128)(2,1)S(1)} collective-permute-done((bf16[256,1536]{1,0:T(8,128)(2,1)S(1)}, bf16[256,1536]{1,0:T(8,128)(2,1)S(1)}, u32[]{:S(2)}, u32[]{:S(2)}) %collective-permute-start.65) | collective-permute-done | bytes 786464 | tf_op jit(solution)/shard_map/ppermute | solution.py:24
  1317.0 16.0 %collective-permute-done.90 = bf16[256,1024]{1,0:T(8,128)(2,1)} collective-permute-done((bf16[256,1024]{1,0:T(8,128)(2,1)}, bf16[256,1024]{1,0:T(8,128)(2,1)}, u32[]{:S(2)}, u32[]{:S(2)}) %collective-permute-start.90) | collective-permute-done | bytes 524320 | tf_op jit(solution)/shard_map/ppermute | solution.py:24
  1334.2 14.5 collective-permute-done.91
  1354.9 38.3 %collective-permute-done.88 = bf16[256,1024]{1,0:T(8,128)(2,1)S(1)} collective-permute-done((bf16[256,1024]{1,0:T(8,128)(2,1)S(1)}, bf16[256,1024]{1,0:T(8,128)(2,1)S(1)}, u32[]{:S(2)}, u32[]{:S(2)}) %collective-permute-start.88) | collective-permute-done | bytes 524320 | tf_op jit(solution)/shard_map/ppermute | solution.py:24
  1410.2 12.3 collective-permute-done.93
  1422.5 21.4 %collective-permute-done.94 = bf16[256,1024]{1,0:T(8,128)(2,1)S(1)} collective-permute-done((bf16[256,1024]{1,0:T(8,128)(2,1)S(1)}, bf16[256,1024]{1,0:T(8,128)(2,1)S(1)}, u32[]{:S(2)}, u32[]{:S(2)}) %collective-permute-start.94) | collective-permute-done | bytes 524320 | tf_op jit(solution)/shard_map/ppermute | solution.py:24
  1445.3 19.3 %copy.200 = f32[256,4,3072]{2,1,0:T(4,128)} copy(f32[256,4,3072]{2,0,1:T(8,128)S(1)} %convert_bitcast_fusion) | data formatting | bytes 25165824
  (636 shorter events, 624.9 us)
Async XLA Ops:
  7.2 228.9 %all-gather.5.cloned.1.call-start = ((), (), s32[]{:S(2)}) async-start(), calls=%async_computation.3 | async-start | bytes 18874368 | tf_op jit(solution)/shard_map/all_gather | solution.py:477
  74.2 373.5 %all-gather.7.cloned.1.call-start = ((), (), s32[]{:S(2)}) async-start(), calls=%async_computation.4 | async-start | bytes 18874368 | tf_op jit(solution)/shard_map/all_gather | solution.py:477
  80.7 61.7 %collective-permute-start.8 = (bf16[256,2048]{1,0:T(8,128)(2,1)S(1)}, bf16[256,2048]{1,0:T(8,128)(2,1)}, u32[]{:S(2)}, u32[]{:S(2)}) collective-permute-start(bf16[256,2048]{1,0:T(8,128)(2,1)S(1)} %reshape.497), channel_id=1, source_target_pairs={{0,3},{1,2},{2,1},{3,0},{4,7},{5,6},{6,5},{7,4},{8,11},{9,10},{10,... | collective-permute-start | bytes 3145736 | tf_op jit(solution)/shard_map/ppermute | solution.py:24
  84.1 68.5 %collective-permute-start.9 = (bf16[256,1664]{1,0:T(8,128)(2,1)}, bf16[256,1664]{1,0:T(8,128)(2,1)}, u32[]{:S(2)}, u32[]{:S(2)}) collective-permute-start(bf16[256,1664]{1,0:T(8,128)(2,1)} %slice.319), channel_id=1, source_target_pairs={{0,8},{8,0},{16,24},{24,16},{1,9},{9,1},{17,25},{25,17},{2,10},{10... | collective-permute-start | bytes 2555912 | tf_op jit(solution)/shard_map/ppermute | solution.py:24
  92.7 62.1 %collective-permute-start.10 = (bf16[256,1664]{1,0:T(8,128)(2,1)}, bf16[256,1664]{1,0:T(8,128)(2,1)S(1)}, u32[]{:S(2)}, u32[]{:S(2)}) collective-permute-start(bf16[256,1664]{1,0:T(8,128)(2,1)} %slice.319), channel_id=1, source_target_pairs={{0,16},{8,24},{16,0},{24,8},{1,17},{9,25},{17,1},{25,9},{2,18},{10... | collective-permute-start | bytes 2555912 | tf_op jit(solution)/shard_map/ppermute | solution.py:24
  224.5 247.1 %all-gather.9.cloned.1.call-start = ((), (), s32[]{:S(2)}) async-start(), calls=%async_computation.5 | async-start | bytes 18874368 | tf_op jit(solution)/shard_map/all_gather | solution.py:477
  318.4 47.3 %collective-permute-start.24 = (bf16[256,2048]{1,0:T(8,128)(2,1)}, bf16[256,2048]{1,0:T(8,128)(2,1)}, u32[]{:S(2)}, u32[]{:S(2)}) collective-permute-start(bf16[256,2048]{1,0:T(8,128)(2,1)} %get-tuple-element.144), channel_id=1, source_target_pairs={{0,2},{1,3},{2,0},{3,1},{4,6},{5,7},{6,4},{7,5},{8,10},{9,11},{10,... | collective-permute-start | bytes 3145736 | tf_op jit(solution)/shard_map/ppermute | solution.py:24
  380.1 514.8 %all-gather.11.cloned.1.call-start = ((), (), s32[]{:S(2)}) async-start(), calls=%async_computation.6 | async-start | bytes 10485760 | tf_op jit(solution)/shard_map/all_gather | solution.py:616
  394.5 46.6 %collective-permute-start.32 = (bf16[256,2048]{1,0:T(8,128)(2,1)S(1)}, bf16[256,2048]{1,0:T(8,128)(2,1)S(1)}, u32[]{:S(2)}, u32[]{:S(2)}) collective-permute-start(bf16[256,2048]{1,0:T(8,128)(2,1)S(1)} %multiply_convert_fusion.2.refs_0_), channel_id=1, source_target_pairs={{0,16},{8,24},{16,0},{24,8},{1,17},{9,25},{17,1},{25,9},{2,18},{10... | collective-permute-start | bytes 3145736 | tf_op jit(solution)/shard_map/ppermute | solution.py:24
  445.3 71.3 %collective-permute-start.34 = (bf16[256,2048]{1,0:T(8,128)(2,1)}, bf16[256,2048]{1,0:T(8,128)(2,1)}, u32[]{:S(2)}, u32[]{:S(2)}) collective-permute-start(bf16[256,2048]{1,0:T(8,128)(2,1)} %broadcast_add_fusion.11), channel_id=1, source_target_pairs={{0,8},{8,0},{16,24},{24,16},{1,9},{9,1},{17,25},{25,17},{2,10},{10... | collective-permute-start | bytes 3145736 | tf_op jit(solution)/shard_map/ppermute | solution.py:24
  445.3 73.5 %collective-permute-start.35 = (bf16[256,2048]{1,0:T(8,128)(2,1)}, bf16[256,2048]{1,0:T(8,128)(2,1)}, u32[]{:S(2)}, u32[]{:S(2)}) collective-permute-start(bf16[256,2048]{1,0:T(8,128)(2,1)} %broadcast_add_fusion.11), channel_id=1, source_target_pairs={{0,24},{8,16},{16,8},{24,0},{1,25},{9,17},{17,9},{25,1},{2,26},{10... | collective-permute-start | bytes 3145736 | tf_op jit(solution)/shard_map/ppermute | solution.py:24
  453.2 852.6 %reduce-scatter.8.cloned.1.call-start = ((), (), s32[]{:S(2)}) async-start(), calls=%async_computation.9 | async-start | bytes 18874368 | tf_op jit(solution)/shard_map/reduce_scatter | solution.py:628
  514.2 49.0 %collective-permute-start.33 = (bf16[256,2048]{1,0:T(8,128)(2,1)}, bf16[256,2048]{1,0:T(8,128)(2,1)S(1)}, u32[]{:S(2)}, u32[]{:S(2)}) collective-permute-start(bf16[256,2048]{1,0:T(8,128)(2,1)} %get-tuple-element.42), channel_id=1, source_target_pairs={{0,16},{8,24},{16,0},{24,8},{1,17},{9,25},{17,1},{25,9},{2,18},{10... | collective-permute-start | bytes 3145736 | tf_op jit(solution)/shard_map/ppermute | solution.py:24
  625.1 48.5 %collective-permute-start.45 = (bf16[256,2048]{1,0:T(8,128)(2,1)S(1)}, bf16[256,2048]{1,0:T(8,128)(2,1)S(1)}, u32[]{:S(2)}, u32[]{:S(2)}) collective-permute-start(bf16[256,2048]{1,0:T(8,128)(2,1)S(1)} %get-tuple-element.119.refs_0_), channel_id=1, source_target_pairs={{0,16},{8,24},{16,0},{24,8},{1,17},{9,25},{17,1},{25,9},{2,18},{10... | collective-permute-start | bytes 3145736 | tf_op jit(solution)/shard_map/ppermute | solution.py:24
  675.5 51.3 %collective-permute-start.47 = (bf16[256,2048]{1,0:T(8,128)(2,1)S(1)}, bf16[256,2048]{1,0:T(8,128)(2,1)}, u32[]{:S(2)}, u32[]{:S(2)}) collective-permute-start(bf16[256,2048]{1,0:T(8,128)(2,1)S(1)} %broadcast_add_fusion.7), channel_id=1, source_target_pairs={{0,8},{8,0},{16,24},{24,16},{1,9},{9,1},{17,25},{25,17},{2,10},{10... | collective-permute-start | bytes 3145736 | tf_op jit(solution)/shard_map/ppermute | solution.py:24
  675.6 53.5 %collective-permute-start.48 = (bf16[256,2048]{1,0:T(8,128)(2,1)S(1)}, bf16[256,2048]{1,0:T(8,128)(2,1)S(1)}, u32[]{:S(2)}, u32[]{:S(2)}) collective-permute-start(bf16[256,2048]{1,0:T(8,128)(2,1)S(1)} %broadcast_add_fusion.7), channel_id=1, source_target_pairs={{0,24},{8,16},{16,8},{24,0},{1,25},{9,17},{17,9},{25,1},{2,26},{10... | collective-permute-start | bytes 3145736 | tf_op jit(solution)/shard_map/ppermute | solution.py:24
  724.2 53.6 %collective-permute-start.46 = (bf16[256,2048]{1,0:T(8,128)(2,1)}, bf16[256,2048]{1,0:T(8,128)(2,1)}, u32[]{:S(2)}, u32[]{:S(2)}) collective-permute-start(bf16[256,2048]{1,0:T(8,128)(2,1)} %get-tuple-element.50), channel_id=1, source_target_pairs={{0,16},{8,24},{16,0},{24,8},{1,17},{9,25},{17,1},{25,9},{2,18},{10... | collective-permute-start | bytes 3145736 | tf_op jit(solution)/shard_map/ppermute | solution.py:24
  809.1 506.1 %reduce-scatter.4.cloned.1.call-start = ((), (), s32[]{:S(2)}) async-start(), calls=%async_computation.7 | async-start | bytes 18874368 | tf_op jit(solution)/shard_map/reduce_scatter | solution.py:628
  811.6 46.6 %collective-permute-start.49 = (bf16[256,2048]{1,0:T(8,128)(2,1)}, bf16[256,2048]{1,0:T(8,128)(2,1)S(1)}, u32[]{:S(2)}, u32[]{:S(2)}) collective-permute-start(bf16[256,2048]{1,0:T(8,128)(2,1)} %copy-done.55), channel_id=1, source_target_pairs={{0,8},{8,0},{16,24},{24,16},{1,9},{9,1},{17,25},{25,17},{2,10},{10... | collective-permute-start | bytes 3145736 | tf_op jit(solution)/shard_map/ppermute | solution.py:24
  889.7 507.0 %reduce-scatter.6.cloned.1.call-start = ((), (), s32[]{:S(2)}) async-start(), calls=%async_computation.8 | async-start | bytes 18874368 | tf_op jit(solution)/shard_map/reduce_scatter | solution.py:628
  1044.4 46.8 %collective-permute-start.57 = (bf16[256,1024]{1,0:T(8,128)(2,1)S(1)}, bf16[256,1024]{1,0:T(8,128)(2,1)S(1)}, u32[]{:S(2)}, u32[]{:S(2)}) collective-permute-start(bf16[256,1024]{1,0:T(8,128)(2,1)S(1)} %get-tuple-element.163), channel_id=1, source_target_pairs={{0,1},{1,0},{2,3},{3,2},{4,5},{5,4},{6,7},{7,6},{8,9},{9,8},{10,11... | collective-permute-start | bytes 1572872 | tf_op jit(solution)/shard_map/ppermute | solution.py:24
  1092.0 74.7 %collective-permute-start.72 = (bf16[256,2048]{1,0:T(8,128)(2,1)}, bf16[256,2048]{1,0:T(8,128)(2,1)}, u32[]{:S(2)}, u32[]{:S(2)}) collective-permute-start(bf16[256,2048]{1,0:T(8,128)(2,1)} %get-tuple-element.116), channel_id=1, source_target_pairs={{0,3},{1,2},{2,1},{3,0},{4,7},{5,6},{6,5},{7,4},{8,11},{9,10},{10,... | collective-permute-start | bytes 3145736 | tf_op jit(solution)/shard_map/ppermute | solution.py:24
  1097.5 98.0 %collective-permute-start.63 = (bf16[1024,1536]{1,0:T(8,128)(2,1)}, bf16[1024,1536]{1,0:T(8,128)(2,1)}, u32[]{:S(2)}, u32[]{:S(2)}) collective-permute-start(bf16[1024,1536]{1,0:T(8,128)(2,1)} %dynamic-slice_bitcast_fusion), channel_id=1, source_target_pairs={{0,4},{4,0},{1,5},{5,1},{2,6},{6,2},{3,7},{7,3},{8,12},{12,8},{9,1... | collective-permute-start | bytes 9437192 | tf_op jit(solution)/shard_map/ppermute | solution.py:24
  1109.6 66.5 %collective-permute-start.82 = (f32[4,2048]{1,0:T(4,128)S(1)}, f32[4,2048]{1,0:T(4,128)S(1)}, u32[]{:S(2)}, u32[]{:S(2)}) collective-permute-start(f32[4,2048]{1,0:T(4,128)S(1)} %pad_maximum_fusion.5), channel_id=1, source_target_pairs={{0,24},{8,16},{16,8},{24,0},{1,25},{9,17},{17,9},{25,1},{2,26},{10... | collective-permute-start | bytes 98312 | tf_op jit(solution)/shard_map/ppermute | solution.py:24
  1121.5 54.7 %collective-permute-start.81 = (f32[4,2048]{1,0:T(4,128)S(1)}, f32[4,2048]{1,0:T(4,128)S(1)}, u32[]{:S(2)}, u32[]{:S(2)}) collective-permute-start(f32[4,2048]{1,0:T(4,128)S(1)} %pad_maximum_fusion.5), channel_id=1, source_target_pairs={{0,16},{8,24},{16,0},{24,8},{1,17},{9,25},{17,1},{25,9},{2,18},{10... | collective-permute-start | bytes 98312 | tf_op jit(solution)/shard_map/ppermute | solution.py:24
  1126.2 49.9 %collective-permute-start.80 = (f32[4,2048]{1,0:T(4,128)S(1)}, f32[4,2048]{1,0:T(4,128)S(1)}, u32[]{:S(2)}, u32[]{:S(2)}) collective-permute-start(f32[4,2048]{1,0:T(4,128)S(1)} %pad_maximum_fusion.5), channel_id=1, source_target_pairs={{0,8},{8,0},{16,24},{24,16},{1,9},{9,1},{17,25},{25,17},{2,10},{10... | collective-permute-start | bytes 98312 | tf_op jit(solution)/shard_map/ppermute | solution.py:24
  1188.1 65.4 %collective-permute-start.86 = (f32[4,2048]{1,0:T(4,128)S(1)}, f32[4,2048]{1,0:T(4,128)S(1)}, u32[]{:S(2)}, u32[]{:S(2)}) collective-permute-start(f32[4,2048]{1,0:T(4,128)S(1)} %add.1070), channel_id=1, source_target_pairs={{0,3},{1,2},{2,1},{3,0},{4,7},{5,6},{6,5},{7,4},{8,11},{9,10},{10,... | collective-permute-start | bytes 98312 | tf_op jit(solution)/shard_map/ppermute | solution.py:24
  1188.9 65.8 %collective-permute-start.84 = (f32[4,2048]{1,0:T(4,128)S(1)}, f32[4,2048]{1,0:T(4,128)S(1)}, u32[]{:S(2)}, u32[]{:S(2)}) collective-permute-start(f32[4,2048]{1,0:T(4,128)S(1)} %add.1070), channel_id=1, source_target_pairs={{0,1},{1,0},{2,3},{3,2},{4,5},{5,4},{6,7},{7,6},{8,9},{9,8},{10,11... | collective-permute-start | bytes 98312 | tf_op jit(solution)/shard_map/ppermute | solution.py:24
  1203.3 59.1 %collective-permute-start.66 = (bf16[256,1536]{1,0:T(8,128)(2,1)S(1)}, bf16[256,1536]{1,0:T(8,128)(2,1)S(1)}, u32[]{:S(2)}, u32[]{:S(2)}) collective-permute-start(bf16[256,1536]{1,0:T(8,128)(2,1)S(1)} %get-tuple-element.146), channel_id=1, source_target_pairs={{0,24},{8,16},{16,8},{24,0},{1,25},{9,17},{17,9},{25,1},{2,26},{10... | collective-permute-start | bytes 2359304 | tf_op jit(solution)/shard_map/ppermute | solution.py:24
  1235.5 49.5 %collective-permute-start.65 = (bf16[256,1536]{1,0:T(8,128)(2,1)S(1)}, bf16[256,1536]{1,0:T(8,128)(2,1)S(1)}, u32[]{:S(2)}, u32[]{:S(2)}) collective-permute-start(bf16[256,1536]{1,0:T(8,128)(2,1)S(1)} %get-tuple-element.147), channel_id=1, source_target_pairs={{0,16},{8,24},{16,0},{24,8},{1,17},{9,25},{17,1},{25,9},{2,18},{10... | collective-permute-start | bytes 2359304 | tf_op jit(solution)/shard_map/ppermute | solution.py:24
  1235.5 49.5 %collective-permute-start.64 = (bf16[256,1536]{1,0:T(8,128)(2,1)S(1)}, bf16[256,1536]{1,0:T(8,128)(2,1)S(1)}, u32[]{:S(2)}, u32[]{:S(2)}) collective-permute-start(bf16[256,1536]{1,0:T(8,128)(2,1)S(1)} %get-tuple-element.145), channel_id=1, source_target_pairs={{0,8},{8,0},{16,24},{24,16},{1,9},{9,1},{17,25},{25,17},{2,10},{10... | collective-permute-start | bytes 2359304 | tf_op jit(solution)/shard_map/ppermute | solution.py:24
  1334.1 59.2 %collective-permute-start.88 = (bf16[256,1024]{1,0:T(8,128)(2,1)S(1)}, bf16[256,1024]{1,0:T(8,128)(2,1)S(1)}, u32[]{:S(2)}, u32[]{:S(2)}) collective-permute-start(bf16[256,1024]{1,0:T(8,128)(2,1)S(1)} %get-tuple-element.153), channel_id=1, source_target_pairs={{0,16},{8,24},{16,0},{24,8},{1,17},{9,25},{17,1},{25,9},{2,18},{10... | collective-permute-start | bytes 1572872 | tf_op jit(solution)/shard_map/ppermute | solution.py:24
  (147 other events, 2501.7 us)
Sparse Core Ops, SparseCore 0:
  74.3 133.7 all-gather.4
  224.6 97.6 all-gather.6
  380.3 91.3 all-gather.8
  473.3 87.6 all-gather.10
  809.2 124.7 reduce-scatter.7
  937.5 133.4 reduce-scatter.3
  1074.5 145.3 reduce-scatter.5

commit v6 on v5

--- a/solution.py
+++ b/solution.py
@@ -265,139 +265,132 @@
     return jnp.sum(jnp.where(slot_choice(place, slots), gate, 0.0), axis=1, keepdims=True)
 
 
-def expert_kernel(count, slots, place, gate, *refs):
-    blocks, (w_gate, w_up, w_down), refs = refs[:count], refs[count : count + 3], refs[count + 3 :]
-    rows, activated, gate_pre, up_pre = refs[-6 - count : -2 - count]
-    partial, (sum_out, sum_tokens) = refs[-2 - count : -2], refs[-2:]
-    expert, chunk = pl.program_id(0), pl.program_id(1)
-
-    def spans():
-        return [(b, slice(b * slots, (b + 1) * slots)) for b in range(count)]
-
-    @pl.when(chunk == 0)
+def spans_of(count, slots):
+    return [(b, slice(b * slots, (b + 1) * slots)) for b in range(count)]
+
+
+def add_tokens(place, b, slots, out, sum_tokens, partial):
+    expert = pl.program_id(0)
+    back = mm(slot_choice(place[0, b], slots).astype(bf16), out, ((0,), (0,)))
+
+    @pl.when(expert == 0)
     def _():
-        for b, span in spans():
-            choice = slot_choice(place[0, b], slots).astype(bf16)
-            rows[0, 0, span] = mm(choice, blocks[b][...], ((1,), (0,))).astype(bf16)
-
+        sum_tokens[b] = back
+
+    @pl.when(expert > 0)
+    def _():
+        sum_tokens[b] += back
+
+    @pl.when(expert == pl.num_programs(0) - 1)
+    def _():
+        partial[b][...] = sum_tokens[b].astype(bf16)
+
+
+def hidden_kernel(count, slots, place, *refs):
+    blocks, w_gate, w_up = refs[:count], refs[count], refs[count + 1]
+    rows, activated, gate_pre, up_pre = refs[-4:]
+    for b, span in spans_of(count, slots):
+        choice = slot_choice(place[0, b], slots).astype(bf16)
+        rows[0, 0, span] = mm(choice, blocks[b][...], ((1,), (0,))).astype(bf16)
     rows_in = rows[0, 0]
     g = mm(rows_in, w_gate[0], ((1,), (0,)))
     u = mm(rows_in, w_up[0], ((1,), (0,)))
-    m = (g * jax.nn.sigmoid(g) * u).astype(bf16)
-    gate_pre[0], up_pre[0], activated[0, 0] = g.astype(bf16), u.astype(bf16), m
-    term = mm(m, w_down[0], ((1,), (1,)))
-
-    @pl.when(chunk == 0)
-    def _():
-        sum_out[...] = term
-
-    @pl.when(chunk > 0)
-    def _():
-        sum_out[...] += term
-
-    @pl.when(chunk == pl.num_programs(1) - 1)
-    def _():
-        for b, span in spans():
-            weight = slot_weight(place[0, b], gate[0, b], slots)
-            out = (sum_out[span] * weight).astype(bf16)
-            back = mm(slot_choice(place[0, b], slots).astype(bf16), out, ((0,), (0,)))
-            add_tokens(expert, b, back, sum_tokens, partial)
-
-
-def add_tokens(expert, b, back, sum_tokens, partial):
-    @pl.when(expert == 0)
-    def _():
-        sum_tokens[b] = back
-
-    @pl.when(expert > 0)
-    def _():
-        sum_tokens[b] += back
-
-    @pl.when(expert == pl.num_programs(0) - 1)
-    def _():
-        partial[b][...] = sum_tokens[b].astype(bf16)
+    gate_pre[0], up_pre[0] = g.astype(bf16), u.astype(bf16)
+    activated[0, 0] = (g * jax.nn.sigmoid(g) * u).astype(bf16)
+
+
+def out_kernel(count, slots, place, gate, activated, w_down, *refs):
+    partial, sum_tokens = refs[:-1], refs[-1]
+    result = mm(activated[0, 0], w_down[0], ((1,), (1,)))
+    for b, span in spans_of(count, slots):
+        out = (result[span] * slot_weight(place[0, b], gate[0, b], slots)).astype(bf16)
+        add_tokens(place, b, slots, out, sum_tokens, partial)
 
 
 def expert_back_kernel(count, slots, place, gate, *refs):
     blocks, (w_gate, w_up, w_down) = refs[:count], refs[count : count + 3]
     gate_pre, up_pre = refs[count + 3 : count + 5]
-    grad_rows, grad_gate, grad_up = refs[-5 - count : -2 - count]
-    partial, (sum_rows, sum_tokens) = refs[-2 - count : -2], refs[-2:]
-    expert, chunk = pl.program_id(0), pl.program_id(1)
-
-    def spans():
-        return [(b, slice(b * slots, (b + 1) * slots)) for b in range(count)]
-
-    @pl.when(chunk == 0)
-    def _():
-        for b, span in spans():
-            choice = slot_choice(place[0, b], slots).astype(bf16)
-            weight = slot_weight(place[0, b], gate[0, b], slots)
-            picked = mm(choice, blocks[b][...], ((1,), (0,)))
-            grad_rows[0, 0, span] = (picked * weight).astype(bf16)
-
+    grad_rows, grad_gate, grad_up = refs[-4 - count : -1 - count]
+    partial, sum_tokens = refs[-1 - count : -1], refs[-1]
+    for b, span in spans_of(count, slots):
+        choice = slot_choice(place[0, b], slots).astype(bf16)
+        weight = slot_weight(place[0, b], gate[0, b], slots)
+        picked = mm(choice, blocks[b][...], ((1,), (0,)))
+        grad_rows[0, 0, span] = (picked * weight).astype(bf16)
     grad_act = mm(grad_rows[0, 0], w_down[0], ((1,), (0,)))
     g, u = gate_pre[0].astype(f32), up_pre[0].astype(f32)
     sigmoid = jax.nn.sigmoid(g)
     dg = (grad_act * u * sigmoid * (1.0 + g * (1.0 - sigmoid))).astype(bf16)
     du = (grad_act * g * sigmoid).astype(bf16)
     grad_gate[0, 0], grad_up[0, 0] = dg, du
-    term = mm(dg, w_gate[0], ((1,), (1,))) + mm(du, w_up[0], ((1,), (1,)))
-
-    @pl.when(chunk == 0)
-    def _():
-        sum_rows[...] = term
-
-    @pl.when(chunk > 0)
-    def _():
-        sum_rows[...] += term
-
-    @pl.when(chunk == pl.num_programs(1) - 1)
-    def _():
-        for b, span in spans():
-            out = sum_rows[span].astype(bf16)
-            back = mm(slot_choice(place[0, b], slots).astype(bf16), out, ((0,), (0,)))
-            add_tokens(expert, b, back, sum_tokens, partial)
-
-
-def run_experts(kernel, group, slots, place, gate, blocks, weights, saved, narrow, prior):
-    experts, width, hidden = weights[0].shape
-    count, (own, _) = len(blocks), blocks[0].shape
-    rows = count * slots
-    step = min(256, hidden)
-    table = pl.BlockSpec((1, count, 1, own), lambda e, f: (e, group, 0, 0))
-    tokens = pl.BlockSpec((own, width), lambda e, f: (0, 0))
-    weight = pl.BlockSpec((1, width, step), lambda e, f: (e, 0, f))
-    local = pl.BlockSpec((1, rows, step), lambda e, f: (e, 0, f))
-    shared_specs = [pl.BlockSpec((1, 1, rows, width), lambda e, f: (e, group, 0, 0))] + [
-        pl.BlockSpec((1, 1, rows, step), lambda e, f: (e, group, 0, f))
-    ] * narrow
-    shared_shapes = [jax.ShapeDtypeStruct((experts, 2, rows, width), bf16)] + [
-        jax.ShapeDtypeStruct((experts, 2, rows, hidden), bf16)
-    ] * narrow
-    local_out = 0 if saved else 2
-    first = 2 + count + 3 + len(saved)
-    return pl.pallas_call(
-        functools.partial(kernel, count, slots),
-        grid=(experts, hidden // step),
-        in_specs=[table, table]
-        + [tokens] * count
-        + [weight] * 3
-        + [local] * len(saved)
-        + [pl.BlockSpec(memory_space=pl.ANY)] * len(prior),
-        out_specs=shared_specs + [local] * local_out + [tokens] * count,
-        out_shape=shared_shapes
-        + [jax.ShapeDtypeStruct((experts, rows, hidden), bf16)] * local_out
-        + [jax.ShapeDtypeStruct((own, width), bf16)] * count,
-        scratch_shapes=[pltpu.VMEM((rows, width), f32), pltpu.VMEM((count, own, width), f32)],
-        input_output_aliases={first + i: i for i in range(len(prior))},
-        compiler_params=pltpu.CompilerParams(vmem_limit_bytes=56 * 2**20),
-        cost_estimate=pl.CostEstimate(
-            flops=experts * rows * width * hidden * 6,
-            bytes_accessed=experts * width * hidden * 8,
-            transcendentals=experts * rows * hidden,
-        ),
-    )(place, gate, *blocks, *weights, *saved, *prior)
+    result = mm(dg, w_gate[0], ((1,), (1,))) + mm(du, w_up[0], ((1,), (1,)))
+    result = result.astype(bf16)
+    for b, span in spans_of(count, slots):
+        add_tokens(place, b, slots, result[span], sum_tokens, partial)
+
+
+class Experts:
+    def __init__(self, group, slots, place, gate, blocks, weights):
+        self.group, self.slots, self.place, self.gate = group, slots, place, gate
+        self.experts, self.width, self.hidden = weights[0].shape
+        self.count, self.own = len(blocks), blocks[0].shape[0]
+        self.rows = self.count * slots
+        group_of = lambda e: (e, group, 0, 0)
+        self.table = pl.BlockSpec((1, self.count, 1, self.own), group_of)
+        self.tokens = pl.BlockSpec((self.own, self.width), lambda e: (0, 0))
+        self.weight = pl.BlockSpec((1, self.width, self.hidden), lambda e: (e, 0, 0))
+        self.local = pl.BlockSpec((1, self.rows, self.hidden), lambda e: (e, 0, 0))
+        self.wide = pl.BlockSpec((1, 1, self.rows, self.width), group_of)
+        self.narrow = pl.BlockSpec((1, 1, self.rows, self.hidden), group_of)
+        self.sums = pltpu.VMEM((self.count, self.own, self.width), f32)
+
+    def shape(self, spec):
+        rows, experts = self.rows, self.experts
+        shapes = [
+            (self.tokens, (self.own, self.width)),
+            (self.local, (experts, rows, self.hidden)),
+            (self.wide, (experts, 2, rows, self.width)),
+            (self.narrow, (experts, 2, rows, self.hidden)),
+        ]
+        [shape] = [shape for known, shape in shapes if known is spec]
+        return jax.ShapeDtypeStruct(shape, bf16)
+
+    def run(self, kernel, ins, outs, scratch, prior=()):
+        specs = [spec for spec, _ in ins] + [pl.BlockSpec(memory_space=pl.ANY)] * len(prior)
+        return pl.pallas_call(
+            functools.partial(kernel, self.count, self.slots),
+            grid=(self.experts,),
+            in_specs=specs,
+            out_specs=outs,
+            out_shape=[self.shape(spec) for spec in outs],
+            scratch_shapes=scratch,
+            input_output_aliases={len(ins) + i: i for i in range(len(prior))},
+            compiler_params=pltpu.CompilerParams(vmem_limit_bytes=58 * 2**20),
+            cost_estimate=pl.CostEstimate(
+                flops=self.experts * self.rows * self.width * self.hidden * 4,
+                bytes_accessed=self.experts * self.width * self.hidden * 6,
+                transcendentals=self.experts * self.rows * self.hidden,
+            ),
+        )(*[array for _, array in ins], *prior)
+
+    def to_hidden(self, blocks, w_gate, w_up, prior):
+        ins = [(self.table, self.place)] + [(self.tokens, block) for block in blocks]
+        ins += [(self.weight, w_gate), (self.weight, w_up)]
+        outs = [self.wide, self.narrow, self.local, self.local]
+        return self.run(hidden_kernel, ins, outs, [], prior)
+
+    def to_tokens(self, activated, w_down):
+        ins = [(self.table, self.place), (self.table, self.gate)]
+        ins += [(self.narrow, activated), (self.weight, w_down)]
+        return self.run(out_kernel, ins, [self.tokens] * self.count, [self.sums])
+
+    def backward(self, blocks, weights, pres, prior):
+        ins = [(self.table, self.place), (self.table, self.gate)]
+        ins += [(self.tokens, block) for block in blocks]
+        ins += [(self.weight, weight) for weight in weights]
+        ins += [(self.local, pre) for pre in pres]
+        outs = [self.wide, self.narrow, self.narrow] + [self.tokens] * self.count
+        return self.run(expert_back_kernel, ins, outs, [self.sums], prior)
 
 
 def dot(spec, left, right):
@@ -452,11 +445,13 @@
         rows = in_order(blocks, "z", start)
         return collect(rows, "o").reshape((width // 2,) + rows.shape[2:])
 
-    def sum_rows(grad):
+    def sum_rows(grad, *others):
         count = grad.shape[1]
         grad = exchange_sum(grad.reshape(CORES, width // 2, count), "c").astype(bf16)
         if outer > 1:
             grad = exchange_sum(grad.reshape(outer, planes * part, count), "o").astype(bf16)
+        if others:
+            grad = after(grad, *others)
         return exchange_sum(grad.reshape(planes, part, count), "z")
 
     def gather_sum(value):
@@ -501,10 +496,11 @@
     inputs = inputs.astype(f32)
 
     mine = in_order(mine_blocks, "s").reshape(part, 4 * cols + PAD)
-    in_blocks = gather_near(mine[:, : 3 * cols + PAD], "z")
-    gate_ready = in_order(gate_blocks, "z", token(mine))
+    seq_tokens = in_order(token_blocks, "s", token(mine)).reshape(seq, width)
+    gate_ready = in_order(gate_blocks, "z", token(seq_tokens))
     w_gate = gather_plane(gate_ready)
-    seq_tokens = in_order(token_blocks, "s", token(gate_ready)).reshape(seq, width).astype(f32)
+    in_blocks = gather_near(after(mine[:, : 3 * cols + PAD], gate_ready), "z")
+    seq_tokens = seq_tokens.astype(f32)
     seq_factor = rms_factor(seq_tokens)
     w_in = stack_rows(in_blocks, token(seq_factor))
     w_in_other = send(w_in, "c", 1)
@@ -538,18 +534,17 @@
 
     place, gate_of = by_group(place), by_group(gate_of)
 
-    def through_planes(block, work):
+    def near_planes(block):
         near = [block] + [None] * (planes - 1)
         for k in groups[0][1:]:
             near[k] = send(block, "z", k)
         later = after(block, *[near[k] for k in groups[0][1:]])
         for k in groups[1]:
             near[k] = send(later, "z", k)
-        first = work(0, [near[k] for k in groups[0]])
+        return [[near[k] for k in group] for group in groups]
+
+    def send_back(first, second):
         got = [first[0]] + [send(first[i], "z", k) for i, k in enumerate(groups[0]) if k]
-        blocks = [near[k] for k in groups[1]]
-        blocks[0] = after(blocks[0], first[0])
-        second = work(1, blocks)
         base = after(total(got), second[0])
         second = [after(part, base) for part in second]
         return second[0], [base] + [send(second[i], "z", k) for i, k in enumerate(groups[1])]
@@ -578,9 +573,10 @@
     up_ready = in_order(up_blocks, "z", token(projected))
     w_up = gather_plane(up_ready)
     out_blocks = gather_near(after(mine[:, 3 * cols + PAD :], up_ready), "z")
+    out_rows = stack_rows(out_blocks, token(q_mean))
     cosine, sine = rope_tables(seq)
     shared = [
-        after(q_mean, up_ready, w_gate),
+        after(q_mean, up_ready, w_gate, out_rows, place),
         k_mean,
         gain_q[None],
         gain_k[None],
@@ -590,7 +586,7 @@
         segment[None],
     ]
     attended, query, keyed, valued, log_total = attend(projected, shared, heads)
-    w_out = collect(stack_rows(out_blocks, token(attended)), "c").reshape(width, cols)
+    w_out = collect(out_rows, "c").reshape(width, cols)
     down_blocks = expert_chunk(2, token(attended))
     attn_out = dot("tc,dc->td", attended, w_out).astype(bf16)
     residual = inputs + exchange_sum(attn_out.reshape(seqs, own, width), "s")
@@ -600,18 +596,18 @@
 
     normed_mid = (residual * rms_factor(residual) * gain_mid).astype(bf16)
     expert_weights = (w_gate, w_up, w_down)
-    pres, kept = [], [()]
-
-    def forward(i, blocks):
-        rows_in, activated, gate_pre, up_pre, *partial = run_experts(
-            expert_kernel, i, slots, place, gate_of, blocks, expert_weights, (), 1, kept[0]
-        )
-        pres.append((gate_pre, up_pre))
-        kept[0] = (rows_in, activated)
-        return partial
-
-    final_out = residual + total(through_planes(normed_mid, forward)[1])
-    rows_in, activated = [v.reshape(seqs, -1, v.shape[-1]) for v in kept[0]]
+    blocks = near_planes(normed_mid)
+    work = [Experts(i, slots, place, gate_of, blocks[i], expert_weights) for i in range(2)]
+    rows_in, activated, *pres = work[0].to_hidden(blocks[0], w_gate, w_up, ())
+    pres = [pres]
+    blocks[1][0] = after(blocks[1][0], pres[0][0])
+    rows_in, activated, *last = work[1].to_hidden(
+        blocks[1], w_gate, w_up, (rows_in, activated)
+    )
+    pres.append(last)
+    partial = [group.to_tokens(activated, w_down) for group in work]
+    final_out = residual + total(send_back(*partial)[1])
+    rows_in, activated = [v.reshape(seqs, -1, v.shape[-1]) for v in (rows_in, activated)]
 
     w_out_all = lax.all_gather(after(w_out, w_up), "s", axis=0)
     valid_f = valid_mask.astype(f32)[:, None]
@@ -634,26 +630,14 @@
 
         return exchange(piece_for, "z", start)
 
-    grads = [()]
-
-    def backward(i, blocks):
-        *shared_grads, first, last = run_experts(
-            expert_back_kernel,
-            i,
-            slots,
-            place,
-            gate_of,
-            blocks,
-            expert_weights,
-            pres[i],
-            2,
-            grads[0],
-        )
-        grads[0] = shared_grads
-        return first, last
-
-    back_last, back_pieces = through_planes(grad_out.astype(bf16), backward)
-    grad_rows, grad_gate, grad_up = [v.reshape(seqs, -1, v.shape[-1]) for v in grads[0]]
+    blocks = near_planes(grad_out.astype(bf16))
+    *grads, first, last = work[0].backward(blocks[0], expert_weights, pres[0], ())
+    partial = [(first, last)]
+    blocks[1][0] = after(blocks[1][0], first)
+    *grads, first, last = work[1].backward(blocks[1], expert_weights, pres[1], grads)
+    partial.append((first, last))
+    back_last, back_pieces = send_back(*partial)
+    grad_rows, grad_gate, grad_up = [v.reshape(seqs, -1, v.shape[-1]) for v in grads]
     grad_w_down = dot("krd,krf->kdf", grad_rows, after(activated, back_last)).astype(bf16)
     back_pieces[0] = after(back_pieces[0], grad_w_down)
     grad_mid = total(back_pieces)
@@ -667,17 +651,20 @@
         lambda i: lax.dynamic_index_in_dim(grad_heads, i, 0, keepdims=False), "s"
     )
     grad_heads = in_order(head_blocks, "s", token(grad_w_gate)).reshape(seq, cols)
-    grad_w_up = dot("krd,krf->kdf", rows_in, after(grad_up, grad_heads)).astype(bf16)
+    low_blocks = gather_near(grad_low, "s")
+    grad_attn_out = in_order(low_blocks, "s", token(grad_w_gate)).reshape(seq, width)
+    grad_w_up = dot("krd,krf->kdf", rows_in, after(grad_up, grad_heads, grad_attn_out))
+    grad_w_up = grad_w_up.astype(bf16)
     up_done = grad_w_up
     grad_w_down, grad_w_gate, grad_w_up = [
         scatter_expert(grad) for grad in (grad_w_down, grad_w_gate, grad_w_up)
     ]
     down_blocks, gate_blocks = to_owners(grad_w_down), to_owners(grad_w_gate)
-    low_blocks = gather_near(grad_low, "s")
+    down_ready = in_order(down_blocks, "z", token(up_done))
+    grad_heads = after(grad_heads, down_ready)
     grad_q, grad_k, grad_v, q_inner, k_inner, gain_q_grad, gain_k_grad = attend_back(
         projected, shared, query, keyed, valued, grad_heads, log_total, heads
     )
-    grad_attn_out = in_order(low_blocks, "s", token(grad_q)).reshape(seq, width)
     grad_w_out = sum_rows(dot("td,tc->dc", grad_attn_out, attended).astype(bf16))
     q_inner, k_inner = over_heads(q_inner[:, 0], k_inner[:, 0], up_done)
 
@@ -701,10 +688,9 @@
 
     grad_normed = whole_of(back_half(w_in), back_half(w_in_other), 1)
     grad_w_qkv = dot("td,tc->dc", normed_in, grad_proj).astype(bf16)
-    down_ready = in_order(down_blocks, "z", token(grad_w_qkv))
-    grad_w_qkv = sum_rows(grad_w_qkv)
     gate_ready = in_order(gate_blocks, "z", token(grad_w_qkv))
-    up_blocks = to_owners(grad_w_up, token(down_ready, gate_ready))
+    grad_w_qkv = sum_rows(grad_w_qkv, gate_ready)
+    up_blocks = to_owners(grad_w_up, token(grad_w_qkv))
     grad_in_norm, gain_in_grad = norm_back(inputs, gain_in, grad_normed)
     grad_tokens = to_outer(grad_resid + grad_in_norm)
 
@@ -723,10 +709,10 @@
         got = exchange(lambda i: lax.dynamic_index_in_dim(grad, i, 0, keepdims=False), "s")
         return in_order(got, "s").astype(f32)
 
-    qkv_rows, out_rows = own_rows(grad_w_qkv), own_rows(grad_w_out)
+    qkv_part, out_part = own_rows(grad_w_qkv), own_rows(grad_w_out)
     grad_attn = jnp.concatenate(
-        [qkv_rows[s, :, i * cols : (i + 1) * cols] for i in range(3) for s in range(seqs)]
-        + [out_rows[s] for s in range(seqs)],
+        [qkv_part[s, :, i * cols : (i + 1) * cols] for i in range(3) for s in range(seqs)]
+        + [out_part[s] for s in range(seqs)],
         axis=1,
     )
     up_ready = in_order(up_blocks, "z")

time: 1490 us -> 1540 us (1.034)
  starting transfers between devices: 182 us -> 258 us
  Pallas kernels: 215 us -> 171 us
    ppermute x96, starting transfers between devices: 181 us -> 244 us  [send(): return lax.ppermute(block, axis, [(i, i ^ step) for i in range(size)])]
    pallas_call x4 -> x6, Pallas kernels: 170 us -> 135 us  [run(): pl.pallas_call(functools.partial(kernel, self.count, self.slots), grid=(s...]
    ppermute x96, waiting for transfers between devices: 533 us -> 554 us  [send(): return lax.ppermute(block, axis, [(i, i ^ step) for i in range(size)])]
    all_gather x3, waiting for transfers between devices: 18.2 us -> 0.02 us  [gather_plane(): chunk = lax.all_gather(chunk, ('s', 'c', 'o'), axis=0, tiled=True)]
    unnamed x182 -> x208, local copies, waits for them, and re-layouts: 67.5 us -> 56.3 us
    add x14 -> x16, other arithmetic: 27.3 us -> 37.5 us  [after(): return value + token(*others).astype(value.dtype)]
    dynamic_update_slice x52 -> x50, local copies, waits for them, and re-layouts: 52.7 us -> 54.6 us  [in_order(): lax.dynamic_update_index_in_dim(stacked, block, (rank ^ k) + start, 0)]
  transfers between devices with their start and end apart: 103 -> 103, of which waited for: 46 -> 39; matrix products, arithmetic and copies ran while one was open for 28% -> 28% of each run, Pallas kernels for 15% -> 11%
where the time goes in v6:
time: 1540 us; the launch traced here: 1520 us
  waiting for transfers between devices  554 us (36%)
  starting transfers between devices  258 us (17%)
  local copies, waits for them, and re-layouts  253 us (16%)
  Pallas kernels  171 us (11%)
  matrix products  115 us (7%)
  other arithmetic  107 us (7%)
  between operations  64.7 us (4%)
    ppermute x96, waiting for transfers between devices, send(): return lax.ppermute(block, axis, [(i, i ^ step) for i in range(size)])  554 us
    ppermute x96, starting transfers between devices, send(): return lax.ppermute(block, axis, [(i, i ^ step) for i in range(size)])  244 us
    pallas_call x6, Pallas kernels, run(): pl.pallas_call(functools.partial(kernel, self.count, self.slots), grid=(s...  135 us
    dot_general x10, matrix products, dot(): return jnp.einsum(spec, left, right, preferred_element_type=f32)  101 us
    unnamed x208, local copies, waits for them, and re-layouts  56.3 us
    dynamic_update_slice x50, local copies, waits for them, and re-layouts, in_order(): lax.dynamic_update_index_in_dim(stacked, block, (rank ^ k) + start, 0)  54.6 us
    add x16, other arithmetic, after(): return value + token(*others).astype(value.dtype)  37.5 us
    another operation x15, local copies, waits for them, and re-layouts, whole(): jax.shard_map(shards, mesh=inner, in_specs=(rows, rows, rows, experts, ro...  33.4 us
  transfers between devices with their start and end apart: 103, of which 39 were waited for; matrix products, arithmetic and copies ran while one was open for 28% of the time, Pallas kernels for 11%

profile of v6, /device:TPU:0, one launch (start us, length us, event | category | flops | bytes accessed | tf_op | source)
XLA Modules:
  0.0 1522.4 jit_solution(17435509260774128909)
XLA Ops:
  39.1 26.2 %collective-permute-done = bf16[64,2176]{1,0:T(8,128)(2,1)} collective-permute-done((bf16[64,2176]{1,0:T(8,128)(2,1)}, bf16[64,2176]{1,0:T(8,128)(2,1)}, u32[]{:S(2)}, u32[]{:S(2)}) %collective-permute-start) | collective-permute-done | bytes 278560 | tf_op jit(solution)/shard_map/ppermute | solution.py:24
  94.5 18.1 %collective-permute-done.7 = bf16[256,1024]{1,0:T(8,128)(2,1)} collective-permute-done((bf16[256,1024]{1,0:T(8,128)(2,1)}, bf16[256,1024]{1,0:T(8,128)(2,1)}, u32[]{:S(2)}, u32[]{:S(2)}) %collective-permute-start.7) | collective-permute-done | bytes 524320 | tf_op jit(solution)/shard_map/ppermute | solution.py:24
  138.5 30.0 %collective-permute-done.9 = bf16[256,1664]{1,0:T(8,128)(2,1)S(1)} collective-permute-done((bf16[256,1664]{1,0:T(8,128)(2,1)}, bf16[256,1664]{1,0:T(8,128)(2,1)S(1)}, u32[]{:S(2)}, u32[]{:S(2)}) %collective-permute-start.9) | collective-permute-done | bytes 852000 | tf_op jit(solution)/shard_map/ppermute | solution.py:24
  169.6 25.4 %collective-permute-done.10 = bf16[256,1664]{1,0:T(8,128)(2,1)S(1)} collective-permute-done((bf16[256,1664]{1,0:T(8,128)(2,1)}, bf16[256,1664]{1,0:T(8,128)(2,1)S(1)}, u32[]{:S(2)}, u32[]{:S(2)}) %collective-permute-start.10) | collective-permute-done | bytes 852000 | tf_op jit(solution)/shard_map/ppermute | solution.py:24
  209.9 14.1 collective-permute-start.16
  342.3 17.6 %shard_map.145 = (bf16[1024,512]{1,0:T(8,128)(2,1)S(1)}, bf16[1024,512]{1,0:T(8,128)(2,1)S(1)}, bf16[1024,512]{1,0:T(8,128)(2,1)S(1)}, bf16[1024,512]{1,0:T(8,128)(2,1)}, f32[4,1024,1]{2,1,0:T(8,128)}) custom-call(f32[1024,1664]{1,0:T(8,128)} %copy-done.13, f32[1024,1664]{1,0:T(8,128)} %copy-done.13, f32[1024,1664]{1,0:T(8,128)} %copy-done.13, ...), custom_call_target="tpu_custom_call" | custom-call | flops 1000000 | bytes 100000 | tf_op jit(solution)/shard_map/pallas_call | solution.py:225
  395.4 21.0 %collective-permute-done.27 = bf16[256,2048]{1,0:T(8,128)(2,1)} collective-permute-done((bf16[256,2048]{1,0:T(8,128)(2,1)}, bf16[256,2048]{1,0:T(8,128)(2,1)}, u32[]{:S(2)}, u32[]{:S(2)}) %collective-permute-start.27) | collective-permute-done | bytes 1048608 | tf_op jit(solution)/shard_map/ppermute | solution.py:24
  444.3 43.1 %collective-permute-done.32.refs_1_ = bf16[256,2048]{1,0:T(8,128)(2,1)S(1)} collective-permute-done((bf16[256,2048]{1,0:T(8,128)(2,1)S(1)}, bf16[256,2048]{1,0:T(8,128)(2,1)S(1)}, u32[]{:S(2)}, u32[]{:S(2)}) %collective-permute-start.32) | collective-permute-done | bytes 1048608 | tf_op jit(solution)/shard_map/ppermute | solution.py:24
  493.5 20.8 %shard_map.146 = (bf16[4,2,288,2048]{3,2,1,0:T(8,128)(2,1)}, bf16[4,2,288,1024]{3,2,1,0:T(8,128)(2,1)}, bf16[4,288,1024]{2,1,0:T(8,128)(2,1)}, bf16[4,288,1024]{2,1,0:T(8,128)(2,1)}) custom-call(s32[4,4,1,256]{3,2,1,0:T(1,128)} %pad_add_fusion.place, bf16[256,2048]{1,0:T(8,128)(2,1)} %copy-done.69, bf16[256,2048]{1,0:T(8,128)(2,1)} %copy-done.88, ...), custom_call_target="tpu_custom_call" | custom-call | flops 9663676416 | bytes 50331648 | tf_op jit(solution)/shard_map/pallas_call | solution.py:360
  538.0 21.2 %shard_map.147 = (bf16[4,2,288,2048]{3,2,1,0:T(8,128)(2,1)}, bf16[4,2,288,1024]{3,2,1,0:T(8,128)(2,1)}, bf16[4,288,1024]{2,1,0:T(8,128)(2,1)}, bf16[4,288,1024]{2,1,0:T(8,128)(2,1)}) custom-call(s32[4,4,1,256]{3,2,1,0:T(1,128)} %pad_add_fusion.place, bf16[256,2048]{1,0:T(8,128)(2,1)} %broadcast_add_fusion.11.refs_0_, ...), custom_call_target="tpu_custom_call", output_to_operand_aliasing={{0}: (5, {}), {1}: (6, {})} | custom-call | flops 9663676416 | bytes 50331648 | tf_op jit(solution)/shard_map/pallas_call | solution.py:360
  559.2 15.0 shard_map.148
  575.7 14.2 shard_map.149
  592.4 27.9 %collective-permute-done.35 = bf16[256,2048]{1,0:T(8,128)(2,1)S(1)} collective-permute-done((bf16[256,2048]{1,0:T(8,128)(2,1)}, bf16[256,2048]{1,0:T(8,128)(2,1)S(1)}, u32[]{:S(2)}, u32[]{:S(2)}) %collective-permute-start.35) | collective-permute-done | bytes 1048608 | tf_op jit(solution)/shard_map/ppermute | solution.py:24
  653.5 18.6 %collective-permute-done.36 = bf16[256,2048]{1,0:T(8,128)(2,1)} collective-permute-done((bf16[256,2048]{1,0:T(8,128)(2,1)}, bf16[256,2048]{1,0:T(8,128)(2,1)}, u32[]{:S(2)}, u32[]{:S(2)}) %collective-permute-start.36) | collective-permute-done | bytes 1048608 | tf_op jit(solution)/shard_map/ppermute | solution.py:24
  682.2 44.9 %collective-permute-done.45.refs_1_ = bf16[256,2048]{1,0:T(8,128)(2,1)S(1)} collective-permute-done((bf16[256,2048]{1,0:T(8,128)(2,1)S(1)}, bf16[256,2048]{1,0:T(8,128)(2,1)S(1)}, u32[]{:S(2)}, u32[]{:S(2)}) %collective-permute-start.45) | collective-permute-done | bytes 1048608 | tf_op jit(solution)/shard_map/ppermute | solution.py:24
  732.5 32.0 %shard_map.150 = (bf16[4,2,288,2048]{3,2,1,0:T(8,128)(2,1)}, bf16[4,2,288,1024]{3,2,1,0:T(8,128)(2,1)}, bf16[4,2,288,1024]{3,2,1,0:T(8,128)(2,1)}, bf16[256,2048]{1,0:T(8,128)(2,1)}, bf16[256,2048]{1,0:T(8,128)(2,1)}) custom-call(s32[4,4,1,256]{3,2,1,0:T(1,128)} %pad_add_fusion.place, f32[4,4,1,256]{3,2,1,0:T(1,128)} %pad_maximum_fusion.7.gate, ...), custom_call_target="tpu_custom_call" | custom-call | flops 9663676416 | bytes 50331648 | tf_op jit(solution)/shard_map/pallas_call | solution.py:360
  780.4 32.2 %shard_map.151 = (bf16[4,2,288,2048]{3,2,1,0:T(8,128)(2,1)}, bf16[4,2,288,1024]{3,2,1,0:T(8,128)(2,1)}, bf16[4,2,288,1024]{3,2,1,0:T(8,128)(2,1)}, bf16[256,2048]{1,0:T(8,128)(2,1)}, bf16[256,2048]{1,0:T(8,128)(2,1)}) custom-call(s32[4,4,1,256]{3,2,1,0:T(1,128)} %pad_add_fusion.place, ...), custom_call_target="tpu_custom_call", output_to_operand_aliasing={{0}: (9, {}), {1}: (10, {}), {2}: (11, {})} | custom-call | flops 9663676416 | bytes 50331648 | tf_op jit(solution)/shard_map/pallas_call | solution.py:360
  835.8 20.7 %convolution_convert_fusion.2 = bf16[4,2048,1024]{2,1,0:T(8,128)(2,1)} fusion(bf16[4,576,2048]{2,1,0:T(8,128)(2,1)} %bitcast.511, bf16[4,576,1024]{2,1,0:T(8,128)(2,1)} %bitcast.524), kind=kOutput, calls=%fused_computation.2 | convolution fusion | flops 9672065024 | bytes 30932992 | tf_op jit(solution)/shard_map/krd,krf->kdf/dot_general | solution.py:397
  856.6 15.1 collective-permute-start.49
  878.8 25.6 %collective-permute-done.49 = bf16[256,2048]{1,0:T(8,128)(2,1)S(1)} collective-permute-done((bf16[256,2048]{1,0:T(8,128)(2,1)}, bf16[256,2048]{1,0:T(8,128)(2,1)S(1)}, u32[]{:S(2)}, u32[]{:S(2)}) %collective-permute-start.49) | collective-permute-done | bytes 1048608 | tf_op jit(solution)/shard_map/ppermute | solution.py:24
  914.8 21.2 %convolution_convert_fusion.1 = bf16[4,2048,1024]{2,1,0:T(8,128)(2,1)} fusion(bf16[4,576,2048]{2,1,0:T(8,128)(2,1)} %bitcast.514, bf16[4,576,1024]{2,1,0:T(8,128)(2,1)} %bitcast.525), kind=kOutput, calls=%fused_computation.1 | convolution fusion | flops 9672065024 | bytes 30932992 | tf_op jit(solution)/shard_map/krd,krf->kdf/dot_general | solution.py:397
  946.8 13.9 collective-permute-start.54
  973.7 38.9 %collective-permute-done.51 = bf16[256,512]{1,0:T(8,128)(2,1)} collective-permute-done((bf16[256,512]{1,0:T(8,128)(2,1)S(1)}, bf16[256,512]{1,0:T(8,128)(2,1)}, u32[]{:S(2)}, u32[]{:S(2)}) %collective-permute-start.51) | collective-permute-done | bytes 262176 | tf_op jit(solution)/shard_map/ppermute | solution.py:24
  1017.9 26.9 %collective-permute-done.52 = bf16[256,512]{1,0:T(8,128)(2,1)} collective-permute-done((bf16[256,512]{1,0:T(8,128)(2,1)S(1)}, bf16[256,512]{1,0:T(8,128)(2,1)}, u32[]{:S(2)}, u32[]{:S(2)}) %collective-permute-start.52) | collective-permute-done | bytes 262176 | tf_op jit(solution)/shard_map/ppermute | solution.py:24
  1064.4 22.3 %convolution_convert_fusion = bf16[4,2048,1024]{2,1,0:T(8,128)(2,1)} fusion(bf16[4,576,2048]{2,1,0:T(8,128)(2,1)} %bitcast.515, bf16[4,576,1024]{2,1,0:T(8,128)(2,1)} %bitcast.526), kind=kOutput, calls=%fused_computation | convolution fusion | flops 9672065024 | bytes 30932992 | tf_op jit(solution)/shard_map/krd,krf->kdf/dot_general | solution.py:397
  1167.9 21.8 %collective-permute-done.58 = bf16[256,1024]{1,0:T(8,128)(2,1)S(1)} collective-permute-done((bf16[256,1024]{1,0:T(8,128)(2,1)}, bf16[256,1024]{1,0:T(8,128)(2,1)S(1)}, u32[]{:S(2)}, u32[]{:S(2)}) %collective-permute-start.58) | collective-permute-done | bytes 524320 | tf_op jit(solution)/shard_map/ppermute | solution.py:24
  1196.3 18.3 %shard_map.152 = (f32[1024,512]{1,0:T(8,128)}, f32[1024,512]{1,0:T(8,128)}, bf16[1024,512]{1,0:T(8,128)(2,1)S(1)}, f32[1024,1]{1,0:T(8,128)S(1)}, f32[1024,1]{1,...) custom-call(f32[1024,1664]{1,0:T(8,128)} %copy-done.13, f32[1024,1664]{1,0:T(8,128)} %copy-done.13, ...), custom_call_target="tpu_custom_call" | custom-call | flops 1000000 | bytes 100000 | tf_op jit(solution)/shard_map/pallas_call | solution.py:243
  1290.1 17.6 %collective-permute-start.70 = (bf16[256,1024]{1,0:T(8,128)(2,1)}, bf16[256,1024]{1,0:T(8,128)(2,1)}, u32[]{:S(2)}, u32[]{:S(2)}) collective-permute-start(bf16[256,1024]{1,0:T(8,128)(2,1)} %get-tuple-element.157), channel_id=1, source_target_pairs={{0,8},{8,0},{16,24},{24,16},{1,9},{9,1},{17,25},{25,17},{2,10},{10... | collective-permute-start | bytes 1572872 | tf_op jit(solution)/shard_map/ppermute | solution.py:24
  1409.3 22.0 %collective-permute-done.74 = bf16[256,1536]{1,0:T(8,128)(2,1)} collective-permute-done((bf16[256,1536]{1,0:T(8,128)(2,1)}, bf16[256,1536]{1,0:T(8,128)(2,1)}, u32[]{:S(2)}, u32[]{:S(2)}) %collective-permute-start.74) | collective-permute-done | bytes 786464 | tf_op jit(solution)/shard_map/ppermute | solution.py:24
  1438.6 14.9 collective-permute-start.93
  1471.7 20.0 %collective-permute-done.94 = bf16[256,1024]{1,0:T(8,128)(2,1)S(1)} collective-permute-done((bf16[256,1024]{1,0:T(8,128)(2,1)S(1)}, bf16[256,1024]{1,0:T(8,128)(2,1)S(1)}, u32[]{:S(2)}, u32[]{:S(2)}) %collective-permute-start.94) | collective-permute-done | bytes 524320 | tf_op jit(solution)/shard_map/ppermute | solution.py:24
  1495.0 19.3 %copy.200 = f32[256,4,3072]{2,1,0:T(4,128)} copy(f32[256,4,3072]{2,0,1:T(8,128)S(1)} %convert_bitcast_fusion) | data formatting | bytes 25165824
  (666 shorter events, 716.8 us)
Async XLA Ops:
  7.2 330.8 %all-gather.5.cloned.1.call-start = ((), (), s32[]{:S(2)}) async-start(), calls=%async_computation.3 | async-start | bytes 18874368 | tf_op jit(solution)/shard_map/all_gather | solution.py:472
  10.5 71.5 %collective-permute-start.3 = (bf16[256,2048]{1,0:T(8,128)(2,1)S(1)}, bf16[256,2048]{1,0:T(8,128)(2,1)}, u32[]{:S(2)}, u32[]{:S(2)}) collective-permute-start(bf16[256,2048]{1,0:T(8,128)(2,1)S(1)} %reshape.512), channel_id=1, source_target_pairs={{0,1},{1,0},{2,3},{3,2},{4,5},{5,4},{6,7},{7,6},{8,9},{9,8},{10,11... | collective-permute-start | bytes 3145736 | tf_op jit(solution)/shard_map/ppermute | solution.py:24
  13.5 72.2 %collective-permute-start.4 = (bf16[256,2048]{1,0:T(8,128)(2,1)S(1)}, bf16[256,2048]{1,0:T(8,128)(2,1)}, u32[]{:S(2)}, u32[]{:S(2)}) collective-permute-start(bf16[256,2048]{1,0:T(8,128)(2,1)S(1)} %reshape.512), channel_id=1, source_target_pairs={{0,2},{1,3},{2,0},{3,1},{4,6},{5,7},{6,4},{7,5},{8,10},{9,11},{10,... | collective-permute-start | bytes 3145736 | tf_op jit(solution)/shard_map/ppermute | solution.py:24
  15.0 72.9 %collective-permute-start.5 = (bf16[256,2048]{1,0:T(8,128)(2,1)S(1)}, bf16[256,2048]{1,0:T(8,128)(2,1)}, u32[]{:S(2)}, u32[]{:S(2)}) collective-permute-start(bf16[256,2048]{1,0:T(8,128)(2,1)S(1)} %reshape.512), channel_id=1, source_target_pairs={{0,3},{1,2},{2,1},{3,0},{4,7},{5,6},{6,5},{7,4},{8,11},{9,10},{10,... | collective-permute-start | bytes 3145736 | tf_op jit(solution)/shard_map/ppermute | solution.py:24
  116.0 377.4 %all-gather.7.cloned.1.call-start = ((), (), s32[]{:S(2)}) async-start(), calls=%async_computation.4 | async-start | bytes 18874368 | tf_op jit(solution)/shard_map/all_gather | solution.py:472
  135.4 59.5 %collective-permute-start.10 = (bf16[256,1664]{1,0:T(8,128)(2,1)}, bf16[256,1664]{1,0:T(8,128)(2,1)S(1)}, u32[]{:S(2)}, u32[]{:S(2)}) collective-permute-start(bf16[256,1664]{1,0:T(8,128)(2,1)} %get-tuple-element.126), channel_id=1, source_target_pairs={{0,16},{8,24},{16,0},{24,8},{1,17},{9,25},{17,1},{25,9},{2,18},{10... | collective-permute-start | bytes 2555912 | tf_op jit(solution)/shard_map/ppermute | solution.py:24
  137.1 58.9 %collective-permute-start.11 = (bf16[256,1664]{1,0:T(8,128)(2,1)}, bf16[256,1664]{1,0:T(8,128)(2,1)}, u32[]{:S(2)}, u32[]{:S(2)}) collective-permute-start(bf16[256,1664]{1,0:T(8,128)(2,1)} %get-tuple-element.126), channel_id=1, source_target_pairs={{0,24},{8,16},{16,8},{24,0},{1,25},{9,17},{17,9},{25,1},{2,26},{10... | collective-permute-start | bytes 2555912 | tf_op jit(solution)/shard_map/ppermute | solution.py:24
  266.9 292.2 %all-gather.9.cloned.1.call-start = ((), (), s32[]{:S(2)}) async-start(), calls=%async_computation.5 | async-start | bytes 18874368 | tf_op jit(solution)/shard_map/all_gather | solution.py:472
  280.0 49.0 %collective-permute-start.22 = (f32[256,16]{0,1:T(8,128)S(1)}, f32[256,16]{0,1:T(8,128)S(1)}, u32[]{:S(2)}, u32[]{:S(2)}) collective-permute-start(f32[256,16]{0,1:T(8,128)S(1)} %get-tuple-element.212), channel_id=1, source_target_pairs={{0,8},{8,0},{16,24},{24,16},{1,9},{9,1},{17,25},{25,17},{2,10},{10... | collective-permute-start | bytes 49160 | tf_op jit(solution)/shard_map/ppermute | solution.py:24
  368.0 48.4 %collective-permute-start.27 = (bf16[256,2048]{1,0:T(8,128)(2,1)}, bf16[256,2048]{1,0:T(8,128)(2,1)}, u32[]{:S(2)}, u32[]{:S(2)}) collective-permute-start(bf16[256,2048]{1,0:T(8,128)(2,1)} %get-tuple-element.147), channel_id=1, source_target_pairs={{0,2},{1,3},{2,0},{3,1},{4,6},{5,7},{6,4},{7,5},{8,10},{9,11},{10,... | collective-permute-start | bytes 3145736 | tf_op jit(solution)/shard_map/ppermute | solution.py:24
  430.7 530.0 %all-gather.11.cloned.1.call-start = ((), (), s32[]{:S(2)}) async-start(), calls=%async_computation.6 | async-start | bytes 10485760 | tf_op jit(solution)/shard_map/all_gather | solution.py:612
  435.6 51.8 %collective-permute-start.32 = (bf16[256,2048]{1,0:T(8,128)(2,1)S(1)}, bf16[256,2048]{1,0:T(8,128)(2,1)S(1)}, u32[]{:S(2)}, u32[]{:S(2)}) collective-permute-start(bf16[256,2048]{1,0:T(8,128)(2,1)S(1)} %multiply_convert_fusion.3.refs_0_), channel_id=1, source_target_pairs={{0,16},{8,24},{16,0},{24,8},{1,17},{9,25},{17,1},{25,9},{2,18},{10... | collective-permute-start | bytes 3145736 | tf_op jit(solution)/shard_map/ppermute | solution.py:24
  522.3 610.9 %reduce-scatter.4.cloned.1.call-start = ((), (), s32[]{:S(2)}) async-start(), calls=%async_computation.7 | async-start | bytes 18874368 | tf_op jit(solution)/shard_map/reduce_scatter | solution.py:624
  730.0 49.4 %collective-permute-start.48 = (bf16[256,2048]{1,0:T(8,128)(2,1)}, bf16[256,2048]{1,0:T(8,128)(2,1)S(1)}, u32[]{:S(2)}, u32[]{:S(2)}) collective-permute-start(bf16[256,2048]{1,0:T(8,128)(2,1)} %broadcast_add_fusion.8), channel_id=1, source_target_pairs={{0,24},{8,16},{16,8},{24,0},{1,25},{9,17},{17,9},{25,1},{2,26},{10... | collective-permute-start | bytes 3145736 | tf_op jit(solution)/shard_map/ppermute | solution.py:24
  767.0 56.1 %collective-permute-start.46 = (bf16[256,2048]{1,0:T(8,128)(2,1)}, bf16[256,2048]{1,0:T(8,128)(2,1)}, u32[]{:S(2)}, u32[]{:S(2)}) collective-permute-start(bf16[256,2048]{1,0:T(8,128)(2,1)} %get-tuple-element.51), channel_id=1, source_target_pairs={{0,16},{8,24},{16,0},{24,8},{1,17},{9,25},{17,1},{25,9},{2,18},{10... | collective-permute-start | bytes 3145736 | tf_op jit(solution)/shard_map/ppermute | solution.py:24
  856.6 423.4 %reduce-scatter.6.cloned.1.call-start = ((), (), s32[]{:S(2)}) async-start(), calls=%async_computation.8 | async-start | bytes 18874368 | tf_op jit(solution)/shard_map/reduce_scatter | solution.py:624
  936.1 500.7 %reduce-scatter.8.cloned.1.call-start = ((), (), s32[]{:S(2)}) async-start(), calls=%async_computation.9 | async-start | bytes 18874368 | tf_op jit(solution)/shard_map/reduce_scatter | solution.py:624
  946.8 101.5 %collective-permute-start.54 = (bf16[256,2048]{1,0:T(8,128)(2,1)}, bf16[256,2048]{1,0:T(8,128)(2,1)}, u32[]{:S(2)}, u32[]{:S(2)}) collective-permute-start(bf16[256,2048]{1,0:T(8,128)(2,1)} %get-tuple-element.117), channel_id=1, source_target_pairs={{0,1},{1,0},{2,3},{3,2},{4,5},{5,4},{6,7},{7,6},{8,9},{9,8},{10,11... | collective-permute-start | bytes 3145736 | tf_op jit(solution)/shard_map/ppermute | solution.py:24
  966.9 83.7 %collective-permute-start.55 = (bf16[256,2048]{1,0:T(8,128)(2,1)}, bf16[256,2048]{1,0:T(8,128)(2,1)}, u32[]{:S(2)}, u32[]{:S(2)}) collective-permute-start(bf16[256,2048]{1,0:T(8,128)(2,1)} %get-tuple-element.117), channel_id=1, source_target_pairs={{0,2},{1,3},{2,0},{3,1},{4,6},{5,7},{6,4},{7,5},{8,10},{9,11},{10,... | collective-permute-start | bytes 3145736 | tf_op jit(solution)/shard_map/ppermute | solution.py:24
  968.5 84.8 %collective-permute-start.56 = (bf16[256,2048]{1,0:T(8,128)(2,1)}, bf16[256,2048]{1,0:T(8,128)(2,1)}, u32[]{:S(2)}, u32[]{:S(2)}) collective-permute-start(bf16[256,2048]{1,0:T(8,128)(2,1)} %get-tuple-element.117), channel_id=1, source_target_pairs={{0,3},{1,2},{2,1},{3,0},{4,7},{5,6},{6,5},{7,4},{8,11},{9,10},{10,... | collective-permute-start | bytes 3145736 | tf_op jit(solution)/shard_map/ppermute | solution.py:24
  970.4 74.4 %collective-permute-start.52 = (bf16[256,512]{1,0:T(8,128)(2,1)S(1)}, bf16[256,512]{1,0:T(8,128)(2,1)}, u32[]{:S(2)}, u32[]{:S(2)}) collective-permute-start(bf16[256,512]{1,0:T(8,128)(2,1)S(1)} %get-tuple-element.175), channel_id=1, source_target_pairs={{0,2},{1,3},{2,0},{3,1},{4,6},{5,7},{6,4},{7,5},{8,10},{9,11},{10,... | collective-permute-start | bytes 786440 | tf_op jit(solution)/shard_map/ppermute | solution.py:24
  1138.8 50.9 %collective-permute-start.58 = (bf16[256,1024]{1,0:T(8,128)(2,1)}, bf16[256,1024]{1,0:T(8,128)(2,1)S(1)}, u32[]{:S(2)}, u32[]{:S(2)}) collective-permute-start(bf16[256,1024]{1,0:T(8,128)(2,1)} %get-tuple-element.166), channel_id=1, source_target_pairs={{0,16},{8,24},{16,0},{24,8},{1,17},{9,25},{17,1},{25,9},{2,18},{10... | collective-permute-start | bytes 1572872 | tf_op jit(solution)/shard_map/ppermute | solution.py:24
  1153.9 67.8 %collective-permute-start.83 = (bf16[64,512]{1,0:T(8,128)(2,1)}, bf16[64,512]{1,0:T(8,128)(2,1)}, u32[]{:S(2)}, u32[]{:S(2)}) collective-permute-start(bf16[64,512]{1,0:T(8,128)(2,1)} %get-tuple-element.199), channel_id=1, source_target_pairs={{0,1},{1,0},{2,3},{3,2},{4,5},{5,4},{6,7},{7,6},{8,9},{9,8},{10,11... | collective-permute-start | bytes 196616 | tf_op jit(solution)/shard_map/ppermute | solution.py:24
  1155.6 101.5 %collective-permute-start.84 = (bf16[64,512]{1,0:T(8,128)(2,1)}, bf16[64,512]{1,0:T(8,128)(2,1)S(1)}, u32[]{:S(2)}, u32[]{:S(2)}) collective-permute-start(bf16[64,512]{1,0:T(8,128)(2,1)} %get-tuple-element.198), channel_id=1, source_target_pairs={{0,2},{1,3},{2,0},{3,1},{4,6},{5,7},{6,4},{7,5},{8,10},{9,11},{10,... | collective-permute-start | bytes 196616 | tf_op jit(solution)/shard_map/ppermute | solution.py:24
  1164.2 95.9 %collective-permute-start.85 = (bf16[64,512]{1,0:T(8,128)(2,1)}, bf16[64,512]{1,0:T(8,128)(2,1)}, u32[]{:S(2)}, u32[]{:S(2)}) collective-permute-start(bf16[64,512]{1,0:T(8,128)(2,1)} %get-tuple-element.197), channel_id=1, source_target_pairs={{0,3},{1,2},{2,1},{3,0},{4,7},{5,6},{6,5},{7,4},{8,11},{9,10},{10,... | collective-permute-start | bytes 196616 | tf_op jit(solution)/shard_map/ppermute | solution.py:24
  1243.3 117.4 %collective-permute-start.69 = (bf16[1024,1536]{1,0:T(8,128)(2,1)}, bf16[1024,1536]{1,0:T(8,128)(2,1)}, u32[]{:S(2)}, u32[]{:S(2)}) collective-permute-start(bf16[1024,1536]{1,0:T(8,128)(2,1)} %dynamic-slice_bitcast_fusion), channel_id=1, source_target_pairs={{0,4},{4,0},{1,5},{5,1},{2,6},{6,2},{3,7},{7,3},{8,12},{12,8},{9,1... | collective-permute-start | bytes 9437192 | tf_op jit(solution)/shard_map/ppermute | solution.py:24
  1260.1 49.8 %collective-permute-start.63 = (bf16[256,1024]{1,0:T(8,128)(2,1)S(1)}, bf16[256,1024]{1,0:T(8,128)(2,1)}, u32[]{:S(2)}, u32[]{:S(2)}) collective-permute-start(bf16[256,1024]{1,0:T(8,128)(2,1)S(1)} %get-tuple-element.162), channel_id=1, source_target_pairs={{0,1},{1,0},{2,3},{3,2},{4,5},{5,4},{6,7},{7,6},{8,9},{9,8},{10,11... | collective-permute-start | bytes 1572872 | tf_op jit(solution)/shard_map/ppermute | solution.py:24
  1269.6 49.4 %collective-permute-start.64 = (bf16[256,1024]{1,0:T(8,128)(2,1)S(1)}, bf16[256,1024]{1,0:T(8,128)(2,1)S(1)}, u32[]{:S(2)}, u32[]{:S(2)}) collective-permute-start(bf16[256,1024]{1,0:T(8,128)(2,1)S(1)} %get-tuple-element.164), channel_id=1, source_target_pairs={{0,2},{1,3},{2,0},{3,1},{4,6},{5,7},{6,4},{7,5},{8,10},{9,11},{10,... | collective-permute-start | bytes 1572872 | tf_op jit(solution)/shard_map/ppermute | solution.py:24
  1272.3 48.0 %collective-permute-start.65 = (bf16[256,1024]{1,0:T(8,128)(2,1)S(1)}, bf16[256,1024]{1,0:T(8,128)(2,1)}, u32[]{:S(2)}, u32[]{:S(2)}) collective-permute-start(bf16[256,1024]{1,0:T(8,128)(2,1)S(1)} %get-tuple-element.163), channel_id=1, source_target_pairs={{0,3},{1,2},{2,1},{3,0},{4,7},{5,6},{6,5},{7,4},{8,11},{9,10},{10,... | collective-permute-start | bytes 1572872 | tf_op jit(solution)/shard_map/ppermute | solution.py:24
  1290.1 50.9 %collective-permute-start.70 = (bf16[256,1024]{1,0:T(8,128)(2,1)}, bf16[256,1024]{1,0:T(8,128)(2,1)}, u32[]{:S(2)}, u32[]{:S(2)}) collective-permute-start(bf16[256,1024]{1,0:T(8,128)(2,1)} %get-tuple-element.157), channel_id=1, source_target_pairs={{0,8},{8,0},{16,24},{24,16},{1,9},{9,1},{17,25},{25,17},{2,10},{10... | collective-permute-start | bytes 1572872 | tf_op jit(solution)/shard_map/ppermute | solution.py:24
  1376.0 55.4 %collective-permute-start.74 = (bf16[256,1536]{1,0:T(8,128)(2,1)}, bf16[256,1536]{1,0:T(8,128)(2,1)}, u32[]{:S(2)}, u32[]{:S(2)}) collective-permute-start(bf16[256,1536]{1,0:T(8,128)(2,1)} %get-tuple-element.150), channel_id=1, source_target_pairs={{0,16},{8,24},{16,0},{24,8},{1,17},{9,25},{17,1},{25,9},{2,18},{10... | collective-permute-start | bytes 2359304 | tf_op jit(solution)/shard_map/ppermute | solution.py:24
  1376.0 55.3 %collective-permute-start.75 = (bf16[256,1536]{1,0:T(8,128)(2,1)}, bf16[256,1536]{1,0:T(8,128)(2,1)}, u32[]{:S(2)}, u32[]{:S(2)}) collective-permute-start(bf16[256,1536]{1,0:T(8,128)(2,1)} %get-tuple-element.149), channel_id=1, source_target_pairs={{0,24},{8,16},{16,8},{24,0},{1,25},{9,17},{17,9},{25,1},{2,26},{10... | collective-permute-start | bytes 2359304 | tf_op jit(solution)/shard_map/ppermute | solution.py:24
  (160 other events, 3009.0 us)
Sparse Core Ops, SparseCore 0:
  116.2 97.3 all-gather.4
  267.0 99.9 all-gather.6
  430.8 94.9 all-gather.8
  527.5 87.6 all-gather.10
  856.7 186.0 reduce-scatter.3
  1046.3 117.4 reduce-scatter.5
  1167.3 154.8 reduce-scatter.7

commit v7 on v6

--- a/solution.py
+++ b/solution.py
@@ -56,6 +56,15 @@
     firsts = [value[(slice(0, 1),) * value.ndim].reshape(()).astype(f32) for value in values]
     total = sum(firsts)
     return (total != total).astype(jnp.int32)
+
+
+def together(work, *operands):
+    shapes = jax.eval_shape(work, *operands)
+
+    def nothing(*_):
+        return jax.tree.map(lambda leaf: jnp.zeros(leaf.shape, leaf.dtype), shapes)
+
+    return lax.cond(token(jax.tree.leaves(operands)[0]) == 0, work, nothing, *operands)
 
 
 def after(value, *others):
@@ -445,14 +454,12 @@
         rows = in_order(blocks, "z", start)
         return collect(rows, "o").reshape((width // 2,) + rows.shape[2:])
 
-    def sum_rows(grad, *others):
+    def sum_cores(grad):
         count = grad.shape[1]
         grad = exchange_sum(grad.reshape(CORES, width // 2, count), "c").astype(bf16)
         if outer > 1:
             grad = exchange_sum(grad.reshape(outer, planes * part, count), "o").astype(bf16)
-        if others:
-            grad = after(grad, *others)
-        return exchange_sum(grad.reshape(planes, part, count), "z")
+        return grad.reshape(planes, part, count)
 
     def gather_sum(value):
         for axis in ("z", "s", "c", "o"):
@@ -461,11 +468,8 @@
 
     by_expert = w_expert.transpose(1, 0, 2)
 
-    def expert_chunk(i, start=0):
-        def piece_for(owner):
-            return lax.dynamic_slice(by_expert, (owner, 0, i * hidden), (1, part, hidden))[0]
-
-        return exchange(piece_for, "z", start)
+    def expert_piece(i, owner):
+        return lax.dynamic_slice(by_expert, (owner, 0, i * hidden), (1, part, hidden))[0]
 
     def gather_plane(ready):
         chunk = ready.reshape(planes * part, hidden)
@@ -487,26 +491,34 @@
         picked = [
             lax.dynamic_slice_in_dim(w_attn, i * width + owner * cols, cols, 1) for i in range(4)
         ]
-        return jnp.concatenate(picked[:3] + [extra] + picked[3:], axis=1)
-
-    mine_blocks = exchange(columns_of, "s")
-    gate_blocks = expert_chunk(0)
+        return jnp.concatenate(picked + [extra], axis=1)
+
     inputs = to_inner(tokens)
-    token_blocks = gather_near(inputs, "s")
+
+    def first_transfers(columns, experts, inputs):
+        return (
+            [columns[0]] + [send(columns[k], "s", k) for k in range(1, seqs)],
+            [experts[0]] + [send(experts[k], "z", k) for k in range(1, planes)],
+            gather_near(inputs, "s"),
+        )
+
+    mine_blocks, gate_blocks, token_blocks = together(
+        first_transfers,
+        [columns_of(rank ^ k) for k in range(seqs)],
+        [expert_piece(0, plane ^ k) for k in range(planes)],
+        inputs,
+    )
     inputs = inputs.astype(f32)
-
     mine = in_order(mine_blocks, "s").reshape(part, 4 * cols + PAD)
-    seq_tokens = in_order(token_blocks, "s", token(mine)).reshape(seq, width)
-    gate_ready = in_order(gate_blocks, "z", token(seq_tokens))
+    gate_ready = in_order(gate_blocks, "z")
     w_gate = gather_plane(gate_ready)
-    in_blocks = gather_near(after(mine[:, : 3 * cols + PAD], gate_ready), "z")
-    seq_tokens = seq_tokens.astype(f32)
+    in_blocks = gather_near(mine, "z")
+    seq_tokens = in_order(token_blocks, "s").reshape(seq, width).astype(f32)
     seq_factor = rms_factor(seq_tokens)
     w_in = stack_rows(in_blocks, token(seq_factor))
     w_in_other = send(w_in, "c", 1)
-    up_blocks = expert_chunk(1, token(w_in))
-
-    side = whole_of(w_in[:, 3 * cols :], w_in_other[:, 3 * cols :], 0)[:, :6].astype(f32).T
+
+    side = whole_of(w_in[:, 4 * cols :], w_in_other[:, 4 * cols :], 0)[:, :6].astype(f32).T
     gain_in, gain_mid = side[0], side[1]
     gain_q = lax.dynamic_slice_in_dim(to_outer(side[2]), rank * cols, cols, 0)
     gain_k = lax.dynamic_slice_in_dim(to_outer(side[3]), rank * cols, cols, 0)
@@ -554,8 +566,23 @@
 
     normed_in = (seq_tokens * seq_factor * gain_in).astype(bf16)
     normed_mine, normed_other = halves(normed_in)
-    projected = jnp.dot(normed_mine, w_in, preferred_element_type=f32) + jnp.dot(
-        normed_other, w_in_other, preferred_element_type=f32
+    w_qkv, w_qkv_other = w_in[:, : 3 * cols], w_in_other[:, : 3 * cols]
+    w_out = whole_of(w_in[:, 3 * cols : 4 * cols], w_in_other[:, 3 * cols : 4 * cols], 0)
+
+    def project(experts, mine, other, weight, weight_other):
+        got = [experts[0]] + [send(experts[k], "z", k) for k in range(1, planes)]
+        projected = jnp.dot(mine, weight, preferred_element_type=f32) + jnp.dot(
+            other, weight_other, preferred_element_type=f32
+        )
+        return got, projected
+
+    up_blocks, projected = together(
+        project,
+        [expert_piece(1, (plane ^ k) + token(w_in)) for k in range(planes)],
+        normed_mine,
+        normed_other,
+        w_qkv,
+        w_qkv_other,
     )
     query_raw = projected[:, :cols]
     key_raw = projected[:, cols : 2 * cols]
@@ -570,13 +597,11 @@
     q_mean, k_mean = over_heads(
         jnp.sum(query_raw * query_raw, axis=-1), jnp.sum(key_raw * key_raw, axis=-1)
     )
-    up_ready = in_order(up_blocks, "z", token(projected))
+    up_ready = in_order(up_blocks, "z")
     w_up = gather_plane(up_ready)
-    out_blocks = gather_near(after(mine[:, 3 * cols + PAD :], up_ready), "z")
-    out_rows = stack_rows(out_blocks, token(q_mean))
     cosine, sine = rope_tables(seq)
     shared = [
-        after(q_mean, up_ready, w_gate, out_rows, place),
+        after(q_mean, up_ready, w_gate, place),
         k_mean,
         gain_q[None],
         gain_k[None],
@@ -586,12 +611,21 @@
         segment[None],
     ]
     attended, query, keyed, valued, log_total = attend(projected, shared, heads)
-    w_out = collect(out_rows, "c").reshape(width, cols)
-    down_blocks = expert_chunk(2, token(attended))
-    attn_out = dot("tc,dc->td", attended, w_out).astype(bf16)
-    residual = inputs + exchange_sum(attn_out.reshape(seqs, own, width), "s")
-    down_ready = in_order(down_blocks, "z", token(residual))
-    residual = after(residual, down_ready)
+    attn_out = dot("tc,dc->td", attended, w_out).astype(bf16).reshape(seqs, own, width)
+
+    def attention_back(parts, experts):
+        return (
+            [parts[0]] + [send(parts[k], "s", k) for k in range(1, seqs)],
+            [experts[0]] + [send(experts[k], "z", k) for k in range(1, planes)],
+        )
+
+    got, down_blocks = together(
+        attention_back,
+        [lax.dynamic_index_in_dim(attn_out, rank ^ k, 0, keepdims=False) for k in range(seqs)],
+        [expert_piece(2, (plane ^ k) + token(projected)) for k in range(planes)],
+    )
+    residual = inputs + sum(piece.astype(f32) for piece in got)
+    down_ready = in_order(down_blocks, "z")
     w_down = gather_plane(down_ready)
 
     normed_mid = (residual * rms_factor(residual) * gain_mid).astype(bf16)
@@ -638,7 +672,7 @@
     partial.append((first, last))
     back_last, back_pieces = send_back(*partial)
     grad_rows, grad_gate, grad_up = [v.reshape(seqs, -1, v.shape[-1]) for v in grads]
-    grad_w_down = dot("krd,krf->kdf", grad_rows, after(activated, back_last)).astype(bf16)
+    grad_w_down = dot("krd,krf->kdf", grad_rows, activated).astype(bf16)
     back_pieces[0] = after(back_pieces[0], grad_w_down)
     grad_mid = total(back_pieces)
     grad_w_gate = dot("krd,krf->kdf", rows_in, after(grad_gate, grad_mid)).astype(bf16)
@@ -651,22 +685,40 @@
         lambda i: lax.dynamic_index_in_dim(grad_heads, i, 0, keepdims=False), "s"
     )
     grad_heads = in_order(head_blocks, "s", token(grad_w_gate)).reshape(seq, cols)
-    low_blocks = gather_near(grad_low, "s")
-    grad_attn_out = in_order(low_blocks, "s", token(grad_w_gate)).reshape(seq, width)
-    grad_w_up = dot("krd,krf->kdf", rows_in, after(grad_up, grad_heads, grad_attn_out))
-    grad_w_up = grad_w_up.astype(bf16)
+    grad_w_down = scatter_expert(grad_w_down)
+    grad_w_gate = scatter_expert(grad_w_gate)
+
+    def attention_grads(experts, low, rows_in, grad_up, grad_heads, raw, *rest):
+        moved = [experts[0]] + [send(experts[k], "z", k) for k in range(1, planes)]
+        near = gather_near(low, "s")
+        grad_w_up = dot("krd,krf->kdf", rows_in, grad_up).astype(bf16)
+        *rest, log_total = rest
+        query, keyed, valued, *shared = rest
+        result = attend_back(
+            raw, shared, query, keyed, valued, after(grad_heads, grad_w_up), log_total, heads
+        )
+        return moved, near, grad_w_up, result
+
+    down_blocks, low_blocks, grad_w_up, result = together(
+        attention_grads,
+        [lax.dynamic_index_in_dim(grad_w_down, plane ^ k, 0, keepdims=False) for k in range(planes)],
+        grad_low,
+        rows_in,
+        grad_up,
+        grad_heads,
+        projected,
+        query,
+        keyed,
+        valued,
+        *shared,
+        log_total,
+    )
+    grad_q, grad_k, grad_v, q_inner, k_inner, gain_q_grad, gain_k_grad = result
     up_done = grad_w_up
-    grad_w_down, grad_w_gate, grad_w_up = [
-        scatter_expert(grad) for grad in (grad_w_down, grad_w_gate, grad_w_up)
-    ]
-    down_blocks, gate_blocks = to_owners(grad_w_down), to_owners(grad_w_gate)
-    down_ready = in_order(down_blocks, "z", token(up_done))
-    grad_heads = after(grad_heads, down_ready)
-    grad_q, grad_k, grad_v, q_inner, k_inner, gain_q_grad, gain_k_grad = attend_back(
-        projected, shared, query, keyed, valued, grad_heads, log_total, heads
-    )
-    grad_w_out = sum_rows(dot("td,tc->dc", grad_attn_out, attended).astype(bf16))
-    q_inner, k_inner = over_heads(q_inner[:, 0], k_inner[:, 0], up_done)
+    grad_w_up = scatter_expert(grad_w_up)
+    grad_attn_out = in_order(low_blocks, "s").reshape(seq, width)
+    grad_w_out = dot("td,tc->dc", grad_attn_out, attended).astype(bf16)
+    q_inner, k_inner = over_heads(q_inner[:, 0], k_inner[:, 0], grad_w_out)
 
     def norm_grad(grad, raw, mean, inner):
         factor = lax.rsqrt(mean + epsilon)
@@ -680,17 +732,31 @@
         ],
         axis=1,
     )
-    grad_padded = jnp.concatenate([grad_proj, jnp.zeros((seq, PAD), bf16)], axis=1)
 
     def back_half(weight):
-        grad = dot("tc,dc->td", grad_padded, weight).astype(bf16)
+        grad = dot("tc,dc->td", grad_proj, weight).astype(bf16)
         return exchange_sum(grad.reshape(seqs, own, width // 2), "s")
 
-    grad_normed = whole_of(back_half(w_in), back_half(w_in_other), 1)
+    grad_normed = whole_of(back_half(w_qkv), back_half(w_qkv_other), 1)
     grad_w_qkv = dot("td,tc->dc", normed_in, grad_proj).astype(bf16)
-    gate_ready = in_order(gate_blocks, "z", token(grad_w_qkv))
-    grad_w_qkv = sum_rows(grad_w_qkv, gate_ready)
+    grad_w_qkv, grad_w_out = sum_cores(grad_w_qkv), sum_cores(grad_w_out)
+
+    def row_transfers(qkv, out, experts):
+        return [
+            [parts[0]] + [send(parts[k], "z", k) for k in range(1, planes)]
+            for parts in (qkv, out, experts)
+        ]
+
+    qkv_blocks, out_blocks, gate_blocks = together(
+        row_transfers,
+        *[
+            [lax.dynamic_index_in_dim(grad, plane ^ k, 0, keepdims=False) for k in range(planes)]
+            for grad in (grad_w_qkv, grad_w_out, grad_w_gate)
+        ],
+    )
+    grad_w_qkv, grad_w_out = total(qkv_blocks), total(out_blocks)
     up_blocks = to_owners(grad_w_up, token(grad_w_qkv))
+    down_ready, gate_ready = in_order(down_blocks, "z"), in_order(gate_blocks, "z")
     grad_in_norm, gain_in_grad = norm_back(inputs, gain_in, grad_normed)
     grad_tokens = to_outer(grad_resid + grad_in_norm)
 

time: 1540 us -> 1530 us (level)
  waiting for transfers between devices: 554 us -> 649 us
  starting transfers between devices: 258 us -> 206 us
    ppermute x96 -> x92, waiting for transfers between devices: 554 us -> 649 us  [send(): return lax.ppermute(block, axis, [(i, i ^ step) for i in range(size)])]
    ppermute x96 -> x92, starting transfers between devices: 244 us -> 204 us  [send(): return lax.ppermute(block, axis, [(i, i ^ step) for i in range(size)])]
    add x16 -> x13, other arithmetic: 37.5 us -> 14.3 us  [after(): return value + token(*others).astype(value.dtype)]
    unnamed x208 -> x178, local copies, waits for them, and re-layouts: 56.3 us -> 48.7 us
    dynamic_update_slice x50 -> x48, local copies, waits for them, and re-layouts: 54.6 us -> 49.1 us  [in_order(): lax.dynamic_update_index_in_dim(stacked, block, (rank ^ k) + start, 0)]
    another operation x15 -> x21, local copies, waits for them, and re-layouts: 33.4 us -> 30.8 us  [whole(): jax.shard_map(shards, mesh=inner, in_specs=(rows, rows, rows, experts, ro...]
  transfers between devices with their start and end apart: 103 -> 99, of which waited for: 39 -> 37; matrix products, arithmetic and copies ran while one was open for 28% -> 25% of each run, Pallas kernels for 11% -> 11%
where the time goes in v7:
time: 1530 us; the launch traced here: 1520 us
  waiting for transfers between devices  649 us (42%)
  local copies, waits for them, and re-layouts  238 us (16%)
  starting transfers between devices  206 us (13%)
  Pallas kernels  170 us (11%)
  matrix products  108 us (7%)
  other arithmetic  92.7 us (6%)
  between operations  50.8 us (3%)
    ppermute x92, waiting for transfers between devices, send(): return lax.ppermute(block, axis, [(i, i ^ step) for i in range(size)])  649 us
    ppermute x92, starting transfers between devices, send(): return lax.ppermute(block, axis, [(i, i ^ step) for i in range(size)])  204 us
    pallas_call x6, Pallas kernels, run(): pl.pallas_call(functools.partial(kernel, self.count, self.slots), grid=(s...  134 us
    dot_general x10, matrix products, dot(): return jnp.einsum(spec, left, right, preferred_element_type=f32)  97.4 us
    dynamic_update_slice x48, local copies, waits for them, and re-layouts, in_order(): lax.dynamic_update_index_in_dim(stacked, block, (rank ^ k) + start, 0)  49.1 us
    unnamed x178, local copies, waits for them, and re-layouts  48.7 us
    another operation x21, local copies, waits for them, and re-layouts, whole(): jax.shard_map(shards, mesh=inner, in_specs=(rows, rows, rows, experts, ro...  30.8 us
  transfers between devices with their start and end apart: 99, of which 37 were waited for; matrix products, arithmetic and copies ran while one was open for 25% of the time, Pallas kernels for 11%

profile of v7, /device:TPU:0, one launch (start us, length us, event | category | flops | bytes accessed | tf_op | source)
XLA Modules:
  0.0 1519.2 jit_solution(16046437311078080376)
XLA Ops:
  21.4 98.9 %conditional.5 = (bf16[1,64,2176]{2,1,0:T(8,128)(2,1)S(1)}, bf16[1,64,2176]{2,1,0:T(8,128)(2,1)}, bf16[1,64,2176]{2,1,0:T(8,128)(2,1)}, bf16[1,64,2176]{2,1,0:T(...) conditional(s32[]{:T(128)} %bitcast.70, () %tuple.158, ...), branch_computations={%region_1.2_spmd, %region_2.3_spmd} | conditional | bytes 42205684 | solution.py:67
  36.4 48.7 %collective-permute-done.2 = bf16[64,2176]{1,0:T(8,128)(2,1)} collective-permute-done((bf16[64,2176]{1,0:T(8,128)(2,1)S(1)}, bf16[64,2176]{1,0:T(8,128)(2,1)}, u32[]{:S(2)}, u32[]{:S(2)}) %collective-permute-start.2) | collective-permute-done | bytes 278560 | tf_op jit(solution)/shard_map/cond/branch_1_fun/ppermute | solution.py:24
  88.0 32.4 %collective-permute-done.4 = bf16[256,1024]{1,0:T(8,128)(2,1)} collective-permute-done((bf16[256,1024]{1,0:T(8,128)(2,1)S(1)}, bf16[256,1024]{1,0:T(8,128)(2,1)}, u32[]{:S(2)}, u32[]{:S(2)}) %collective-permute-start.4) | collective-permute-done | bytes 524320 | tf_op jit(solution)/shard_map/cond/branch_1_fun/ppermute | solution.py:24
  157.3 32.6 %collective-permute-done.33 = bf16[256,2176]{1,0:T(8,128)(2,1)} collective-permute-done((bf16[256,2176]{1,0:T(8,128)(2,1)S(1)}, bf16[256,2176]{1,0:T(8,128)(2,1)}, u32[]{:S(2)}, u32[]{:S(2)}) %collective-permute-start.33) | collective-permute-done | bytes 1114144 | tf_op jit(solution)/shard_map/ppermute | solution.py:24
  192.2 26.3 %collective-permute-done.34 = bf16[256,2176]{1,0:T(8,128)(2,1)} collective-permute-done((bf16[256,2176]{1,0:T(8,128)(2,1)S(1)}, bf16[256,2176]{1,0:T(8,128)(2,1)}, u32[]{:S(2)}, u32[]{:S(2)}) %collective-permute-start.34) | collective-permute-done | bytes 1114144 | tf_op jit(solution)/shard_map/ppermute | solution.py:24
  244.3 68.4 %conditional.6 = (f32[1024,1536]{1,0:T(8,128)}, bf16[1,256,1024]{2,1,0:T(8,128)(2,1)S(1)}, bf16[1,256,1024]{2,1,0:T(8,128)(2,1)}, bf16[1,256,1024]{2,1,0:T(8,128)(2,1)}, bf16[1,256,1024]{2,1,0:T(8,128)(2,1)}) conditional(s32[]{:T(128)} %bitcast.82, () %tuple.160, (pred[]{:T(512)}, bf16[1024,2048]{1,0:T(8,128)(2,1)}, bf16[1024,2048]{1,0:T(8,128)(2,1)}, ...), branch_computations={%region_4.5_spmd, %region_5.6_spmd} | conditional | flops 6446120960 | bytes 97518480 | solution.py:67
  253.5 20.9 %collective-permute-start.24 = (bf16[256,1024]{1,0:T(8,128)(2,1)S(1)}, bf16[256,1024]{1,0:T(8,128)(2,1)}, u32[]{:S(2)}, u32[]{:S(2)}) collective-permute-start(bf16[256,1024]{1,0:T(8,128)(2,1)S(1)} %get-tuple-element.1107), channel_id=1, source_target_pairs={{0,8},{8,0},{16,24},{24,16},{1,9},{9,1},{17,25},{25,17},{2,10},{10... | collective-permute-start | bytes 1572872 | tf_op jit(solution)/shard_map/cond/branch_1_fun/ppermute | solution.py:24
  376.6 90.5 %conditional.7 = (f32[256,2048]{1,0:T(8,128)}, f32[256,2048]{1,0:T(8,128)}, f32[256,2048]{1,0:T(8,128)}, f32[256,2048]{1,0:T(8,128)S(1)}, bf16[1,256,1024]{2,1,0...) conditional(s32[]{:T(128)} %bitcast.108, () %tuple.162, ...), branch_computations={%region_9.10_spmd, %region_10.11_spmd} | conditional | flops 3670034 | bytes 62915144 | solution.py:67
  397.4 30.8 %collective-permute-done.11 = bf16[256,2048]{1,0:T(8,128)(2,1)S(1)} collective-permute-done((bf16[256,2048]{1,0:T(8,128)(2,1)}, bf16[256,2048]{1,0:T(8,128)(2,1)S(1)}, u32[]{:S(2)}, u32[]{:S(2)}) %collective-permute-start.11) | collective-permute-done | bytes 1048608 | tf_op jit(solution)/shard_map/cond/branch_1_fun/ppermute | solution.py:24
  430.3 18.9 %collective-permute-done.10 = bf16[256,2048]{1,0:T(8,128)(2,1)S(1)} collective-permute-done((bf16[256,2048]{1,0:T(8,128)(2,1)}, bf16[256,2048]{1,0:T(8,128)(2,1)S(1)}, u32[]{:S(2)}, u32[]{:S(2)}) %collective-permute-start.10) | collective-permute-done | bytes 1048608 | tf_op jit(solution)/shard_map/cond/branch_1_fun/ppermute | solution.py:24
  483.7 43.6 %collective-permute-done.43.refs_1_ = bf16[256,2048]{1,0:T(8,128)(2,1)S(1)} collective-permute-done((bf16[256,2048]{1,0:T(8,128)(2,1)S(1)}, bf16[256,2048]{1,0:T(8,128)(2,1)S(1)}, u32[]{:S(2)}, u32[]{:S(2)}) %collective-permute-start.43) | collective-permute-done | bytes 1048608 | tf_op jit(solution)/shard_map/ppermute | solution.py:24
  534.8 20.8 %shard_map.146 = (bf16[4,2,288,2048]{3,2,1,0:T(8,128)(2,1)}, bf16[4,2,288,1024]{3,2,1,0:T(8,128)(2,1)}, bf16[4,288,1024]{2,1,0:T(8,128)(2,1)}, bf16[4,288,1024]{2,1,0:T(8,128)(2,1)}) custom-call(s32[4,4,1,256]{3,2,1,0:T(1,128)} %pad_add_fusion.place, bf16[256,2048]{1,0:T(8,128)(2,1)} %copy-done.61, bf16[256,2048]{1,0:T(8,128)(2,1)} %copy-done.87, ...), custom_call_target="tpu_custom_call" | custom-call | flops 9663676416 | bytes 50331648 | tf_op jit(solution)/shard_map/pallas_call | solution.py:369
  581.0 20.8 %shard_map.147 = (bf16[4,2,288,2048]{3,2,1,0:T(8,128)(2,1)}, bf16[4,2,288,1024]{3,2,1,0:T(8,128)(2,1)}, bf16[4,288,1024]{2,1,0:T(8,128)(2,1)}, bf16[4,288,1024]{2,1,0:T(8,128)(2,1)}) custom-call(s32[4,4,1,256]{3,2,1,0:T(1,128)} %pad_add_fusion.place, bf16[256,2048]{1,0:T(8,128)(2,1)} %broadcast_add_fusion.8.refs_0_, ...), custom_call_target="tpu_custom_call", output_to_operand_aliasing={{0}: (5, {}), {1}: (6, {})} | custom-call | flops 9663676416 | bytes 50331648 | tf_op jit(solution)/shard_map/pallas_call | solution.py:369
  635.5 27.7 %collective-permute-done.46 = bf16[256,2048]{1,0:T(8,128)(2,1)S(1)} collective-permute-done((bf16[256,2048]{1,0:T(8,128)(2,1)}, bf16[256,2048]{1,0:T(8,128)(2,1)S(1)}, u32[]{:S(2)}, u32[]{:S(2)}) %collective-permute-start.46) | collective-permute-done | bytes 1048608 | tf_op jit(solution)/shard_map/ppermute | solution.py:24
  696.3 19.7 %collective-permute-done.47 = bf16[256,2048]{1,0:T(8,128)(2,1)} collective-permute-done((bf16[256,2048]{1,0:T(8,128)(2,1)}, bf16[256,2048]{1,0:T(8,128)(2,1)}, u32[]{:S(2)}, u32[]{:S(2)}) %collective-permute-start.47) | collective-permute-done | bytes 1048608 | tf_op jit(solution)/shard_map/ppermute | solution.py:24
  725.1 45.0 %collective-permute-done.56.refs_1_ = bf16[256,2048]{1,0:T(8,128)(2,1)S(1)} collective-permute-done((bf16[256,2048]{1,0:T(8,128)(2,1)S(1)}, bf16[256,2048]{1,0:T(8,128)(2,1)S(1)}, u32[]{:S(2)}, u32[]{:S(2)}) %collective-permute-start.56) | collective-permute-done | bytes 1048608 | tf_op jit(solution)/shard_map/ppermute | solution.py:24
  776.2 31.9 %shard_map.150 = (bf16[4,2,288,2048]{3,2,1,0:T(8,128)(2,1)}, bf16[4,2,288,1024]{3,2,1,0:T(8,128)(2,1)}, bf16[4,2,288,1024]{3,2,1,0:T(8,128)(2,1)}, bf16[256,2048]{1,0:T(8,128)(2,1)}, bf16[256,2048]{1,0:T(8,128)(2,1)}) custom-call(s32[4,4,1,256]{3,2,1,0:T(1,128)} %pad_add_fusion.place, f32[4,4,1,256]{3,2,1,0:T(1,128)} %pad_maximum_fusion.8.gate, ...), custom_call_target="tpu_custom_call" | custom-call | flops 9663676416 | bytes 50331648 | tf_op jit(solution)/shard_map/pallas_call | solution.py:369
  823.0 32.1 %shard_map.151 = (bf16[4,2,288,2048]{3,2,1,0:T(8,128)(2,1)}, bf16[4,2,288,1024]{3,2,1,0:T(8,128)(2,1)}, bf16[4,2,288,1024]{3,2,1,0:T(8,128)(2,1)}, bf16[256,2048]{1,0:T(8,128)(2,1)}, bf16[256,2048]{1,0:T(8,128)(2,1)}) custom-call(s32[4,4,1,256]{3,2,1,0:T(1,128)} %pad_add_fusion.place, ...), custom_call_target="tpu_custom_call", output_to_operand_aliasing={{0}: (9, {}), {1}: (10, {}), {2}: (11, {})} | custom-call | flops 9663676416 | bytes 50331648 | tf_op jit(solution)/shard_map/pallas_call | solution.py:369
  855.1 20.5 %convolution_convert_fusion.2 = bf16[4,2048,1024]{2,1,0:T(8,128)(2,1)} fusion(bf16[4,576,2048]{2,1,0:T(8,128)(2,1)} %bitcast.445, bf16[4,576,1024]{2,1,0:T(8,128)(2,1)} %bitcast.457), kind=kOutput, calls=%fused_computation.52 | convolution fusion | flops 9672065024 | bytes 30932992 | tf_op jit(solution)/shard_map/krd,krf->kdf/dot_general | solution.py:406
  880.8 42.0 %collective-permute-done.57 = bf16[256,2048]{1,0:T(8,128)(2,1)S(1)} collective-permute-done((bf16[256,2048]{1,0:T(8,128)(2,1)}, bf16[256,2048]{1,0:T(8,128)(2,1)S(1)}, u32[]{:S(2)}, u32[]{:S(2)}) %collective-permute-start.57) | collective-permute-done | bytes 1048608 | tf_op jit(solution)/shard_map/ppermute | solution.py:24
  929.3 23.8 %collective-permute-done.61 = bf16[256,2048]{1,0:T(8,128)(2,1)S(1)} collective-permute-done((bf16[256,2048]{1,0:T(8,128)(2,1)S(1)}, bf16[256,2048]{1,0:T(8,128)(2,1)S(1)}, u32[]{:S(2)}, u32[]{:S(2)}) %collective-permute-start.61) | collective-permute-done | bytes 1048608 | tf_op jit(solution)/shard_map/ppermute | solution.py:24
  953.1 19.8 %collective-permute-done.60 = bf16[256,2048]{1,0:T(8,128)(2,1)S(1)} collective-permute-done((bf16[256,2048]{1,0:T(8,128)(2,1)S(1)}, bf16[256,2048]{1,0:T(8,128)(2,1)S(1)}, u32[]{:S(2)}, u32[]{:S(2)}) %collective-permute-start.60) | collective-permute-done | bytes 1048608 | tf_op jit(solution)/shard_map/ppermute | solution.py:24
  979.7 20.7 %convolution_convert_fusion.1 = bf16[4,2048,1024]{2,1,0:T(8,128)(2,1)} fusion(bf16[4,576,2048]{2,1,0:T(8,128)(2,1)} %bitcast.446, bf16[4,576,1024]{2,1,0:T(8,128)(2,1)} %bitcast.456), kind=kOutput, calls=%fused_computation.51 | convolution fusion | flops 9672065024 | bytes 30932992 | tf_op jit(solution)/shard_map/krd,krf->kdf/dot_general | solution.py:406
  1026.2 80.3 %conditional.8 = (bf16[4,2048,1024]{2,1,0:T(8,128)(2,1)}, f32[1024,512]{1,0:T(8,128)}, f32[1024,512]{1,0:T(8,128)}, bf16[1024,512]{1,0:T(8,128)(2,1)}, bf16[1,25...) conditional(s32[]{:T(128)} %bitcast.135, () %tuple.164, ...), branch_computations={%region_19.20_spmd, %region_20.21_spmd} | conditional | flops 9673589760 | bytes 67316080 | solution.py:67
  1036.2 20.9 %convolution_convert_fusion = bf16[4,2048,1024]{2,1,0:T(8,128)(2,1)} fusion(bf16[4,576,2048]{2,1,0:T(8,128)(2,1)} %get-tuple-element.452, bf16[4,576,1024]{2,1,0:T(8,128)(2,1)} %bitcast.455), kind=kOutput, calls=%fused_computation.42 | convolution fusion | flops 9672065024 | bytes 30932992 | tf_op jit(solution)/shard_map/cond/branch_1_fun/krd,krf->kdf/dot_general | solution.py:406
  1068.2 18.3 %branch_1_fun.1 = (f32[1024,512]{1,0:T(8,128)}, f32[1024,512]{1,0:T(8,128)}, bf16[1024,512]{1,0:T(8,128)(2,1)}, f32[1024,1]{1,0:T(8,128)S(1)}, f32[1024,1]{1,0:T...) custom-call(f32[1024,1536]{1,0:T(8,128)} %get-tuple-element.454.q_raw.k_raw, ...), custom_call_target="tpu_custom_call" | custom-call | flops 1000000 | bytes 100000 | tf_op jit(solution)/shard_map/cond/branch_1_fun/pallas_call | solution.py:252
  1086.9 19.3 %collective-permute-done.32 = bf16[256,2048]{1,0:T(8,128)(2,1)} collective-permute-done((bf16[256,2048]{1,0:T(8,128)(2,1)}, bf16[256,2048]{1,0:T(8,128)(2,1)}, u32[]{:S(2)}, u32[]{:S(2)}) %collective-permute-start.32) | collective-permute-done | bytes 1048608 | tf_op jit(solution)/shard_map/cond/branch_1_fun/ppermute | solution.py:24
  1271.6 131.5 %conditional.9 = (f32[256,1536]{1,0:T(8,128)S(1)}, f32[256,1536]{1,0:T(8,128)S(1)}, f32[256,1536]{1,0:T(8,128)S(1)}, f32[256,512]{1,0:T(8,128)S(1)}, f32[256,512...) conditional(s32[]{:T(128)} %bitcast.173, () %tuple.166, ...), branch_computations={%region_23.24_spmd, %region_24.25_spmd} | conditional | flops 3145728 | bytes 53477932 | solution.py:67
  1284.1 37.4 %collective-permute-start.17 = (bf16[256,512]{1,0:T(8,128)(2,1)S(1)}, bf16[256,512]{1,0:T(8,128)(2,1)S(1)}, u32[]{:S(2)}, u32[]{:S(2)}) collective-permute-start(bf16[256,512]{1,0:T(8,128)(2,1)S(1)} %get-tuple-element.1127), channel_id=1, source_target_pairs={{0,8},{8,0},{16,24},{24,16},{1,9},{9,1},{17,25},{25,17},{2,10},{10... | collective-permute-start | bytes 786440 | tf_op jit(solution)/shard_map/cond/branch_1_fun/ppermute | solution.py:24
  1321.8 42.7 %collective-permute-done.18 = bf16[256,512]{1,0:T(8,128)(2,1)S(1)} collective-permute-done((bf16[256,512]{1,0:T(8,128)(2,1)S(1)}, bf16[256,512]{1,0:T(8,128)(2,1)S(1)}, u32[]{:S(2)}, u32[]{:S(2)}) %collective-permute-start.18) | collective-permute-done | bytes 262176 | tf_op jit(solution)/shard_map/cond/branch_1_fun/ppermute | solution.py:24
  1465.6 22.8 %collective-permute-done.90 = bf16[256,1024]{1,0:T(8,128)(2,1)S(1)} collective-permute-done((bf16[256,1024]{1,0:T(8,128)(2,1)S(1)}, bf16[256,1024]{1,0:T(8,128)(2,1)S(1)}, u32[]{:S(2)}, u32[]{:S(2)}) %collective-permute-start.90) | collective-permute-done | bytes 524320 | tf_op jit(solution)/shard_map/ppermute | solution.py:24
  1491.7 19.3 %copy.228 = f32[256,4,3072]{2,1,0:T(4,128)} copy(f32[256,4,3072]{2,0,1:T(8,128)S(1)} %convert_bitcast_fusion) | data formatting | bytes 25165824
  (663 shorter events, 704.9 us)
Async XLA Ops:
  7.2 341.6 %all-gather.5.cloned.1.call-start = ((), (), s32[]{:S(2)}) async-start(), calls=%async_computation.3 | async-start | bytes 18874368 | tf_op jit(solution)/shard_map/all_gather | solution.py:476
  30.8 56.9 %collective-permute-start.3 = (bf16[256,1024]{1,0:T(8,128)(2,1)S(1)}, bf16[256,1024]{1,0:T(8,128)(2,1)}, u32[]{:S(2)}, u32[]{:S(2)}) collective-permute-start(bf16[256,1024]{1,0:T(8,128)(2,1)S(1)} %get-tuple-element.1103), channel_id=1, source_target_pairs={{0,8},{8,0},{16,24},{24,16},{1,9},{9,1},{17,25},{25,17},{2,10},{10... | collective-permute-start | bytes 1572872 | tf_op jit(solution)/shard_map/cond/branch_1_fun/ppermute | solution.py:24
  32.4 88.0 %collective-permute-start.6 = (bf16[256,2048]{1,0:T(8,128)(2,1)S(1)}, bf16[256,2048]{1,0:T(8,128)(2,1)}, u32[]{:S(2)}, u32[]{:S(2)}) collective-permute-start(bf16[256,2048]{1,0:T(8,128)(2,1)S(1)} %get-tuple-element.430), channel_id=1, source_target_pairs={{0,1},{1,0},{2,3},{3,2},{4,5},{5,4},{6,7},{7,6},{8,9},{9,8},{10,11... | collective-permute-start | bytes 3145736 | tf_op jit(solution)/shard_map/cond/branch_1_fun/ppermute | solution.py:24
  32.9 87.4 %collective-permute-start.7 = (bf16[256,2048]{1,0:T(8,128)(2,1)S(1)}, bf16[256,2048]{1,0:T(8,128)(2,1)}, u32[]{:S(2)}, u32[]{:S(2)}) collective-permute-start(bf16[256,2048]{1,0:T(8,128)(2,1)S(1)} %get-tuple-element.430), channel_id=1, source_target_pairs={{0,2},{1,3},{2,0},{3,1},{4,6},{5,7},{6,4},{7,5},{8,10},{9,11},{10,... | collective-permute-start | bytes 3145736 | tf_op jit(solution)/shard_map/cond/branch_1_fun/ppermute | solution.py:24
  33.4 86.9 %collective-permute-start.8 = (bf16[256,2048]{1,0:T(8,128)(2,1)S(1)}, bf16[256,2048]{1,0:T(8,128)(2,1)}, u32[]{:S(2)}, u32[]{:S(2)}) collective-permute-start(bf16[256,2048]{1,0:T(8,128)(2,1)S(1)} %get-tuple-element.430), channel_id=1, source_target_pairs={{0,3},{1,2},{2,1},{3,0},{4,7},{5,6},{6,5},{7,4},{8,11},{9,10},{10,... | collective-permute-start | bytes 3145736 | tf_op jit(solution)/shard_map/cond/branch_1_fun/ppermute | solution.py:24
  35.9 49.2 %collective-permute-start.2 = (bf16[64,2176]{1,0:T(8,128)(2,1)S(1)}, bf16[64,2176]{1,0:T(8,128)(2,1)}, u32[]{:S(2)}, u32[]{:S(2)}) collective-permute-start(bf16[64,2176]{1,0:T(8,128)(2,1)S(1)} %copy-done.64), channel_id=1, source_target_pairs={{0,3},{1,2},{2,1},{3,0},{4,7},{5,6},{6,5},{7,4},{8,11},{9,10},{10,... | collective-permute-start | bytes 835592 | tf_op jit(solution)/shard_map/cond/branch_1_fun/ppermute | solution.py:24
  126.9 407.9 %all-gather.7.cloned.1.call-start = ((), (), s32[]{:S(2)}) async-start(), calls=%async_computation.4 | async-start | bytes 18874368 | tf_op jit(solution)/shard_map/all_gather | solution.py:476
  130.5 59.3 %collective-permute-start.33 = (bf16[256,2176]{1,0:T(8,128)(2,1)S(1)}, bf16[256,2176]{1,0:T(8,128)(2,1)}, u32[]{:S(2)}, u32[]{:S(2)}) collective-permute-start(bf16[256,2176]{1,0:T(8,128)(2,1)S(1)} %bitcast.458), channel_id=1, source_target_pairs={{0,8},{8,0},{16,24},{24,16},{1,9},{9,1},{17,25},{25,17},{2,10},{10... | collective-permute-start | bytes 3342344 | tf_op jit(solution)/shard_map/ppermute | solution.py:24
  142.3 76.2 %collective-permute-start.34 = (bf16[256,2176]{1,0:T(8,128)(2,1)S(1)}, bf16[256,2176]{1,0:T(8,128)(2,1)}, u32[]{:S(2)}, u32[]{:S(2)}) collective-permute-start(bf16[256,2176]{1,0:T(8,128)(2,1)S(1)} %bitcast.459), channel_id=1, source_target_pairs={{0,16},{8,24},{16,0},{24,8},{1,17},{9,25},{17,1},{25,9},{2,18},{10... | collective-permute-start | bytes 3342344 | tf_op jit(solution)/shard_map/ppermute | solution.py:24
  143.5 77.3 %collective-permute-start.35 = (bf16[256,2176]{1,0:T(8,128)(2,1)S(1)}, bf16[256,2176]{1,0:T(8,128)(2,1)}, u32[]{:S(2)}, u32[]{:S(2)}) collective-permute-start(bf16[256,2176]{1,0:T(8,128)(2,1)S(1)} %bitcast.460), channel_id=1, source_target_pairs={{0,24},{8,16},{16,8},{24,0},{1,25},{9,17},{17,9},{25,1},{2,26},{10... | collective-permute-start | bytes 3342344 | tf_op jit(solution)/shard_map/ppermute | solution.py:24
  319.2 282.5 %all-gather.9.cloned.1.call-start = ((), (), s32[]{:S(2)}) async-start(), calls=%async_computation.5 | async-start | bytes 18874368 | tf_op jit(solution)/shard_map/all_gather | solution.py:476
  378.6 49.6 %collective-permute-start.11 = (bf16[256,2048]{1,0:T(8,128)(2,1)}, bf16[256,2048]{1,0:T(8,128)(2,1)S(1)}, u32[]{:S(2)}, u32[]{:S(2)}) collective-permute-start(bf16[256,2048]{1,0:T(8,128)(2,1)} %get-tuple-element.1117), channel_id=1, source_target_pairs={{0,3},{1,2},{2,1},{3,0},{4,7},{5,6},{6,5},{7,4},{8,11},{9,10},{10,... | collective-permute-start | bytes 3145736 | tf_op jit(solution)/shard_map/cond/branch_1_fun/ppermute | solution.py:24
  380.1 69.0 %collective-permute-start.10 = (bf16[256,2048]{1,0:T(8,128)(2,1)}, bf16[256,2048]{1,0:T(8,128)(2,1)S(1)}, u32[]{:S(2)}, u32[]{:S(2)}) collective-permute-start(bf16[256,2048]{1,0:T(8,128)(2,1)} %get-tuple-element.1116), channel_id=1, source_target_pairs={{0,2},{1,3},{2,0},{3,1},{4,6},{5,7},{6,4},{7,5},{8,10},{9,11},{10,... | collective-permute-start | bytes 3145736 | tf_op jit(solution)/shard_map/cond/branch_1_fun/ppermute | solution.py:24
  381.5 79.7 %collective-permute-start.9 = (bf16[256,2048]{1,0:T(8,128)(2,1)}, bf16[256,2048]{1,0:T(8,128)(2,1)}, u32[]{:S(2)}, u32[]{:S(2)}) collective-permute-start(bf16[256,2048]{1,0:T(8,128)(2,1)} %get-tuple-element.1115), channel_id=1, source_target_pairs={{0,1},{1,0},{2,3},{3,2},{4,5},{5,4},{6,7},{7,6},{8,9},{9,8},{10,11... | collective-permute-start | bytes 3145736 | tf_op jit(solution)/shard_map/cond/branch_1_fun/ppermute | solution.py:24
  394.5 72.5 %collective-permute-start.12 = (bf16[256,1024]{1,0:T(8,128)(2,1)S(1)}, bf16[256,1024]{1,0:T(8,128)(2,1)}, u32[]{:S(2)}, u32[]{:S(2)}) collective-permute-start(bf16[256,1024]{1,0:T(8,128)(2,1)S(1)} %get-tuple-element.1113), channel_id=1, source_target_pairs={{0,8},{8,0},{16,24},{24,16},{1,9},{9,1},{17,25},{25,17},{2,10},{10... | collective-permute-start | bytes 1572872 | tf_op jit(solution)/shard_map/cond/branch_1_fun/ppermute | solution.py:24
  396.2 70.8 %collective-permute-start.13 = (bf16[256,1024]{1,0:T(8,128)(2,1)S(1)}, bf16[256,1024]{1,0:T(8,128)(2,1)}, u32[]{:S(2)}, u32[]{:S(2)}) collective-permute-start(bf16[256,1024]{1,0:T(8,128)(2,1)S(1)} %get-tuple-element.1112), channel_id=1, source_target_pairs={{0,16},{8,24},{16,0},{24,8},{1,17},{9,25},{17,1},{25,9},{2,18},{10... | collective-permute-start | bytes 1572872 | tf_op jit(solution)/shard_map/cond/branch_1_fun/ppermute | solution.py:24
  476.4 528.7 %all-gather.11.cloned.1.call-start = ((), (), s32[]{:S(2)}) async-start(), calls=%async_computation.7 | async-start | bytes 10485760 | tf_op jit(solution)/shard_map/all_gather | solution.py:646
  562.3 455.8 %reduce-scatter.4.cloned.1.call-start = ((), (), s32[]{:S(2)}) async-start(), calls=%async_computation.6 | async-start | bytes 18874368 | tf_op jit(solution)/shard_map/reduce_scatter | solution.py:658
  875.6 396.0 %reduce-scatter.6.cloned.1.call-start = ((), (), s32[]{:S(2)}) async-start(), calls=%async_computation.8 | async-start | bytes 18874368 | tf_op jit(solution)/shard_map/reduce_scatter | solution.py:658
  1000.5 437.6 %reduce-scatter.8.cloned.1.call-start = ((), (), s32[]{:S(2)}) async-start(), calls=%async_computation.9 | async-start | bytes 18874368 | tf_op jit(solution)/shard_map/reduce_scatter | solution.py:658
  1026.2 60.7 %collective-permute-start.30 = (bf16[256,2048]{1,0:T(8,128)(2,1)}, bf16[256,2048]{1,0:T(8,128)(2,1)}, u32[]{:S(2)}, u32[]{:S(2)}) collective-permute-start(bf16[256,2048]{1,0:T(8,128)(2,1)} %get-tuple-element.485), channel_id=1, source_target_pairs={{0,1},{1,0},{2,3},{3,2},{4,5},{5,4},{6,7},{7,6},{8,9},{9,8},{10,11... | collective-permute-start | bytes 3145736 | tf_op jit(solution)/shard_map/cond/branch_1_fun/ppermute | solution.py:24
  1027.2 59.8 %collective-permute-start.31 = (bf16[256,2048]{1,0:T(8,128)(2,1)}, bf16[256,2048]{1,0:T(8,128)(2,1)}, u32[]{:S(2)}, u32[]{:S(2)}) collective-permute-start(bf16[256,2048]{1,0:T(8,128)(2,1)} %get-tuple-element.485), channel_id=1, source_target_pairs={{0,2},{1,3},{2,0},{3,1},{4,6},{5,7},{6,4},{7,5},{8,10},{9,11},{10,... | collective-permute-start | bytes 3145736 | tf_op jit(solution)/shard_map/cond/branch_1_fun/ppermute | solution.py:24
  1027.8 78.5 %collective-permute-start.32 = (bf16[256,2048]{1,0:T(8,128)(2,1)}, bf16[256,2048]{1,0:T(8,128)(2,1)}, u32[]{:S(2)}, u32[]{:S(2)}) collective-permute-start(bf16[256,2048]{1,0:T(8,128)(2,1)} %get-tuple-element.485), channel_id=1, source_target_pairs={{0,3},{1,2},{2,1},{3,0},{4,7},{5,6},{6,5},{7,4},{8,11},{9,10},{10,... | collective-permute-start | bytes 3145736 | tf_op jit(solution)/shard_map/cond/branch_1_fun/ppermute | solution.py:24
  1032.2 54.7 %collective-permute-start.28 = (bf16[256,1024]{1,0:T(8,128)(2,1)}, bf16[256,1024]{1,0:T(8,128)(2,1)}, u32[]{:S(2)}, u32[]{:S(2)}) collective-permute-start(bf16[256,1024]{1,0:T(8,128)(2,1)} %get-tuple-element.1109), channel_id=1, source_target_pairs={{0,16},{8,24},{16,0},{24,8},{1,17},{9,25},{17,1},{25,9},{2,18},{10... | collective-permute-start | bytes 1572872 | tf_op jit(solution)/shard_map/cond/branch_1_fun/ppermute | solution.py:24
  1134.7 50.5 %collective-permute-start.55 = (f32[8,128]{1,0:T(8,128)S(1)}, f32[8,128]{1,0:T(8,128)S(1)}, u32[]{:S(2)}, u32[]{:S(2)}) collective-permute-start(f32[8,128]{1,0:T(8,128)S(1)} %broadcast_in_dim.338), channel_id=1, source_target_pairs={{0,4},{4,0},{1,5},{5,1},{2,6},{6,2},{3,7},{7,3},{8,12},{12,8},{9,1... | collective-permute-start | bytes 12296 | tf_op jit(solution)/shard_map/ppermute | solution.py:24
  1187.5 77.2 %collective-permute-start.74 = (bf16[1024,1536]{1,0:T(8,128)(2,1)}, bf16[1024,1536]{1,0:T(8,128)(2,1)}, u32[]{:S(2)}, u32[]{:S(2)}) collective-permute-start(bf16[1024,1536]{1,0:T(8,128)(2,1)} %dynamic-slice_bitcast_fusion.26), channel_id=1, source_target_pairs={{0,4},{4,0},{1,5},{5,1},{2,6},{6,2},{3,7},{7,3},{8,12},{12,8},{9,1... | collective-permute-start | bytes 9437192 | tf_op jit(solution)/shard_map/ppermute | solution.py:24
  1196.8 65.4 %collective-permute-start.75 = (bf16[1024,512]{1,0:T(8,128)(2,1)}, bf16[1024,512]{1,0:T(8,128)(2,1)}, u32[]{:S(2)}, u32[]{:S(2)}) collective-permute-start(bf16[1024,512]{1,0:T(8,128)(2,1)} %dynamic-slice_bitcast_fusion.27), channel_id=1, source_target_pairs={{0,4},{4,0},{1,5},{5,1},{2,6},{6,2},{3,7},{7,3},{8,12},{12,8},{9,1... | collective-permute-start | bytes 3145736 | tf_op jit(solution)/shard_map/ppermute | solution.py:24
  1274.1 94.0 %collective-permute-start.22 = (bf16[256,1536]{1,0:T(8,128)(2,1)S(1)}, bf16[256,1536]{1,0:T(8,128)(2,1)S(1)}, u32[]{:S(2)}, u32[]{:S(2)}) collective-permute-start(bf16[256,1536]{1,0:T(8,128)(2,1)S(1)} %get-tuple-element.1118), channel_id=1, source_target_pairs={{0,24},{8,16},{16,8},{24,0},{1,25},{9,17},{17,9},{25,1},{2,26},{10... | collective-permute-start | bytes 2359304 | tf_op jit(solution)/shard_map/cond/branch_1_fun/ppermute | solution.py:24
  1277.0 93.3 %collective-permute-start.16 = (bf16[256,1536]{1,0:T(8,128)(2,1)S(1)}, bf16[256,1536]{1,0:T(8,128)(2,1)S(1)}, u32[]{:S(2)}, u32[]{:S(2)}) collective-permute-start(bf16[256,1536]{1,0:T(8,128)(2,1)S(1)} %get-tuple-element.1119), channel_id=1, source_target_pairs={{0,16},{8,24},{16,0},{24,8},{1,17},{9,25},{17,1},{25,9},{2,18},{10... | collective-permute-start | bytes 2359304 | tf_op jit(solution)/shard_map/cond/branch_1_fun/ppermute | solution.py:24
  1277.0 93.3 %collective-permute-start.15 = (bf16[256,1536]{1,0:T(8,128)(2,1)S(1)}, bf16[256,1536]{1,0:T(8,128)(2,1)S(1)}, u32[]{:S(2)}, u32[]{:S(2)}) collective-permute-start(bf16[256,1536]{1,0:T(8,128)(2,1)S(1)} %get-tuple-element.1120), channel_id=1, source_target_pairs={{0,8},{8,0},{16,24},{24,16},{1,9},{9,1},{17,25},{25,17},{2,10},{10... | collective-permute-start | bytes 2359304 | tf_op jit(solution)/shard_map/cond/branch_1_fun/ppermute | solution.py:24
  1278.6 85.9 %collective-permute-start.18 = (bf16[256,512]{1,0:T(8,128)(2,1)S(1)}, bf16[256,512]{1,0:T(8,128)(2,1)S(1)}, u32[]{:S(2)}, u32[]{:S(2)}) collective-permute-start(bf16[256,512]{1,0:T(8,128)(2,1)S(1)} %get-tuple-element.1126), channel_id=1, source_target_pairs={{0,16},{8,24},{16,0},{24,8},{1,17},{9,25},{17,1},{25,9},{2,18},{10... | collective-permute-start | bytes 786440 | tf_op jit(solution)/shard_map/cond/branch_1_fun/ppermute | solution.py:24
  1284.1 80.4 %collective-permute-start.17 = (bf16[256,512]{1,0:T(8,128)(2,1)S(1)}, bf16[256,512]{1,0:T(8,128)(2,1)S(1)}, u32[]{:S(2)}, u32[]{:S(2)}) collective-permute-start(bf16[256,512]{1,0:T(8,128)(2,1)S(1)} %get-tuple-element.1127), channel_id=1, source_target_pairs={{0,8},{8,0},{16,24},{24,16},{1,9},{9,1},{17,25},{25,17},{2,10},{10... | collective-permute-start | bytes 786440 | tf_op jit(solution)/shard_map/cond/branch_1_fun/ppermute | solution.py:24
  (157 other events, 2402.2 us)
Sparse Core Ops, SparseCore 0:
  127.0 104.6 all-gather.4
  319.4 144.2 all-gather.6
  476.5 89.8 all-gather.8
  568.1 87.5 all-gather.10
  875.7 117.3 reduce-scatter.3
  1000.6 151.7 reduce-scatter.5
  1156.0 130.2 reduce-scatter.7

commit v8 on v6

--- a/solution.py
+++ b/solution.py
@@ -47,8 +47,16 @@
     return [piece_for(rank)] + [send(piece_for(rank ^ k), axis, k) for k in range(1, size)]
 
 
+def swap(pieces, axis):
+    return lax.all_to_all(pieces, axis, split_axis=0, concat_axis=0, tiled=True)
+
+
+def exchange_by_rank(pieces, axis):
+    return exchange(lambda i: lax.dynamic_index_in_dim(pieces, i, 0, keepdims=False), axis)
+
+
 def exchange_sum(pieces, axis):
-    got = exchange(lambda i: lax.dynamic_index_in_dim(pieces, i, 0, keepdims=False), axis)
+    got = exchange_by_rank(pieces, axis)
     return sum(piece.astype(f32) for piece in got)
 
 
@@ -445,14 +453,12 @@
         rows = in_order(blocks, "z", start)
         return collect(rows, "o").reshape((width // 2,) + rows.shape[2:])
 
-    def sum_rows(grad, *others):
+    def sum_cores(grad):
         count = grad.shape[1]
-        grad = exchange_sum(grad.reshape(CORES, width // 2, count), "c").astype(bf16)
+        grad = exchange_sum(grad.reshape(CORES, width // 2, count), "c")
         if outer > 1:
-            grad = exchange_sum(grad.reshape(outer, planes * part, count), "o").astype(bf16)
-        if others:
-            grad = after(grad, *others)
-        return exchange_sum(grad.reshape(planes, part, count), "z")
+            grad = exchange_sum(grad.astype(bf16).reshape(outer, planes * part, count), "o")
+        return grad
 
     def gather_sum(value):
         for axis in ("z", "s", "c", "o"):
@@ -483,30 +489,43 @@
         axis=1,
     )
 
-    def columns_of(owner):
+    inputs = to_inner(tokens)
+    column_rows, extra_rows = rows_dev * 4 * cols // width, rows_dev * PAD // width
+    extra = jnp.pad(extra.reshape(extra_rows, width), ((0, -extra_rows % 8), (0, 0)))
+
+    def message_to(owner):
         picked = [
             lax.dynamic_slice_in_dim(w_attn, i * width + owner * cols, cols, 1) for i in range(4)
         ]
-        return jnp.concatenate(picked[:3] + [extra] + picked[3:], axis=1)
-
-    mine_blocks = exchange(columns_of, "s")
+        picked = jnp.concatenate(picked, axis=1).reshape(column_rows, width)
+        return jnp.concatenate([inputs, picked, extra], axis=0)
+
+    messages = exchange(message_to, "s")
     gate_blocks = expert_chunk(0)
-    inputs = to_inner(tokens)
-    token_blocks = gather_near(inputs, "s")
+    last = own + column_rows
+    columns = [
+        jnp.concatenate(
+            [
+                message[own:last].reshape(rows_dev, 4 * cols),
+                message[last : last + extra_rows].reshape(rows_dev, PAD),
+            ],
+            axis=1,
+        )
+        for message in messages
+    ]
+    mine = in_order(columns, "s").reshape(part, 4 * cols + PAD)
+    seq_tokens = in_order([message[:own] for message in messages], "s")
+    seq_tokens = seq_tokens.reshape(seq, width).astype(f32)
     inputs = inputs.astype(f32)
-
-    mine = in_order(mine_blocks, "s").reshape(part, 4 * cols + PAD)
-    seq_tokens = in_order(token_blocks, "s", token(mine)).reshape(seq, width)
-    gate_ready = in_order(gate_blocks, "z", token(seq_tokens))
+    gate_ready = in_order(gate_blocks, "z", token(mine))
     w_gate = gather_plane(gate_ready)
-    in_blocks = gather_near(after(mine[:, : 3 * cols + PAD], gate_ready), "z")
-    seq_tokens = seq_tokens.astype(f32)
+    in_blocks = gather_near(after(mine, gate_ready), "z")
     seq_factor = rms_factor(seq_tokens)
     w_in = stack_rows(in_blocks, token(seq_factor))
     w_in_other = send(w_in, "c", 1)
     up_blocks = expert_chunk(1, token(w_in))
 
-    side = whole_of(w_in[:, 3 * cols :], w_in_other[:, 3 * cols :], 0)[:, :6].astype(f32).T
+    side = whole_of(w_in[:, 4 * cols :], w_in_other[:, 4 * cols :], 0)[:, :6].astype(f32).T
     gain_in, gain_mid = side[0], side[1]
     gain_q = lax.dynamic_slice_in_dim(to_outer(side[2]), rank * cols, cols, 0)
     gain_k = lax.dynamic_slice_in_dim(to_outer(side[3]), rank * cols, cols, 0)
@@ -554,8 +573,10 @@
 
     normed_in = (seq_tokens * seq_factor * gain_in).astype(bf16)
     normed_mine, normed_other = halves(normed_in)
-    projected = jnp.dot(normed_mine, w_in, preferred_element_type=f32) + jnp.dot(
-        normed_other, w_in_other, preferred_element_type=f32
+    w_qkv, w_qkv_other = w_in[:, : 3 * cols], w_in_other[:, : 3 * cols]
+    w_out = whole_of(w_in[:, 3 * cols : 4 * cols], w_in_other[:, 3 * cols : 4 * cols], 0)
+    projected = jnp.dot(normed_mine, w_qkv, preferred_element_type=f32) + jnp.dot(
+        normed_other, w_qkv_other, preferred_element_type=f32
     )
     query_raw = projected[:, :cols]
     key_raw = projected[:, cols : 2 * cols]
@@ -572,11 +593,9 @@
     )
     up_ready = in_order(up_blocks, "z", token(projected))
     w_up = gather_plane(up_ready)
-    out_blocks = gather_near(after(mine[:, 3 * cols + PAD :], up_ready), "z")
-    out_rows = stack_rows(out_blocks, token(q_mean))
     cosine, sine = rope_tables(seq)
     shared = [
-        after(q_mean, up_ready, w_gate, out_rows, place),
+        after(q_mean, up_ready, w_gate, place, w_out),
         k_mean,
         gain_q[None],
         gain_k[None],
@@ -586,10 +605,10 @@
         segment[None],
     ]
     attended, query, keyed, valued, log_total = attend(projected, shared, heads)
-    w_out = collect(out_rows, "c").reshape(width, cols)
     down_blocks = expert_chunk(2, token(attended))
     attn_out = dot("tc,dc->td", attended, w_out).astype(bf16)
-    residual = inputs + exchange_sum(attn_out.reshape(seqs, own, width), "s")
+    got = exchange_sum(attn_out.reshape(seqs, own, width), "s")
+    residual = inputs + got
     down_ready = in_order(down_blocks, "z", token(residual))
     residual = after(residual, down_ready)
     w_down = gather_plane(down_ready)
@@ -599,14 +618,15 @@
     blocks = near_planes(normed_mid)
     work = [Experts(i, slots, place, gate_of, blocks[i], expert_weights) for i in range(2)]
     rows_in, activated, *pres = work[0].to_hidden(blocks[0], w_gate, w_up, ())
+    first = work[0].to_tokens(activated, w_down)
     pres = [pres]
-    blocks[1][0] = after(blocks[1][0], pres[0][0])
+    blocks[1][0] = after(blocks[1][0], first[0])
     rows_in, activated, *last = work[1].to_hidden(
         blocks[1], w_gate, w_up, (rows_in, activated)
     )
     pres.append(last)
-    partial = [group.to_tokens(activated, w_down) for group in work]
-    final_out = residual + total(send_back(*partial)[1])
+    second = work[1].to_tokens(activated, w_down)
+    final_out = residual + total(send_back(first, second)[1])
     rows_in, activated = [v.reshape(seqs, -1, v.shape[-1]) for v in (rows_in, activated)]
 
     w_out_all = lax.all_gather(after(w_out, w_up), "s", axis=0)
@@ -623,12 +643,6 @@
         grad = grad.reshape(seqs * width, hidden)
         grad = lax.psum_scatter(grad, ("s", "c", "o"), scatter_dimension=0, tiled=True)
         return grad.reshape(planes, part, hidden)
-
-    def to_owners(grad, start=0):
-        def piece_for(owner):
-            return lax.dynamic_index_in_dim(grad, owner, 0, keepdims=False)
-
-        return exchange(piece_for, "z", start)
 
     blocks = near_planes(grad_out.astype(bf16))
     *grads, first, last = work[0].backward(blocks[0], expert_weights, pres[0], ())
@@ -651,22 +665,21 @@
         lambda i: lax.dynamic_index_in_dim(grad_heads, i, 0, keepdims=False), "s"
     )
     grad_heads = in_order(head_blocks, "s", token(grad_w_gate)).reshape(seq, cols)
-    low_blocks = gather_near(grad_low, "s")
-    grad_attn_out = in_order(low_blocks, "s", token(grad_w_gate)).reshape(seq, width)
-    grad_w_up = dot("krd,krf->kdf", rows_in, after(grad_up, grad_heads, grad_attn_out))
-    grad_w_up = grad_w_up.astype(bf16)
+    grad_w_up = dot("krd,krf->kdf", rows_in, after(grad_up, grad_heads)).astype(bf16)
     up_done = grad_w_up
     grad_w_down, grad_w_gate, grad_w_up = [
         scatter_expert(grad) for grad in (grad_w_down, grad_w_gate, grad_w_up)
     ]
-    down_blocks, gate_blocks = to_owners(grad_w_down), to_owners(grad_w_gate)
-    down_ready = in_order(down_blocks, "z", token(up_done))
-    grad_heads = after(grad_heads, down_ready)
+    low_blocks = gather_near(after(grad_low, grad_heads), "s")
+    down_ready = swap(grad_w_down, "z")
     grad_q, grad_k, grad_v, q_inner, k_inner, gain_q_grad, gain_k_grad = attend_back(
-        projected, shared, query, keyed, valued, grad_heads, log_total, heads
-    )
-    grad_w_out = sum_rows(dot("td,tc->dc", grad_attn_out, attended).astype(bf16))
-    q_inner, k_inner = over_heads(q_inner[:, 0], k_inner[:, 0], up_done)
+        projected, shared, query, keyed, valued, after(grad_heads, up_done), log_total, heads
+    )
+    grad_attn_out = in_order(low_blocks, "s", token(grad_q)).reshape(seq, width)
+    down_ready = after(down_ready, grad_q)
+    q_inner = after(q_inner, down_ready, grad_attn_out)
+    grad_w_out = dot("td,tc->dc", grad_attn_out, attended).astype(bf16)
+    q_inner, k_inner = over_heads(q_inner[:, 0], k_inner[:, 0], grad_w_out)
 
     def norm_grad(grad, raw, mean, inner):
         factor = lax.rsqrt(mean + epsilon)
@@ -680,17 +693,18 @@
         ],
         axis=1,
     )
-    grad_padded = jnp.concatenate([grad_proj, jnp.zeros((seq, PAD), bf16)], axis=1)
 
     def back_half(weight):
-        grad = dot("tc,dc->td", grad_padded, weight).astype(bf16)
+        grad = dot("tc,dc->td", grad_proj, weight).astype(bf16)
         return exchange_sum(grad.reshape(seqs, own, width // 2), "s")
 
-    grad_normed = whole_of(back_half(w_in), back_half(w_in_other), 1)
+    grad_normed = whole_of(back_half(w_qkv), back_half(w_qkv_other), 1)
     grad_w_qkv = dot("td,tc->dc", normed_in, grad_proj).astype(bf16)
-    gate_ready = in_order(gate_blocks, "z", token(grad_w_qkv))
-    grad_w_qkv = sum_rows(grad_w_qkv, gate_ready)
-    up_blocks = to_owners(grad_w_up, token(grad_w_qkv))
+    summed = jnp.concatenate([sum_cores(grad_w_qkv), sum_cores(grad_w_out)], axis=1)
+    summed = summed.astype(bf16).reshape(planes, part, 4 * cols)
+    gate_ready = swap(grad_w_gate, "z")
+    grad_attn = after(exchange_sum(summed, "z"), gate_ready).astype(bf16)
+    up_ready = swap(after(grad_w_up, grad_attn), "z")
     grad_in_norm, gain_in_grad = norm_back(inputs, gain_in, grad_normed)
     grad_tokens = to_outer(grad_resid + grad_in_norm)
 
@@ -704,18 +718,11 @@
     row = (lax.axis_index(("c", "o", "z")) * seqs + rank) * rows_dev
     grad_gains = lax.dynamic_slice_in_dim(gains, row, rows_dev, 1).T
 
-    def own_rows(grad):
-        grad = grad.astype(bf16).reshape(seqs, rows_dev, grad.shape[1])
-        got = exchange(lambda i: lax.dynamic_index_in_dim(grad, i, 0, keepdims=False), "s")
-        return in_order(got, "s").astype(f32)
-
-    qkv_part, out_part = own_rows(grad_w_qkv), own_rows(grad_w_out)
+    got = exchange_by_rank(grad_attn.reshape(seqs, rows_dev, 4 * cols), "s")
+    got = in_order(got, "s").astype(f32)
     grad_attn = jnp.concatenate(
-        [qkv_part[s, :, i * cols : (i + 1) * cols] for i in range(3) for s in range(seqs)]
-        + [out_part[s] for s in range(seqs)],
-        axis=1,
-    )
-    up_ready = in_order(up_blocks, "z")
+        [got[s, :, i * cols : (i + 1) * cols] for i in range(4) for s in range(seqs)], axis=1
+    )
     grad_expert = jnp.concatenate([gate_ready, up_ready, down_ready], axis=2)
     grad_expert = grad_expert.astype(f32).transpose(1, 0, 2)
     return (

time: 1540 us -> 1420 us (0.922)
  starting transfers between devices: 258 us -> 148 us
  local copies, waits for them, and re-layouts: 253 us -> 235 us
    ppermute x96 -> x74, starting transfers between devices: 244 us -> 133 us  [send(): return lax.ppermute(block, axis, [(i, i ^ step) for i in range(size)])]
    all_to_all x0 -> x3, waiting for transfers between devices: none -> 34.9 us  [swap(): return lax.all_to_all(pieces, axis, split_axis=0, concat_axis=0, tiled=True)]
    ppermute x96 -> x74, waiting for transfers between devices: 554 us -> 525 us  [send(): return lax.ppermute(block, axis, [(i, i ^ step) for i in range(size)])]
    dynamic_update_slice x50 -> x31, local copies, waits for them, and re-layouts: 54.6 us -> 41.6 us  [in_order(): lax.dynamic_update_index_in_dim(stacked, block, (rank ^ k) + start, 0)]
    unnamed x208 -> x196, local copies, waits for them, and re-layouts: 56.3 us -> 62.2 us
    another operation x15 -> x10, local copies, waits for them, and re-layouts: 33.4 us -> 28.1 us  [whole(): jax.shard_map(shards, mesh=inner, in_specs=(rows, rows, rows, experts, ro...]
    add x16 -> x20, other arithmetic: 37.5 us -> 38.7 us  [after(): return value + token(*others).astype(value.dtype)]
  transfers between devices with their start and end apart: 103 -> 84, of which waited for: 39 -> 32; matrix products, arithmetic and copies ran while one was open for 28% -> 28% of each run, Pallas kernels for 11% -> 12%
where the time goes in v8:
time: 1420 us; the launch traced here: 1410 us
  waiting for transfers between devices  563 us (40%)
  local copies, waits for them, and re-layouts  235 us (17%)
  Pallas kernels  172 us (12%)
  starting transfers between devices  148 us (10%)
  other arithmetic  117 us (8%)
  matrix products  109 us (8%)
  between operations  62.2 us (4%)
    ppermute x74, waiting for transfers between devices, send(): return lax.ppermute(block, axis, [(i, i ^ step) for i in range(size)])  525 us
    pallas_call x6, Pallas kernels, run(): pl.pallas_call(functools.partial(kernel, self.count, self.slots), grid=(s...  136 us
    ppermute x74, starting transfers between devices, send(): return lax.ppermute(block, axis, [(i, i ^ step) for i in range(size)])  133 us
    dot_general x10, matrix products, dot(): return jnp.einsum(spec, left, right, preferred_element_type=f32)  97.1 us
    unnamed x196, local copies, waits for them, and re-layouts  62.2 us
    dynamic_update_slice x31, local copies, waits for them, and re-layouts, in_order(): lax.dynamic_update_index_in_dim(stacked, block, (rank ^ k) + start, 0)  41.6 us
    add x20, other arithmetic, after(): return value + token(*others).astype(value.dtype)  38.7 us
    all_to_all x3, waiting for transfers between devices, swap(): return lax.all_to_all(pieces, axis, split_axis=0, concat_axis=0, tiled=True)  34.9 us
  transfers between devices with their start and end apart: 84, of which 32 were waited for; matrix products, arithmetic and copies ran while one was open for 28% of the time, Pallas kernels for 12%

profile of v8, /device:TPU:0, one launch (start us, length us, event | category | flops | bytes accessed | tf_op | source)
XLA Modules:
  0.0 1406.1 jit_solution(17853080363097808464)
XLA Ops:
  43.2 14.1 %collective-permute-done = bf16[328,2048]{1,0:T(8,128)(2,1)} collective-permute-done((bf16[328,2048]{1,0:T(8,128)(2,1)}, bf16[328,2048]{1,0:T(8,128)(2,1)}, u32[]{:S(2)}, u32[]{:S(2)}) %collective-permute-start) | collective-permute-done | bytes 1343520 | tf_op jit(solution)/shard_map/ppermute | solution.py:24
  62.3 24.5 %collective-permute-done.1 = bf16[328,2048]{1,0:T(8,128)(2,1)} collective-permute-done((bf16[328,2048]{1,0:T(8,128)(2,1)}, bf16[328,2048]{1,0:T(8,128)(2,1)}, u32[]{:S(2)}, u32[]{:S(2)}) %collective-permute-start.1) | collective-permute-done | bytes 1343520 | tf_op jit(solution)/shard_map/ppermute | solution.py:24
  124.9 38.1 %collective-permute-done.6 = bf16[256,2176]{1,0:T(8,128)(2,1)} collective-permute-done((bf16[256,2176]{1,0:T(8,128)(2,1)S(1)}, bf16[256,2176]{1,0:T(8,128)(2,1)}, u32[]{:S(2)}, u32[]{:S(2)}) %collective-permute-start.6) | collective-permute-done | bytes 1114144 | tf_op jit(solution)/shard_map/ppermute | solution.py:24
  165.5 28.9 %collective-permute-done.7 = bf16[256,2176]{1,0:T(8,128)(2,1)S(1)} collective-permute-done((bf16[256,2176]{1,0:T(8,128)(2,1)S(1)}, bf16[256,2176]{1,0:T(8,128)(2,1)S(1)}, u32[]{:S(2)}, u32[]{:S(2)}) %collective-permute-start.7) | collective-permute-done | bytes 1114144 | tf_op jit(solution)/shard_map/ppermute | solution.py:24
  209.2 19.9 %collective-permute-start.13 = (bf16[256,1024]{1,0:T(8,128)(2,1)}, bf16[256,1024]{1,0:T(8,128)(2,1)}, u32[]{:S(2)}, u32[]{:S(2)}) collective-permute-start(bf16[256,1024]{1,0:T(8,128)(2,1)} %bitcast.418), channel_id=1, source_target_pairs={{0,8},{8,0},{16,24},{24,16},{1,9},{9,1},{17,25},{25,17},{2,10},{10... | collective-permute-start | bytes 1572872 | tf_op jit(solution)/shard_map/ppermute | solution.py:24
  305.0 17.8 %shard_map.145 = (bf16[1024,512]{1,0:T(8,128)(2,1)S(1)}, bf16[1024,512]{1,0:T(8,128)(2,1)S(1)}, bf16[1024,512]{1,0:T(8,128)(2,1)S(1)}, bf16[1024,512]{1,0:T(8,128)(2,1)}, f32[4,1024,1]{2,1,0:T(8,128)}) custom-call(f32[1024,1536]{1,0:T(8,128)} %copy-done.15, f32[1024,1536]{1,0:T(8,128)} %copy-done.15, f32[1024,1536]{1,0:T(8,128)} %copy-done.15, ...), custom_call_target="tpu_custom_call" | custom-call | flops 1000000 | bytes 100000 | tf_op jit(solution)/shard_map/pallas_call | solution.py:233
  346.5 31.4 %collective-permute-done.21 = bf16[256,2048]{1,0:T(8,128)(2,1)} collective-permute-done((bf16[256,2048]{1,0:T(8,128)(2,1)}, bf16[256,2048]{1,0:T(8,128)(2,1)}, u32[]{:S(2)}, u32[]{:S(2)}) %collective-permute-start.21) | collective-permute-done | bytes 1048608 | tf_op jit(solution)/shard_map/ppermute | solution.py:24
  380.5 18.7 %collective-permute-done.20 = bf16[256,2048]{1,0:T(8,128)(2,1)} collective-permute-done((bf16[256,2048]{1,0:T(8,128)(2,1)}, bf16[256,2048]{1,0:T(8,128)(2,1)}, u32[]{:S(2)}, u32[]{:S(2)}) %collective-permute-start.20) | collective-permute-done | bytes 1048608 | tf_op jit(solution)/shard_map/ppermute | solution.py:24
  399.2 13.9 collective-permute-done.19
  436.5 43.9 %collective-permute-done.25.refs_1_ = bf16[256,2048]{1,0:T(8,128)(2,1)S(1)} collective-permute-done((bf16[256,2048]{1,0:T(8,128)(2,1)S(1)}, bf16[256,2048]{1,0:T(8,128)(2,1)S(1)}, u32[]{:S(2)}, u32[]{:S(2)}) %collective-permute-start.25) | collective-permute-done | bytes 1048608 | tf_op jit(solution)/shard_map/ppermute | solution.py:24
  493.8 21.1 %shard_map.146 = (bf16[4,2,288,2048]{3,2,1,0:T(8,128)(2,1)}, bf16[4,2,288,1024]{3,2,1,0:T(8,128)(2,1)}, bf16[4,288,1024]{2,1,0:T(8,128)(2,1)}, bf16[4,288,1024]{2,1,0:T(8,128)(2,1)}) custom-call(s32[4,4,1,256]{3,2,1,0:T(1,128)} %pad_add_fusion.place, bf16[256,2048]{1,0:T(8,128)(2,1)} %copy-done.66, bf16[256,2048]{1,0:T(8,128)(2,1)} %copy-done.80, ...), custom_call_target="tpu_custom_call" | custom-call | flops 9663676416 | bytes 50331648 | tf_op jit(solution)/shard_map/pallas_call | solution.py:368
  517.7 14.8 %shard_map.147 = (bf16[256,2048]{1,0:T(8,128)(2,1)}, bf16[256,2048]{1,0:T(8,128)(2,1)}) custom-call(s32[4,4,1,256]{3,2,1,0:T(1,128)} %pad_add_fusion.place, f32[4,4,1,256]{3,2,1,0:T(1,128)} %pad_maximum_fusion.9.gate, bf16[4,2,288,1024]{3,2,1,0:T(8,128)(2,1)} %get-tuple-element.41.activated.refs_5_, bf16[4,2048,1024]{2,1,0:T(8,128)(2,1)} %bitcast.447), custom_call_target="tpu_custom_call" | custom-call | flops 9663676416 | bytes 50331648 | tf_op jit(solution)/shard_map/pallas_call | solution.py:368
  539.7 20.8 %shard_map.148 = (bf16[4,2,288,2048]{3,2,1,0:T(8,128)(2,1)}, bf16[4,2,288,1024]{3,2,1,0:T(8,128)(2,1)}, bf16[4,288,1024]{2,1,0:T(8,128)(2,1)}, bf16[4,288,1024]{2,1,0:T(8,128)(2,1)}) custom-call(s32[4,4,1,256]{3,2,1,0:T(1,128)} %pad_add_fusion.place, bf16[256,2048]{1,0:T(8,128)(2,1)} %broadcast_add_fusion.15.refs_0_, ...), custom_call_target="tpu_custom_call", output_to_operand_aliasing={{0}: (5, {}), {1}: (6, {})} | custom-call | flops 9663676416 | bytes 50331648 | tf_op jit(solution)/shard_map/pallas_call | solution.py:368
  560.5 15.0 %shard_map.149 = (bf16[256,2048]{1,0:T(8,128)(2,1)}, bf16[256,2048]{1,0:T(8,128)(2,1)}) custom-call(s32[4,4,1,256]{3,2,1,0:T(1,128)} %pad_add_fusion.place, f32[4,4,1,256]{3,2,1,0:T(1,128)} %pad_maximum_fusion.9.gate, bf16[4,2,288,1024]{3,2,1,0:T(8,128)(2,1)} %get-tuple-element.45.activated, bf16[4,2048,1024]{2,1,0:T(8,128)(2,1)} %bitcast.448), custom_call_target="tpu_custom_call" | custom-call | flops 9663676416 | bytes 50331648 | tf_op jit(solution)/shard_map/pallas_call | solution.py:368
  619.5 19.0 %collective-permute-done.29 = bf16[256,2048]{1,0:T(8,128)(2,1)} collective-permute-done((bf16[256,2048]{1,0:T(8,128)(2,1)}, bf16[256,2048]{1,0:T(8,128)(2,1)}, u32[]{:S(2)}, u32[]{:S(2)}) %collective-permute-start.29) | collective-permute-done | bytes 1048608 | tf_op jit(solution)/shard_map/ppermute | solution.py:24
  646.6 47.9 %collective-permute-done.38.refs_1_ = bf16[256,2048]{1,0:T(8,128)(2,1)S(1)} collective-permute-done((bf16[256,2048]{1,0:T(8,128)(2,1)S(1)}, bf16[256,2048]{1,0:T(8,128)(2,1)S(1)}, u32[]{:S(2)}, u32[]{:S(2)}) %collective-permute-start.38) | collective-permute-done | bytes 1048608 | tf_op jit(solution)/shard_map/ppermute | solution.py:24
  698.4 32.0 %shard_map.150 = (bf16[4,2,288,2048]{3,2,1,0:T(8,128)(2,1)}, bf16[4,2,288,1024]{3,2,1,0:T(8,128)(2,1)}, bf16[4,2,288,1024]{3,2,1,0:T(8,128)(2,1)}, bf16[256,2048]{1,0:T(8,128)(2,1)}, bf16[256,2048]{1,0:T(8,128)(2,1)}) custom-call(s32[4,4,1,256]{3,2,1,0:T(1,128)} %pad_add_fusion.place, f32[4,4,1,256]{3,2,1,0:T(1,128)} %pad_maximum_fusion.9.gate, ...), custom_call_target="tpu_custom_call" | custom-call | flops 9663676416 | bytes 50331648 | tf_op jit(solution)/shard_map/pallas_call | solution.py:368
  747.9 32.0 %shard_map.151 = (bf16[4,2,288,2048]{3,2,1,0:T(8,128)(2,1)}, bf16[4,2,288,1024]{3,2,1,0:T(8,128)(2,1)}, bf16[4,2,288,1024]{3,2,1,0:T(8,128)(2,1)}, bf16[256,2048]{1,0:T(8,128)(2,1)}, bf16[256,2048]{1,0:T(8,128)(2,1)}) custom-call(s32[4,4,1,256]{3,2,1,0:T(1,128)} %pad_add_fusion.place, ...), custom_call_target="tpu_custom_call", output_to_operand_aliasing={{0}: (9, {}), {1}: (10, {}), {2}: (11, {})} | custom-call | flops 9663676416 | bytes 50331648 | tf_op jit(solution)/shard_map/pallas_call | solution.py:368
  803.8 20.7 %convolution_convert_fusion.2 = bf16[4,2048,1024]{2,1,0:T(8,128)(2,1)} fusion(bf16[4,576,2048]{2,1,0:T(8,128)(2,1)} %bitcast.457, bf16[4,576,1024]{2,1,0:T(8,128)(2,1)} %bitcast.470), kind=kOutput, calls=%fused_computation.2 | convolution fusion | flops 9672065024 | bytes 30932992 | tf_op jit(solution)/shard_map/krd,krf->kdf/dot_general | solution.py:405
  827.3 13.9 collective-permute-start.42
  854.1 19.9 %collective-permute-done.42 = bf16[256,2048]{1,0:T(8,128)(2,1)S(1)} collective-permute-done((bf16[256,2048]{1,0:T(8,128)(2,1)}, bf16[256,2048]{1,0:T(8,128)(2,1)S(1)}, u32[]{:S(2)}, u32[]{:S(2)}) %collective-permute-start.42) | collective-permute-done | bytes 1048608 | tf_op jit(solution)/shard_map/ppermute | solution.py:24
  884.5 21.0 %convolution_convert_fusion.1 = bf16[4,2048,1024]{2,1,0:T(8,128)(2,1)} fusion(bf16[4,576,2048]{2,1,0:T(8,128)(2,1)} %bitcast.462, bf16[4,576,1024]{2,1,0:T(8,128)(2,1)} %bitcast.471), kind=kOutput, calls=%fused_computation.1 | convolution fusion | flops 9672065024 | bytes 30932992 | tf_op jit(solution)/shard_map/krd,krf->kdf/dot_general | solution.py:405
  928.7 12.0 collective-permute-done.45
  951.7 22.4 %convolution_convert_fusion = bf16[4,2048,1024]{2,1,0:T(8,128)(2,1)} fusion(bf16[4,576,2048]{2,1,0:T(8,128)(2,1)} %bitcast.463, bf16[4,576,1024]{2,1,0:T(8,128)(2,1)} %bitcast.472), kind=kOutput, calls=%fused_computation | convolution fusion | flops 9672065024 | bytes 30932992 | tf_op jit(solution)/shard_map/krd,krf->kdf/dot_general | solution.py:405
  983.9 18.8 %shard_map.152 = (f32[1024,512]{1,0:T(8,128)}, f32[1024,512]{1,0:T(8,128)}, bf16[1024,512]{1,0:T(8,128)(2,1)S(1)}, f32[1024,1]{1,0:T(8,128)S(1)}, f32[1024,1]{1,...) custom-call(f32[1024,1536]{1,0:T(8,128)} %copy-done.15, f32[1024,1536]{1,0:T(8,128)} %copy-done.15, ...), custom_call_target="tpu_custom_call" | custom-call | flops 1000000 | bytes 100000 | tf_op jit(solution)/shard_map/pallas_call | solution.py:251
  1029.2 29.5 %collective-permute-done.47 = bf16[256,2048]{1,0:T(8,128)(2,1)} collective-permute-done((bf16[256,2048]{1,0:T(8,128)(2,1)}, bf16[256,2048]{1,0:T(8,128)(2,1)}, u32[]{:S(2)}, u32[]{:S(2)}) %collective-permute-start.47) | collective-permute-done | bytes 1048608 | tf_op jit(solution)/shard_map/ppermute | solution.py:24
  1063.4 27.4 %collective-permute-done.49 = bf16[256,2048]{1,0:T(8,128)(2,1)S(1)} collective-permute-done((bf16[256,2048]{1,0:T(8,128)(2,1)}, bf16[256,2048]{1,0:T(8,128)(2,1)S(1)}, u32[]{:S(2)}, u32[]{:S(2)}) %collective-permute-start.49) | collective-permute-done | bytes 1048608 | tf_op jit(solution)/shard_map/ppermute | solution.py:24
  1186.9 13.6 collective-permute-done.69
  1200.5 11.9 collective-permute-done.68
  1249.5 61.7 %collective-permute-done.62 = bf16[256,2048]{1,0:T(8,128)(2,1)} collective-permute-done((bf16[256,2048]{1,0:T(8,128)(2,1)}, bf16[256,2048]{1,0:T(8,128)(2,1)}, u32[]{:S(2)}, u32[]{:S(2)}) %collective-permute-start.62) | collective-permute-done | bytes 1048608 | tf_op jit(solution)/shard_map/ppermute | solution.py:24
  1339.9 34.9 %all-to-all-done.2 = bf16[4,256,1024]{2,1,0:T(8,128)(2,1)} async-done(((bf16[4,256,1024]{2,1,0:T(8,128)(2,1)}), bf16[4,256,1024]{2,1,0:T(8,128)(2,1)}, u32[]{:S(2)}, u32[]{:S(2)}) %all-to-all-start.2) | async-done | bytes 2097184 | tf_op jit(solution)/shard_map/all_to_all | solution.py:51
  1378.4 19.3 %copy.174 = f32[256,4,3072]{2,1,0:T(4,128)} copy(f32[256,4,3072]{2,0,1:T(8,128)S(1)} %convert_bitcast_fusion) | data formatting | bytes 25165824
  (598 shorter events, 563.1 us)
Async XLA Ops:
  7.2 293.7 %all-gather.5.cloned.1.call-start = ((), (), s32[]{:S(2)}) async-start(), calls=%async_computation.6 | async-start | bytes 18874368 | tf_op jit(solution)/shard_map/all_gather | solution.py:478
  26.7 60.0 %collective-permute-start.1 = (bf16[328,2048]{1,0:T(8,128)(2,1)}, bf16[328,2048]{1,0:T(8,128)(2,1)}, u32[]{:S(2)}, u32[]{:S(2)}) collective-permute-start(bf16[328,2048]{1,0:T(8,128)(2,1)} %get-tuple-element.150), channel_id=1, source_target_pairs={{0,2},{1,3},{2,0},{3,1},{4,6},{5,7},{6,4},{7,5},{8,10},{9,11},{10,... | collective-permute-start | bytes 4030472 | tf_op jit(solution)/shard_map/ppermute | solution.py:24
  28.2 59.3 %collective-permute-start.2 = (bf16[328,2048]{1,0:T(8,128)(2,1)}, bf16[328,2048]{1,0:T(8,128)(2,1)}, u32[]{:S(2)}, u32[]{:S(2)}) collective-permute-start(bf16[328,2048]{1,0:T(8,128)(2,1)} %get-tuple-element.148), channel_id=1, source_target_pairs={{0,3},{1,2},{2,1},{3,0},{4,7},{5,6},{6,5},{7,4},{8,11},{9,10},{10,... | collective-permute-start | bytes 4030472 | tf_op jit(solution)/shard_map/ppermute | solution.py:24
  37.2 59.8 %collective-permute-start.3 = (bf16[256,1024]{1,0:T(8,128)(2,1)}, bf16[256,1024]{1,0:T(8,128)(2,1)}, u32[]{:S(2)}, u32[]{:S(2)}) collective-permute-start(bf16[256,1024]{1,0:T(8,128)(2,1)} %bitcast.421), channel_id=1, source_target_pairs={{0,8},{8,0},{16,24},{24,16},{1,9},{9,1},{17,25},{25,17},{2,10},{10... | collective-permute-start | bytes 1572872 | tf_op jit(solution)/shard_map/ppermute | solution.py:24
  40.2 58.6 %collective-permute-start.4 = (bf16[256,1024]{1,0:T(8,128)(2,1)}, bf16[256,1024]{1,0:T(8,128)(2,1)}, u32[]{:S(2)}, u32[]{:S(2)}) collective-permute-start(bf16[256,1024]{1,0:T(8,128)(2,1)} %bitcast.420), channel_id=1, source_target_pairs={{0,16},{8,24},{16,0},{24,8},{1,17},{9,25},{17,1},{25,9},{2,18},{10... | collective-permute-start | bytes 1572872 | tf_op jit(solution)/shard_map/ppermute | solution.py:24
  102.6 385.4 %all-gather.7.cloned.1.call-start = ((), (), s32[]{:S(2)}) async-start(), calls=%async_computation.7 | async-start | bytes 18874368 | tf_op jit(solution)/shard_map/all_gather | solution.py:478
  118.2 76.2 %collective-permute-start.7 = (bf16[256,2176]{1,0:T(8,128)(2,1)S(1)}, bf16[256,2176]{1,0:T(8,128)(2,1)S(1)}, u32[]{:S(2)}, u32[]{:S(2)}) collective-permute-start(bf16[256,2176]{1,0:T(8,128)(2,1)S(1)} %broadcast_add_fusion.5), channel_id=1, source_target_pairs={{0,16},{8,24},{16,0},{24,8},{1,17},{9,25},{17,1},{25,9},{2,18},{10... | collective-permute-start | bytes 3342344 | tf_op jit(solution)/shard_map/ppermute | solution.py:24
  120.9 74.6 %collective-permute-start.8 = (bf16[256,2176]{1,0:T(8,128)(2,1)S(1)}, bf16[256,2176]{1,0:T(8,128)(2,1)}, u32[]{:S(2)}, u32[]{:S(2)}) collective-permute-start(bf16[256,2176]{1,0:T(8,128)(2,1)S(1)} %broadcast_add_fusion.5), channel_id=1, source_target_pairs={{0,24},{8,16},{16,8},{24,0},{1,25},{9,17},{17,9},{25,1},{2,26},{10... | collective-permute-start | bytes 3342344 | tf_op jit(solution)/shard_map/ppermute | solution.py:24
  272.2 245.5 %all-gather.9.cloned.1.call-start = ((), (), s32[]{:S(2)}) async-start(), calls=%async_computation.8 | async-start | bytes 18874368 | tf_op jit(solution)/shard_map/all_gather | solution.py:478
  328.3 49.7 %collective-permute-start.21 = (bf16[256,2048]{1,0:T(8,128)(2,1)}, bf16[256,2048]{1,0:T(8,128)(2,1)}, u32[]{:S(2)}, u32[]{:S(2)}) collective-permute-start(bf16[256,2048]{1,0:T(8,128)(2,1)} %get-tuple-element.138), channel_id=1, source_target_pairs={{0,3},{1,2},{2,1},{3,0},{4,7},{5,6},{6,5},{7,4},{8,11},{9,10},{10,... | collective-permute-start | bytes 3145736 | tf_op jit(solution)/shard_map/ppermute | solution.py:24
  329.8 69.4 %collective-permute-start.20 = (bf16[256,2048]{1,0:T(8,128)(2,1)}, bf16[256,2048]{1,0:T(8,128)(2,1)}, u32[]{:S(2)}, u32[]{:S(2)}) collective-permute-start(bf16[256,2048]{1,0:T(8,128)(2,1)} %get-tuple-element.139), channel_id=1, source_target_pairs={{0,2},{1,3},{2,0},{3,1},{4,6},{5,7},{6,4},{7,5},{8,10},{9,11},{10,... | collective-permute-start | bytes 3145736 | tf_op jit(solution)/shard_map/ppermute | solution.py:24
  331.1 82.0 %collective-permute-start.19 = (bf16[256,2048]{1,0:T(8,128)(2,1)}, bf16[256,2048]{1,0:T(8,128)(2,1)}, u32[]{:S(2)}, u32[]{:S(2)}) collective-permute-start(bf16[256,2048]{1,0:T(8,128)(2,1)} %get-tuple-element.137), channel_id=1, source_target_pairs={{0,1},{1,0},{2,3},{3,2},{4,5},{5,4},{6,7},{7,6},{8,9},{9,8},{10,11... | collective-permute-start | bytes 3145736 | tf_op jit(solution)/shard_map/ppermute | solution.py:24
  342.3 79.8 %collective-permute-start.22 = (bf16[256,1024]{1,0:T(8,128)(2,1)}, bf16[256,1024]{1,0:T(8,128)(2,1)}, u32[]{:S(2)}, u32[]{:S(2)}) collective-permute-start(bf16[256,1024]{1,0:T(8,128)(2,1)} %bitcast.415), channel_id=1, source_target_pairs={{0,8},{8,0},{16,24},{24,16},{1,9},{9,1},{17,25},{25,17},{2,10},{10... | collective-permute-start | bytes 1572872 | tf_op jit(solution)/shard_map/ppermute | solution.py:24
  344.2 79.7 %collective-permute-start.23 = (bf16[256,1024]{1,0:T(8,128)(2,1)}, bf16[256,1024]{1,0:T(8,128)(2,1)}, u32[]{:S(2)}, u32[]{:S(2)}) collective-permute-start(bf16[256,1024]{1,0:T(8,128)(2,1)} %bitcast.414), channel_id=1, source_target_pairs={{0,16},{8,24},{16,0},{24,8},{1,17},{9,25},{17,1},{25,9},{2,18},{10... | collective-permute-start | bytes 1572872 | tf_op jit(solution)/shard_map/ppermute | solution.py:24
  427.7 482.9 %all-gather.11.cloned.1.call-start = ((), (), s32[]{:S(2)}) async-start(), calls=%async_computation.9 | async-start | bytes 10485760 | tf_op jit(solution)/shard_map/all_gather | solution.py:632
  484.5 52.9 %collective-permute-start.27 = (bf16[256,2048]{1,0:T(8,128)(2,1)}, bf16[256,2048]{1,0:T(8,128)(2,1)}, u32[]{:S(2)}, u32[]{:S(2)}) collective-permute-start(bf16[256,2048]{1,0:T(8,128)(2,1)} %broadcast_add_fusion.16), channel_id=1, source_target_pairs={{0,8},{8,0},{16,24},{24,16},{1,9},{9,1},{17,25},{25,17},{2,10},{10... | collective-permute-start | bytes 3145736 | tf_op jit(solution)/shard_map/ppermute | solution.py:24
  485.1 54.6 %collective-permute-start.28 = (bf16[256,2048]{1,0:T(8,128)(2,1)}, bf16[256,2048]{1,0:T(8,128)(2,1)}, u32[]{:S(2)}, u32[]{:S(2)}) collective-permute-start(bf16[256,2048]{1,0:T(8,128)(2,1)} %broadcast_add_fusion.16), channel_id=1, source_target_pairs={{0,24},{8,16},{16,8},{24,0},{1,25},{9,17},{17,9},{25,1},{2,26},{10... | collective-permute-start | bytes 3145736 | tf_op jit(solution)/shard_map/ppermute | solution.py:24
  493.7 482.9 %reduce-scatter.4.cloned.1.call-start = ((), (), s32[]{:S(2)}) async-start(), calls=%async_computation.10 | async-start | bytes 18874368 | tf_op jit(solution)/shard_map/reduce_scatter | solution.py:644
  732.9 58.2 %collective-permute-start.39 = (bf16[256,2048]{1,0:T(8,128)(2,1)}, bf16[256,2048]{1,0:T(8,128)(2,1)}, u32[]{:S(2)}, u32[]{:S(2)}) collective-permute-start(bf16[256,2048]{1,0:T(8,128)(2,1)} %get-tuple-element.51), channel_id=1, source_target_pairs={{0,16},{8,24},{16,0},{24,8},{1,17},{9,25},{17,1},{25,9},{2,18},{10... | collective-permute-start | bytes 3145736 | tf_op jit(solution)/shard_map/ppermute | solution.py:24
  824.5 331.0 %reduce-scatter.6.cloned.1.call-start = ((), (), s32[]{:S(2)}) async-start(), calls=%async_computation.11 | async-start | bytes 18874368 | tf_op jit(solution)/shard_map/reduce_scatter | solution.py:644
  905.5 414.0 %reduce-scatter.8.cloned.1.call-start = ((), (), s32[]{:S(2)}) async-start(), calls=%async_computation.12 | async-start | bytes 18874368 | tf_op jit(solution)/shard_map/reduce_scatter | solution.py:644
  976.6 116.4 %all-to-all-start = ((bf16[4,256,1024]{2,1,0:T(8,128)(2,1)}), bf16[4,256,1024]{2,1,0:T(8,128)(2,1)}, u32[]{:S(2)}, u32[]{:S(2)}) async-start(bf16[4,256,1024]{2,1,0:T(8,128)(2,1)} %bitcast.487), calls=%async_computation.1 | async-start | bytes 4194304 | tf_op jit(solution)/shard_map/all_to_all | solution.py:51
  1010.0 51.1 %collective-permute-start.48 = (bf16[256,2048]{1,0:T(8,128)(2,1)}, bf16[256,2048]{1,0:T(8,128)(2,1)}, u32[]{:S(2)}, u32[]{:S(2)}) collective-permute-start(bf16[256,2048]{1,0:T(8,128)(2,1)} %get-tuple-element.109), channel_id=1, source_target_pairs={{0,2},{1,3},{2,0},{3,1},{4,6},{5,7},{6,4},{7,5},{8,10},{9,11},{10,... | collective-permute-start | bytes 3145736 | tf_op jit(solution)/shard_map/ppermute | solution.py:24
  1021.2 69.6 %collective-permute-start.49 = (bf16[256,2048]{1,0:T(8,128)(2,1)}, bf16[256,2048]{1,0:T(8,128)(2,1)S(1)}, u32[]{:S(2)}, u32[]{:S(2)}) collective-permute-start(bf16[256,2048]{1,0:T(8,128)(2,1)} %get-tuple-element.109), channel_id=1, source_target_pairs={{0,3},{1,2},{2,1},{3,0},{4,7},{5,6},{6,5},{7,4},{8,11},{9,10},{10,... | collective-permute-start | bytes 3145736 | tf_op jit(solution)/shard_map/ppermute | solution.py:24
  1028.8 103.2 %collective-permute-start.36 = (f32[8,128]{1,0:T(8,128)S(1)}, f32[8,128]{1,0:T(8,128)S(1)}, u32[]{:S(2)}, u32[]{:S(2)}) collective-permute-start(f32[8,128]{1,0:T(8,128)S(1)} %broadcast_in_dim.215), channel_id=1, source_target_pairs={{0,3},{1,2},{2,1},{3,0},{4,7},{5,6},{6,5},{7,4},{8,11},{9,10},{10,... | collective-permute-start | bytes 12296 | tf_op jit(solution)/shard_map/ppermute | solution.py:24
  1028.9 108.8 %collective-permute-start.35 = (f32[8,128]{1,0:T(8,128)S(1)}, f32[8,128]{1,0:T(8,128)S(1)}, u32[]{:S(2)}, u32[]{:S(2)}) collective-permute-start(f32[8,128]{1,0:T(8,128)S(1)} %broadcast_in_dim.215), channel_id=1, source_target_pairs={{0,2},{1,3},{2,0},{3,1},{4,6},{5,7},{6,4},{7,5},{8,10},{9,11},{10,... | collective-permute-start | bytes 12296 | tf_op jit(solution)/shard_map/ppermute | solution.py:24
  1132.0 80.6 %collective-permute-start.59 = (bf16[1024,1536]{1,0:T(8,128)(2,1)}, bf16[1024,1536]{1,0:T(8,128)(2,1)}, u32[]{:S(2)}, u32[]{:S(2)}) collective-permute-start(bf16[1024,1536]{1,0:T(8,128)(2,1)} %dynamic-slice_bitcast_fusion), channel_id=1, source_target_pairs={{0,4},{4,0},{1,5},{5,1},{2,6},{6,2},{3,7},{7,3},{8,12},{12,8},{9,1... | collective-permute-start | bytes 9437192 | tf_op jit(solution)/shard_map/ppermute | solution.py:24
  1155.6 91.4 %all-to-all-start.1 = ((bf16[4,256,1024]{2,1,0:T(8,128)(2,1)}), bf16[4,256,1024]{2,1,0:T(8,128)(2,1)}, u32[]{:S(2)}, u32[]{:S(2)}) async-start(bf16[4,256,1024]{2,1,0:T(8,128)(2,1)} %bitcast.486), calls=%async_computation.3 | async-start | bytes 4194304 | tf_op jit(solution)/shard_map/all_to_all | solution.py:51
  1161.2 61.4 %collective-permute-start.37 = (f32[8,128]{1,0:T(8,128)S(1)}, f32[8,128]{1,0:T(8,128)S(1)}, u32[]{:S(2)}, u32[]{:S(2)}) collective-permute-start(f32[8,128]{1,0:T(8,128)S(1)} %broadcast_in_dim.216), channel_id=1, source_target_pairs={{0,4},{4,0},{1,5},{5,1},{2,6},{6,2},{3,7},{7,3},{8,12},{12,8},{9,1... | collective-permute-start | bytes 12296 | tf_op jit(solution)/shard_map/ppermute | solution.py:24
  1219.7 91.5 %collective-permute-start.62 = (bf16[256,2048]{1,0:T(8,128)(2,1)}, bf16[256,2048]{1,0:T(8,128)(2,1)}, u32[]{:S(2)}, u32[]{:S(2)}) collective-permute-start(bf16[256,2048]{1,0:T(8,128)(2,1)} %get-tuple-element.135), channel_id=1, source_target_pairs={{0,16},{8,24},{16,0},{24,8},{1,17},{9,25},{17,1},{25,9},{2,18},{10... | collective-permute-start | bytes 3145736 | tf_op jit(solution)/shard_map/ppermute | solution.py:24
  1220.0 91.2 %collective-permute-start.61 = (bf16[256,2048]{1,0:T(8,128)(2,1)}, bf16[256,2048]{1,0:T(8,128)(2,1)}, u32[]{:S(2)}, u32[]{:S(2)}) collective-permute-start(bf16[256,2048]{1,0:T(8,128)(2,1)} %get-tuple-element.134), channel_id=1, source_target_pairs={{0,8},{8,0},{16,24},{24,16},{1,9},{9,1},{17,25},{25,17},{2,10},{10... | collective-permute-start | bytes 3145736 | tf_op jit(solution)/shard_map/ppermute | solution.py:24
  1322.5 52.3 %all-to-all-start.2 = ((bf16[4,256,1024]{2,1,0:T(8,128)(2,1)}), bf16[4,256,1024]{2,1,0:T(8,128)(2,1)}, u32[]{:S(2)}, u32[]{:S(2)}) async-start(bf16[4,256,1024]{2,1,0:T(8,128)(2,1)} %bitcast.193), calls=%async_computation.5 | async-start | bytes 4194304 | tf_op jit(solution)/shard_map/all_to_all | solution.py:51
  (135 other events, 2107.7 us)
Sparse Core Ops, SparseCore 0:
  102.7 90.1 all-gather.4
  272.3 143.2 all-gather.6
  427.8 89.8 all-gather.8
  519.4 87.6 all-gather.10
  824.7 135.1 reduce-scatter.3
  963.3 174.2 reduce-scatter.5
  1141.1 117.2 reduce-scatter.7

commit v9 on v8

--- a/solution.py
+++ b/solution.py
@@ -465,7 +465,7 @@
             value = sum(gather_near(jnp.broadcast_to(value, (8, PAD)), axis))[0, 0]
         return value
 
-    by_expert = w_expert.transpose(1, 0, 2)
+    by_expert = lax.optimization_barrier(w_expert.transpose(1, 0, 2))
 
     def expert_chunk(i, start=0):
         def piece_for(owner):
@@ -489,6 +489,28 @@
         axis=1,
     )
 
+    routed = jnp.stack(
+        gather_near(jnp.concatenate([routes.astype(f32), gate_weights], axis=1), "z")
+    )
+    route_all, gate_all = routed[..., :TOP].astype(jnp.int32), routed[..., TOP:]
+    expert_ids = jnp.arange(seqs) * planes + plane
+    match = route_all[:, :, None, :] == expert_ids[None, None, :, None]
+    used = jnp.any(match, axis=-1)
+    gate_of = jnp.sum(jnp.where(match, gate_all[:, :, None, :], 0.0), axis=-1)
+    before = (jnp.arange(own)[:, None] > jnp.arange(own)[None, :]).astype(bf16)
+    place = dot("tu,buk->btk", before, used.astype(bf16)).astype(jnp.int32)
+    place = jnp.where(used, place, -1)
+    slots = -(-capacity // 16) * 16
+    place = place.transpose(2, 0, 1)[:, :, None, :]
+    gate_of = gate_of.transpose(2, 0, 1)[:, :, None, :]
+
+    groups = [[k for k in range(planes) if k % 2 == odd] for odd in range(2)]
+
+    def by_group(table):
+        return jnp.concatenate([table[:, k : k + 1] for group in groups for k in group], axis=1)
+
+    place, gate_of = by_group(place), by_group(gate_of)
+
     inputs = to_inner(tokens)
     column_rows, extra_rows = rows_dev * 4 * cols // width, rows_dev * PAD // width
     extra = jnp.pad(extra.reshape(extra_rows, width), ((0, -extra_rows % 8), (0, 0)))
@@ -502,6 +524,7 @@
 
     messages = exchange(message_to, "s")
     gate_blocks = expert_chunk(0)
+    up_blocks = expert_chunk(1, token(*gate_blocks))
     last = own + column_rows
     columns = [
         jnp.concatenate(
@@ -519,11 +542,12 @@
     inputs = inputs.astype(f32)
     gate_ready = in_order(gate_blocks, "z", token(mine))
     w_gate = gather_plane(gate_ready)
-    in_blocks = gather_near(after(mine, gate_ready), "z")
+    up_ready = in_order(up_blocks, "z", token(seq_tokens, place, gate_of))
+    w_up = gather_plane(up_ready)
+    in_blocks = gather_near(after(mine, up_ready), "z")
     seq_factor = rms_factor(seq_tokens)
     w_in = stack_rows(in_blocks, token(seq_factor))
     w_in_other = send(w_in, "c", 1)
-    up_blocks = expert_chunk(1, token(w_in))
 
     side = whole_of(w_in[:, 4 * cols :], w_in_other[:, 4 * cols :], 0)[:, :6].astype(f32).T
     gain_in, gain_mid = side[0], side[1]
@@ -531,27 +555,6 @@
     gain_k = lax.dynamic_slice_in_dim(to_outer(side[3]), rank * cols, cols, 0)
     total_count = jnp.sum(side[4, ::rows_dev]) * 128.0 + jnp.sum(side[5, ::rows_dev])
 
-    routed = jnp.stack(
-        gather_near(jnp.concatenate([routes.astype(f32), gate_weights], axis=1), "z")
-    )
-    route_all, gate_all = routed[..., :TOP].astype(jnp.int32), routed[..., TOP:]
-    expert_ids = jnp.arange(seqs) * planes + plane
-    match = route_all[:, :, None, :] == expert_ids[None, None, :, None]
-    used = jnp.any(match, axis=-1)
-    gate_of = jnp.sum(jnp.where(match, gate_all[:, :, None, :], 0.0), axis=-1)
-    before = (jnp.arange(own)[:, None] > jnp.arange(own)[None, :]).astype(bf16)
-    place = dot("tu,buk->btk", before, used.astype(bf16)).astype(jnp.int32)
-    place = jnp.where(used, place, -1)
-    slots = -(-capacity // 16) * 16
-    place = place.transpose(2, 0, 1)[:, :, None, :]
-    gate_of = gate_of.transpose(2, 0, 1)[:, :, None, :]
-
-    groups = [[k for k in range(planes) if k % 2 == odd] for odd in range(2)]
-
-    def by_group(table):
-        return jnp.concatenate([table[:, k : k + 1] for group in groups for k in group], axis=1)
-
-    place, gate_of = by_group(place), by_group(gate_of)
 
     def near_planes(block):
         near = [block] + [None] * (planes - 1)
@@ -591,11 +594,9 @@
     q_mean, k_mean = over_heads(
         jnp.sum(query_raw * query_raw, axis=-1), jnp.sum(key_raw * key_raw, axis=-1)
     )
-    up_ready = in_order(up_blocks, "z", token(projected))
-    w_up = gather_plane(up_ready)
     cosine, sine = rope_tables(seq)
     shared = [
-        after(q_mean, up_ready, w_gate, place, w_out),
+        after(q_mean, w_gate, w_out),
         k_mean,
         gain_q[None],
         gain_k[None],
@@ -713,6 +714,7 @@
         return to_inner(lax.dynamic_update_slice_in_dim(full, local, rank * cols, 0))
 
     gains = jnp.stack([gain_in_grad, gain_mid_grad, widen(gain_q_grad[0]), widen(gain_k_grad[0])])
+    gains = after(gains, grad_attn)
     for axis in ("z", "c", "s", "o"):
         gains = sum(gather_near(gains, axis))
     row = (lax.axis_index(("c", "o", "z")) * seqs + rank) * rows_dev

time: 1420 us -> 1440 us (1.014)
  local copies, waits for them, and re-layouts: 235 us -> 216 us
  waiting for transfers between devices: 563 us -> 582 us
    another operation x10 -> x7, local copies, waits for them, and re-layouts: 28.1 us -> 6.45 us  [whole(): jax.shard_map(shards, mesh=inner, in_specs=(rows, rows, rows, experts, ro...]
    ppermute x74, waiting for transfers between devices: 525 us -> 544 us  [send(): return lax.ppermute(block, axis, [(i, i ^ step) for i in range(size)])]
    ppermute x74, starting transfers between devices: 133 us -> 149 us  [send(): return lax.ppermute(block, axis, [(i, i ^ step) for i in range(size)])]
    unnamed x196 -> x190, local copies, waits for them, and re-layouts: 62.2 us -> 59.7 us
    slice x33 -> x36, local copies, waits for them, and re-layouts: 28.5 us -> 30.8 us  [token(): value[(slice(0, 1),) * value.ndim].reshape(()).astype(f32)]
    add x20 -> x21, other arithmetic: 38.7 us -> 38.4 us  [after(): return value + token(*others).astype(value.dtype)]
    dynamic_update_slice x31 -> x30, local copies, waits for them, and re-layouts: 41.6 us -> 41.7 us  [in_order(): lax.dynamic_update_index_in_dim(stacked, block, (rank ^ k) + start, 0)]
  transfers between devices with their start and end apart: 84 -> 84, of which waited for: 32 -> 36; matrix products, arithmetic and copies ran while one was open for 28% -> 27% of each run, Pallas kernels for 12% -> 12%
where the time goes in v9:
time: 1440 us; the launch traced here: 1430 us
  waiting for transfers between devices  582 us (40%)
  local copies, waits for them, and re-layouts  216 us (15%)
  Pallas kernels  172 us (12%)
  starting transfers between devices  162 us (11%)
  other arithmetic  123 us (9%)
  matrix products  112 us (8%)
  between operations  62.6 us (4%)
    ppermute x74, waiting for transfers between devices, send(): return lax.ppermute(block, axis, [(i, i ^ step) for i in range(size)])  544 us
    ppermute x74, starting transfers between devices, send(): return lax.ppermute(block, axis, [(i, i ^ step) for i in range(size)])  149 us
    pallas_call x6, Pallas kernels, run(): pl.pallas_call(functools.partial(kernel, self.count, self.slots), grid=(s...  135 us
    dot_general x10, matrix products, dot(): return jnp.einsum(spec, left, right, preferred_element_type=f32)  99.8 us
    unnamed x190, local copies, waits for them, and re-layouts  59.7 us
    dynamic_update_slice x30, local copies, waits for them, and re-layouts, in_order(): lax.dynamic_update_index_in_dim(stacked, block, (rank ^ k) + start, 0)  41.7 us
    add x21, other arithmetic, after(): return value + token(*others).astype(value.dtype)  38.4 us
    slice x36, local copies, waits for them, and re-layouts, token(): value[(slice(0, 1),) * value.ndim].reshape(()).astype(f32)  30.8 us
  transfers between devices with their start and end apart: 84, of which 36 were waited for; matrix products, arithmetic and copies ran while one was open for 27% of the time, Pallas kernels for 12%

profile of v9, /device:TPU:0, one launch (start us, length us, event | category | flops | bytes accessed | tf_op | source)
XLA Modules:
  0.0 1429.5 jit_solution(2312033126005133180)
XLA Ops:
  43.6 18.8 %collective-permute-done.3 = bf16[256,1024]{1,0:T(8,128)(2,1)S(1)} collective-permute-done((bf16[256,1024]{1,0:T(8,128)(2,1)S(1)}, bf16[256,1024]{1,0:T(8,128)(2,1)S(1)}, u32[]{:S(2)}, u32[]{:S(2)}) %collective-permute-start.3) | collective-permute-done | bytes 524320 | tf_op jit(solution)/shard_map/ppermute | solution.py:24
  139.7 14.9 %collective-permute-done.10 = bf16[256,1024]{1,0:T(8,128)(2,1)} collective-permute-done((bf16[256,1024]{1,0:T(8,128)(2,1)}, bf16[256,1024]{1,0:T(8,128)(2,1)}, u32[]{:S(2)}, u32[]{:S(2)}) %collective-permute-start.10) | collective-permute-done | bytes 524320 | tf_op jit(solution)/shard_map/ppermute | solution.py:24
  181.4 39.8 %collective-permute-done.12 = bf16[256,2176]{1,0:T(8,128)(2,1)S(1)} collective-permute-done((bf16[256,2176]{1,0:T(8,128)(2,1)S(1)}, bf16[256,2176]{1,0:T(8,128)(2,1)S(1)}, u32[]{:S(2)}, u32[]{:S(2)}) %collective-permute-start.12) | collective-permute-done | bytes 1114144 | tf_op jit(solution)/shard_map/ppermute | solution.py:24
  222.4 29.0 %collective-permute-done.13 = bf16[256,2176]{1,0:T(8,128)(2,1)S(1)} collective-permute-done((bf16[256,2176]{1,0:T(8,128)(2,1)S(1)}, bf16[256,2176]{1,0:T(8,128)(2,1)S(1)}, u32[]{:S(2)}, u32[]{:S(2)}) %collective-permute-start.13) | collective-permute-done | bytes 1114144 | tf_op jit(solution)/shard_map/ppermute | solution.py:24
  294.2 17.6 %shard_map.145 = (bf16[1024,512]{1,0:T(8,128)(2,1)S(1)}, bf16[1024,512]{1,0:T(8,128)(2,1)S(1)}, bf16[1024,512]{1,0:T(8,128)(2,1)S(1)}, bf16[1024,512]{1,0:T(8,128)(2,1)}, f32[4,1024,1]{2,1,0:T(8,128)}) custom-call(f32[1024,1536]{1,0:T(8,128)} %copy-done.15, f32[1024,1536]{1,0:T(8,128)} %copy-done.15, f32[1024,1536]{1,0:T(8,128)} %copy-done.15, ...), custom_call_target="tpu_custom_call" | custom-call | flops 1000000 | bytes 100000 | tf_op jit(solution)/shard_map/pallas_call | solution.py:233
  322.7 22.0 %collective-permute-done.21 = bf16[256,2048]{1,0:T(8,128)(2,1)} collective-permute-done((bf16[256,2048]{1,0:T(8,128)(2,1)}, bf16[256,2048]{1,0:T(8,128)(2,1)}, u32[]{:S(2)}, u32[]{:S(2)}) %collective-permute-start.21) | collective-permute-done | bytes 1048608 | tf_op jit(solution)/shard_map/ppermute | solution.py:24
  344.7 20.7 %collective-permute-done.20 = bf16[256,2048]{1,0:T(8,128)(2,1)} collective-permute-done((bf16[256,2048]{1,0:T(8,128)(2,1)}, bf16[256,2048]{1,0:T(8,128)(2,1)}, u32[]{:S(2)}, u32[]{:S(2)}) %collective-permute-start.20) | collective-permute-done | bytes 1048608 | tf_op jit(solution)/shard_map/ppermute | solution.py:24
  376.5 21.5 %collective-permute-start.22 = (bf16[256,1024]{1,0:T(8,128)(2,1)}, bf16[256,1024]{1,0:T(8,128)(2,1)}, u32[]{:S(2)}, u32[]{:S(2)}) collective-permute-start(bf16[256,1024]{1,0:T(8,128)(2,1)} %get-tuple-element.124), channel_id=1, source_target_pairs={{0,8},{8,0},{16,24},{24,16},{1,9},{9,1},{17,25},{25,17},{2,10},{10... | collective-permute-start | bytes 1572872 | tf_op jit(solution)/shard_map/ppermute | solution.py:24
  400.9 20.3 %collective-permute-done.22 = bf16[256,1024]{1,0:T(8,128)(2,1)} collective-permute-done((bf16[256,1024]{1,0:T(8,128)(2,1)}, bf16[256,1024]{1,0:T(8,128)(2,1)}, u32[]{:S(2)}, u32[]{:S(2)}) %collective-permute-start.22) | collective-permute-done | bytes 524320 | tf_op jit(solution)/shard_map/ppermute | solution.py:24
  423.1 13.4 collective-permute-done.23
  462.2 37.9 %collective-permute-done.25.refs_1_ = bf16[256,2048]{1,0:T(8,128)(2,1)} collective-permute-done((bf16[256,2048]{1,0:T(8,128)(2,1)}, bf16[256,2048]{1,0:T(8,128)(2,1)}, u32[]{:S(2)}, u32[]{:S(2)}) %collective-permute-start.25) | collective-permute-done | bytes 1048608 | tf_op jit(solution)/shard_map/ppermute | solution.py:24
  506.7 20.7 %shard_map.146 = (bf16[4,2,288,2048]{3,2,1,0:T(8,128)(2,1)}, bf16[4,2,288,1024]{3,2,1,0:T(8,128)(2,1)}, bf16[4,288,1024]{2,1,0:T(8,128)(2,1)}, bf16[4,288,1024]{2,1,0:T(8,128)(2,1)}) custom-call(s32[4,4,1,256]{3,2,1,0:T(1,128)} %pad_add_fusion.place, bf16[256,2048]{1,0:T(8,128)(2,1)} %multiply_convert_fusion.3.refs_0_, ...), custom_call_target="tpu_custom_call" | custom-call | flops 9663676416 | bytes 50331648 | tf_op jit(solution)/shard_map/pallas_call | solution.py:368
  536.2 14.8 %shard_map.147 = (bf16[256,2048]{1,0:T(8,128)(2,1)}, bf16[256,2048]{1,0:T(8,128)(2,1)}) custom-call(s32[4,4,1,256]{3,2,1,0:T(1,128)} %pad_add_fusion.place, f32[4,4,1,256]{3,2,1,0:T(1,128)} %pad_maximum_fusion.8.gate, bf16[4,2,288,1024]{3,2,1,0:T(8,128)(2,1)} %get-tuple-element.41.activated.refs_5_, bf16[4,2048,1024]{2,1,0:T(8,128)(2,1)} %bitcast.428), custom_call_target="tpu_custom_call" | custom-call | flops 9663676416 | bytes 50331648 | tf_op jit(solution)/shard_map/pallas_call | solution.py:368
  558.2 20.7 %shard_map.148 = (bf16[4,2,288,2048]{3,2,1,0:T(8,128)(2,1)}, bf16[4,2,288,1024]{3,2,1,0:T(8,128)(2,1)}, bf16[4,288,1024]{2,1,0:T(8,128)(2,1)}, bf16[4,288,1024]{2,1,0:T(8,128)(2,1)}) custom-call(s32[4,4,1,256]{3,2,1,0:T(1,128)} %pad_add_fusion.place, bf16[256,2048]{1,0:T(8,128)(2,1)} %broadcast_add_fusion.15.refs_0_, ...), custom_call_target="tpu_custom_call", output_to_operand_aliasing={{0}: (5, {}), {1}: (6, {})} | custom-call | flops 9663676416 | bytes 50331648 | tf_op jit(solution)/shard_map/pallas_call | solution.py:368
  578.9 14.9 %shard_map.149 = (bf16[256,2048]{1,0:T(8,128)(2,1)}, bf16[256,2048]{1,0:T(8,128)(2,1)}) custom-call(s32[4,4,1,256]{3,2,1,0:T(1,128)} %pad_add_fusion.place, f32[4,4,1,256]{3,2,1,0:T(1,128)} %pad_maximum_fusion.8.gate, bf16[4,2,288,1024]{3,2,1,0:T(8,128)(2,1)} %get-tuple-element.45.activated, bf16[4,2048,1024]{2,1,0:T(8,128)(2,1)} %bitcast.429), custom_call_target="tpu_custom_call" | custom-call | flops 9663676416 | bytes 50331648 | tf_op jit(solution)/shard_map/pallas_call | solution.py:368
  637.8 19.1 %collective-permute-done.29 = bf16[256,2048]{1,0:T(8,128)(2,1)} collective-permute-done((bf16[256,2048]{1,0:T(8,128)(2,1)}, bf16[256,2048]{1,0:T(8,128)(2,1)}, u32[]{:S(2)}, u32[]{:S(2)}) %collective-permute-start.29) | collective-permute-done | bytes 1048608 | tf_op jit(solution)/shard_map/ppermute | solution.py:24
  665.1 47.9 %collective-permute-done.38.refs_1_ = bf16[256,2048]{1,0:T(8,128)(2,1)S(1)} collective-permute-done((bf16[256,2048]{1,0:T(8,128)(2,1)S(1)}, bf16[256,2048]{1,0:T(8,128)(2,1)S(1)}, u32[]{:S(2)}, u32[]{:S(2)}) %collective-permute-start.38) | collective-permute-done | bytes 1048608 | tf_op jit(solution)/shard_map/ppermute | solution.py:24
  716.9 31.9 %shard_map.150 = (bf16[4,2,288,2048]{3,2,1,0:T(8,128)(2,1)}, bf16[4,2,288,1024]{3,2,1,0:T(8,128)(2,1)}, bf16[4,2,288,1024]{3,2,1,0:T(8,128)(2,1)}, bf16[256,2048]{1,0:T(8,128)(2,1)}, bf16[256,2048]{1,0:T(8,128)(2,1)}) custom-call(s32[4,4,1,256]{3,2,1,0:T(1,128)} %pad_add_fusion.place, f32[4,4,1,256]{3,2,1,0:T(1,128)} %pad_maximum_fusion.8.gate, ...), custom_call_target="tpu_custom_call" | custom-call | flops 9663676416 | bytes 50331648 | tf_op jit(solution)/shard_map/pallas_call | solution.py:368
  766.4 32.2 %shard_map.151 = (bf16[4,2,288,2048]{3,2,1,0:T(8,128)(2,1)}, bf16[4,2,288,1024]{3,2,1,0:T(8,128)(2,1)}, bf16[4,2,288,1024]{3,2,1,0:T(8,128)(2,1)}, bf16[256,2048]{1,0:T(8,128)(2,1)}, bf16[256,2048]{1,0:T(8,128)(2,1)}) custom-call(s32[4,4,1,256]{3,2,1,0:T(1,128)} %pad_add_fusion.place, ...), custom_call_target="tpu_custom_call", output_to_operand_aliasing={{0}: (9, {}), {1}: (10, {}), {2}: (11, {})} | custom-call | flops 9663676416 | bytes 50331648 | tf_op jit(solution)/shard_map/pallas_call | solution.py:368
  822.1 20.7 %convolution_convert_fusion.2 = bf16[4,2048,1024]{2,1,0:T(8,128)(2,1)} fusion(bf16[4,576,2048]{2,1,0:T(8,128)(2,1)} %bitcast.442, bf16[4,576,1024]{2,1,0:T(8,128)(2,1)} %bitcast.458), kind=kOutput, calls=%fused_computation.2 | convolution fusion | flops 9672065024 | bytes 30932992 | tf_op jit(solution)/shard_map/krd,krf->kdf/dot_general | solution.py:405
  845.6 14.1 collective-permute-start.42
  872.4 19.9 %collective-permute-done.42 = bf16[256,2048]{1,0:T(8,128)(2,1)S(1)} collective-permute-done((bf16[256,2048]{1,0:T(8,128)(2,1)}, bf16[256,2048]{1,0:T(8,128)(2,1)S(1)}, u32[]{:S(2)}, u32[]{:S(2)}) %collective-permute-start.42) | collective-permute-done | bytes 1048608 | tf_op jit(solution)/shard_map/ppermute | solution.py:24
  902.8 21.0 %convolution_convert_fusion.1 = bf16[4,2048,1024]{2,1,0:T(8,128)(2,1)} fusion(bf16[4,576,2048]{2,1,0:T(8,128)(2,1)} %bitcast.447, bf16[4,576,1024]{2,1,0:T(8,128)(2,1)} %bitcast.459), kind=kOutput, calls=%fused_computation.1 | convolution fusion | flops 9672065024 | bytes 30932992 | tf_op jit(solution)/shard_map/krd,krf->kdf/dot_general | solution.py:405
  969.7 22.3 %convolution_convert_fusion = bf16[4,2048,1024]{2,1,0:T(8,128)(2,1)} fusion(bf16[4,576,2048]{2,1,0:T(8,128)(2,1)} %bitcast.448, bf16[4,576,1024]{2,1,0:T(8,128)(2,1)} %bitcast.460), kind=kOutput, calls=%fused_computation | convolution fusion | flops 9672065024 | bytes 30932992 | tf_op jit(solution)/shard_map/krd,krf->kdf/dot_general | solution.py:405
  997.1 18.9 %shard_map.152 = (f32[1024,512]{1,0:T(8,128)}, f32[1024,512]{1,0:T(8,128)}, bf16[1024,512]{1,0:T(8,128)(2,1)S(1)}, f32[1024,1]{1,0:T(8,128)S(1)}, f32[1024,1]{1,...) custom-call(f32[1024,1536]{1,0:T(8,128)} %copy-done.15, f32[1024,1536]{1,0:T(8,128)} %copy-done.15, ...), custom_call_target="tpu_custom_call" | custom-call | flops 1000000 | bytes 100000 | tf_op jit(solution)/shard_map/pallas_call | solution.py:251
  1032.9 41.0 %collective-permute-done.47 = bf16[256,2048]{1,0:T(8,128)(2,1)} collective-permute-done((bf16[256,2048]{1,0:T(8,128)(2,1)}, bf16[256,2048]{1,0:T(8,128)(2,1)}, u32[]{:S(2)}, u32[]{:S(2)}) %collective-permute-start.47) | collective-permute-done | bytes 1048608 | tf_op jit(solution)/shard_map/ppermute | solution.py:24
  1085.6 23.6 %collective-permute-done.49 = bf16[256,2048]{1,0:T(8,128)(2,1)} collective-permute-done((bf16[256,2048]{1,0:T(8,128)(2,1)}, bf16[256,2048]{1,0:T(8,128)(2,1)}, u32[]{:S(2)}, u32[]{:S(2)}) %collective-permute-start.49) | collective-permute-done | bytes 1048608 | tf_op jit(solution)/shard_map/ppermute | solution.py:24
  1239.2 15.7 %collective-permute-done.58 = bf16[256,1024]{1,0:T(8,128)(2,1)S(1)} collective-permute-done((bf16[256,1024]{1,0:T(8,128)(2,1)S(1)}, bf16[256,1024]{1,0:T(8,128)(2,1)S(1)}, u32[]{:S(2)}, u32[]{:S(2)}) %collective-permute-start.58) | collective-permute-done | bytes 524320 | tf_op jit(solution)/shard_map/ppermute | solution.py:24
  1259.1 14.2 collective-permute-done.56
  1287.6 31.8 %collective-permute-done.62 = bf16[256,2048]{1,0:T(8,128)(2,1)} collective-permute-done((bf16[256,2048]{1,0:T(8,128)(2,1)}, bf16[256,2048]{1,0:T(8,128)(2,1)}, u32[]{:S(2)}, u32[]{:S(2)}) %collective-permute-start.62) | collective-permute-done | bytes 1048608 | tf_op jit(solution)/shard_map/ppermute | solution.py:24
  1369.6 28.6 %all-to-all-done.2 = bf16[4,256,1024]{2,1,0:T(8,128)(2,1)} async-done(((bf16[4,256,1024]{2,1,0:T(8,128)(2,1)}), bf16[4,256,1024]{2,1,0:T(8,128)(2,1)}, u32[]{:S(2)}, u32[]{:S(2)}) %all-to-all-start.2) | async-done | bytes 2097184 | tf_op jit(solution)/shard_map/all_to_all | solution.py:51
  1401.8 19.3 %copy.135 = f32[256,4,3072]{2,1,0:T(4,128)} copy(f32[256,4,3072]{2,0,1:T(8,128)S(1)} %convert_bitcast_fusion) | data formatting | bytes 25165824
  (594 shorter events, 617.5 us)
Async XLA Ops:
  7.2 283.5 %all-gather.5.cloned.1.call-start = ((), (), s32[]{:S(2)}) async-start(), calls=%async_computation.6 | async-start | bytes 18874368 | tf_op jit(solution)/shard_map/all_gather | solution.py:478
  23.8 57.0 %collective-permute-start = (bf16[328,2048]{1,0:T(8,128)(2,1)}, bf16[328,2048]{1,0:T(8,128)(2,1)}, u32[]{:S(2)}, u32[]{:S(2)}) collective-permute-start(bf16[328,2048]{1,0:T(8,128)(2,1)} %get-tuple-element.149), channel_id=1, source_target_pairs={{0,1},{1,0},{2,3},{3,2},{4,5},{5,4},{6,7},{7,6},{8,9},{9,8},{10,11... | collective-permute-start | bytes 4030472 | tf_op jit(solution)/shard_map/ppermute | solution.py:24
  26.8 60.0 %collective-permute-start.1 = (bf16[328,2048]{1,0:T(8,128)(2,1)}, bf16[328,2048]{1,0:T(8,128)(2,1)}, u32[]{:S(2)}, u32[]{:S(2)}) collective-permute-start(bf16[328,2048]{1,0:T(8,128)(2,1)} %get-tuple-element.150), channel_id=1, source_target_pairs={{0,2},{1,3},{2,0},{3,1},{4,6},{5,7},{6,4},{7,5},{8,10},{9,11},{10,... | collective-permute-start | bytes 4030472 | tf_op jit(solution)/shard_map/ppermute | solution.py:24
  28.3 59.3 %collective-permute-start.2 = (bf16[328,2048]{1,0:T(8,128)(2,1)}, bf16[328,2048]{1,0:T(8,128)(2,1)}, u32[]{:S(2)}, u32[]{:S(2)}) collective-permute-start(bf16[328,2048]{1,0:T(8,128)(2,1)} %get-tuple-element.148), channel_id=1, source_target_pairs={{0,3},{1,2},{2,1},{3,0},{4,7},{5,6},{6,5},{7,4},{8,11},{9,10},{10,... | collective-permute-start | bytes 4030472 | tf_op jit(solution)/shard_map/ppermute | solution.py:24
  101.3 355.1 %all-gather.7.cloned.1.call-start = ((), (), s32[]{:S(2)}) async-start(), calls=%async_computation.7 | async-start | bytes 18874368 | tf_op jit(solution)/shard_map/all_gather | solution.py:478
  158.2 378.0 %all-gather.9.cloned.1.call-start = ((), (), s32[]{:S(2)}) async-start(), calls=%async_computation.8 | async-start | bytes 18874368 | tf_op jit(solution)/shard_map/all_gather | solution.py:478
  166.3 54.9 %collective-permute-start.12 = (bf16[256,2176]{1,0:T(8,128)(2,1)S(1)}, bf16[256,2176]{1,0:T(8,128)(2,1)S(1)}, u32[]{:S(2)}, u32[]{:S(2)}) collective-permute-start(bf16[256,2176]{1,0:T(8,128)(2,1)S(1)} %broadcast_add_fusion.5), channel_id=1, source_target_pairs={{0,8},{8,0},{16,24},{24,16},{1,9},{9,1},{17,25},{25,17},{2,10},{10... | collective-permute-start | bytes 3342344 | tf_op jit(solution)/shard_map/ppermute | solution.py:24
  175.3 76.2 %collective-permute-start.13 = (bf16[256,2176]{1,0:T(8,128)(2,1)S(1)}, bf16[256,2176]{1,0:T(8,128)(2,1)S(1)}, u32[]{:S(2)}, u32[]{:S(2)}) collective-permute-start(bf16[256,2176]{1,0:T(8,128)(2,1)S(1)} %broadcast_add_fusion.5), channel_id=1, source_target_pairs={{0,16},{8,24},{16,0},{24,8},{1,17},{9,25},{17,1},{25,9},{2,18},{10... | collective-permute-start | bytes 3342344 | tf_op jit(solution)/shard_map/ppermute | solution.py:24
  175.3 77.2 %collective-permute-start.14 = (bf16[256,2176]{1,0:T(8,128)(2,1)S(1)}, bf16[256,2176]{1,0:T(8,128)(2,1)S(1)}, u32[]{:S(2)}, u32[]{:S(2)}) collective-permute-start(bf16[256,2176]{1,0:T(8,128)(2,1)S(1)} %broadcast_add_fusion.5), channel_id=1, source_target_pairs={{0,24},{8,16},{16,8},{24,0},{1,25},{9,17},{17,9},{25,1},{2,26},{10... | collective-permute-start | bytes 3342344 | tf_op jit(solution)/shard_map/ppermute | solution.py:24
  439.2 489.6 %all-gather.11.cloned.1.call-start = ((), (), s32[]{:S(2)}) async-start(), calls=%async_computation.9 | async-start | bytes 10485760 | tf_op jit(solution)/shard_map/all_gather | solution.py:633
  445.1 55.1 %collective-permute-start.25 = (bf16[256,2048]{1,0:T(8,128)(2,1)}, bf16[256,2048]{1,0:T(8,128)(2,1)}, u32[]{:S(2)}, u32[]{:S(2)}) collective-permute-start(bf16[256,2048]{1,0:T(8,128)(2,1)} %multiply_convert_fusion.3.refs_0_), channel_id=1, source_target_pairs={{0,16},{8,24},{16,0},{24,8},{1,17},{9,25},{17,1},{25,9},{2,18},{10... | collective-permute-start | bytes 3145736 | tf_op jit(solution)/shard_map/ppermute | solution.py:24
  462.2 563.0 %reduce-scatter.4.cloned.1.call-start = ((), (), s32[]{:S(2)}) async-start(), calls=%async_computation.10 | async-start | bytes 18874368 | tf_op jit(solution)/shard_map/reduce_scatter | solution.py:645
  505.5 50.5 %collective-permute-start.27 = (bf16[256,2048]{1,0:T(8,128)(2,1)}, bf16[256,2048]{1,0:T(8,128)(2,1)}, u32[]{:S(2)}, u32[]{:S(2)}) collective-permute-start(bf16[256,2048]{1,0:T(8,128)(2,1)} %broadcast_add_fusion.16), channel_id=1, source_target_pairs={{0,8},{8,0},{16,24},{24,16},{1,9},{9,1},{17,25},{25,17},{2,10},{10... | collective-permute-start | bytes 3145736 | tf_op jit(solution)/shard_map/ppermute | solution.py:24
  505.5 52.7 %collective-permute-start.28 = (bf16[256,2048]{1,0:T(8,128)(2,1)}, bf16[256,2048]{1,0:T(8,128)(2,1)}, u32[]{:S(2)}, u32[]{:S(2)}) collective-permute-start(bf16[256,2048]{1,0:T(8,128)(2,1)} %broadcast_add_fusion.16), channel_id=1, source_target_pairs={{0,24},{8,16},{16,8},{24,0},{1,25},{9,17},{17,9},{25,1},{2,26},{10... | collective-permute-start | bytes 3145736 | tf_op jit(solution)/shard_map/ppermute | solution.py:24
  553.5 49.0 %collective-permute-start.26 = (bf16[256,2048]{1,0:T(8,128)(2,1)}, bf16[256,2048]{1,0:T(8,128)(2,1)S(1)}, u32[]{:S(2)}, u32[]{:S(2)}) collective-permute-start(bf16[256,2048]{1,0:T(8,128)(2,1)} %get-tuple-element.43), channel_id=1, source_target_pairs={{0,16},{8,24},{16,0},{24,8},{1,17},{9,25},{17,1},{25,9},{2,18},{10... | collective-permute-start | bytes 3145736 | tf_op jit(solution)/shard_map/ppermute | solution.py:24
  715.9 49.5 %collective-permute-start.41 = (bf16[256,2048]{1,0:T(8,128)(2,1)}, bf16[256,2048]{1,0:T(8,128)(2,1)S(1)}, u32[]{:S(2)}, u32[]{:S(2)}) collective-permute-start(bf16[256,2048]{1,0:T(8,128)(2,1)} %broadcast_add_fusion.12), channel_id=1, source_target_pairs={{0,24},{8,16},{16,8},{24,0},{1,25},{9,17},{17,9},{25,1},{2,26},{10... | collective-permute-start | bytes 3145736 | tf_op jit(solution)/shard_map/ppermute | solution.py:24
  751.3 58.3 %collective-permute-start.39 = (bf16[256,2048]{1,0:T(8,128)(2,1)}, bf16[256,2048]{1,0:T(8,128)(2,1)}, u32[]{:S(2)}, u32[]{:S(2)}) collective-permute-start(bf16[256,2048]{1,0:T(8,128)(2,1)} %get-tuple-element.51), channel_id=1, source_target_pairs={{0,16},{8,24},{16,0},{24,8},{1,17},{9,25},{17,1},{25,9},{2,18},{10... | collective-permute-start | bytes 3145736 | tf_op jit(solution)/shard_map/ppermute | solution.py:24
  842.8 332.9 %reduce-scatter.6.cloned.1.call-start = ((), (), s32[]{:S(2)}) async-start(), calls=%async_computation.11 | async-start | bytes 18874368 | tf_op jit(solution)/shard_map/reduce_scatter | solution.py:645
  923.8 419.1 %reduce-scatter.8.cloned.1.call-start = ((), (), s32[]{:S(2)}) async-start(), calls=%async_computation.12 | async-start | bytes 18874368 | tf_op jit(solution)/shard_map/reduce_scatter | solution.py:645
  1025.1 48.8 %collective-permute-start.47 = (bf16[256,2048]{1,0:T(8,128)(2,1)}, bf16[256,2048]{1,0:T(8,128)(2,1)}, u32[]{:S(2)}, u32[]{:S(2)}) collective-permute-start(bf16[256,2048]{1,0:T(8,128)(2,1)} %get-tuple-element.109), channel_id=1, source_target_pairs={{0,1},{1,0},{2,3},{3,2},{4,5},{5,4},{6,7},{7,6},{8,9},{9,8},{10,11... | collective-permute-start | bytes 3145736 | tf_op jit(solution)/shard_map/ppermute | solution.py:24
  1025.1 93.6 %all-to-all-start = ((bf16[4,256,1024]{2,1,0:T(8,128)(2,1)}), bf16[4,256,1024]{2,1,0:T(8,128)(2,1)S(1)}, u32[]{:S(2)}, u32[]{:S(2)}) async-start(bf16[4,256,1024]{2,1,0:T(8,128)(2,1)} %bitcast.475), calls=%async_computation.1 | async-start | bytes 4194304 | tf_op jit(solution)/shard_map/all_to_all | solution.py:51
  1029.1 54.2 %collective-permute-start.48 = (bf16[256,2048]{1,0:T(8,128)(2,1)}, bf16[256,2048]{1,0:T(8,128)(2,1)}, u32[]{:S(2)}, u32[]{:S(2)}) collective-permute-start(bf16[256,2048]{1,0:T(8,128)(2,1)} %get-tuple-element.109), channel_id=1, source_target_pairs={{0,2},{1,3},{2,0},{3,1},{4,6},{5,7},{6,4},{7,5},{8,10},{9,11},{10,... | collective-permute-start | bytes 3145736 | tf_op jit(solution)/shard_map/ppermute | solution.py:24
  1029.2 79.9 %collective-permute-start.49 = (bf16[256,2048]{1,0:T(8,128)(2,1)}, bf16[256,2048]{1,0:T(8,128)(2,1)}, u32[]{:S(2)}, u32[]{:S(2)}) collective-permute-start(bf16[256,2048]{1,0:T(8,128)(2,1)} %get-tuple-element.109), channel_id=1, source_target_pairs={{0,3},{1,2},{2,1},{3,0},{4,7},{5,6},{6,5},{7,4},{8,11},{9,10},{10,... | collective-permute-start | bytes 3145736 | tf_op jit(solution)/shard_map/ppermute | solution.py:24
  1148.3 49.0 %collective-permute-start.59 = (bf16[1024,1536]{1,0:T(8,128)(2,1)}, bf16[1024,1536]{1,0:T(8,128)(2,1)}, u32[]{:S(2)}, u32[]{:S(2)}) collective-permute-start(bf16[1024,1536]{1,0:T(8,128)(2,1)} %dynamic-slice_bitcast_fusion), channel_id=1, source_target_pairs={{0,4},{4,0},{1,5},{5,1},{2,6},{6,2},{3,7},{7,3},{8,12},{12,8},{9,1... | collective-permute-start | bytes 9437192 | tf_op jit(solution)/shard_map/ppermute | solution.py:24
  1175.7 109.4 %all-to-all-start.1 = ((bf16[4,256,1024]{2,1,0:T(8,128)(2,1)}), bf16[4,256,1024]{2,1,0:T(8,128)(2,1)}, u32[]{:S(2)}, u32[]{:S(2)}) async-start(bf16[4,256,1024]{2,1,0:T(8,128)(2,1)} %bitcast.474), calls=%async_computation.3 | async-start | bytes 4194304 | tf_op jit(solution)/shard_map/all_to_all | solution.py:51
  1197.3 57.6 %collective-permute-start.58 = (bf16[256,1024]{1,0:T(8,128)(2,1)S(1)}, bf16[256,1024]{1,0:T(8,128)(2,1)S(1)}, u32[]{:S(2)}, u32[]{:S(2)}) collective-permute-start(bf16[256,1024]{1,0:T(8,128)(2,1)S(1)} %get-tuple-element.141), channel_id=1, source_target_pairs={{0,3},{1,2},{2,1},{3,0},{4,7},{5,6},{6,5},{7,4},{8,11},{9,10},{10,... | collective-permute-start | bytes 1572872 | tf_op jit(solution)/shard_map/ppermute | solution.py:24
  1200.7 58.4 %collective-permute-start.57 = (bf16[256,1024]{1,0:T(8,128)(2,1)S(1)}, bf16[256,1024]{1,0:T(8,128)(2,1)}, u32[]{:S(2)}, u32[]{:S(2)}) collective-permute-start(bf16[256,1024]{1,0:T(8,128)(2,1)S(1)} %get-tuple-element.142), channel_id=1, source_target_pairs={{0,2},{1,3},{2,0},{3,1},{4,6},{5,7},{6,4},{7,5},{8,10},{9,11},{10,... | collective-permute-start | bytes 1572872 | tf_op jit(solution)/shard_map/ppermute | solution.py:24
  1214.2 59.0 %collective-permute-start.56 = (bf16[256,1024]{1,0:T(8,128)(2,1)S(1)}, bf16[256,1024]{1,0:T(8,128)(2,1)}, u32[]{:S(2)}, u32[]{:S(2)}) collective-permute-start(bf16[256,1024]{1,0:T(8,128)(2,1)S(1)} %get-tuple-element.140), channel_id=1, source_target_pairs={{0,1},{1,0},{2,3},{3,2},{4,5},{5,4},{6,7},{7,6},{8,9},{9,8},{10,11... | collective-permute-start | bytes 1572872 | tf_op jit(solution)/shard_map/ppermute | solution.py:24
  1225.0 62.6 %collective-permute-start.63 = (bf16[256,2048]{1,0:T(8,128)(2,1)}, bf16[256,2048]{1,0:T(8,128)(2,1)}, u32[]{:S(2)}, u32[]{:S(2)}) collective-permute-start(bf16[256,2048]{1,0:T(8,128)(2,1)} %get-tuple-element.136), channel_id=1, source_target_pairs={{0,24},{8,16},{16,8},{24,0},{1,25},{9,17},{17,9},{25,1},{2,26},{10... | collective-permute-start | bytes 3145736 | tf_op jit(solution)/shard_map/ppermute | solution.py:24
  1236.2 83.2 %collective-permute-start.62 = (bf16[256,2048]{1,0:T(8,128)(2,1)}, bf16[256,2048]{1,0:T(8,128)(2,1)}, u32[]{:S(2)}, u32[]{:S(2)}) collective-permute-start(bf16[256,2048]{1,0:T(8,128)(2,1)} %get-tuple-element.135), channel_id=1, source_target_pairs={{0,16},{8,24},{16,0},{24,8},{1,17},{9,25},{17,1},{25,9},{2,18},{10... | collective-permute-start | bytes 3145736 | tf_op jit(solution)/shard_map/ppermute | solution.py:24
  1254.9 64.5 %collective-permute-start.61 = (bf16[256,2048]{1,0:T(8,128)(2,1)}, bf16[256,2048]{1,0:T(8,128)(2,1)}, u32[]{:S(2)}, u32[]{:S(2)}) collective-permute-start(bf16[256,2048]{1,0:T(8,128)(2,1)} %get-tuple-element.134), channel_id=1, source_target_pairs={{0,8},{8,0},{16,24},{24,16},{1,9},{9,1},{17,25},{25,17},{2,10},{10... | collective-permute-start | bytes 3145736 | tf_op jit(solution)/shard_map/ppermute | solution.py:24
  1345.9 52.3 %all-to-all-start.2 = ((bf16[4,256,1024]{2,1,0:T(8,128)(2,1)}), bf16[4,256,1024]{2,1,0:T(8,128)(2,1)}, u32[]{:S(2)}, u32[]{:S(2)}) async-start(bf16[4,256,1024]{2,1,0:T(8,128)(2,1)} %bitcast.194), calls=%async_computation.5 | async-start | bytes 4194304 | tf_op jit(solution)/shard_map/all_to_all | solution.py:51
  (136 other events, 1908.1 us)
Sparse Core Ops, SparseCore 0:
  101.4 92.9 all-gather.4
  196.8 89.8 all-gather.6
  439.4 96.7 all-gather.8
  537.9 87.5 all-gather.10
  843.0 134.9 reduce-scatter.3
  981.4 157.1 reduce-scatter.5
  1142.1 164.1 reduce-scatter.7

commit v10 on v9

--- a/solution.py
+++ b/solution.py
@@ -548,6 +548,7 @@
     seq_factor = rms_factor(seq_tokens)
     w_in = stack_rows(in_blocks, token(seq_factor))
     w_in_other = send(w_in, "c", 1)
+    down_blocks = expert_chunk(2, token(w_in))
 
     side = whole_of(w_in[:, 4 * cols :], w_in_other[:, 4 * cols :], 0)[:, :6].astype(f32).T
     gain_in, gain_mid = side[0], side[1]
@@ -606,13 +607,11 @@
         segment[None],
     ]
     attended, query, keyed, valued, log_total = attend(projected, shared, heads)
-    down_blocks = expert_chunk(2, token(attended))
-    attn_out = dot("tc,dc->td", attended, w_out).astype(bf16)
+    down_ready = in_order(down_blocks, "z", token(attended))
+    w_down = gather_plane(down_ready)
+    attn_out = dot("tc,dc->td", after(attended, down_ready), w_out).astype(bf16)
     got = exchange_sum(attn_out.reshape(seqs, own, width), "s")
     residual = inputs + got
-    down_ready = in_order(down_blocks, "z", token(residual))
-    residual = after(residual, down_ready)
-    w_down = gather_plane(down_ready)
 
     normed_mid = (residual * rms_factor(residual) * gain_mid).astype(bf16)
     expert_weights = (w_gate, w_up, w_down)
@@ -634,8 +633,6 @@
     valid_f = valid_mask.astype(f32)[:, None]
     difference = final_out - to_inner(teacher).astype(f32)
     squared = jnp.sum(valid_f * difference * difference)
-    squared = gather_sum(squared)
-    loss_value = squared / (total_count * width)
     grad_out = (
         to_inner(cotangent).astype(f32) + 2.0 / (total_count * width) * valid_f * difference
     )
@@ -661,6 +658,8 @@
     grad_resid = grad_out + grad_resid_norm
 
     grad_low = grad_resid.astype(bf16)
+    grad_attn_out = swap(jnp.broadcast_to(grad_low[None], (seqs, own, width)), "s")
+    grad_attn_out = grad_attn_out.reshape(seq, width)
     grad_heads = dot("td,sdc->stc", grad_low, w_out_all).astype(bf16)
     head_blocks = exchange(
         lambda i: lax.dynamic_index_in_dim(grad_heads, i, 0, keepdims=False), "s"
@@ -671,16 +670,12 @@
     grad_w_down, grad_w_gate, grad_w_up = [
         scatter_expert(grad) for grad in (grad_w_down, grad_w_gate, grad_w_up)
     ]
-    low_blocks = gather_near(after(grad_low, grad_heads), "s")
     down_ready = swap(grad_w_down, "z")
     grad_q, grad_k, grad_v, q_inner, k_inner, gain_q_grad, gain_k_grad = attend_back(
         projected, shared, query, keyed, valued, after(grad_heads, up_done), log_total, heads
     )
-    grad_attn_out = in_order(low_blocks, "s", token(grad_q)).reshape(seq, width)
-    down_ready = after(down_ready, grad_q)
-    q_inner = after(q_inner, down_ready, grad_attn_out)
     grad_w_out = dot("td,tc->dc", grad_attn_out, attended).astype(bf16)
-    q_inner, k_inner = over_heads(q_inner[:, 0], k_inner[:, 0], grad_w_out)
+    q_inner, k_inner = over_heads(q_inner[:, 0], k_inner[:, 0])
 
     def norm_grad(grad, raw, mean, inner):
         factor = lax.rsqrt(mean + epsilon)
@@ -699,13 +694,14 @@
         grad = dot("tc,dc->td", grad_proj, weight).astype(bf16)
         return exchange_sum(grad.reshape(seqs, own, width // 2), "s")
 
-    grad_normed = whole_of(back_half(w_qkv), back_half(w_qkv_other), 1)
     grad_w_qkv = dot("td,tc->dc", normed_in, grad_proj).astype(bf16)
     summed = jnp.concatenate([sum_cores(grad_w_qkv), sum_cores(grad_w_out)], axis=1)
     summed = summed.astype(bf16).reshape(planes, part, 4 * cols)
-    gate_ready = swap(grad_w_gate, "z")
-    grad_attn = after(exchange_sum(summed, "z"), gate_ready).astype(bf16)
-    up_ready = swap(after(grad_w_up, grad_attn), "z")
+    gate_ready = swap(after(grad_w_gate, down_ready), "z")
+    grad_proj = after(grad_proj, summed)
+    grad_normed = whole_of(back_half(w_qkv), back_half(w_qkv_other), 1)
+    grad_attn = jnp.sum(swap(summed, "z").astype(f32), axis=0).astype(bf16)
+    up_ready = swap(after(grad_w_up, grad_attn, gate_ready), "z")
     grad_in_norm, gain_in_grad = norm_back(inputs, gain_in, grad_normed)
     grad_tokens = to_outer(grad_resid + grad_in_norm)
 
@@ -715,6 +711,7 @@
 
     gains = jnp.stack([gain_in_grad, gain_mid_grad, widen(gain_q_grad[0]), widen(gain_k_grad[0])])
     gains = after(gains, grad_attn)
+    loss_value = gather_sum(after(squared, grad_attn)) / (total_count * width)
     for axis in ("z", "c", "s", "o"):
         gains = sum(gather_near(gains, axis))
     row = (lax.axis_index(("c", "o", "z")) * seqs + rank) * rows_dev

time: 1440 us -> 1560 us (1.083)
  waiting for transfers between devices: 582 us -> 707 us
    all_to_all x3 -> x5, waiting for transfers between devices: 28.6 us -> 164 us  [swap(): return lax.all_to_all(pieces, axis, split_axis=0, concat_axis=0, tiled=True)]
    ppermute x74 -> x68, waiting for transfers between devices: 544 us -> 474 us  [send(): return lax.ppermute(block, axis, [(i, i ^ step) for i in range(size)])]
    all_gather x3, waiting for transfers between devices: 8.83 us -> 68.5 us  [gather_plane(): chunk = lax.all_gather(chunk, ('s', 'c', 'o'), axis=0, tiled=True)]
    ppermute x74 -> x68, starting transfers between devices: 149 us -> 126 us  [send(): return lax.ppermute(block, axis, [(i, i ^ step) for i in range(size)])]
    unnamed x190 -> x170, local copies, waits for them, and re-layouts: 59.7 us -> 78.4 us
    dynamic_update_slice x30 -> x26, local copies, waits for them, and re-layouts: 41.7 us -> 26.2 us  [in_order(): lax.dynamic_update_index_in_dim(stacked, block, (rank ^ k) + start, 0)]
    add x21 -> x20, other arithmetic: 38.4 us -> 41.2 us  [after(): return value + token(*others).astype(value.dtype)]
  transfers between devices with their start and end apart: 84 -> 80, of which waited for: 36 -> 32; matrix products, arithmetic and copies ran while one was open for 27% -> 25% of each run, Pallas kernels for 12% -> 11%
where the time goes in v10:
time: 1560 us; the launch traced here: 1550 us
  waiting for transfers between devices  707 us (45%)
  local copies, waits for them, and re-layouts  218 us (14%)
  Pallas kernels  172 us (11%)
  starting transfers between devices  151 us (10%)
  other arithmetic  128 us (8%)
  matrix products  109 us (7%)
  between operations  62 us (4%)
    ppermute x68, waiting for transfers between devices, send(): return lax.ppermute(block, axis, [(i, i ^ step) for i in range(size)])  474 us
    all_to_all x5, waiting for transfers between devices, swap(): return lax.all_to_all(pieces, axis, split_axis=0, concat_axis=0, tiled=True)  164 us
    pallas_call x6, Pallas kernels, run(): pl.pallas_call(functools.partial(kernel, self.count, self.slots), grid=(s...  135 us
    ppermute x68, starting transfers between devices, send(): return lax.ppermute(block, axis, [(i, i ^ step) for i in range(size)])  126 us
    dot_general x10, matrix products, dot(): return jnp.einsum(spec, left, right, preferred_element_type=f32)  98.7 us
    unnamed x170, local copies, waits for them, and re-layouts  78.4 us
    all_gather x3, waiting for transfers between devices, gather_plane(): chunk = lax.all_gather(chunk, ('s', 'c', 'o'), axis=0, tiled=True)  68.5 us
    add x20, other arithmetic, after(): return value + token(*others).astype(value.dtype)  41.2 us
  transfers between devices with their start and end apart: 80, of which 32 were waited for; matrix products, arithmetic and copies ran while one was open for 25% of the time, Pallas kernels for 11%

profile of v10, /device:TPU:0, one launch (start us, length us, event | category | flops | bytes accessed | tf_op | source)
XLA Modules:
  0.0 1548.1 jit_solution(1087498314097764694)
XLA Ops:
  56.8 13.9 collective-permute-done.3
  75.6 14.9 collective-permute-done.4
  140.9 18.1 %collective-permute-done.10 = bf16[256,1024]{1,0:T(8,128)(2,1)} collective-permute-done((bf16[256,1024]{1,0:T(8,128)(2,1)}, bf16[256,1024]{1,0:T(8,128)(2,1)}, u32[]{:S(2)}, u32[]{:S(2)}) %collective-permute-start.10) | collective-permute-done | bytes 524320 | tf_op jit(solution)/shard_map/ppermute | solution.py:24
  173.4 39.6 %collective-permute-done.12 = bf16[256,2176]{1,0:T(8,128)(2,1)S(1)} collective-permute-done((bf16[256,2176]{1,0:T(8,128)(2,1)S(1)}, bf16[256,2176]{1,0:T(8,128)(2,1)S(1)}, u32[]{:S(2)}, u32[]{:S(2)}) %collective-permute-start.12) | collective-permute-done | bytes 1114144 | tf_op jit(solution)/shard_map/ppermute | solution.py:24
  213.2 33.4 %collective-permute-done.13 = bf16[256,2176]{1,0:T(8,128)(2,1)S(1)} collective-permute-done((bf16[256,2176]{1,0:T(8,128)(2,1)S(1)}, bf16[256,2176]{1,0:T(8,128)(2,1)S(1)}, u32[]{:S(2)}, u32[]{:S(2)}) %collective-permute-start.13) | collective-permute-done | bytes 1114144 | tf_op jit(solution)/shard_map/ppermute | solution.py:24
  259.9 19.6 %collective-permute-start.19 = (bf16[256,1024]{1,0:T(8,128)(2,1)}, bf16[256,1024]{1,0:T(8,128)(2,1)}, u32[]{:S(2)}, u32[]{:S(2)}) collective-permute-start(bf16[256,1024]{1,0:T(8,128)(2,1)} %get-tuple-element.127), channel_id=1, source_target_pairs={{0,8},{8,0},{16,24},{24,16},{1,9},{9,1},{17,25},{25,17},{2,10},{10... | collective-permute-start | bytes 1572872 | tf_op jit(solution)/shard_map/ppermute | solution.py:24
  308.4 54.4 %all-gather.5.cloned.1.call-done = bf16[8192,1024]{1,0:T(8,128)(2,1)} async-done(((bf16[1024,1024]{1,0:T(8,128)(2,1)}), bf16[8192,1024]{1,0:T(8,128)(2,1)}) %all-gather.5.cloned.1.call-update) | async-done | bytes 16777232 | tf_op jit(solution)/shard_map/all_gather | solution.py:478
  366.4 17.9 %shard_map.145 = (bf16[1024,512]{1,0:T(8,128)(2,1)S(1)}, bf16[1024,512]{1,0:T(8,128)(2,1)S(1)}, bf16[1024,512]{1,0:T(8,128)(2,1)S(1)}, bf16[1024,512]{1,0:T(8,128)(2,1)}, f32[4,1024,1]{2,1,0:T(8,128)}) custom-call(f32[1024,1536]{1,0:T(8,128)} %copy-done.14, f32[1024,1536]{1,0:T(8,128)} %copy-done.14, f32[1024,1536]{1,0:T(8,128)} %copy-done.14, ...), custom_call_target="tpu_custom_call" | custom-call | flops 1000000 | bytes 100000 | tf_op jit(solution)/shard_map/pallas_call | solution.py:233
  407.7 45.7 %collective-permute-done.24 = bf16[256,2048]{1,0:T(8,128)(2,1)S(1)} collective-permute-done((bf16[256,2048]{1,0:T(8,128)(2,1)S(1)}, bf16[256,2048]{1,0:T(8,128)(2,1)S(1)}, u32[]{:S(2)}, u32[]{:S(2)}) %collective-permute-start.24) | collective-permute-done | bytes 1048608 | tf_op jit(solution)/shard_map/ppermute | solution.py:24
  453.5 22.0 %collective-permute-done.23 = bf16[256,2048]{1,0:T(8,128)(2,1)S(1)} collective-permute-done((bf16[256,2048]{1,0:T(8,128)(2,1)S(1)}, bf16[256,2048]{1,0:T(8,128)(2,1)S(1)}, u32[]{:S(2)}, u32[]{:S(2)}) %collective-permute-start.23) | collective-permute-done | bytes 1048608 | tf_op jit(solution)/shard_map/ppermute | solution.py:24
  475.5 21.7 %collective-permute-done.22 = bf16[256,2048]{1,0:T(8,128)(2,1)S(1)} collective-permute-done((bf16[256,2048]{1,0:T(8,128)(2,1)S(1)}, bf16[256,2048]{1,0:T(8,128)(2,1)S(1)}, u32[]{:S(2)}, u32[]{:S(2)}) %collective-permute-start.22) | collective-permute-done | bytes 1048608 | tf_op jit(solution)/shard_map/ppermute | solution.py:24
  510.1 38.6 %collective-permute-done.25.refs_1_ = bf16[256,2048]{1,0:T(8,128)(2,1)} collective-permute-done((bf16[256,2048]{1,0:T(8,128)(2,1)}, bf16[256,2048]{1,0:T(8,128)(2,1)}, u32[]{:S(2)}, u32[]{:S(2)}) %collective-permute-start.25) | collective-permute-done | bytes 1048608 | tf_op jit(solution)/shard_map/ppermute | solution.py:24
  557.4 21.0 %shard_map.146 = (bf16[4,2,288,2048]{3,2,1,0:T(8,128)(2,1)}, bf16[4,2,288,1024]{3,2,1,0:T(8,128)(2,1)}, bf16[4,288,1024]{2,1,0:T(8,128)(2,1)}, bf16[4,288,1024]{2,1,0:T(8,128)(2,1)}) custom-call(s32[4,4,1,256]{3,2,1,0:T(1,128)} %pad_add_fusion.place, bf16[256,2048]{1,0:T(8,128)(2,1)} %multiply_convert_fusion.3.refs_0_, ...), custom_call_target="tpu_custom_call" | custom-call | flops 9663676416 | bytes 50331648 | tf_op jit(solution)/shard_map/pallas_call | solution.py:368
  578.4 14.1 all-gather.9.cloned.1.call-done
  592.5 14.8 shard_map.147
  614.6 20.6 %shard_map.148 = (bf16[4,2,288,2048]{3,2,1,0:T(8,128)(2,1)}, bf16[4,2,288,1024]{3,2,1,0:T(8,128)(2,1)}, bf16[4,288,1024]{2,1,0:T(8,128)(2,1)}, bf16[4,288,1024]{2,1,0:T(8,128)(2,1)}) custom-call(s32[4,4,1,256]{3,2,1,0:T(1,128)} %pad_add_fusion.place, bf16[256,2048]{1,0:T(8,128)(2,1)} %broadcast_add_fusion.14.refs_0_, ...), custom_call_target="tpu_custom_call", output_to_operand_aliasing={{0}: (5, {}), {1}: (6, {})} | custom-call | flops 9663676416 | bytes 50331648 | tf_op jit(solution)/shard_map/pallas_call | solution.py:368
  635.2 15.0 shard_map.149
  694.2 19.1 %collective-permute-done.29 = bf16[256,2048]{1,0:T(8,128)(2,1)} collective-permute-done((bf16[256,2048]{1,0:T(8,128)(2,1)}, bf16[256,2048]{1,0:T(8,128)(2,1)}, u32[]{:S(2)}, u32[]{:S(2)}) %collective-permute-start.29) | collective-permute-done | bytes 1048608 | tf_op jit(solution)/shard_map/ppermute | solution.py:24
  721.3 47.9 %collective-permute-done.31.refs_1_ = bf16[256,2048]{1,0:T(8,128)(2,1)S(1)} collective-permute-done((bf16[256,2048]{1,0:T(8,128)(2,1)S(1)}, bf16[256,2048]{1,0:T(8,128)(2,1)S(1)}, u32[]{:S(2)}, u32[]{:S(2)}) %collective-permute-start.31) | collective-permute-done | bytes 1048608 | tf_op jit(solution)/shard_map/ppermute | solution.py:24
  773.1 31.8 %shard_map.150 = (bf16[4,2,288,2048]{3,2,1,0:T(8,128)(2,1)}, bf16[4,2,288,1024]{3,2,1,0:T(8,128)(2,1)}, bf16[4,2,288,1024]{3,2,1,0:T(8,128)(2,1)}, bf16[256,2048]{1,0:T(8,128)(2,1)}, bf16[256,2048]{1,0:T(8,128)(2,1)}) custom-call(s32[4,4,1,256]{3,2,1,0:T(1,128)} %pad_add_fusion.place, f32[4,4,1,256]{3,2,1,0:T(1,128)} %pad_maximum_fusion.9.gate, ...), custom_call_target="tpu_custom_call" | custom-call | flops 9663676416 | bytes 50331648 | tf_op jit(solution)/shard_map/pallas_call | solution.py:368
  822.5 32.2 %shard_map.151 = (bf16[4,2,288,2048]{3,2,1,0:T(8,128)(2,1)}, bf16[4,2,288,1024]{3,2,1,0:T(8,128)(2,1)}, bf16[4,2,288,1024]{3,2,1,0:T(8,128)(2,1)}, bf16[256,2048]{1,0:T(8,128)(2,1)}, bf16[256,2048]{1,0:T(8,128)(2,1)}) custom-call(s32[4,4,1,256]{3,2,1,0:T(1,128)} %pad_add_fusion.place, ...), custom_call_target="tpu_custom_call", output_to_operand_aliasing={{0}: (9, {}), {1}: (10, {}), {2}: (11, {})} | custom-call | flops 9663676416 | bytes 50331648 | tf_op jit(solution)/shard_map/pallas_call | solution.py:368
  878.4 20.7 %convolution_convert_fusion.2 = bf16[4,2048,1024]{2,1,0:T(8,128)(2,1)} fusion(bf16[4,576,2048]{2,1,0:T(8,128)(2,1)} %bitcast.420, bf16[4,576,1024]{2,1,0:T(8,128)(2,1)} %bitcast.443), kind=kOutput, calls=%fused_computation.2 | convolution fusion | flops 9672065024 | bytes 30932992 | tf_op jit(solution)/shard_map/krd,krf->kdf/dot_general | solution.py:405
  901.9 14.1 collective-permute-start.35
  928.6 19.9 %collective-permute-done.35 = bf16[256,2048]{1,0:T(8,128)(2,1)S(1)} collective-permute-done((bf16[256,2048]{1,0:T(8,128)(2,1)}, bf16[256,2048]{1,0:T(8,128)(2,1)S(1)}, u32[]{:S(2)}, u32[]{:S(2)}) %collective-permute-start.35) | collective-permute-done | bytes 1048608 | tf_op jit(solution)/shard_map/ppermute | solution.py:24
  958.9 21.0 %convolution_convert_fusion.1 = bf16[4,2048,1024]{2,1,0:T(8,128)(2,1)} fusion(bf16[4,576,2048]{2,1,0:T(8,128)(2,1)} %bitcast.423, bf16[4,576,1024]{2,1,0:T(8,128)(2,1)} %bitcast.444), kind=kOutput, calls=%fused_computation.1 | convolution fusion | flops 9672065024 | bytes 30932992 | tf_op jit(solution)/shard_map/krd,krf->kdf/dot_general | solution.py:405
  1025.9 22.3 %convolution_convert_fusion = bf16[4,2048,1024]{2,1,0:T(8,128)(2,1)} fusion(bf16[4,576,2048]{2,1,0:T(8,128)(2,1)} %bitcast.424, bf16[4,576,1024]{2,1,0:T(8,128)(2,1)} %bitcast.445), kind=kOutput, calls=%fused_computation | convolution fusion | flops 9672065024 | bytes 30932992 | tf_op jit(solution)/shard_map/krd,krf->kdf/dot_general | solution.py:405
  1053.4 18.8 %shard_map.152 = (f32[1024,512]{1,0:T(8,128)}, f32[1024,512]{1,0:T(8,128)}, bf16[1024,512]{1,0:T(8,128)(2,1)S(1)}, f32[1024,1]{1,0:T(8,128)S(1)}, f32[1024,1]{1,...) custom-call(f32[1024,1536]{1,0:T(8,128)} %copy-done.14, f32[1024,1536]{1,0:T(8,128)} %copy-done.14, ...), custom_call_target="tpu_custom_call" | custom-call | flops 1000000 | bytes 100000 | tf_op jit(solution)/shard_map/pallas_call | solution.py:251
  1104.5 60.2 %all-to-all-done = bf16[4,256,2048]{2,1,0:T(8,128)(2,1)} async-done(((bf16[4,256,2048]{2,1,0:T(8,128)(2,1)}), bf16[4,256,2048]{2,1,0:T(8,128)(2,1)}, u32[]{:S(2)}, u32[]{:S(2)}) %all-to-all-start) | async-done | bytes 4194336 | tf_op jit(solution)/shard_map/all_to_all | solution.py:51
  1200.2 78.8 %all-to-all-done.1 = bf16[4,256,2048]{2,1,0:T(8,128)(2,1)} async-done(((bf16[4,256,2048]{2,1,0:T(8,128)(2,1)}), bf16[4,256,2048]{2,1,0:T(8,128)(2,1)}, u32[]{:S(2)}, u32[]{:S(2)}) %all-to-all-start.1) | async-done | bytes 4194336 | tf_op jit(solution)/shard_map/all_to_all | solution.py:51
  1394.2 31.0 %collective-permute-done.63 = f32[4,2048]{1,0:T(4,128)S(1)} collective-permute-done((f32[4,2048]{1,0:T(4,128)S(1)}, f32[4,2048]{1,0:T(4,128)S(1)}, u32[]{:S(2)}, u32[]{:S(2)}) %collective-permute-start.63) | collective-permute-done | bytes 32800 | tf_op jit(solution)/shard_map/ppermute | solution.py:24
  1491.4 25.3 %all-to-all-done.4 = bf16[4,256,1024]{2,1,0:T(8,128)(2,1)} async-done(((bf16[4,256,1024]{2,1,0:T(8,128)(2,1)}), bf16[4,256,1024]{2,1,0:T(8,128)(2,1)}, u32[]{:S(2)}, u32[]{:S(2)}) %all-to-all-start.4) | async-done | bytes 2097184 | tf_op jit(solution)/shard_map/all_to_all | solution.py:51
  1520.3 19.3 %copy.135 = f32[256,4,3072]{2,1,0:T(4,128)} copy(f32[256,4,3072]{2,0,1:T(8,128)S(1)} %convert_bitcast_fusion) | data formatting | bytes 25165824
  (559 shorter events, 598.6 us)
Async XLA Ops:
  7.2 355.7 %all-gather.5.cloned.1.call-start = ((), (), s32[]{:S(2)}) async-start(), calls=%async_computation.8 | async-start | bytes 18874368 | tf_op jit(solution)/shard_map/all_gather | solution.py:478
  30.8 63.7 %collective-permute-start = (bf16[328,2048]{1,0:T(8,128)(2,1)}, bf16[328,2048]{1,0:T(8,128)(2,1)}, u32[]{:S(2)}, u32[]{:S(2)}) collective-permute-start(bf16[328,2048]{1,0:T(8,128)(2,1)} %get-tuple-element.148), channel_id=1, source_target_pairs={{0,1},{1,0},{2,3},{3,2},{4,5},{5,4},{6,7},{7,6},{8,9},{9,8},{10,11... | collective-permute-start | bytes 4030472 | tf_op jit(solution)/shard_map/ppermute | solution.py:24
  32.5 64.4 %collective-permute-start.1 = (bf16[328,2048]{1,0:T(8,128)(2,1)}, bf16[328,2048]{1,0:T(8,128)(2,1)}, u32[]{:S(2)}, u32[]{:S(2)}) collective-permute-start(bf16[328,2048]{1,0:T(8,128)(2,1)} %get-tuple-element.149), channel_id=1, source_target_pairs={{0,2},{1,3},{2,0},{3,1},{4,6},{5,7},{6,4},{7,5},{8,10},{9,11},{10,... | collective-permute-start | bytes 4030472 | tf_op jit(solution)/shard_map/ppermute | solution.py:24
  163.2 49.8 %collective-permute-start.12 = (bf16[256,2176]{1,0:T(8,128)(2,1)S(1)}, bf16[256,2176]{1,0:T(8,128)(2,1)S(1)}, u32[]{:S(2)}, u32[]{:S(2)}) collective-permute-start(bf16[256,2176]{1,0:T(8,128)(2,1)S(1)} %broadcast_add_fusion.5), channel_id=1, source_target_pairs={{0,8},{8,0},{16,24},{24,16},{1,9},{9,1},{17,25},{25,17},{2,10},{10... | collective-permute-start | bytes 3342344 | tf_op jit(solution)/shard_map/ppermute | solution.py:24
  170.4 76.2 %collective-permute-start.13 = (bf16[256,2176]{1,0:T(8,128)(2,1)S(1)}, bf16[256,2176]{1,0:T(8,128)(2,1)S(1)}, u32[]{:S(2)}, u32[]{:S(2)}) collective-permute-start(bf16[256,2176]{1,0:T(8,128)(2,1)S(1)} %broadcast_add_fusion.5), channel_id=1, source_target_pairs={{0,16},{8,24},{16,0},{24,8},{1,17},{9,25},{17,1},{25,9},{2,18},{10... | collective-permute-start | bytes 3342344 | tf_op jit(solution)/shard_map/ppermute | solution.py:24
  171.4 75.3 %collective-permute-start.14 = (bf16[256,2176]{1,0:T(8,128)(2,1)S(1)}, bf16[256,2176]{1,0:T(8,128)(2,1)S(1)}, u32[]{:S(2)}, u32[]{:S(2)}) collective-permute-start(bf16[256,2176]{1,0:T(8,128)(2,1)S(1)} %broadcast_add_fusion.5), channel_id=1, source_target_pairs={{0,24},{8,16},{16,8},{24,0},{1,25},{9,17},{17,9},{25,1},{2,26},{10... | collective-permute-start | bytes 3342344 | tf_op jit(solution)/shard_map/ppermute | solution.py:24
  256.3 248.0 %all-gather.7.cloned.1.call-start = ((), (), s32[]{:S(2)}) async-start(), calls=%async_computation.9 | async-start | bytes 18874368 | tf_op jit(solution)/shard_map/all_gather | solution.py:478
  257.0 335.4 %all-gather.9.cloned.1.call-start = ((), (), s32[]{:S(2)}) async-start(), calls=%async_computation.10 | async-start | bytes 18874368 | tf_op jit(solution)/shard_map/all_gather | solution.py:478
  259.9 132.6 %collective-permute-start.19 = (bf16[256,1024]{1,0:T(8,128)(2,1)}, bf16[256,1024]{1,0:T(8,128)(2,1)}, u32[]{:S(2)}, u32[]{:S(2)}) collective-permute-start(bf16[256,1024]{1,0:T(8,128)(2,1)} %get-tuple-element.127), channel_id=1, source_target_pairs={{0,8},{8,0},{16,24},{24,16},{1,9},{9,1},{17,25},{25,17},{2,10},{10... | collective-permute-start | bytes 1572872 | tf_op jit(solution)/shard_map/ppermute | solution.py:24
  279.5 114.9 %collective-permute-start.20 = (bf16[256,1024]{1,0:T(8,128)(2,1)}, bf16[256,1024]{1,0:T(8,128)(2,1)S(1)}, u32[]{:S(2)}, u32[]{:S(2)}) collective-permute-start(bf16[256,1024]{1,0:T(8,128)(2,1)} %get-tuple-element.126), channel_id=1, source_target_pairs={{0,16},{8,24},{16,0},{24,8},{1,17},{9,25},{17,1},{25,9},{2,18},{10... | collective-permute-start | bytes 1572872 | tf_op jit(solution)/shard_map/ppermute | solution.py:24
  306.4 88.8 %collective-permute-start.21 = (bf16[256,1024]{1,0:T(8,128)(2,1)}, bf16[256,1024]{1,0:T(8,128)(2,1)}, u32[]{:S(2)}, u32[]{:S(2)}) collective-permute-start(bf16[256,1024]{1,0:T(8,128)(2,1)} %get-tuple-element.124), channel_id=1, source_target_pairs={{0,24},{8,16},{16,8},{24,0},{1,25},{9,17},{17,9},{25,1},{2,26},{10... | collective-permute-start | bytes 1572872 | tf_op jit(solution)/shard_map/ppermute | solution.py:24
  397.1 588.3 %all-gather.11.cloned.1.call-start = ((), (), s32[]{:S(2)}) async-start(), calls=%async_computation.11 | async-start | bytes 10485760 | tf_op jit(solution)/shard_map/all_gather | solution.py:632
  404.2 49.3 %collective-permute-start.24 = (bf16[256,2048]{1,0:T(8,128)(2,1)S(1)}, bf16[256,2048]{1,0:T(8,128)(2,1)S(1)}, u32[]{:S(2)}, u32[]{:S(2)}) collective-permute-start(bf16[256,2048]{1,0:T(8,128)(2,1)S(1)} %get-tuple-element.137), channel_id=1, source_target_pairs={{0,3},{1,2},{2,1},{3,0},{4,7},{5,6},{6,5},{7,4},{8,11},{9,10},{10,... | collective-permute-start | bytes 3145736 | tf_op jit(solution)/shard_map/ppermute | solution.py:24
  405.7 69.8 %collective-permute-start.23 = (bf16[256,2048]{1,0:T(8,128)(2,1)S(1)}, bf16[256,2048]{1,0:T(8,128)(2,1)S(1)}, u32[]{:S(2)}, u32[]{:S(2)}) collective-permute-start(bf16[256,2048]{1,0:T(8,128)(2,1)S(1)} %get-tuple-element.138), channel_id=1, source_target_pairs={{0,2},{1,3},{2,0},{3,1},{4,6},{5,7},{6,4},{7,5},{8,10},{9,11},{10,... | collective-permute-start | bytes 3145736 | tf_op jit(solution)/shard_map/ppermute | solution.py:24
  407.2 90.0 %collective-permute-start.22 = (bf16[256,2048]{1,0:T(8,128)(2,1)S(1)}, bf16[256,2048]{1,0:T(8,128)(2,1)S(1)}, u32[]{:S(2)}, u32[]{:S(2)}) collective-permute-start(bf16[256,2048]{1,0:T(8,128)(2,1)S(1)} %get-tuple-element.136), channel_id=1, source_target_pairs={{0,1},{1,0},{2,3},{3,2},{4,5},{5,4},{6,7},{7,6},{8,9},{9,8},{10,11... | collective-permute-start | bytes 3145736 | tf_op jit(solution)/shard_map/ppermute | solution.py:24
  510.0 768.9 %reduce-scatter.6.cloned.1.call-start = ((), (), s32[]{:S(2)}) async-start(), calls=%async_computation.13 | async-start | bytes 18874368 | tf_op jit(solution)/shard_map/reduce_scatter | solution.py:642
  554.1 58.1 %collective-permute-start.27 = (bf16[256,2048]{1,0:T(8,128)(2,1)}, bf16[256,2048]{1,0:T(8,128)(2,1)}, u32[]{:S(2)}, u32[]{:S(2)}) collective-permute-start(bf16[256,2048]{1,0:T(8,128)(2,1)} %broadcast_add_fusion.15), channel_id=1, source_target_pairs={{0,8},{8,0},{16,24},{24,16},{1,9},{9,1},{17,25},{25,17},{2,10},{10... | collective-permute-start | bytes 3145736 | tf_op jit(solution)/shard_map/ppermute | solution.py:24
  554.5 60.1 %collective-permute-start.28 = (bf16[256,2048]{1,0:T(8,128)(2,1)}, bf16[256,2048]{1,0:T(8,128)(2,1)}, u32[]{:S(2)}, u32[]{:S(2)}) collective-permute-start(bf16[256,2048]{1,0:T(8,128)(2,1)} %broadcast_add_fusion.15), channel_id=1, source_target_pairs={{0,24},{8,16},{16,8},{24,0},{1,25},{9,17},{17,9},{25,1},{2,26},{10... | collective-permute-start | bytes 3145736 | tf_op jit(solution)/shard_map/ppermute | solution.py:24
  772.1 49.5 %collective-permute-start.34 = (bf16[256,2048]{1,0:T(8,128)(2,1)}, bf16[256,2048]{1,0:T(8,128)(2,1)S(1)}, u32[]{:S(2)}, u32[]{:S(2)}) collective-permute-start(bf16[256,2048]{1,0:T(8,128)(2,1)} %broadcast_add_fusion.11), channel_id=1, source_target_pairs={{0,24},{8,16},{16,8},{24,0},{1,25},{9,17},{17,9},{25,1},{2,26},{10... | collective-permute-start | bytes 3145736 | tf_op jit(solution)/shard_map/ppermute | solution.py:24
  807.4 58.4 %collective-permute-start.32 = (bf16[256,2048]{1,0:T(8,128)(2,1)}, bf16[256,2048]{1,0:T(8,128)(2,1)}, u32[]{:S(2)}, u32[]{:S(2)}) collective-permute-start(bf16[256,2048]{1,0:T(8,128)(2,1)} %get-tuple-element.54), channel_id=1, source_target_pairs={{0,16},{8,24},{16,0},{24,8},{1,17},{9,25},{17,1},{25,9},{2,18},{10... | collective-permute-start | bytes 3145736 | tf_op jit(solution)/shard_map/ppermute | solution.py:24
  899.1 480.9 %reduce-scatter.4.cloned.1.call-start = ((), (), s32[]{:S(2)}) async-start(), calls=%async_computation.12 | async-start | bytes 18874368 | tf_op jit(solution)/shard_map/reduce_scatter | solution.py:642
  980.0 481.9 %reduce-scatter.8.cloned.1.call-start = ((), (), s32[]{:S(2)}) async-start(), calls=%async_computation.14 | async-start | bytes 18874368 | tf_op jit(solution)/shard_map/reduce_scatter | solution.py:642
  1082.7 82.0 %all-to-all-start = ((bf16[4,256,2048]{2,1,0:T(8,128)(2,1)}), bf16[4,256,2048]{2,1,0:T(8,128)(2,1)}, u32[]{:S(2)}, u32[]{:S(2)}) async-start(bf16[4,256,2048]{2,1,0:T(8,128)(2,1)} %broadcast_in_dim.216), calls=%async_computation | async-start | bytes 8388608 | tf_op jit(solution)/shard_map/all_to_all | solution.py:51
  1104.5 66.4 %collective-permute-start.43 = (bf16[1024,1536]{1,0:T(8,128)(2,1)}, bf16[1024,1536]{1,0:T(8,128)(2,1)}, u32[]{:S(2)}, u32[]{:S(2)}) collective-permute-start(bf16[1024,1536]{1,0:T(8,128)(2,1)} %dynamic-slice_bitcast_fusion), channel_id=1, source_target_pairs={{0,4},{4,0},{1,5},{5,1},{2,6},{6,2},{3,7},{7,3},{8,12},{12,8},{9,1... | collective-permute-start | bytes 9437192 | tf_op jit(solution)/shard_map/ppermute | solution.py:24
  1179.7 99.2 %all-to-all-start.1 = ((bf16[4,256,2048]{2,1,0:T(8,128)(2,1)}), bf16[4,256,2048]{2,1,0:T(8,128)(2,1)}, u32[]{:S(2)}, u32[]{:S(2)}) async-start(bf16[4,256,2048]{2,1,0:T(8,128)(2,1)} %pad_maximum_fusion), calls=%async_computation.1 | async-start | bytes 8388608 | tf_op jit(solution)/shard_map/all_to_all | solution.py:51
  1196.7 98.2 %collective-permute-start.54 = (bf16[256,1024]{1,0:T(8,128)(2,1)}, bf16[256,1024]{1,0:T(8,128)(2,1)}, u32[]{:S(2)}, u32[]{:S(2)}) collective-permute-start(bf16[256,1024]{1,0:T(8,128)(2,1)} %get-tuple-element.143), channel_id=1, source_target_pairs={{0,3},{1,2},{2,1},{3,0},{4,7},{5,6},{6,5},{7,4},{8,11},{9,10},{10,... | collective-permute-start | bytes 1572872 | tf_op jit(solution)/shard_map/ppermute | solution.py:24
  1198.6 106.8 %collective-permute-start.53 = (bf16[256,1024]{1,0:T(8,128)(2,1)S(1)}, bf16[256,1024]{1,0:T(8,128)(2,1)}, u32[]{:S(2)}, u32[]{:S(2)}) collective-permute-start(bf16[256,1024]{1,0:T(8,128)(2,1)S(1)} %get-tuple-element.144), channel_id=1, source_target_pairs={{0,2},{1,3},{2,0},{3,1},{4,6},{5,7},{6,4},{7,5},{8,10},{9,11},{10,... | collective-permute-start | bytes 1572872 | tf_op jit(solution)/shard_map/ppermute | solution.py:24
  1199.5 105.9 %collective-permute-start.52 = (bf16[256,1024]{1,0:T(8,128)(2,1)S(1)}, bf16[256,1024]{1,0:T(8,128)(2,1)}, u32[]{:S(2)}, u32[]{:S(2)}) collective-permute-start(bf16[256,1024]{1,0:T(8,128)(2,1)S(1)} %get-tuple-element.142), channel_id=1, source_target_pairs={{0,1},{1,0},{2,3},{3,2},{4,5},{5,4},{6,7},{7,6},{8,9},{9,8},{10,11... | collective-permute-start | bytes 1572872 | tf_op jit(solution)/shard_map/ppermute | solution.py:24
  1278.9 98.6 %all-to-all-start.2 = ((bf16[4,256,1024]{2,1,0:T(8,128)(2,1)}), bf16[4,256,1024]{2,1,0:T(8,128)(2,1)}, u32[]{:S(2)}, u32[]{:S(2)}) async-start(bf16[4,256,1024]{2,1,0:T(8,128)(2,1)} %bitcast.458), calls=%async_computation.4 | async-start | bytes 4194304 | tf_op jit(solution)/shard_map/all_to_all | solution.py:51
  1383.1 76.9 %all-to-all-start.3 = ((bf16[4,256,1024]{2,1,0:T(8,128)(2,1)}), bf16[4,256,1024]{2,1,0:T(8,128)(2,1)S(1)}, u32[]{:S(2)}, u32[]{:S(2)}) async-start(bf16[4,256,1024]{2,1,0:T(8,128)(2,1)} %bitcast.426), calls=%async_computation.5 | async-start | bytes 4194304 | tf_op jit(solution)/shard_map/all_to_all | solution.py:51
  1394.1 49.2 %collective-permute-start.51 = (f32[8,128]{1,0:T(8,128)S(1)}, f32[8,128]{1,0:T(8,128)S(1)}, u32[]{:S(2)}, u32[]{:S(2)}) collective-permute-start(f32[8,128]{1,0:T(8,128)S(1)} %broadcast_in_dim.219), channel_id=1, source_target_pairs={{0,4},{4,0},{1,5},{5,1},{2,6},{6,2},{3,7},{7,3},{8,12},{12,8},{9,1... | collective-permute-start | bytes 12296 | tf_op jit(solution)/shard_map/ppermute | solution.py:24
  1465.0 51.7 %all-to-all-start.4 = ((bf16[4,256,1024]{2,1,0:T(8,128)(2,1)}), bf16[4,256,1024]{2,1,0:T(8,128)(2,1)}, u32[]{:S(2)}, u32[]{:S(2)}) async-start(bf16[4,256,1024]{2,1,0:T(8,128)(2,1)} %bitcast.427), calls=%async_computation.7 | async-start | bytes 4194304 | tf_op jit(solution)/shard_map/all_to_all | solution.py:51
  (122 other events, 2046.4 us)
Sparse Core Ops, SparseCore 0:
  256.4 106.3 all-gather.4
  365.3 134.7 all-gather.6
  502.6 89.8 all-gather.8
  594.2 87.6 all-gather.10
  899.2 134.9 reduce-scatter.5
  1037.6 158.7 reduce-scatter.3
  1200.0 138.2 reduce-scatter.7

commit v11 on v9

--- a/solution.py
+++ b/solution.py
@@ -546,8 +546,9 @@
     w_up = gather_plane(up_ready)
     in_blocks = gather_near(after(mine, up_ready), "z")
     seq_factor = rms_factor(seq_tokens)
-    w_in = stack_rows(in_blocks, token(seq_factor))
+    w_in = stack_rows(in_blocks, token(seq_factor, w_gate))
     w_in_other = send(w_in, "c", 1)
+    down_blocks = expert_chunk(2, token(w_in))
 
     side = whole_of(w_in[:, 4 * cols :], w_in_other[:, 4 * cols :], 0)[:, :6].astype(f32).T
     gain_in, gain_mid = side[0], side[1]
@@ -594,9 +595,11 @@
     q_mean, k_mean = over_heads(
         jnp.sum(query_raw * query_raw, axis=-1), jnp.sum(key_raw * key_raw, axis=-1)
     )
+    down_ready = in_order(down_blocks, "z", token(projected))
+    w_down = gather_plane(down_ready)
     cosine, sine = rope_tables(seq)
     shared = [
-        after(q_mean, w_gate, w_out),
+        after(q_mean, w_out, down_ready),
         k_mean,
         gain_q[None],
         gain_k[None],
@@ -606,13 +609,9 @@
         segment[None],
     ]
     attended, query, keyed, valued, log_total = attend(projected, shared, heads)
-    down_blocks = expert_chunk(2, token(attended))
     attn_out = dot("tc,dc->td", attended, w_out).astype(bf16)
     got = exchange_sum(attn_out.reshape(seqs, own, width), "s")
     residual = inputs + got
-    down_ready = in_order(down_blocks, "z", token(residual))
-    residual = after(residual, down_ready)
-    w_down = gather_plane(down_ready)
 
     normed_mid = (residual * rms_factor(residual) * gain_mid).astype(bf16)
     expert_weights = (w_gate, w_up, w_down)
@@ -634,8 +633,6 @@
     valid_f = valid_mask.astype(f32)[:, None]
     difference = final_out - to_inner(teacher).astype(f32)
     squared = jnp.sum(valid_f * difference * difference)
-    squared = gather_sum(squared)
-    loss_value = squared / (total_count * width)
     grad_out = (
         to_inner(cotangent).astype(f32) + 2.0 / (total_count * width) * valid_f * difference
     )
@@ -695,15 +692,17 @@
         axis=1,
     )
 
-    def back_half(weight):
-        grad = dot("tc,dc->td", grad_proj, weight).astype(bf16)
-        return exchange_sum(grad.reshape(seqs, own, width // 2), "s")
-
-    grad_normed = whole_of(back_half(w_qkv), back_half(w_qkv_other), 1)
     grad_w_qkv = dot("td,tc->dc", normed_in, grad_proj).astype(bf16)
     summed = jnp.concatenate([sum_cores(grad_w_qkv), sum_cores(grad_w_out)], axis=1)
     summed = summed.astype(bf16).reshape(planes, part, 4 * cols)
     gate_ready = swap(grad_w_gate, "z")
+    late_proj = after(grad_proj, summed)
+    grad_normed = jnp.concatenate(
+        [dot("tc,dc->td", late_proj, weight).astype(bf16) for weight in (w_qkv, w_qkv_other)],
+        axis=1,
+    )
+    grad_normed = exchange_sum(grad_normed.reshape(seqs, own, width), "s")
+    grad_normed = whole_of(grad_normed[:, : width // 2], grad_normed[:, width // 2 :], 1)
     grad_attn = after(exchange_sum(summed, "z"), gate_ready).astype(bf16)
     up_ready = swap(after(grad_w_up, grad_attn), "z")
     grad_in_norm, gain_in_grad = norm_back(inputs, gain_in, grad_normed)
@@ -715,6 +714,7 @@
 
     gains = jnp.stack([gain_in_grad, gain_mid_grad, widen(gain_q_grad[0]), widen(gain_k_grad[0])])
     gains = after(gains, grad_attn)
+    loss_value = gather_sum(after(squared, grad_attn)) / (total_count * width)
     for axis in ("z", "c", "s", "o"):
         gains = sum(gather_near(gains, axis))
     row = (lax.axis_index(("c", "o", "z")) * seqs + rank) * rows_dev

time: 1440 us -> 1460 us (1.014)
  starting transfers between devices: 162 us -> 179 us
    ppermute x74 -> x71, waiting for transfers between devices: 544 us -> 510 us  [send(): return lax.ppermute(block, axis, [(i, i ^ step) for i in range(size)])]
    all_to_all x3, waiting for transfers between devices: 28.6 us -> 45 us  [swap(): return lax.all_to_all(pieces, axis, split_axis=0, concat_axis=0, tiled=True)]
    ppermute x74 -> x71, starting transfers between devices: 149 us -> 164 us  [send(): return lax.ppermute(block, axis, [(i, i ^ step) for i in range(size)])]
    dynamic_update_slice x30 -> x29, local copies, waits for them, and re-layouts: 41.7 us -> 36.6 us  [in_order(): lax.dynamic_update_index_in_dim(stacked, block, (rank ^ k) + start, 0)]
    unnamed x190 -> x182, local copies, waits for them, and re-layouts: 59.7 us -> 62.4 us
    slice x36 -> x37, local copies, waits for them, and re-layouts: 30.8 us -> 31.3 us  [token(): value[(slice(0, 1),) * value.ndim].reshape(()).astype(f32)]
  transfers between devices with their start and end apart: 84 -> 81, of which waited for: 36 -> 34; matrix products, arithmetic and copies ran while one was open for 27% -> 27% of each run, Pallas kernels for 12% -> 12%
where the time goes in v11:
time: 1460 us; the launch traced here: 1450 us
  waiting for transfers between devices  573 us (39%)
  local copies, waits for them, and re-layouts  223 us (15%)
  starting transfers between devices  179 us (12%)
  Pallas kernels  171 us (12%)
  other arithmetic  129 us (9%)
  matrix products  109 us (7%)
  between operations  63.5 us (4%)
    ppermute x71, waiting for transfers between devices, send(): return lax.ppermute(block, axis, [(i, i ^ step) for i in range(size)])  510 us
    ppermute x71, starting transfers between devices, send(): return lax.ppermute(block, axis, [(i, i ^ step) for i in range(size)])  164 us
    pallas_call x6, Pallas kernels, run(): pl.pallas_call(functools.partial(kernel, self.count, self.slots), grid=(s...  134 us
    dot_general x10, matrix products, dot(): return jnp.einsum(spec, left, right, preferred_element_type=f32)  96.9 us
    unnamed x182, local copies, waits for them, and re-layouts  62.4 us
    all_to_all x3, waiting for transfers between devices, swap(): return lax.all_to_all(pieces, axis, split_axis=0, concat_axis=0, tiled=True)  45 us
    add x21, other arithmetic, after(): return value + token(*others).astype(value.dtype)  40.9 us
    dynamic_update_slice x29, local copies, waits for them, and re-layouts, in_order(): lax.dynamic_update_index_in_dim(stacked, block, (rank ^ k) + start, 0)  36.6 us
  transfers between devices with their start and end apart: 81, of which 34 were waited for; matrix products, arithmetic and copies ran while one was open for 27% of the time, Pallas kernels for 12%

profile of v11, /device:TPU:0, one launch (start us, length us, event | category | flops | bytes accessed | tf_op | source)
XLA Modules:
  0.0 1447.6 jit_solution(12699482635497844109)
XLA Ops:
  43.6 18.8 %collective-permute-done.3 = bf16[256,1024]{1,0:T(8,128)(2,1)S(1)} collective-permute-done((bf16[256,1024]{1,0:T(8,128)(2,1)S(1)}, bf16[256,1024]{1,0:T(8,128)(2,1)S(1)}, u32[]{:S(2)}, u32[]{:S(2)}) %collective-permute-start.3) | collective-permute-done | bytes 524320 | tf_op jit(solution)/shard_map/ppermute | solution.py:24
  139.7 14.9 %collective-permute-done.10 = bf16[256,1024]{1,0:T(8,128)(2,1)} collective-permute-done((bf16[256,1024]{1,0:T(8,128)(2,1)}, bf16[256,1024]{1,0:T(8,128)(2,1)}, u32[]{:S(2)}, u32[]{:S(2)}) %collective-permute-start.10) | collective-permute-done | bytes 524320 | tf_op jit(solution)/shard_map/ppermute | solution.py:24
  176.5 17.9 %all-gather.5.cloned.1.call-done = bf16[8192,1024]{1,0:T(8,128)(2,1)} async-done(((bf16[1024,1024]{1,0:T(8,128)(2,1)}), bf16[8192,1024]{1,0:T(8,128)(2,1)}) %all-gather.5.cloned.1.call-update) | async-done | bytes 16777232 | tf_op jit(solution)/shard_map/all_gather | solution.py:478
  200.5 19.5 %collective-permute-done.12 = bf16[256,2176]{1,0:T(8,128)(2,1)} collective-permute-done((bf16[256,2176]{1,0:T(8,128)(2,1)S(1)}, bf16[256,2176]{1,0:T(8,128)(2,1)}, u32[]{:S(2)}, u32[]{:S(2)}) %collective-permute-start.12) | collective-permute-done | bytes 1114144 | tf_op jit(solution)/shard_map/ppermute | solution.py:24
  222.4 27.8 %collective-permute-done.13 = bf16[256,2176]{1,0:T(8,128)(2,1)} collective-permute-done((bf16[256,2176]{1,0:T(8,128)(2,1)S(1)}, bf16[256,2176]{1,0:T(8,128)(2,1)}, u32[]{:S(2)}, u32[]{:S(2)}) %collective-permute-start.13) | collective-permute-done | bytes 1114144 | tf_op jit(solution)/shard_map/ppermute | solution.py:24
  288.8 20.5 %collective-permute-start.19 = (bf16[256,1024]{1,0:T(8,128)(2,1)}, bf16[256,1024]{1,0:T(8,128)(2,1)}, u32[]{:S(2)}, u32[]{:S(2)}) collective-permute-start(bf16[256,1024]{1,0:T(8,128)(2,1)} %get-tuple-element.124), channel_id=1, source_target_pairs={{0,8},{8,0},{16,24},{24,16},{1,9},{9,1},{17,25},{25,17},{2,10},{10... | collective-permute-start | bytes 1572872 | tf_op jit(solution)/shard_map/ppermute | solution.py:24
  311.9 20.6 %collective-permute-done.19 = bf16[256,1024]{1,0:T(8,128)(2,1)} collective-permute-done((bf16[256,1024]{1,0:T(8,128)(2,1)}, bf16[256,1024]{1,0:T(8,128)(2,1)}, u32[]{:S(2)}, u32[]{:S(2)}) %collective-permute-start.19) | collective-permute-done | bytes 524320 | tf_op jit(solution)/shard_map/ppermute | solution.py:24
  365.3 18.0 %shard_map.145 = (bf16[1024,512]{1,0:T(8,128)(2,1)S(1)}, bf16[1024,512]{1,0:T(8,128)(2,1)S(1)}, bf16[1024,512]{1,0:T(8,128)(2,1)S(1)}, bf16[1024,512]{1,0:T(8,128)(2,1)}, f32[4,1024,1]{2,1,0:T(8,128)}) custom-call(f32[1024,1536]{1,0:T(8,128)} %copy-done.15, f32[1024,1536]{1,0:T(8,128)} %copy-done.15, f32[1024,1536]{1,0:T(8,128)} %copy-done.15, ...), custom_call_target="tpu_custom_call" | custom-call | flops 1000000 | bytes 100000 | tf_op jit(solution)/shard_map/pallas_call | solution.py:233
  389.7 27.2 %collective-permute-done.24 = bf16[256,2048]{1,0:T(8,128)(2,1)S(1)} collective-permute-done((bf16[256,2048]{1,0:T(8,128)(2,1)S(1)}, bf16[256,2048]{1,0:T(8,128)(2,1)S(1)}, u32[]{:S(2)}, u32[]{:S(2)}) %collective-permute-start.24) | collective-permute-done | bytes 1048608 | tf_op jit(solution)/shard_map/ppermute | solution.py:24
  416.9 30.0 %collective-permute-done.23 = bf16[256,2048]{1,0:T(8,128)(2,1)S(1)} collective-permute-done((bf16[256,2048]{1,0:T(8,128)(2,1)S(1)}, bf16[256,2048]{1,0:T(8,128)(2,1)S(1)}, u32[]{:S(2)}, u32[]{:S(2)}) %collective-permute-start.23) | collective-permute-done | bytes 1048608 | tf_op jit(solution)/shard_map/ppermute | solution.py:24
  470.1 37.4 %collective-permute-done.25.refs_1_ = bf16[256,2048]{1,0:T(8,128)(2,1)} collective-permute-done((bf16[256,2048]{1,0:T(8,128)(2,1)}, bf16[256,2048]{1,0:T(8,128)(2,1)}, u32[]{:S(2)}, u32[]{:S(2)}) %collective-permute-start.25) | collective-permute-done | bytes 1048608 | tf_op jit(solution)/shard_map/ppermute | solution.py:24
  513.9 20.8 %shard_map.146 = (bf16[4,2,288,2048]{3,2,1,0:T(8,128)(2,1)}, bf16[4,2,288,1024]{3,2,1,0:T(8,128)(2,1)}, bf16[4,288,1024]{2,1,0:T(8,128)(2,1)}, bf16[4,288,1024]{2,1,0:T(8,128)(2,1)}) custom-call(s32[4,4,1,256]{3,2,1,0:T(1,128)} %pad_add_fusion.place, bf16[256,2048]{1,0:T(8,128)(2,1)} %multiply_convert_fusion.3.refs_0_, ...), custom_call_target="tpu_custom_call" | custom-call | flops 9663676416 | bytes 50331648 | tf_op jit(solution)/shard_map/pallas_call | solution.py:368
  534.7 14.2 shard_map.147
  563.0 20.7 %shard_map.148 = (bf16[4,2,288,2048]{3,2,1,0:T(8,128)(2,1)}, bf16[4,2,288,1024]{3,2,1,0:T(8,128)(2,1)}, bf16[4,288,1024]{2,1,0:T(8,128)(2,1)}, bf16[4,288,1024]{2,1,0:T(8,128)(2,1)}) custom-call(s32[4,4,1,256]{3,2,1,0:T(1,128)} %pad_add_fusion.place, bf16[256,2048]{1,0:T(8,128)(2,1)} %broadcast_add_fusion.15.refs_0_, ...), custom_call_target="tpu_custom_call", output_to_operand_aliasing={{0}: (5, {}), {1}: (6, {})} | custom-call | flops 9663676416 | bytes 50331648 | tf_op jit(solution)/shard_map/pallas_call | solution.py:368
  583.7 14.3 shard_map.149
  612.9 15.8 %collective-permute-start.29 = (bf16[256,2048]{1,0:T(8,128)(2,1)}, bf16[256,2048]{1,0:T(8,128)(2,1)}, u32[]{:S(2)}, u32[]{:S(2)}) collective-permute-start(bf16[256,2048]{1,0:T(8,128)(2,1)} %broadcast_add_fusion.14), channel_id=1, source_target_pairs={{0,8},{8,0},{16,24},{24,16},{1,9},{9,1},{17,25},{25,17},{2,10},{10... | collective-permute-start | bytes 3145736 | tf_op jit(solution)/shard_map/ppermute | solution.py:24
  669.1 47.0 %collective-permute-done.31.refs_1_ = bf16[256,2048]{1,0:T(8,128)(2,1)S(1)} collective-permute-done((bf16[256,2048]{1,0:T(8,128)(2,1)S(1)}, bf16[256,2048]{1,0:T(8,128)(2,1)S(1)}, u32[]{:S(2)}, u32[]{:S(2)}) %collective-permute-start.31) | collective-permute-done | bytes 1048608 | tf_op jit(solution)/shard_map/ppermute | solution.py:24
  721.4 32.0 %shard_map.150 = (bf16[4,2,288,2048]{3,2,1,0:T(8,128)(2,1)}, bf16[4,2,288,1024]{3,2,1,0:T(8,128)(2,1)}, bf16[4,2,288,1024]{3,2,1,0:T(8,128)(2,1)}, bf16[256,2048]{1,0:T(8,128)(2,1)}, bf16[256,2048]{1,0:T(8,128)(2,1)}) custom-call(s32[4,4,1,256]{3,2,1,0:T(1,128)} %pad_add_fusion.place, f32[4,4,1,256]{3,2,1,0:T(1,128)} %pad_maximum_fusion.9.gate, ...), custom_call_target="tpu_custom_call" | custom-call | flops 9663676416 | bytes 50331648 | tf_op jit(solution)/shard_map/pallas_call | solution.py:368
  769.1 32.2 %shard_map.151 = (bf16[4,2,288,2048]{3,2,1,0:T(8,128)(2,1)}, bf16[4,2,288,1024]{3,2,1,0:T(8,128)(2,1)}, bf16[4,2,288,1024]{3,2,1,0:T(8,128)(2,1)}, bf16[256,2048]{1,0:T(8,128)(2,1)}, bf16[256,2048]{1,0:T(8,128)(2,1)}) custom-call(s32[4,4,1,256]{3,2,1,0:T(1,128)} %pad_add_fusion.place, ...), custom_call_target="tpu_custom_call", output_to_operand_aliasing={{0}: (9, {}), {1}: (10, {}), {2}: (11, {})} | custom-call | flops 9663676416 | bytes 50331648 | tf_op jit(solution)/shard_map/pallas_call | solution.py:368
  825.6 20.7 %convolution_convert_fusion.2 = bf16[4,2048,1024]{2,1,0:T(8,128)(2,1)} fusion(bf16[4,576,2048]{2,1,0:T(8,128)(2,1)} %bitcast.432, bf16[4,576,1024]{2,1,0:T(8,128)(2,1)} %bitcast.447), kind=kOutput, calls=%fused_computation.2 | convolution fusion | flops 9672065024 | bytes 30932992 | tf_op jit(solution)/shard_map/krd,krf->kdf/dot_general | solution.py:405
  875.8 21.3 %collective-permute-done.35 = bf16[256,2048]{1,0:T(8,128)(2,1)S(1)} collective-permute-done((bf16[256,2048]{1,0:T(8,128)(2,1)}, bf16[256,2048]{1,0:T(8,128)(2,1)S(1)}, u32[]{:S(2)}, u32[]{:S(2)}) %collective-permute-start.35) | collective-permute-done | bytes 1048608 | tf_op jit(solution)/shard_map/ppermute | solution.py:24
  907.8 20.9 %convolution_convert_fusion.1 = bf16[4,2048,1024]{2,1,0:T(8,128)(2,1)} fusion(bf16[4,576,2048]{2,1,0:T(8,128)(2,1)} %bitcast.437, bf16[4,576,1024]{2,1,0:T(8,128)(2,1)} %bitcast.448), kind=kOutput, calls=%fused_computation.1 | convolution fusion | flops 9672065024 | bytes 30932992 | tf_op jit(solution)/shard_map/krd,krf->kdf/dot_general | solution.py:405
  973.2 22.3 %convolution_convert_fusion = bf16[4,2048,1024]{2,1,0:T(8,128)(2,1)} fusion(bf16[4,576,2048]{2,1,0:T(8,128)(2,1)} %bitcast.438, bf16[4,576,1024]{2,1,0:T(8,128)(2,1)} %bitcast.449), kind=kOutput, calls=%fused_computation | convolution fusion | flops 9672065024 | bytes 30932992 | tf_op jit(solution)/shard_map/krd,krf->kdf/dot_general | solution.py:405
  1005.4 18.8 %shard_map.152 = (f32[1024,512]{1,0:T(8,128)}, f32[1024,512]{1,0:T(8,128)}, bf16[1024,512]{1,0:T(8,128)(2,1)S(1)}, f32[1024,1]{1,0:T(8,128)S(1)}, f32[1024,1]{1,...) custom-call(f32[1024,1536]{1,0:T(8,128)} %copy-done.15, f32[1024,1536]{1,0:T(8,128)} %copy-done.15, ...), custom_call_target="tpu_custom_call" | custom-call | flops 1000000 | bytes 100000 | tf_op jit(solution)/shard_map/pallas_call | solution.py:251
  1037.2 45.1 %collective-permute-done.40 = bf16[256,2048]{1,0:T(8,128)(2,1)} collective-permute-done((bf16[256,2048]{1,0:T(8,128)(2,1)}, bf16[256,2048]{1,0:T(8,128)(2,1)}, u32[]{:S(2)}, u32[]{:S(2)}) %collective-permute-start.40) | collective-permute-done | bytes 1048608 | tf_op jit(solution)/shard_map/ppermute | solution.py:24
  1088.1 24.2 %collective-permute-done.42 = bf16[256,2048]{1,0:T(8,128)(2,1)S(1)} collective-permute-done((bf16[256,2048]{1,0:T(8,128)(2,1)}, bf16[256,2048]{1,0:T(8,128)(2,1)S(1)}, u32[]{:S(2)}, u32[]{:S(2)}) %collective-permute-start.42) | collective-permute-done | bytes 1048608 | tf_op jit(solution)/shard_map/ppermute | solution.py:24
  1199.9 23.8 %collective-permute-done.50 = bf16[256,2048]{1,0:T(8,128)(2,1)} collective-permute-done((bf16[256,2048]{1,0:T(8,128)(2,1)}, bf16[256,2048]{1,0:T(8,128)(2,1)}, u32[]{:S(2)}, u32[]{:S(2)}) %collective-permute-start.50) | collective-permute-done | bytes 1048608 | tf_op jit(solution)/shard_map/ppermute | solution.py:24
  1235.3 21.0 %all-to-all-done.1 = bf16[4,256,1024]{2,1,0:T(8,128)(2,1)} async-done(((bf16[4,256,1024]{2,1,0:T(8,128)(2,1)}), bf16[4,256,1024]{2,1,0:T(8,128)(2,1)}, u32[]{:S(2)}, u32[]{:S(2)}) %all-to-all-start.1) | async-done | bytes 2097184 | tf_op jit(solution)/shard_map/all_to_all | solution.py:51
  1258.8 41.5 %collective-permute-done.49 = bf16[256,2048]{1,0:T(8,128)(2,1)} collective-permute-done((bf16[256,2048]{1,0:T(8,128)(2,1)}, bf16[256,2048]{1,0:T(8,128)(2,1)}, u32[]{:S(2)}, u32[]{:S(2)}) %collective-permute-start.49) | collective-permute-done | bytes 1048608 | tf_op jit(solution)/shard_map/ppermute | solution.py:24
  1324.1 14.1 collective-permute-start.65
  1392.3 24.0 %all-to-all-done.2 = bf16[4,256,1024]{2,1,0:T(8,128)(2,1)} async-done(((bf16[4,256,1024]{2,1,0:T(8,128)(2,1)}), bf16[4,256,1024]{2,1,0:T(8,128)(2,1)}, u32[]{:S(2)}, u32[]{:S(2)}) %all-to-all-start.2) | async-done | bytes 2097184 | tf_op jit(solution)/shard_map/all_to_all | solution.py:51
  1419.9 19.3 %copy.140 = f32[256,4,3072]{2,1,0:T(4,128)} copy(f32[256,4,3072]{2,0,1:T(8,128)S(1)} %convert_bitcast_fusion) | data formatting | bytes 25165824
  (582 shorter events, 617.5 us)
Async XLA Ops:
  7.2 187.2 %all-gather.5.cloned.1.call-start = ((), (), s32[]{:S(2)}) async-start(), calls=%async_computation.6 | async-start | bytes 18874368 | tf_op jit(solution)/shard_map/all_gather | solution.py:478
  23.8 57.0 %collective-permute-start = (bf16[328,2048]{1,0:T(8,128)(2,1)}, bf16[328,2048]{1,0:T(8,128)(2,1)}, u32[]{:S(2)}, u32[]{:S(2)}) collective-permute-start(bf16[328,2048]{1,0:T(8,128)(2,1)} %get-tuple-element.148), channel_id=1, source_target_pairs={{0,1},{1,0},{2,3},{3,2},{4,5},{5,4},{6,7},{7,6},{8,9},{9,8},{10,11... | collective-permute-start | bytes 4030472 | tf_op jit(solution)/shard_map/ppermute | solution.py:24
  26.7 60.0 %collective-permute-start.1 = (bf16[328,2048]{1,0:T(8,128)(2,1)}, bf16[328,2048]{1,0:T(8,128)(2,1)}, u32[]{:S(2)}, u32[]{:S(2)}) collective-permute-start(bf16[328,2048]{1,0:T(8,128)(2,1)} %get-tuple-element.149), channel_id=1, source_target_pairs={{0,2},{1,3},{2,0},{3,1},{4,6},{5,7},{6,4},{7,5},{8,10},{9,11},{10,... | collective-permute-start | bytes 4030472 | tf_op jit(solution)/shard_map/ppermute | solution.py:24
  28.2 59.3 %collective-permute-start.2 = (bf16[328,2048]{1,0:T(8,128)(2,1)}, bf16[328,2048]{1,0:T(8,128)(2,1)}, u32[]{:S(2)}, u32[]{:S(2)}) collective-permute-start(bf16[328,2048]{1,0:T(8,128)(2,1)} %get-tuple-element.147), channel_id=1, source_target_pairs={{0,3},{1,2},{2,1},{3,0},{4,7},{5,6},{6,5},{7,4},{8,11},{9,10},{10,... | collective-permute-start | bytes 4030472 | tf_op jit(solution)/shard_map/ppermute | solution.py:24
  101.3 363.0 %all-gather.7.cloned.1.call-start = ((), (), s32[]{:S(2)}) async-start(), calls=%async_computation.7 | async-start | bytes 18874368 | tf_op jit(solution)/shard_map/all_gather | solution.py:478
  158.1 376.6 %all-gather.9.cloned.1.call-start = ((), (), s32[]{:S(2)}) async-start(), calls=%async_computation.8 | async-start | bytes 18874368 | tf_op jit(solution)/shard_map/all_gather | solution.py:478
  165.0 55.0 %collective-permute-start.12 = (bf16[256,2176]{1,0:T(8,128)(2,1)S(1)}, bf16[256,2176]{1,0:T(8,128)(2,1)}, u32[]{:S(2)}, u32[]{:S(2)}) collective-permute-start(bf16[256,2176]{1,0:T(8,128)(2,1)S(1)} %broadcast_add_fusion.5), channel_id=1, source_target_pairs={{0,8},{8,0},{16,24},{24,16},{1,9},{9,1},{17,25},{25,17},{2,10},{10... | collective-permute-start | bytes 3342344 | tf_op jit(solution)/shard_map/ppermute | solution.py:24
  173.9 76.3 %collective-permute-start.13 = (bf16[256,2176]{1,0:T(8,128)(2,1)S(1)}, bf16[256,2176]{1,0:T(8,128)(2,1)}, u32[]{:S(2)}, u32[]{:S(2)}) collective-permute-start(bf16[256,2176]{1,0:T(8,128)(2,1)S(1)} %broadcast_add_fusion.5), channel_id=1, source_target_pairs={{0,16},{8,24},{16,0},{24,8},{1,17},{9,25},{17,1},{25,9},{2,18},{10... | collective-permute-start | bytes 3342344 | tf_op jit(solution)/shard_map/ppermute | solution.py:24
  173.9 78.6 %collective-permute-start.14 = (bf16[256,2176]{1,0:T(8,128)(2,1)S(1)}, bf16[256,2176]{1,0:T(8,128)(2,1)}, u32[]{:S(2)}, u32[]{:S(2)}) collective-permute-start(bf16[256,2176]{1,0:T(8,128)(2,1)S(1)} %broadcast_add_fusion.5), channel_id=1, source_target_pairs={{0,24},{8,16},{16,8},{24,0},{1,25},{9,17},{17,9},{25,1},{2,26},{10... | collective-permute-start | bytes 3342344 | tf_op jit(solution)/shard_map/ppermute | solution.py:24
  349.1 584.5 %all-gather.11.cloned.1.call-start = ((), (), s32[]{:S(2)}) async-start(), calls=%async_computation.9 | async-start | bytes 10485760 | tf_op jit(solution)/shard_map/all_gather | solution.py:632
  388.1 58.8 %collective-permute-start.23 = (bf16[256,2048]{1,0:T(8,128)(2,1)S(1)}, bf16[256,2048]{1,0:T(8,128)(2,1)S(1)}, u32[]{:S(2)}, u32[]{:S(2)}) collective-permute-start(bf16[256,2048]{1,0:T(8,128)(2,1)S(1)} %get-tuple-element.142), channel_id=1, source_target_pairs={{0,2},{1,3},{2,0},{3,1},{4,6},{5,7},{6,4},{7,5},{8,10},{9,11},{10,... | collective-permute-start | bytes 3145736 | tf_op jit(solution)/shard_map/ppermute | solution.py:24
  389.2 57.8 %collective-permute-start.22 = (bf16[256,2048]{1,0:T(8,128)(2,1)S(1)}, bf16[256,2048]{1,0:T(8,128)(2,1)S(1)}, u32[]{:S(2)}, u32[]{:S(2)}) collective-permute-start(bf16[256,2048]{1,0:T(8,128)(2,1)S(1)} %get-tuple-element.140), channel_id=1, source_target_pairs={{0,1},{1,0},{2,3},{3,2},{4,5},{5,4},{6,7},{7,6},{8,9},{9,8},{10,11... | collective-permute-start | bytes 3145736 | tf_op jit(solution)/shard_map/ppermute | solution.py:24
  450.4 57.1 %collective-permute-start.25 = (bf16[256,2048]{1,0:T(8,128)(2,1)}, bf16[256,2048]{1,0:T(8,128)(2,1)}, u32[]{:S(2)}, u32[]{:S(2)}) collective-permute-start(bf16[256,2048]{1,0:T(8,128)(2,1)} %multiply_convert_fusion.3.refs_0_), channel_id=1, source_target_pairs={{0,16},{8,24},{16,0},{24,8},{1,17},{9,25},{17,1},{25,9},{2,18},{10... | collective-permute-start | bytes 3145736 | tf_op jit(solution)/shard_map/ppermute | solution.py:24
  470.1 528.0 %reduce-scatter.4.cloned.1.call-start = ((), (), s32[]{:S(2)}) async-start(), calls=%async_computation.10 | async-start | bytes 18874368 | tf_op jit(solution)/shard_map/reduce_scatter | solution.py:642
  512.9 50.2 %collective-permute-start.28 = (bf16[256,2048]{1,0:T(8,128)(2,1)}, bf16[256,2048]{1,0:T(8,128)(2,1)}, u32[]{:S(2)}, u32[]{:S(2)}) collective-permute-start(bf16[256,2048]{1,0:T(8,128)(2,1)} %broadcast_add_fusion.16), channel_id=1, source_target_pairs={{0,24},{8,16},{16,8},{24,0},{1,25},{9,17},{17,9},{25,1},{2,26},{10... | collective-permute-start | bytes 3145736 | tf_op jit(solution)/shard_map/ppermute | solution.py:24
  551.5 55.3 %collective-permute-start.26 = (bf16[256,2048]{1,0:T(8,128)(2,1)}, bf16[256,2048]{1,0:T(8,128)(2,1)S(1)}, u32[]{:S(2)}, u32[]{:S(2)}) collective-permute-start(bf16[256,2048]{1,0:T(8,128)(2,1)} %get-tuple-element.43), channel_id=1, source_target_pairs={{0,16},{8,24},{16,0},{24,8},{1,17},{9,25},{17,1},{25,9},{2,18},{10... | collective-permute-start | bytes 3145736 | tf_op jit(solution)/shard_map/ppermute | solution.py:24
  719.0 49.1 %collective-permute-start.34 = (bf16[256,2048]{1,0:T(8,128)(2,1)}, bf16[256,2048]{1,0:T(8,128)(2,1)S(1)}, u32[]{:S(2)}, u32[]{:S(2)}) collective-permute-start(bf16[256,2048]{1,0:T(8,128)(2,1)} %broadcast_add_fusion.12), channel_id=1, source_target_pairs={{0,24},{8,16},{16,8},{24,0},{1,25},{9,17},{17,9},{25,1},{2,26},{10... | collective-permute-start | bytes 3145736 | tf_op jit(solution)/shard_map/ppermute | solution.py:24
  755.9 57.0 %collective-permute-start.32 = (bf16[256,2048]{1,0:T(8,128)(2,1)}, bf16[256,2048]{1,0:T(8,128)(2,1)}, u32[]{:S(2)}, u32[]{:S(2)}) collective-permute-start(bf16[256,2048]{1,0:T(8,128)(2,1)} %get-tuple-element.54), channel_id=1, source_target_pairs={{0,16},{8,24},{16,0},{24,8},{1,17},{9,25},{17,1},{25,9},{2,18},{10... | collective-permute-start | bytes 3145736 | tf_op jit(solution)/shard_map/ppermute | solution.py:24
  846.4 310.5 %reduce-scatter.6.cloned.1.call-start = ((), (), s32[]{:S(2)}) async-start(), calls=%async_computation.11 | async-start | bytes 18874368 | tf_op jit(solution)/shard_map/reduce_scatter | solution.py:642
  928.8 430.8 %reduce-scatter.8.cloned.1.call-start = ((), (), s32[]{:S(2)}) async-start(), calls=%async_computation.12 | async-start | bytes 18874368 | tf_op jit(solution)/shard_map/reduce_scatter | solution.py:642
  998.1 116.4 %all-to-all-start = ((bf16[4,256,1024]{2,1,0:T(8,128)(2,1)}), bf16[4,256,1024]{2,1,0:T(8,128)(2,1)}, u32[]{:S(2)}, u32[]{:S(2)}) async-start(bf16[4,256,1024]{2,1,0:T(8,128)(2,1)} %bitcast.464), calls=%async_computation.1 | async-start | bytes 4194304 | tf_op jit(solution)/shard_map/all_to_all | solution.py:51
  1033.5 48.8 %collective-permute-start.40 = (bf16[256,2048]{1,0:T(8,128)(2,1)}, bf16[256,2048]{1,0:T(8,128)(2,1)}, u32[]{:S(2)}, u32[]{:S(2)}) collective-permute-start(bf16[256,2048]{1,0:T(8,128)(2,1)} %get-tuple-element.109), channel_id=1, source_target_pairs={{0,1},{1,0},{2,3},{3,2},{4,5},{5,4},{6,7},{7,6},{8,9},{9,8},{10,11... | collective-permute-start | bytes 3145736 | tf_op jit(solution)/shard_map/ppermute | solution.py:24
  1035.5 51.6 %collective-permute-start.41 = (bf16[256,2048]{1,0:T(8,128)(2,1)}, bf16[256,2048]{1,0:T(8,128)(2,1)S(1)}, u32[]{:S(2)}, u32[]{:S(2)}) collective-permute-start(bf16[256,2048]{1,0:T(8,128)(2,1)} %get-tuple-element.109), channel_id=1, source_target_pairs={{0,2},{1,3},{2,0},{3,1},{4,6},{5,7},{6,4},{7,5},{8,10},{9,11},{10,... | collective-permute-start | bytes 3145736 | tf_op jit(solution)/shard_map/ppermute | solution.py:24
  1035.5 76.8 %collective-permute-start.42 = (bf16[256,2048]{1,0:T(8,128)(2,1)}, bf16[256,2048]{1,0:T(8,128)(2,1)S(1)}, u32[]{:S(2)}, u32[]{:S(2)}) collective-permute-start(bf16[256,2048]{1,0:T(8,128)(2,1)} %get-tuple-element.109), channel_id=1, source_target_pairs={{0,3},{1,2},{2,1},{3,0},{4,7},{5,6},{6,5},{7,4},{8,11},{9,10},{10,... | collective-permute-start | bytes 3145736 | tf_op jit(solution)/shard_map/ppermute | solution.py:24
  1156.8 99.4 %all-to-all-start.1 = ((bf16[4,256,1024]{2,1,0:T(8,128)(2,1)}), bf16[4,256,1024]{2,1,0:T(8,128)(2,1)}, u32[]{:S(2)}, u32[]{:S(2)}) async-start(bf16[4,256,1024]{2,1,0:T(8,128)(2,1)} %bitcast.463), calls=%async_computation.3 | async-start | bytes 4194304 | tf_op jit(solution)/shard_map/all_to_all | solution.py:51
  1169.9 53.7 %collective-permute-start.50 = (bf16[256,2048]{1,0:T(8,128)(2,1)}, bf16[256,2048]{1,0:T(8,128)(2,1)}, u32[]{:S(2)}, u32[]{:S(2)}) collective-permute-start(bf16[256,2048]{1,0:T(8,128)(2,1)} %get-tuple-element.139), channel_id=1, source_target_pairs={{0,24},{8,16},{16,8},{24,0},{1,25},{9,17},{17,9},{25,1},{2,26},{10... | collective-permute-start | bytes 3145736 | tf_op jit(solution)/shard_map/ppermute | solution.py:24
  1173.7 126.6 %collective-permute-start.49 = (bf16[256,2048]{1,0:T(8,128)(2,1)}, bf16[256,2048]{1,0:T(8,128)(2,1)}, u32[]{:S(2)}, u32[]{:S(2)}) collective-permute-start(bf16[256,2048]{1,0:T(8,128)(2,1)} %get-tuple-element.138), channel_id=1, source_target_pairs={{0,16},{8,24},{16,0},{24,8},{1,17},{9,25},{17,1},{25,9},{2,18},{10... | collective-permute-start | bytes 3145736 | tf_op jit(solution)/shard_map/ppermute | solution.py:24
  1173.7 126.6 %collective-permute-start.48 = (bf16[256,2048]{1,0:T(8,128)(2,1)}, bf16[256,2048]{1,0:T(8,128)(2,1)}, u32[]{:S(2)}, u32[]{:S(2)}) collective-permute-start(bf16[256,2048]{1,0:T(8,128)(2,1)} %get-tuple-element.137), channel_id=1, source_target_pairs={{0,8},{8,0},{16,24},{24,16},{1,9},{9,1},{17,25},{25,17},{2,10},{10... | collective-permute-start | bytes 3145736 | tf_op jit(solution)/shard_map/ppermute | solution.py:24
  1199.9 108.1 %collective-permute-start.60 = (bf16[256,2048]{1,0:T(8,128)(2,1)}, bf16[256,2048]{1,0:T(8,128)(2,1)}, u32[]{:S(2)}, u32[]{:S(2)}) collective-permute-start(bf16[256,2048]{1,0:T(8,128)(2,1)} %get-tuple-element.135), channel_id=1, source_target_pairs={{0,3},{1,2},{2,1},{3,0},{4,7},{5,6},{6,5},{7,4},{8,11},{9,10},{10,... | collective-permute-start | bytes 3145736 | tf_op jit(solution)/shard_map/ppermute | solution.py:24
  1199.9 111.1 %collective-permute-start.59 = (bf16[256,2048]{1,0:T(8,128)(2,1)}, bf16[256,2048]{1,0:T(8,128)(2,1)}, u32[]{:S(2)}, u32[]{:S(2)}) collective-permute-start(bf16[256,2048]{1,0:T(8,128)(2,1)} %get-tuple-element.136), channel_id=1, source_target_pairs={{0,2},{1,3},{2,0},{3,1},{4,6},{5,7},{6,4},{7,5},{8,10},{9,11},{10,... | collective-permute-start | bytes 3145736 | tf_op jit(solution)/shard_map/ppermute | solution.py:24
  1223.6 87.3 %collective-permute-start.58 = (bf16[256,2048]{1,0:T(8,128)(2,1)}, bf16[256,2048]{1,0:T(8,128)(2,1)}, u32[]{:S(2)}, u32[]{:S(2)}) collective-permute-start(bf16[256,2048]{1,0:T(8,128)(2,1)} %get-tuple-element.134), channel_id=1, source_target_pairs={{0,1},{1,0},{2,3},{3,2},{4,5},{5,4},{6,7},{7,6},{8,9},{9,8},{10,11... | collective-permute-start | bytes 3145736 | tf_op jit(solution)/shard_map/ppermute | solution.py:24
  1362.7 53.6 %all-to-all-start.2 = ((bf16[4,256,1024]{2,1,0:T(8,128)(2,1)}), bf16[4,256,1024]{2,1,0:T(8,128)(2,1)}, u32[]{:S(2)}, u32[]{:S(2)}) async-start(bf16[4,256,1024]{2,1,0:T(8,128)(2,1)} %bitcast.190), calls=%async_computation.5 | async-start | bytes 4194304 | tf_op jit(solution)/shard_map/all_to_all | solution.py:51
  (129 other events, 1879.7 us)
Sparse Core Ops, SparseCore 0:
  101.4 92.9 all-gather.4
  196.8 89.8 all-gather.6
  349.2 136.0 all-gather.8
  487.0 91.8 all-gather.10
  846.5 135.1 reduce-scatter.3
  985.1 156.6 reduce-scatter.5
  1145.3 160.7 reduce-scatter.7

commit v12 on v11

--- a/solution.py
+++ b/solution.py
@@ -546,9 +546,8 @@
     w_up = gather_plane(up_ready)
     in_blocks = gather_near(after(mine, up_ready), "z")
     seq_factor = rms_factor(seq_tokens)
-    w_in = stack_rows(in_blocks, token(seq_factor, w_gate))
+    w_in = stack_rows(in_blocks, token(seq_factor))
     w_in_other = send(w_in, "c", 1)
-    down_blocks = expert_chunk(2, token(w_in))
 
     side = whole_of(w_in[:, 4 * cols :], w_in_other[:, 4 * cols :], 0)[:, :6].astype(f32).T
     gain_in, gain_mid = side[0], side[1]
@@ -595,11 +594,9 @@
     q_mean, k_mean = over_heads(
         jnp.sum(query_raw * query_raw, axis=-1), jnp.sum(key_raw * key_raw, axis=-1)
     )
-    down_ready = in_order(down_blocks, "z", token(projected))
-    w_down = gather_plane(down_ready)
     cosine, sine = rope_tables(seq)
     shared = [
-        after(q_mean, w_out, down_ready),
+        after(q_mean, w_gate, w_out),
         k_mean,
         gain_q[None],
         gain_k[None],
@@ -609,9 +606,20 @@
         segment[None],
     ]
     attended, query, keyed, valued, log_total = attend(projected, shared, heads)
+    start = token(attended)
+    down_blocks = exchange(
+        lambda owner: lax.dynamic_slice(
+            w_expert, (0, owner, 2 * hidden), (part, 1, hidden)
+        )[:, 0],
+        "z",
+        start,
+    )
     attn_out = dot("tc,dc->td", attended, w_out).astype(bf16)
     got = exchange_sum(attn_out.reshape(seqs, own, width), "s")
     residual = inputs + got
+    down_ready = in_order(down_blocks, "z", token(residual))
+    residual = after(residual, down_ready)
+    w_down = gather_plane(down_ready)
 
     normed_mid = (residual * rms_factor(residual) * gain_mid).astype(bf16)
     expert_weights = (w_gate, w_up, w_down)
@@ -703,8 +711,9 @@
     )
     grad_normed = exchange_sum(grad_normed.reshape(seqs, own, width), "s")
     grad_normed = whole_of(grad_normed[:, : width // 2], grad_normed[:, width // 2 :], 1)
-    grad_attn = after(exchange_sum(summed, "z"), gate_ready).astype(bf16)
-    up_ready = swap(after(grad_w_up, grad_attn), "z")
+    row_blocks = exchange_by_rank(summed, "z")
+    grad_attn = after(total(row_blocks), gate_ready).astype(bf16)
+    up_ready = swap(after(grad_w_up, row_blocks[1]), "z")
     grad_in_norm, gain_in_grad = norm_back(inputs, gain_in, grad_normed)
     grad_tokens = to_outer(grad_resid + grad_in_norm)
 

time: 1460 us -> 1410 us (0.966)
  waiting for transfers between devices: 573 us -> 524 us
    ppermute x71, waiting for transfers between devices: 510 us -> 471 us  [send(): return lax.ppermute(block, axis, [(i, i ^ step) for i in range(size)])]
    dynamic_update_slice x29 -> x31, local copies, waits for them, and re-layouts: 36.6 us -> 41.9 us  [in_order(): lax.dynamic_update_index_in_dim(stacked, block, (rank ^ k) + start, 0)]
    slice x37 -> x38, local copies, waits for them, and re-layouts: 31.3 us -> 32 us  [token(): value[(slice(0, 1),) * value.ndim].reshape(()).astype(f32)]
  transfers between devices with their start and end apart: 81 -> 81, of which waited for: 34 -> 31; matrix products, arithmetic and copies ran while one was open for 27% -> 28% of each run, Pallas kernels for 12% -> 12%
where the time goes in v12:
time: 1410 us; the launch traced here: 1400 us
  waiting for transfers between devices  524 us (37%)
  local copies, waits for them, and re-layouts  229 us (16%)
  starting transfers between devices  172 us (12%)
  Pallas kernels  172 us (12%)
  other arithmetic  131 us (9%)
  matrix products  109 us (8%)
  between operations  66 us (5%)
    ppermute x71, waiting for transfers between devices, send(): return lax.ppermute(block, axis, [(i, i ^ step) for i in range(size)])  471 us
    ppermute x71, starting transfers between devices, send(): return lax.ppermute(block, axis, [(i, i ^ step) for i in range(size)])  157 us
    pallas_call x6, Pallas kernels, run(): pl.pallas_call(functools.partial(kernel, self.count, self.slots), grid=(s...  136 us
    dot_general x10, matrix products, dot(): return jnp.einsum(spec, left, right, preferred_element_type=f32)  96.9 us
    unnamed x182, local copies, waits for them, and re-layouts  62.2 us
    all_to_all x3, waiting for transfers between devices, swap(): return lax.all_to_all(pieces, axis, split_axis=0, concat_axis=0, tiled=True)  45 us
    dynamic_update_slice x31, local copies, waits for them, and re-layouts, in_order(): lax.dynamic_update_index_in_dim(stacked, block, (rank ^ k) + start, 0)  41.9 us
    add x21, other arithmetic, after(): return value + token(*others).astype(value.dtype)  40.8 us
  transfers between devices with their start and end apart: 81, of which 31 were waited for; matrix products, arithmetic and copies ran while one was open for 28% of the time, Pallas kernels for 12%

profile of v12, /device:TPU:0, one launch (start us, length us, event | category | flops | bytes accessed | tf_op | source)
XLA Modules:
  0.0 1402.1 jit_solution(5518092801603308747)
XLA Ops:
  43.6 18.8 %collective-permute-done.3 = bf16[256,1024]{1,0:T(8,128)(2,1)S(1)} collective-permute-done((bf16[256,1024]{1,0:T(8,128)(2,1)S(1)}, bf16[256,1024]{1,0:T(8,128)(2,1)S(1)}, u32[]{:S(2)}, u32[]{:S(2)}) %collective-permute-start.3) | collective-permute-done | bytes 524320 | tf_op jit(solution)/shard_map/ppermute | solution.py:24
  139.7 14.9 %collective-permute-done.10 = bf16[256,1024]{1,0:T(8,128)(2,1)} collective-permute-done((bf16[256,1024]{1,0:T(8,128)(2,1)}, bf16[256,1024]{1,0:T(8,128)(2,1)}, u32[]{:S(2)}, u32[]{:S(2)}) %collective-permute-start.10) | collective-permute-done | bytes 524320 | tf_op jit(solution)/shard_map/ppermute | solution.py:24
  181.4 39.8 %collective-permute-done.12 = bf16[256,2176]{1,0:T(8,128)(2,1)S(1)} collective-permute-done((bf16[256,2176]{1,0:T(8,128)(2,1)S(1)}, bf16[256,2176]{1,0:T(8,128)(2,1)S(1)}, u32[]{:S(2)}, u32[]{:S(2)}) %collective-permute-start.12) | collective-permute-done | bytes 1114144 | tf_op jit(solution)/shard_map/ppermute | solution.py:24
  222.3 29.1 %collective-permute-done.13 = bf16[256,2176]{1,0:T(8,128)(2,1)S(1)} collective-permute-done((bf16[256,2176]{1,0:T(8,128)(2,1)S(1)}, bf16[256,2176]{1,0:T(8,128)(2,1)S(1)}, u32[]{:S(2)}, u32[]{:S(2)}) %collective-permute-start.13) | collective-permute-done | bytes 1114144 | tf_op jit(solution)/shard_map/ppermute | solution.py:24
  294.2 17.7 %shard_map.145 = (bf16[1024,512]{1,0:T(8,128)(2,1)S(1)}, bf16[1024,512]{1,0:T(8,128)(2,1)S(1)}, bf16[1024,512]{1,0:T(8,128)(2,1)S(1)}, bf16[1024,512]{1,0:T(8,128)(2,1)}, f32[4,1024,1]{2,1,0:T(8,128)}) custom-call(f32[1024,1536]{1,0:T(8,128)} %copy-done.15, f32[1024,1536]{1,0:T(8,128)} %copy-done.15, f32[1024,1536]{1,0:T(8,128)} %copy-done.15, ...), custom_call_target="tpu_custom_call" | custom-call | flops 1000000 | bytes 100000 | tf_op jit(solution)/shard_map/pallas_call | solution.py:233
  325.2 21.8 %collective-permute-start.22 = (bf16[256,1024]{1,0:T(8,128)(2,1)}, bf16[256,1024]{1,0:T(8,128)(2,1)}, u32[]{:S(2)}, u32[]{:S(2)}) collective-permute-start(bf16[256,1024]{1,0:T(8,128)(2,1)} %get-tuple-element.122), channel_id=1, source_target_pairs={{0,8},{8,0},{16,24},{24,16},{1,9},{9,1},{17,25},{25,17},{2,10},{10... | collective-permute-start | bytes 1572872 | tf_op jit(solution)/shard_map/ppermute | solution.py:24
  349.6 15.9 %collective-permute-done.20 = bf16[256,2048]{1,0:T(8,128)(2,1)} collective-permute-done((bf16[256,2048]{1,0:T(8,128)(2,1)}, bf16[256,2048]{1,0:T(8,128)(2,1)}, u32[]{:S(2)}, u32[]{:S(2)}) %collective-permute-start.20) | collective-permute-done | bytes 1048608 | tf_op jit(solution)/shard_map/ppermute | solution.py:24
  390.7 19.3 %collective-permute-start.25 = (bf16[256,2048]{1,0:T(8,128)(2,1)}, bf16[256,2048]{1,0:T(8,128)(2,1)}, u32[]{:S(2)}, u32[]{:S(2)}) collective-permute-start(bf16[256,2048]{1,0:T(8,128)(2,1)} %multiply_convert_fusion.3.refs_0_), channel_id=1, source_target_pairs={{0,16},{8,24},{16,0},{24,8},{1,17},{9,25},{17,1},{25,9},{2,18},{10... | collective-permute-start | bytes 3145736 | tf_op jit(solution)/shard_map/ppermute | solution.py:24
  417.1 39.0 %collective-permute-done.25.refs_1_ = bf16[256,2048]{1,0:T(8,128)(2,1)} collective-permute-done((bf16[256,2048]{1,0:T(8,128)(2,1)}, bf16[256,2048]{1,0:T(8,128)(2,1)}, u32[]{:S(2)}, u32[]{:S(2)}) %collective-permute-start.25) | collective-permute-done | bytes 1048608 | tf_op jit(solution)/shard_map/ppermute | solution.py:24
  462.6 20.9 %shard_map.146 = (bf16[4,2,288,2048]{3,2,1,0:T(8,128)(2,1)}, bf16[4,2,288,1024]{3,2,1,0:T(8,128)(2,1)}, bf16[4,288,1024]{2,1,0:T(8,128)(2,1)}, bf16[4,288,1024]{2,1,0:T(8,128)(2,1)}) custom-call(s32[4,4,1,256]{3,2,1,0:T(1,128)} %pad_add_fusion.place, bf16[256,2048]{1,0:T(8,128)(2,1)} %multiply_convert_fusion.3.refs_0_, ...), custom_call_target="tpu_custom_call" | custom-call | flops 9663676416 | bytes 50331648 | tf_op jit(solution)/shard_map/pallas_call | solution.py:368
  491.1 14.8 %shard_map.147 = (bf16[256,2048]{1,0:T(8,128)(2,1)}, bf16[256,2048]{1,0:T(8,128)(2,1)}) custom-call(s32[4,4,1,256]{3,2,1,0:T(1,128)} %pad_add_fusion.place, f32[4,4,1,256]{3,2,1,0:T(1,128)} %pad_maximum_fusion.9.gate, bf16[4,2,288,1024]{3,2,1,0:T(8,128)(2,1)} %get-tuple-element.41.activated.refs_5_, bf16[4,2048,1024]{2,1,0:T(8,128)(2,1)} %bitcast.414), custom_call_target="tpu_custom_call" | custom-call | flops 9663676416 | bytes 50331648 | tf_op jit(solution)/shard_map/pallas_call | solution.py:368
  513.1 20.7 %shard_map.148 = (bf16[4,2,288,2048]{3,2,1,0:T(8,128)(2,1)}, bf16[4,2,288,1024]{3,2,1,0:T(8,128)(2,1)}, bf16[4,288,1024]{2,1,0:T(8,128)(2,1)}, bf16[4,288,1024]{2,1,0:T(8,128)(2,1)}) custom-call(s32[4,4,1,256]{3,2,1,0:T(1,128)} %pad_add_fusion.place, bf16[256,2048]{1,0:T(8,128)(2,1)} %broadcast_add_fusion.15.refs_0_, ...), custom_call_target="tpu_custom_call", output_to_operand_aliasing={{0}: (5, {}), {1}: (6, {})} | custom-call | flops 9663676416 | bytes 50331648 | tf_op jit(solution)/shard_map/pallas_call | solution.py:368
  533.8 14.9 %shard_map.149 = (bf16[256,2048]{1,0:T(8,128)(2,1)}, bf16[256,2048]{1,0:T(8,128)(2,1)}) custom-call(s32[4,4,1,256]{3,2,1,0:T(1,128)} %pad_add_fusion.place, f32[4,4,1,256]{3,2,1,0:T(1,128)} %pad_maximum_fusion.9.gate, bf16[4,2,288,1024]{3,2,1,0:T(8,128)(2,1)} %get-tuple-element.45.activated, bf16[4,2048,1024]{2,1,0:T(8,128)(2,1)} %bitcast.415), custom_call_target="tpu_custom_call" | custom-call | flops 9663676416 | bytes 50331648 | tf_op jit(solution)/shard_map/pallas_call | solution.py:368
  592.7 19.2 %collective-permute-done.29 = bf16[256,2048]{1,0:T(8,128)(2,1)} collective-permute-done((bf16[256,2048]{1,0:T(8,128)(2,1)}, bf16[256,2048]{1,0:T(8,128)(2,1)}, u32[]{:S(2)}, u32[]{:S(2)}) %collective-permute-start.29) | collective-permute-done | bytes 1048608 | tf_op jit(solution)/shard_map/ppermute | solution.py:24
  620.0 47.9 %collective-permute-done.31.refs_1_ = bf16[256,2048]{1,0:T(8,128)(2,1)S(1)} collective-permute-done((bf16[256,2048]{1,0:T(8,128)(2,1)S(1)}, bf16[256,2048]{1,0:T(8,128)(2,1)S(1)}, u32[]{:S(2)}, u32[]{:S(2)}) %collective-permute-start.31) | collective-permute-done | bytes 1048608 | tf_op jit(solution)/shard_map/ppermute | solution.py:24
  671.8 32.0 %shard_map.150 = (bf16[4,2,288,2048]{3,2,1,0:T(8,128)(2,1)}, bf16[4,2,288,1024]{3,2,1,0:T(8,128)(2,1)}, bf16[4,2,288,1024]{3,2,1,0:T(8,128)(2,1)}, bf16[256,2048]{1,0:T(8,128)(2,1)}, bf16[256,2048]{1,0:T(8,128)(2,1)}) custom-call(s32[4,4,1,256]{3,2,1,0:T(1,128)} %pad_add_fusion.place, f32[4,4,1,256]{3,2,1,0:T(1,128)} %pad_maximum_fusion.9.gate, ...), custom_call_target="tpu_custom_call" | custom-call | flops 9663676416 | bytes 50331648 | tf_op jit(solution)/shard_map/pallas_call | solution.py:368
  721.3 32.2 %shard_map.151 = (bf16[4,2,288,2048]{3,2,1,0:T(8,128)(2,1)}, bf16[4,2,288,1024]{3,2,1,0:T(8,128)(2,1)}, bf16[4,2,288,1024]{3,2,1,0:T(8,128)(2,1)}, bf16[256,2048]{1,0:T(8,128)(2,1)}, bf16[256,2048]{1,0:T(8,128)(2,1)}) custom-call(s32[4,4,1,256]{3,2,1,0:T(1,128)} %pad_add_fusion.place, ...), custom_call_target="tpu_custom_call", output_to_operand_aliasing={{0}: (9, {}), {1}: (10, {}), {2}: (11, {})} | custom-call | flops 9663676416 | bytes 50331648 | tf_op jit(solution)/shard_map/pallas_call | solution.py:368
  777.0 20.7 %convolution_convert_fusion.2 = bf16[4,2048,1024]{2,1,0:T(8,128)(2,1)} fusion(bf16[4,576,2048]{2,1,0:T(8,128)(2,1)} %bitcast.430, bf16[4,576,1024]{2,1,0:T(8,128)(2,1)} %bitcast.444), kind=kOutput, calls=%fused_computation.2 | convolution fusion | flops 9672065024 | bytes 30932992 | tf_op jit(solution)/shard_map/krd,krf->kdf/dot_general | solution.py:405
  800.6 14.1 %collective-permute-start.35 = (bf16[256,2048]{1,0:T(8,128)(2,1)}, bf16[256,2048]{1,0:T(8,128)(2,1)S(1)}, u32[]{:S(2)}, u32[]{:S(2)}) collective-permute-start(bf16[256,2048]{1,0:T(8,128)(2,1)} %copy-done.62), channel_id=1, source_target_pairs={{0,8},{8,0},{16,24},{24,16},{1,9},{9,1},{17,25},{25,17},{2,10},{10... | collective-permute-start | bytes 3145736 | tf_op jit(solution)/shard_map/ppermute | solution.py:24
  827.3 19.9 %collective-permute-done.35 = bf16[256,2048]{1,0:T(8,128)(2,1)S(1)} collective-permute-done((bf16[256,2048]{1,0:T(8,128)(2,1)}, bf16[256,2048]{1,0:T(8,128)(2,1)S(1)}, u32[]{:S(2)}, u32[]{:S(2)}) %collective-permute-start.35) | collective-permute-done | bytes 1048608 | tf_op jit(solution)/shard_map/ppermute | solution.py:24
  857.7 21.0 %convolution_convert_fusion.1 = bf16[4,2048,1024]{2,1,0:T(8,128)(2,1)} fusion(bf16[4,576,2048]{2,1,0:T(8,128)(2,1)} %bitcast.435, bf16[4,576,1024]{2,1,0:T(8,128)(2,1)} %bitcast.445), kind=kOutput, calls=%fused_computation.1 | convolution fusion | flops 9672065024 | bytes 30932992 | tf_op jit(solution)/shard_map/krd,krf->kdf/dot_general | solution.py:405
  901.9 11.8 collective-permute-done.38
  924.7 22.3 %convolution_convert_fusion = bf16[4,2048,1024]{2,1,0:T(8,128)(2,1)} fusion(bf16[4,576,2048]{2,1,0:T(8,128)(2,1)} %bitcast.436, bf16[4,576,1024]{2,1,0:T(8,128)(2,1)} %bitcast.446), kind=kOutput, calls=%fused_computation | convolution fusion | flops 9672065024 | bytes 30932992 | tf_op jit(solution)/shard_map/krd,krf->kdf/dot_general | solution.py:405
  957.0 18.9 %shard_map.152 = (f32[1024,512]{1,0:T(8,128)}, f32[1024,512]{1,0:T(8,128)}, bf16[1024,512]{1,0:T(8,128)(2,1)S(1)}, f32[1024,1]{1,0:T(8,128)S(1)}, f32[1024,1]{1,...) custom-call(f32[1024,1536]{1,0:T(8,128)} %copy-done.15, f32[1024,1536]{1,0:T(8,128)} %copy-done.15, ...), custom_call_target="tpu_custom_call" | custom-call | flops 1000000 | bytes 100000 | tf_op jit(solution)/shard_map/pallas_call | solution.py:251
  988.8 45.1 %collective-permute-done.40 = bf16[256,2048]{1,0:T(8,128)(2,1)} collective-permute-done((bf16[256,2048]{1,0:T(8,128)(2,1)}, bf16[256,2048]{1,0:T(8,128)(2,1)}, u32[]{:S(2)}, u32[]{:S(2)}) %collective-permute-start.40) | collective-permute-done | bytes 1048608 | tf_op jit(solution)/shard_map/ppermute | solution.py:24
  1037.3 26.7 %collective-permute-done.42 = bf16[256,2048]{1,0:T(8,128)(2,1)S(1)} collective-permute-done((bf16[256,2048]{1,0:T(8,128)(2,1)}, bf16[256,2048]{1,0:T(8,128)(2,1)S(1)}, u32[]{:S(2)}, u32[]{:S(2)}) %collective-permute-start.42) | collective-permute-done | bytes 1048608 | tf_op jit(solution)/shard_map/ppermute | solution.py:24
  1151.5 23.8 %collective-permute-done.50 = bf16[256,2048]{1,0:T(8,128)(2,1)} collective-permute-done((bf16[256,2048]{1,0:T(8,128)(2,1)}, bf16[256,2048]{1,0:T(8,128)(2,1)}, u32[]{:S(2)}, u32[]{:S(2)}) %collective-permute-start.50) | collective-permute-done | bytes 1048608 | tf_op jit(solution)/shard_map/ppermute | solution.py:24
  1187.1 21.0 %all-to-all-done.1 = bf16[4,256,1024]{2,1,0:T(8,128)(2,1)} async-done(((bf16[4,256,1024]{2,1,0:T(8,128)(2,1)}), bf16[4,256,1024]{2,1,0:T(8,128)(2,1)}, u32[]{:S(2)}, u32[]{:S(2)}) %all-to-all-start.1) | async-done | bytes 2097184 | tf_op jit(solution)/shard_map/all_to_all | solution.py:51
  1210.5 41.5 %collective-permute-done.49 = bf16[256,2048]{1,0:T(8,128)(2,1)} collective-permute-done((bf16[256,2048]{1,0:T(8,128)(2,1)}, bf16[256,2048]{1,0:T(8,128)(2,1)}, u32[]{:S(2)}, u32[]{:S(2)}) %collective-permute-start.49) | collective-permute-done | bytes 1048608 | tf_op jit(solution)/shard_map/ppermute | solution.py:24
  1275.9 14.1 %collective-permute-start.65 = (f32[4,2048]{1,0:T(4,128)S(1)}, f32[4,2048]{1,0:T(4,128)S(1)}, u32[]{:S(2)}, u32[]{:S(2)}) collective-permute-start(f32[4,2048]{1,0:T(4,128)S(1)} %maximum_add_fusion.1), channel_id=1, source_target_pairs={{0,16},{8,24},{16,0},{24,8},{1,17},{9,25},{17,1},{25,9},{2,18},{10... | collective-permute-start | bytes 98312 | tf_op jit(solution)/shard_map/ppermute | solution.py:24
  1346.7 24.0 %all-to-all-done.2 = bf16[4,256,1024]{2,1,0:T(8,128)(2,1)} async-done(((bf16[4,256,1024]{2,1,0:T(8,128)(2,1)}), bf16[4,256,1024]{2,1,0:T(8,128)(2,1)}, u32[]{:S(2)}, u32[]{:S(2)}) %all-to-all-start.2) | async-done | bytes 2097184 | tf_op jit(solution)/shard_map/all_to_all | solution.py:51
  1374.4 19.3 %copy.155 = f32[256,4,3072]{2,1,0:T(4,128)} copy(f32[256,4,3072]{2,0,1:T(8,128)S(1)} %convert_bitcast_fusion) | data formatting | bytes 25165824
  (585 shorter events, 572.9 us)
Async XLA Ops:
  7.2 283.4 %all-gather.5.cloned.1.call-start = ((), (), s32[]{:S(2)}) async-start(), calls=%async_computation.6 | async-start | bytes 18874368 | tf_op jit(solution)/shard_map/all_gather | solution.py:478
  23.8 57.0 %collective-permute-start = (bf16[328,2048]{1,0:T(8,128)(2,1)}, bf16[328,2048]{1,0:T(8,128)(2,1)}, u32[]{:S(2)}, u32[]{:S(2)}) collective-permute-start(bf16[328,2048]{1,0:T(8,128)(2,1)} %get-tuple-element.147), channel_id=1, source_target_pairs={{0,1},{1,0},{2,3},{3,2},{4,5},{5,4},{6,7},{7,6},{8,9},{9,8},{10,11... | collective-permute-start | bytes 4030472 | tf_op jit(solution)/shard_map/ppermute | solution.py:24
  26.7 60.0 %collective-permute-start.1 = (bf16[328,2048]{1,0:T(8,128)(2,1)}, bf16[328,2048]{1,0:T(8,128)(2,1)}, u32[]{:S(2)}, u32[]{:S(2)}) collective-permute-start(bf16[328,2048]{1,0:T(8,128)(2,1)} %get-tuple-element.148), channel_id=1, source_target_pairs={{0,2},{1,3},{2,0},{3,1},{4,6},{5,7},{6,4},{7,5},{8,10},{9,11},{10,... | collective-permute-start | bytes 4030472 | tf_op jit(solution)/shard_map/ppermute | solution.py:24
  28.2 59.3 %collective-permute-start.2 = (bf16[328,2048]{1,0:T(8,128)(2,1)}, bf16[328,2048]{1,0:T(8,128)(2,1)}, u32[]{:S(2)}, u32[]{:S(2)}) collective-permute-start(bf16[328,2048]{1,0:T(8,128)(2,1)} %get-tuple-element.146), channel_id=1, source_target_pairs={{0,3},{1,2},{2,1},{3,0},{4,7},{5,6},{6,5},{7,4},{8,11},{9,10},{10,... | collective-permute-start | bytes 4030472 | tf_op jit(solution)/shard_map/ppermute | solution.py:24
  101.3 310.0 %all-gather.7.cloned.1.call-start = ((), (), s32[]{:S(2)}) async-start(), calls=%async_computation.7 | async-start | bytes 18874368 | tf_op jit(solution)/shard_map/all_gather | solution.py:478
  158.1 333.0 %all-gather.9.cloned.1.call-start = ((), (), s32[]{:S(2)}) async-start(), calls=%async_computation.8 | async-start | bytes 18874368 | tf_op jit(solution)/shard_map/all_gather | solution.py:478
  166.3 54.9 %collective-permute-start.12 = (bf16[256,2176]{1,0:T(8,128)(2,1)S(1)}, bf16[256,2176]{1,0:T(8,128)(2,1)S(1)}, u32[]{:S(2)}, u32[]{:S(2)}) collective-permute-start(bf16[256,2176]{1,0:T(8,128)(2,1)S(1)} %broadcast_add_fusion.5), channel_id=1, source_target_pairs={{0,8},{8,0},{16,24},{24,16},{1,9},{9,1},{17,25},{25,17},{2,10},{10... | collective-permute-start | bytes 3342344 | tf_op jit(solution)/shard_map/ppermute | solution.py:24
  175.3 76.2 %collective-permute-start.13 = (bf16[256,2176]{1,0:T(8,128)(2,1)S(1)}, bf16[256,2176]{1,0:T(8,128)(2,1)S(1)}, u32[]{:S(2)}, u32[]{:S(2)}) collective-permute-start(bf16[256,2176]{1,0:T(8,128)(2,1)S(1)} %broadcast_add_fusion.5), channel_id=1, source_target_pairs={{0,16},{8,24},{16,0},{24,8},{1,17},{9,25},{17,1},{25,9},{2,18},{10... | collective-permute-start | bytes 3342344 | tf_op jit(solution)/shard_map/ppermute | solution.py:24
  175.3 77.2 %collective-permute-start.14 = (bf16[256,2176]{1,0:T(8,128)(2,1)S(1)}, bf16[256,2176]{1,0:T(8,128)(2,1)S(1)}, u32[]{:S(2)}, u32[]{:S(2)}) collective-permute-start(bf16[256,2176]{1,0:T(8,128)(2,1)S(1)} %broadcast_add_fusion.5), channel_id=1, source_target_pairs={{0,24},{8,16},{16,8},{24,0},{1,25},{9,17},{17,9},{25,1},{2,26},{10... | collective-permute-start | bytes 3342344 | tf_op jit(solution)/shard_map/ppermute | solution.py:24
  325.2 50.3 %collective-permute-start.22 = (bf16[256,1024]{1,0:T(8,128)(2,1)}, bf16[256,1024]{1,0:T(8,128)(2,1)}, u32[]{:S(2)}, u32[]{:S(2)}) collective-permute-start(bf16[256,1024]{1,0:T(8,128)(2,1)} %get-tuple-element.122), channel_id=1, source_target_pairs={{0,8},{8,0},{16,24},{24,16},{1,9},{9,1},{17,25},{25,17},{2,10},{10... | collective-permute-start | bytes 1572872 | tf_op jit(solution)/shard_map/ppermute | solution.py:24
  384.8 498.9 %all-gather.11.cloned.1.call-start = ((), (), s32[]{:S(2)}) async-start(), calls=%async_computation.9 | async-start | bytes 10485760 | tf_op jit(solution)/shard_map/all_gather | solution.py:640
  390.7 65.4 %collective-permute-start.25 = (bf16[256,2048]{1,0:T(8,128)(2,1)}, bf16[256,2048]{1,0:T(8,128)(2,1)}, u32[]{:S(2)}, u32[]{:S(2)}) collective-permute-start(bf16[256,2048]{1,0:T(8,128)(2,1)} %multiply_convert_fusion.3.refs_0_), channel_id=1, source_target_pairs={{0,16},{8,24},{16,0},{24,8},{1,17},{9,25},{17,1},{25,9},{2,18},{10... | collective-permute-start | bytes 3145736 | tf_op jit(solution)/shard_map/ppermute | solution.py:24
  417.1 532.5 %reduce-scatter.4.cloned.1.call-start = ((), (), s32[]{:S(2)}) async-start(), calls=%async_computation.10 | async-start | bytes 18874368 | tf_op jit(solution)/shard_map/reduce_scatter | solution.py:650
  461.6 49.3 %collective-permute-start.27 = (bf16[256,2048]{1,0:T(8,128)(2,1)}, bf16[256,2048]{1,0:T(8,128)(2,1)}, u32[]{:S(2)}, u32[]{:S(2)}) collective-permute-start(bf16[256,2048]{1,0:T(8,128)(2,1)} %broadcast_add_fusion.16), channel_id=1, source_target_pairs={{0,8},{8,0},{16,24},{24,16},{1,9},{9,1},{17,25},{25,17},{2,10},{10... | collective-permute-start | bytes 3145736 | tf_op jit(solution)/shard_map/ppermute | solution.py:24
  461.6 51.5 %collective-permute-start.28 = (bf16[256,2048]{1,0:T(8,128)(2,1)}, bf16[256,2048]{1,0:T(8,128)(2,1)}, u32[]{:S(2)}, u32[]{:S(2)}) collective-permute-start(bf16[256,2048]{1,0:T(8,128)(2,1)} %broadcast_add_fusion.16), channel_id=1, source_target_pairs={{0,24},{8,16},{16,8},{24,0},{1,25},{9,17},{17,9},{25,1},{2,26},{10... | collective-permute-start | bytes 3145736 | tf_op jit(solution)/shard_map/ppermute | solution.py:24
  508.4 49.0 %collective-permute-start.26 = (bf16[256,2048]{1,0:T(8,128)(2,1)}, bf16[256,2048]{1,0:T(8,128)(2,1)S(1)}, u32[]{:S(2)}, u32[]{:S(2)}) collective-permute-start(bf16[256,2048]{1,0:T(8,128)(2,1)} %get-tuple-element.43), channel_id=1, source_target_pairs={{0,16},{8,24},{16,0},{24,8},{1,17},{9,25},{17,1},{25,9},{2,18},{10... | collective-permute-start | bytes 3145736 | tf_op jit(solution)/shard_map/ppermute | solution.py:24
  670.8 49.5 %collective-permute-start.34 = (bf16[256,2048]{1,0:T(8,128)(2,1)}, bf16[256,2048]{1,0:T(8,128)(2,1)S(1)}, u32[]{:S(2)}, u32[]{:S(2)}) collective-permute-start(bf16[256,2048]{1,0:T(8,128)(2,1)} %broadcast_add_fusion.12), channel_id=1, source_target_pairs={{0,24},{8,16},{16,8},{24,0},{1,25},{9,17},{17,9},{25,1},{2,26},{10... | collective-permute-start | bytes 3145736 | tf_op jit(solution)/shard_map/ppermute | solution.py:24
  706.3 58.2 %collective-permute-start.32 = (bf16[256,2048]{1,0:T(8,128)(2,1)}, bf16[256,2048]{1,0:T(8,128)(2,1)}, u32[]{:S(2)}, u32[]{:S(2)}) collective-permute-start(bf16[256,2048]{1,0:T(8,128)(2,1)} %get-tuple-element.54), channel_id=1, source_target_pairs={{0,16},{8,24},{16,0},{24,8},{1,17},{9,25},{17,1},{25,9},{2,18},{10... | collective-permute-start | bytes 3145736 | tf_op jit(solution)/shard_map/ppermute | solution.py:24
  797.8 310.8 %reduce-scatter.6.cloned.1.call-start = ((), (), s32[]{:S(2)}) async-start(), calls=%async_computation.11 | async-start | bytes 18874368 | tf_op jit(solution)/shard_map/reduce_scatter | solution.py:650
  878.7 435.4 %reduce-scatter.8.cloned.1.call-start = ((), (), s32[]{:S(2)}) async-start(), calls=%async_computation.12 | async-start | bytes 18874368 | tf_op jit(solution)/shard_map/reduce_scatter | solution.py:650
  949.6 116.6 %all-to-all-start = ((bf16[4,256,1024]{2,1,0:T(8,128)(2,1)}), bf16[4,256,1024]{2,1,0:T(8,128)(2,1)}, u32[]{:S(2)}, u32[]{:S(2)}) async-start(bf16[4,256,1024]{2,1,0:T(8,128)(2,1)} %bitcast.461), calls=%async_computation.1 | async-start | bytes 4194304 | tf_op jit(solution)/shard_map/all_to_all | solution.py:51
  985.1 48.8 %collective-permute-start.40 = (bf16[256,2048]{1,0:T(8,128)(2,1)}, bf16[256,2048]{1,0:T(8,128)(2,1)}, u32[]{:S(2)}, u32[]{:S(2)}) collective-permute-start(bf16[256,2048]{1,0:T(8,128)(2,1)} %get-tuple-element.109), channel_id=1, source_target_pairs={{0,1},{1,0},{2,3},{3,2},{4,5},{5,4},{6,7},{7,6},{8,9},{9,8},{10,11... | collective-permute-start | bytes 3145736 | tf_op jit(solution)/shard_map/ppermute | solution.py:24
  985.1 51.1 %collective-permute-start.41 = (bf16[256,2048]{1,0:T(8,128)(2,1)}, bf16[256,2048]{1,0:T(8,128)(2,1)S(1)}, u32[]{:S(2)}, u32[]{:S(2)}) collective-permute-start(bf16[256,2048]{1,0:T(8,128)(2,1)} %get-tuple-element.109), channel_id=1, source_target_pairs={{0,2},{1,3},{2,0},{3,1},{4,6},{5,7},{6,4},{7,5},{8,10},{9,11},{10,... | collective-permute-start | bytes 3145736 | tf_op jit(solution)/shard_map/ppermute | solution.py:24
  985.1 78.8 %collective-permute-start.42 = (bf16[256,2048]{1,0:T(8,128)(2,1)}, bf16[256,2048]{1,0:T(8,128)(2,1)S(1)}, u32[]{:S(2)}, u32[]{:S(2)}) collective-permute-start(bf16[256,2048]{1,0:T(8,128)(2,1)} %get-tuple-element.109), channel_id=1, source_target_pairs={{0,3},{1,2},{2,1},{3,0},{4,7},{5,6},{6,5},{7,4},{8,11},{9,10},{10,... | collective-permute-start | bytes 3145736 | tf_op jit(solution)/shard_map/ppermute | solution.py:24
  1108.6 99.5 %all-to-all-start.1 = ((bf16[4,256,1024]{2,1,0:T(8,128)(2,1)}), bf16[4,256,1024]{2,1,0:T(8,128)(2,1)}, u32[]{:S(2)}, u32[]{:S(2)}) async-start(bf16[4,256,1024]{2,1,0:T(8,128)(2,1)} %bitcast.460), calls=%async_computation.3 | async-start | bytes 4194304 | tf_op jit(solution)/shard_map/all_to_all | solution.py:51
  1121.7 53.7 %collective-permute-start.50 = (bf16[256,2048]{1,0:T(8,128)(2,1)}, bf16[256,2048]{1,0:T(8,128)(2,1)}, u32[]{:S(2)}, u32[]{:S(2)}) collective-permute-start(bf16[256,2048]{1,0:T(8,128)(2,1)} %get-tuple-element.138), channel_id=1, source_target_pairs={{0,24},{8,16},{16,8},{24,0},{1,25},{9,17},{17,9},{25,1},{2,26},{10... | collective-permute-start | bytes 3145736 | tf_op jit(solution)/shard_map/ppermute | solution.py:24
  1125.5 126.6 %collective-permute-start.49 = (bf16[256,2048]{1,0:T(8,128)(2,1)}, bf16[256,2048]{1,0:T(8,128)(2,1)}, u32[]{:S(2)}, u32[]{:S(2)}) collective-permute-start(bf16[256,2048]{1,0:T(8,128)(2,1)} %get-tuple-element.137), channel_id=1, source_target_pairs={{0,16},{8,24},{16,0},{24,8},{1,17},{9,25},{17,1},{25,9},{2,18},{10... | collective-permute-start | bytes 3145736 | tf_op jit(solution)/shard_map/ppermute | solution.py:24
  1125.5 126.6 %collective-permute-start.48 = (bf16[256,2048]{1,0:T(8,128)(2,1)}, bf16[256,2048]{1,0:T(8,128)(2,1)}, u32[]{:S(2)}, u32[]{:S(2)}) collective-permute-start(bf16[256,2048]{1,0:T(8,128)(2,1)} %get-tuple-element.136), channel_id=1, source_target_pairs={{0,8},{8,0},{16,24},{24,16},{1,9},{9,1},{17,25},{25,17},{2,10},{10... | collective-permute-start | bytes 3145736 | tf_op jit(solution)/shard_map/ppermute | solution.py:24
  1151.5 108.2 %collective-permute-start.60 = (bf16[256,2048]{1,0:T(8,128)(2,1)}, bf16[256,2048]{1,0:T(8,128)(2,1)}, u32[]{:S(2)}, u32[]{:S(2)}) collective-permute-start(bf16[256,2048]{1,0:T(8,128)(2,1)} %get-tuple-element.134), channel_id=1, source_target_pairs={{0,3},{1,2},{2,1},{3,0},{4,7},{5,6},{6,5},{7,4},{8,11},{9,10},{10,... | collective-permute-start | bytes 3145736 | tf_op jit(solution)/shard_map/ppermute | solution.py:24
  1151.5 111.2 %collective-permute-start.59 = (bf16[256,2048]{1,0:T(8,128)(2,1)}, bf16[256,2048]{1,0:T(8,128)(2,1)}, u32[]{:S(2)}, u32[]{:S(2)}) collective-permute-start(bf16[256,2048]{1,0:T(8,128)(2,1)} %get-tuple-element.135), channel_id=1, source_target_pairs={{0,2},{1,3},{2,0},{3,1},{4,6},{5,7},{6,4},{7,5},{8,10},{9,11},{10,... | collective-permute-start | bytes 3145736 | tf_op jit(solution)/shard_map/ppermute | solution.py:24
  1175.4 87.4 %collective-permute-start.58 = (bf16[256,2048]{1,0:T(8,128)(2,1)}, bf16[256,2048]{1,0:T(8,128)(2,1)}, u32[]{:S(2)}, u32[]{:S(2)}) collective-permute-start(bf16[256,2048]{1,0:T(8,128)(2,1)} %get-tuple-element.133), channel_id=1, source_target_pairs={{0,1},{1,0},{2,3},{3,2},{4,5},{5,4},{6,7},{7,6},{8,9},{9,8},{10,11... | collective-permute-start | bytes 3145736 | tf_op jit(solution)/shard_map/ppermute | solution.py:24
  1317.1 53.6 %all-to-all-start.2 = ((bf16[4,256,1024]{2,1,0:T(8,128)(2,1)}), bf16[4,256,1024]{2,1,0:T(8,128)(2,1)}, u32[]{:S(2)}, u32[]{:S(2)}) async-start(bf16[4,256,1024]{2,1,0:T(8,128)(2,1)} %bitcast.191), calls=%async_computation.5 | async-start | bytes 4194304 | tf_op jit(solution)/shard_map/all_to_all | solution.py:51
  (129 other events, 1839.5 us)
Sparse Core Ops, SparseCore 0:
  101.4 92.9 all-gather.4
  196.8 89.8 all-gather.6
  385.0 106.0 all-gather.8
  492.8 87.6 all-gather.10
  797.9 134.9 reduce-scatter.3
  936.3 157.1 reduce-scatter.5
  1097.0 160.7 reduce-scatter.7

commit v13 on v12

--- a/solution.py
+++ b/solution.py
@@ -709,11 +709,14 @@
         [dot("tc,dc->td", late_proj, weight).astype(bf16) for weight in (w_qkv, w_qkv_other)],
         axis=1,
     )
-    grad_normed = exchange_sum(grad_normed.reshape(seqs, own, width), "s")
-    grad_normed = whole_of(grad_normed[:, : width // 2], grad_normed[:, width // 2 :], 1)
+    normed_blocks = exchange_by_rank(grad_normed.reshape(seqs, own, width), "s")
     row_blocks = exchange_by_rank(summed, "z")
     grad_attn = after(total(row_blocks), gate_ready).astype(bf16)
-    up_ready = swap(after(grad_w_up, row_blocks[1]), "z")
+    grad_w_up = after(grad_w_up, grad_attn)
+    up_ready = swap(grad_w_up, "z")
+    normed_blocks[0] = after(normed_blocks[0], grad_w_up)
+    grad_normed = total(normed_blocks)
+    grad_normed = whole_of(grad_normed[:, : width // 2], grad_normed[:, width // 2 :], 1)
     grad_in_norm, gain_in_grad = norm_back(inputs, gain_in, grad_normed)
     grad_tokens = to_outer(grad_resid + grad_in_norm)
 
@@ -722,8 +725,8 @@
         return to_inner(lax.dynamic_update_slice_in_dim(full, local, rank * cols, 0))
 
     gains = jnp.stack([gain_in_grad, gain_mid_grad, widen(gain_q_grad[0]), widen(gain_k_grad[0])])
-    gains = after(gains, grad_attn)
-    loss_value = gather_sum(after(squared, grad_attn)) / (total_count * width)
+    gains = after(gains, grad_w_up)
+    loss_value = gather_sum(after(squared, grad_w_up)) / (total_count * width)
     for axis in ("z", "c", "s", "o"):
         gains = sum(gather_near(gains, axis))
     row = (lax.axis_index(("c", "o", "z")) * seqs + rank) * rows_dev

time: 1410 us -> 1420 us (level)
    ppermute x71, waiting for transfers between devices: 471 us -> 497 us  [send(): return lax.ppermute(block, axis, [(i, i ^ step) for i in range(size)])]
    all_to_all x3, waiting for transfers between devices: 45 us -> 23.1 us  [swap(): return lax.all_to_all(pieces, axis, split_axis=0, concat_axis=0, tiled=True)]
    unnamed x182 -> x186, local copies, waits for them, and re-layouts: 62.2 us -> 63.5 us
  transfers between devices with their start and end apart: 81 -> 81, of which waited for: 31 -> 32; matrix products, arithmetic and copies ran while one was open for 28% -> 28% of each run, Pallas kernels for 12% -> 12%
where the time goes in v13:
time: 1420 us; the launch traced here: 1410 us
  waiting for transfers between devices  528 us (37%)
  local copies, waits for them, and re-layouts  230 us (16%)
  starting transfers between devices  177 us (12%)
  Pallas kernels  172 us (12%)
  other arithmetic  127 us (9%)
  matrix products  109 us (8%)
  between operations  66 us (5%)
    ppermute x71, waiting for transfers between devices, send(): return lax.ppermute(block, axis, [(i, i ^ step) for i in range(size)])  497 us
    ppermute x71, starting transfers between devices, send(): return lax.ppermute(block, axis, [(i, i ^ step) for i in range(size)])  163 us
    pallas_call x6, Pallas kernels, run(): pl.pallas_call(functools.partial(kernel, self.count, self.slots), grid=(s...  136 us
    dot_general x10, matrix products, dot(): return jnp.einsum(spec, left, right, preferred_element_type=f32)  96.8 us
    unnamed x186, local copies, waits for them, and re-layouts  63.5 us
    dynamic_update_slice x31, local copies, waits for them, and re-layouts, in_order(): lax.dynamic_update_index_in_dim(stacked, block, (rank ^ k) + start, 0)  41.9 us
    add x21, other arithmetic, after(): return value + token(*others).astype(value.dtype)  39.5 us
    slice x38, local copies, waits for them, and re-layouts, token(): value[(slice(0, 1),) * value.ndim].reshape(()).astype(f32)  31.3 us
  transfers between devices with their start and end apart: 81, of which 32 were waited for; matrix products, arithmetic and copies ran while one was open for 28% of the time, Pallas kernels for 12%

profile of v13, /device:TPU:0, one launch (start us, length us, event | category | flops | bytes accessed | tf_op | source)
XLA Modules:
  0.0 1409.3 jit_solution(9156418731733805898)
XLA Ops:
  43.6 18.8 %collective-permute-done.3 = bf16[256,1024]{1,0:T(8,128)(2,1)S(1)} collective-permute-done((bf16[256,1024]{1,0:T(8,128)(2,1)S(1)}, bf16[256,1024]{1,0:T(8,128)(2,1)S(1)}, u32[]{:S(2)}, u32[]{:S(2)}) %collective-permute-start.3) | collective-permute-done | bytes 524320 | tf_op jit(solution)/shard_map/ppermute | solution.py:24
  139.7 14.9 %collective-permute-done.10 = bf16[256,1024]{1,0:T(8,128)(2,1)} collective-permute-done((bf16[256,1024]{1,0:T(8,128)(2,1)}, bf16[256,1024]{1,0:T(8,128)(2,1)}, u32[]{:S(2)}, u32[]{:S(2)}) %collective-permute-start.10) | collective-permute-done | bytes 524320 | tf_op jit(solution)/shard_map/ppermute | solution.py:24
  181.4 39.8 %collective-permute-done.12 = bf16[256,2176]{1,0:T(8,128)(2,1)S(1)} collective-permute-done((bf16[256,2176]{1,0:T(8,128)(2,1)S(1)}, bf16[256,2176]{1,0:T(8,128)(2,1)S(1)}, u32[]{:S(2)}, u32[]{:S(2)}) %collective-permute-start.12) | collective-permute-done | bytes 1114144 | tf_op jit(solution)/shard_map/ppermute | solution.py:24
  222.4 29.0 %collective-permute-done.13 = bf16[256,2176]{1,0:T(8,128)(2,1)S(1)} collective-permute-done((bf16[256,2176]{1,0:T(8,128)(2,1)S(1)}, bf16[256,2176]{1,0:T(8,128)(2,1)S(1)}, u32[]{:S(2)}, u32[]{:S(2)}) %collective-permute-start.13) | collective-permute-done | bytes 1114144 | tf_op jit(solution)/shard_map/ppermute | solution.py:24
  294.2 17.6 %shard_map.145 = (bf16[1024,512]{1,0:T(8,128)(2,1)S(1)}, bf16[1024,512]{1,0:T(8,128)(2,1)S(1)}, bf16[1024,512]{1,0:T(8,128)(2,1)S(1)}, bf16[1024,512]{1,0:T(8,128)(2,1)}, f32[4,1024,1]{2,1,0:T(8,128)}) custom-call(f32[1024,1536]{1,0:T(8,128)} %copy-done.15, f32[1024,1536]{1,0:T(8,128)} %copy-done.15, f32[1024,1536]{1,0:T(8,128)} %copy-done.15, ...), custom_call_target="tpu_custom_call" | custom-call | flops 1000000 | bytes 100000 | tf_op jit(solution)/shard_map/pallas_call | solution.py:233
  325.2 21.7 %collective-permute-start.22 = (bf16[256,1024]{1,0:T(8,128)(2,1)}, bf16[256,1024]{1,0:T(8,128)(2,1)}, u32[]{:S(2)}, u32[]{:S(2)}) collective-permute-start(bf16[256,1024]{1,0:T(8,128)(2,1)} %get-tuple-element.122), channel_id=1, source_target_pairs={{0,8},{8,0},{16,24},{24,16},{1,9},{9,1},{17,25},{25,17},{2,10},{10... | collective-permute-start | bytes 1572872 | tf_op jit(solution)/shard_map/ppermute | solution.py:24
  349.5 15.9 %collective-permute-done.20 = bf16[256,2048]{1,0:T(8,128)(2,1)} collective-permute-done((bf16[256,2048]{1,0:T(8,128)(2,1)}, bf16[256,2048]{1,0:T(8,128)(2,1)}, u32[]{:S(2)}, u32[]{:S(2)}) %collective-permute-start.20) | collective-permute-done | bytes 1048608 | tf_op jit(solution)/shard_map/ppermute | solution.py:24
  390.6 19.3 %collective-permute-start.25 = (bf16[256,2048]{1,0:T(8,128)(2,1)}, bf16[256,2048]{1,0:T(8,128)(2,1)}, u32[]{:S(2)}, u32[]{:S(2)}) collective-permute-start(bf16[256,2048]{1,0:T(8,128)(2,1)} %multiply_convert_fusion.3.refs_0_), channel_id=1, source_target_pairs={{0,16},{8,24},{16,0},{24,8},{1,17},{9,25},{17,1},{25,9},{2,18},{10... | collective-permute-start | bytes 3145736 | tf_op jit(solution)/shard_map/ppermute | solution.py:24
  417.0 39.1 %collective-permute-done.25.refs_1_ = bf16[256,2048]{1,0:T(8,128)(2,1)} collective-permute-done((bf16[256,2048]{1,0:T(8,128)(2,1)}, bf16[256,2048]{1,0:T(8,128)(2,1)}, u32[]{:S(2)}, u32[]{:S(2)}) %collective-permute-start.25) | collective-permute-done | bytes 1048608 | tf_op jit(solution)/shard_map/ppermute | solution.py:24
  462.5 20.9 %shard_map.146 = (bf16[4,2,288,2048]{3,2,1,0:T(8,128)(2,1)}, bf16[4,2,288,1024]{3,2,1,0:T(8,128)(2,1)}, bf16[4,288,1024]{2,1,0:T(8,128)(2,1)}, bf16[4,288,1024]{2,1,0:T(8,128)(2,1)}) custom-call(s32[4,4,1,256]{3,2,1,0:T(1,128)} %pad_add_fusion.place, bf16[256,2048]{1,0:T(8,128)(2,1)} %multiply_convert_fusion.3.refs_0_, ...), custom_call_target="tpu_custom_call" | custom-call | flops 9663676416 | bytes 50331648 | tf_op jit(solution)/shard_map/pallas_call | solution.py:368
  491.0 14.8 %shard_map.147 = (bf16[256,2048]{1,0:T(8,128)(2,1)}, bf16[256,2048]{1,0:T(8,128)(2,1)}) custom-call(s32[4,4,1,256]{3,2,1,0:T(1,128)} %pad_add_fusion.place, f32[4,4,1,256]{3,2,1,0:T(1,128)} %pad_maximum_fusion.9.gate, bf16[4,2,288,1024]{3,2,1,0:T(8,128)(2,1)} %get-tuple-element.41.activated.refs_5_, bf16[4,2048,1024]{2,1,0:T(8,128)(2,1)} %bitcast.415), custom_call_target="tpu_custom_call" | custom-call | flops 9663676416 | bytes 50331648 | tf_op jit(solution)/shard_map/pallas_call | solution.py:368
  513.0 20.7 %shard_map.148 = (bf16[4,2,288,2048]{3,2,1,0:T(8,128)(2,1)}, bf16[4,2,288,1024]{3,2,1,0:T(8,128)(2,1)}, bf16[4,288,1024]{2,1,0:T(8,128)(2,1)}, bf16[4,288,1024]{2,1,0:T(8,128)(2,1)}) custom-call(s32[4,4,1,256]{3,2,1,0:T(1,128)} %pad_add_fusion.place, bf16[256,2048]{1,0:T(8,128)(2,1)} %broadcast_add_fusion.15.refs_0_, ...), custom_call_target="tpu_custom_call", output_to_operand_aliasing={{0}: (5, {}), {1}: (6, {})} | custom-call | flops 9663676416 | bytes 50331648 | tf_op jit(solution)/shard_map/pallas_call | solution.py:368
  533.7 14.9 %shard_map.149 = (bf16[256,2048]{1,0:T(8,128)(2,1)}, bf16[256,2048]{1,0:T(8,128)(2,1)}) custom-call(s32[4,4,1,256]{3,2,1,0:T(1,128)} %pad_add_fusion.place, f32[4,4,1,256]{3,2,1,0:T(1,128)} %pad_maximum_fusion.9.gate, bf16[4,2,288,1024]{3,2,1,0:T(8,128)(2,1)} %get-tuple-element.45.activated, bf16[4,2048,1024]{2,1,0:T(8,128)(2,1)} %bitcast.416), custom_call_target="tpu_custom_call" | custom-call | flops 9663676416 | bytes 50331648 | tf_op jit(solution)/shard_map/pallas_call | solution.py:368
  592.6 19.2 %collective-permute-done.29 = bf16[256,2048]{1,0:T(8,128)(2,1)} collective-permute-done((bf16[256,2048]{1,0:T(8,128)(2,1)}, bf16[256,2048]{1,0:T(8,128)(2,1)}, u32[]{:S(2)}, u32[]{:S(2)}) %collective-permute-start.29) | collective-permute-done | bytes 1048608 | tf_op jit(solution)/shard_map/ppermute | solution.py:24
  619.9 47.9 %collective-permute-done.31.refs_1_ = bf16[256,2048]{1,0:T(8,128)(2,1)S(1)} collective-permute-done((bf16[256,2048]{1,0:T(8,128)(2,1)S(1)}, bf16[256,2048]{1,0:T(8,128)(2,1)S(1)}, u32[]{:S(2)}, u32[]{:S(2)}) %collective-permute-start.31) | collective-permute-done | bytes 1048608 | tf_op jit(solution)/shard_map/ppermute | solution.py:24
  671.7 32.0 %shard_map.150 = (bf16[4,2,288,2048]{3,2,1,0:T(8,128)(2,1)}, bf16[4,2,288,1024]{3,2,1,0:T(8,128)(2,1)}, bf16[4,2,288,1024]{3,2,1,0:T(8,128)(2,1)}, bf16[256,2048]{1,0:T(8,128)(2,1)}, bf16[256,2048]{1,0:T(8,128)(2,1)}) custom-call(s32[4,4,1,256]{3,2,1,0:T(1,128)} %pad_add_fusion.place, f32[4,4,1,256]{3,2,1,0:T(1,128)} %pad_maximum_fusion.9.gate, ...), custom_call_target="tpu_custom_call" | custom-call | flops 9663676416 | bytes 50331648 | tf_op jit(solution)/shard_map/pallas_call | solution.py:368
  721.2 32.2 %shard_map.151 = (bf16[4,2,288,2048]{3,2,1,0:T(8,128)(2,1)}, bf16[4,2,288,1024]{3,2,1,0:T(8,128)(2,1)}, bf16[4,2,288,1024]{3,2,1,0:T(8,128)(2,1)}, bf16[256,2048]{1,0:T(8,128)(2,1)}, bf16[256,2048]{1,0:T(8,128)(2,1)}) custom-call(s32[4,4,1,256]{3,2,1,0:T(1,128)} %pad_add_fusion.place, ...), custom_call_target="tpu_custom_call", output_to_operand_aliasing={{0}: (9, {}), {1}: (10, {}), {2}: (11, {})} | custom-call | flops 9663676416 | bytes 50331648 | tf_op jit(solution)/shard_map/pallas_call | solution.py:368
  777.0 20.7 %convolution_convert_fusion.2 = bf16[4,2048,1024]{2,1,0:T(8,128)(2,1)} fusion(bf16[4,576,2048]{2,1,0:T(8,128)(2,1)} %bitcast.431, bf16[4,576,1024]{2,1,0:T(8,128)(2,1)} %bitcast.447), kind=kOutput, calls=%fused_computation.2 | convolution fusion | flops 9672065024 | bytes 30932992 | tf_op jit(solution)/shard_map/krd,krf->kdf/dot_general | solution.py:405
  800.5 14.1 %collective-permute-start.35 = (bf16[256,2048]{1,0:T(8,128)(2,1)}, bf16[256,2048]{1,0:T(8,128)(2,1)S(1)}, u32[]{:S(2)}, u32[]{:S(2)}) collective-permute-start(bf16[256,2048]{1,0:T(8,128)(2,1)} %copy-done.64), channel_id=1, source_target_pairs={{0,8},{8,0},{16,24},{24,16},{1,9},{9,1},{17,25},{25,17},{2,10},{10... | collective-permute-start | bytes 3145736 | tf_op jit(solution)/shard_map/ppermute | solution.py:24
  827.3 19.9 %collective-permute-done.35 = bf16[256,2048]{1,0:T(8,128)(2,1)S(1)} collective-permute-done((bf16[256,2048]{1,0:T(8,128)(2,1)}, bf16[256,2048]{1,0:T(8,128)(2,1)S(1)}, u32[]{:S(2)}, u32[]{:S(2)}) %collective-permute-start.35) | collective-permute-done | bytes 1048608 | tf_op jit(solution)/shard_map/ppermute | solution.py:24
  857.7 21.0 %convolution_convert_fusion.1 = bf16[4,2048,1024]{2,1,0:T(8,128)(2,1)} fusion(bf16[4,576,2048]{2,1,0:T(8,128)(2,1)} %bitcast.436, bf16[4,576,1024]{2,1,0:T(8,128)(2,1)} %bitcast.448), kind=kOutput, calls=%fused_computation.1 | convolution fusion | flops 9672065024 | bytes 30932992 | tf_op jit(solution)/shard_map/krd,krf->kdf/dot_general | solution.py:405
  901.9 11.7 collective-permute-done.38
  924.5 22.3 %convolution_convert_fusion = bf16[4,2048,1024]{2,1,0:T(8,128)(2,1)} fusion(bf16[4,576,2048]{2,1,0:T(8,128)(2,1)} %bitcast.437, bf16[4,576,1024]{2,1,0:T(8,128)(2,1)} %bitcast.449), kind=kOutput, calls=%fused_computation | convolution fusion | flops 9672065024 | bytes 30932992 | tf_op jit(solution)/shard_map/krd,krf->kdf/dot_general | solution.py:405
  956.8 18.9 %shard_map.152 = (f32[1024,512]{1,0:T(8,128)}, f32[1024,512]{1,0:T(8,128)}, bf16[1024,512]{1,0:T(8,128)(2,1)S(1)}, f32[1024,1]{1,0:T(8,128)S(1)}, f32[1024,1]{1,...) custom-call(f32[1024,1536]{1,0:T(8,128)} %copy-done.15, f32[1024,1536]{1,0:T(8,128)} %copy-done.15, ...), custom_call_target="tpu_custom_call" | custom-call | flops 1000000 | bytes 100000 | tf_op jit(solution)/shard_map/pallas_call | solution.py:251
  988.7 45.1 %collective-permute-done.40 = bf16[256,2048]{1,0:T(8,128)(2,1)} collective-permute-done((bf16[256,2048]{1,0:T(8,128)(2,1)}, bf16[256,2048]{1,0:T(8,128)(2,1)}, u32[]{:S(2)}, u32[]{:S(2)}) %collective-permute-start.40) | collective-permute-done | bytes 1048608 | tf_op jit(solution)/shard_map/ppermute | solution.py:24
  1037.1 26.8 %collective-permute-done.42 = bf16[256,2048]{1,0:T(8,128)(2,1)S(1)} collective-permute-done((bf16[256,2048]{1,0:T(8,128)(2,1)}, bf16[256,2048]{1,0:T(8,128)(2,1)S(1)}, u32[]{:S(2)}, u32[]{:S(2)}) %collective-permute-start.42) | collective-permute-done | bytes 1048608 | tf_op jit(solution)/shard_map/ppermute | solution.py:24
  1152.2 23.9 %collective-permute-done.50 = bf16[256,2048]{1,0:T(8,128)(2,1)} collective-permute-done((bf16[256,2048]{1,0:T(8,128)(2,1)}, bf16[256,2048]{1,0:T(8,128)(2,1)}, u32[]{:S(2)}, u32[]{:S(2)}) %collective-permute-start.50) | collective-permute-done | bytes 1048608 | tf_op jit(solution)/shard_map/ppermute | solution.py:24
  1185.7 23.1 %all-to-all-done.1 = bf16[4,256,1024]{2,1,0:T(8,128)(2,1)} async-done(((bf16[4,256,1024]{2,1,0:T(8,128)(2,1)}), bf16[4,256,1024]{2,1,0:T(8,128)(2,1)}, u32[]{:S(2)}, u32[]{:S(2)}) %all-to-all-start.1) | async-done | bytes 2097184 | tf_op jit(solution)/shard_map/all_to_all | solution.py:51
  1211.3 41.6 %collective-permute-done.49 = bf16[256,2048]{1,0:T(8,128)(2,1)} collective-permute-done((bf16[256,2048]{1,0:T(8,128)(2,1)}, bf16[256,2048]{1,0:T(8,128)(2,1)}, u32[]{:S(2)}, u32[]{:S(2)}) %collective-permute-start.49) | collective-permute-done | bytes 1048608 | tf_op jit(solution)/shard_map/ppermute | solution.py:24
  1266.7 19.7 %collective-permute-start.52 = (f32[8,128]{1,0:T(8,128)S(1)}, f32[8,128]{1,0:T(8,128)S(1)}, u32[]{:S(2)}, u32[]{:S(2)}) collective-permute-start(f32[8,128]{1,0:T(8,128)S(1)} %broadcast_in_dim.225), channel_id=1, source_target_pairs={{0,16},{8,24},{16,0},{24,8},{1,17},{9,25},{17,1},{25,9},{2,18},{10... | collective-permute-start | bytes 12296 | tf_op jit(solution)/shard_map/ppermute | solution.py:24
  1318.1 21.6 %collective-permute-done.64 = f32[4,2048]{1,0:T(4,128)S(1)} collective-permute-done((f32[4,2048]{1,0:T(4,128)S(1)}, f32[4,2048]{1,0:T(4,128)S(1)}, u32[]{:S(2)}, u32[]{:S(2)}) %collective-permute-start.64) | collective-permute-done | bytes 32800 | tf_op jit(solution)/shard_map/ppermute | solution.py:24
  1381.5 19.3 %copy.155 = f32[256,4,3072]{2,1,0:T(4,128)} copy(f32[256,4,3072]{2,0,1:T(8,128)S(1)} %convert_bitcast_fusion) | data formatting | bytes 25165824
  (589 shorter events, 574.8 us)
Async XLA Ops:
  7.2 283.4 %all-gather.5.cloned.1.call-start = ((), (), s32[]{:S(2)}) async-start(), calls=%async_computation.6 | async-start | bytes 18874368 | tf_op jit(solution)/shard_map/all_gather | solution.py:478
  23.8 57.0 %collective-permute-start = (bf16[328,2048]{1,0:T(8,128)(2,1)}, bf16[328,2048]{1,0:T(8,128)(2,1)}, u32[]{:S(2)}, u32[]{:S(2)}) collective-permute-start(bf16[328,2048]{1,0:T(8,128)(2,1)} %get-tuple-element.147), channel_id=1, source_target_pairs={{0,1},{1,0},{2,3},{3,2},{4,5},{5,4},{6,7},{7,6},{8,9},{9,8},{10,11... | collective-permute-start | bytes 4030472 | tf_op jit(solution)/shard_map/ppermute | solution.py:24
  26.7 60.0 %collective-permute-start.1 = (bf16[328,2048]{1,0:T(8,128)(2,1)}, bf16[328,2048]{1,0:T(8,128)(2,1)}, u32[]{:S(2)}, u32[]{:S(2)}) collective-permute-start(bf16[328,2048]{1,0:T(8,128)(2,1)} %get-tuple-element.148), channel_id=1, source_target_pairs={{0,2},{1,3},{2,0},{3,1},{4,6},{5,7},{6,4},{7,5},{8,10},{9,11},{10,... | collective-permute-start | bytes 4030472 | tf_op jit(solution)/shard_map/ppermute | solution.py:24
  28.2 59.3 %collective-permute-start.2 = (bf16[328,2048]{1,0:T(8,128)(2,1)}, bf16[328,2048]{1,0:T(8,128)(2,1)}, u32[]{:S(2)}, u32[]{:S(2)}) collective-permute-start(bf16[328,2048]{1,0:T(8,128)(2,1)} %get-tuple-element.146), channel_id=1, source_target_pairs={{0,3},{1,2},{2,1},{3,0},{4,7},{5,6},{6,5},{7,4},{8,11},{9,10},{10,... | collective-permute-start | bytes 4030472 | tf_op jit(solution)/shard_map/ppermute | solution.py:24
  101.3 309.9 %all-gather.7.cloned.1.call-start = ((), (), s32[]{:S(2)}) async-start(), calls=%async_computation.7 | async-start | bytes 18874368 | tf_op jit(solution)/shard_map/all_gather | solution.py:478
  158.1 332.8 %all-gather.9.cloned.1.call-start = ((), (), s32[]{:S(2)}) async-start(), calls=%async_computation.8 | async-start | bytes 18874368 | tf_op jit(solution)/shard_map/all_gather | solution.py:478
  166.3 54.9 %collective-permute-start.12 = (bf16[256,2176]{1,0:T(8,128)(2,1)S(1)}, bf16[256,2176]{1,0:T(8,128)(2,1)S(1)}, u32[]{:S(2)}, u32[]{:S(2)}) collective-permute-start(bf16[256,2176]{1,0:T(8,128)(2,1)S(1)} %broadcast_add_fusion.5), channel_id=1, source_target_pairs={{0,8},{8,0},{16,24},{24,16},{1,9},{9,1},{17,25},{25,17},{2,10},{10... | collective-permute-start | bytes 3342344 | tf_op jit(solution)/shard_map/ppermute | solution.py:24
  175.3 76.2 %collective-permute-start.13 = (bf16[256,2176]{1,0:T(8,128)(2,1)S(1)}, bf16[256,2176]{1,0:T(8,128)(2,1)S(1)}, u32[]{:S(2)}, u32[]{:S(2)}) collective-permute-start(bf16[256,2176]{1,0:T(8,128)(2,1)S(1)} %broadcast_add_fusion.5), channel_id=1, source_target_pairs={{0,16},{8,24},{16,0},{24,8},{1,17},{9,25},{17,1},{25,9},{2,18},{10... | collective-permute-start | bytes 3342344 | tf_op jit(solution)/shard_map/ppermute | solution.py:24
  175.3 77.2 %collective-permute-start.14 = (bf16[256,2176]{1,0:T(8,128)(2,1)S(1)}, bf16[256,2176]{1,0:T(8,128)(2,1)S(1)}, u32[]{:S(2)}, u32[]{:S(2)}) collective-permute-start(bf16[256,2176]{1,0:T(8,128)(2,1)S(1)} %broadcast_add_fusion.5), channel_id=1, source_target_pairs={{0,24},{8,16},{16,8},{24,0},{1,25},{9,17},{17,9},{25,1},{2,26},{10... | collective-permute-start | bytes 3342344 | tf_op jit(solution)/shard_map/ppermute | solution.py:24
  325.2 50.3 %collective-permute-start.22 = (bf16[256,1024]{1,0:T(8,128)(2,1)}, bf16[256,1024]{1,0:T(8,128)(2,1)}, u32[]{:S(2)}, u32[]{:S(2)}) collective-permute-start(bf16[256,1024]{1,0:T(8,128)(2,1)} %get-tuple-element.122), channel_id=1, source_target_pairs={{0,8},{8,0},{16,24},{24,16},{1,9},{9,1},{17,25},{25,17},{2,10},{10... | collective-permute-start | bytes 1572872 | tf_op jit(solution)/shard_map/ppermute | solution.py:24
  384.8 499.0 %all-gather.11.cloned.1.call-start = ((), (), s32[]{:S(2)}) async-start(), calls=%async_computation.9 | async-start | bytes 10485760 | tf_op jit(solution)/shard_map/all_gather | solution.py:640
  390.6 65.4 %collective-permute-start.25 = (bf16[256,2048]{1,0:T(8,128)(2,1)}, bf16[256,2048]{1,0:T(8,128)(2,1)}, u32[]{:S(2)}, u32[]{:S(2)}) collective-permute-start(bf16[256,2048]{1,0:T(8,128)(2,1)} %multiply_convert_fusion.3.refs_0_), channel_id=1, source_target_pairs={{0,16},{8,24},{16,0},{24,8},{1,17},{9,25},{17,1},{25,9},{2,18},{10... | collective-permute-start | bytes 3145736 | tf_op jit(solution)/shard_map/ppermute | solution.py:24
  416.9 532.5 %reduce-scatter.6.cloned.1.call-start = ((), (), s32[]{:S(2)}) async-start(), calls=%async_computation.11 | async-start | bytes 18874368 | tf_op jit(solution)/shard_map/reduce_scatter | solution.py:650
  461.5 49.3 %collective-permute-start.27 = (bf16[256,2048]{1,0:T(8,128)(2,1)}, bf16[256,2048]{1,0:T(8,128)(2,1)}, u32[]{:S(2)}, u32[]{:S(2)}) collective-permute-start(bf16[256,2048]{1,0:T(8,128)(2,1)} %broadcast_add_fusion.16), channel_id=1, source_target_pairs={{0,8},{8,0},{16,24},{24,16},{1,9},{9,1},{17,25},{25,17},{2,10},{10... | collective-permute-start | bytes 3145736 | tf_op jit(solution)/shard_map/ppermute | solution.py:24
  461.5 51.5 %collective-permute-start.28 = (bf16[256,2048]{1,0:T(8,128)(2,1)}, bf16[256,2048]{1,0:T(8,128)(2,1)}, u32[]{:S(2)}, u32[]{:S(2)}) collective-permute-start(bf16[256,2048]{1,0:T(8,128)(2,1)} %broadcast_add_fusion.16), channel_id=1, source_target_pairs={{0,24},{8,16},{16,8},{24,0},{1,25},{9,17},{17,9},{25,1},{2,26},{10... | collective-permute-start | bytes 3145736 | tf_op jit(solution)/shard_map/ppermute | solution.py:24
  508.3 49.0 %collective-permute-start.26 = (bf16[256,2048]{1,0:T(8,128)(2,1)}, bf16[256,2048]{1,0:T(8,128)(2,1)S(1)}, u32[]{:S(2)}, u32[]{:S(2)}) collective-permute-start(bf16[256,2048]{1,0:T(8,128)(2,1)} %get-tuple-element.43), channel_id=1, source_target_pairs={{0,16},{8,24},{16,0},{24,8},{1,17},{9,25},{17,1},{25,9},{2,18},{10... | collective-permute-start | bytes 3145736 | tf_op jit(solution)/shard_map/ppermute | solution.py:24
  670.7 49.5 %collective-permute-start.33 = (bf16[256,2048]{1,0:T(8,128)(2,1)}, bf16[256,2048]{1,0:T(8,128)(2,1)S(1)}, u32[]{:S(2)}, u32[]{:S(2)}) collective-permute-start(bf16[256,2048]{1,0:T(8,128)(2,1)} %broadcast_add_fusion.12), channel_id=1, source_target_pairs={{0,24},{8,16},{16,8},{24,0},{1,25},{9,17},{17,9},{25,1},{2,26},{10... | collective-permute-start | bytes 3145736 | tf_op jit(solution)/shard_map/ppermute | solution.py:24
  706.2 58.2 %collective-permute-start.34 = (bf16[256,2048]{1,0:T(8,128)(2,1)}, bf16[256,2048]{1,0:T(8,128)(2,1)}, u32[]{:S(2)}, u32[]{:S(2)}) collective-permute-start(bf16[256,2048]{1,0:T(8,128)(2,1)} %get-tuple-element.58), channel_id=1, source_target_pairs={{0,16},{8,24},{16,0},{24,8},{1,17},{9,25},{17,1},{25,9},{2,18},{10... | collective-permute-start | bytes 3145736 | tf_op jit(solution)/shard_map/ppermute | solution.py:24
  797.7 311.7 %reduce-scatter.8.cloned.1.call-start = ((), (), s32[]{:S(2)}) async-start(), calls=%async_computation.12 | async-start | bytes 18874368 | tf_op jit(solution)/shard_map/reduce_scatter | solution.py:650
  878.7 379.7 %reduce-scatter.4.cloned.1.call-start = ((), (), s32[]{:S(2)}) async-start(), calls=%async_computation.10 | async-start | bytes 18874368 | tf_op jit(solution)/shard_map/reduce_scatter | solution.py:650
  949.4 116.7 %all-to-all-start = ((bf16[4,256,1024]{2,1,0:T(8,128)(2,1)}), bf16[4,256,1024]{2,1,0:T(8,128)(2,1)}, u32[]{:S(2)}, u32[]{:S(2)}) async-start(bf16[4,256,1024]{2,1,0:T(8,128)(2,1)} %bitcast.464), calls=%async_computation.2 | async-start | bytes 4194304 | tf_op jit(solution)/shard_map/all_to_all | solution.py:51
  985.0 48.8 %collective-permute-start.40 = (bf16[256,2048]{1,0:T(8,128)(2,1)}, bf16[256,2048]{1,0:T(8,128)(2,1)}, u32[]{:S(2)}, u32[]{:S(2)}) collective-permute-start(bf16[256,2048]{1,0:T(8,128)(2,1)} %get-tuple-element.109), channel_id=1, source_target_pairs={{0,1},{1,0},{2,3},{3,2},{4,5},{5,4},{6,7},{7,6},{8,9},{9,8},{10,11... | collective-permute-start | bytes 3145736 | tf_op jit(solution)/shard_map/ppermute | solution.py:24
  985.0 51.1 %collective-permute-start.41 = (bf16[256,2048]{1,0:T(8,128)(2,1)}, bf16[256,2048]{1,0:T(8,128)(2,1)S(1)}, u32[]{:S(2)}, u32[]{:S(2)}) collective-permute-start(bf16[256,2048]{1,0:T(8,128)(2,1)} %get-tuple-element.109), channel_id=1, source_target_pairs={{0,2},{1,3},{2,0},{3,1},{4,6},{5,7},{6,4},{7,5},{8,10},{9,11},{10,... | collective-permute-start | bytes 3145736 | tf_op jit(solution)/shard_map/ppermute | solution.py:24
  985.0 78.9 %collective-permute-start.42 = (bf16[256,2048]{1,0:T(8,128)(2,1)}, bf16[256,2048]{1,0:T(8,128)(2,1)S(1)}, u32[]{:S(2)}, u32[]{:S(2)}) collective-permute-start(bf16[256,2048]{1,0:T(8,128)(2,1)} %get-tuple-element.109), channel_id=1, source_target_pairs={{0,3},{1,2},{2,1},{3,0},{4,7},{5,6},{6,5},{7,4},{8,11},{9,10},{10,... | collective-permute-start | bytes 3145736 | tf_op jit(solution)/shard_map/ppermute | solution.py:24
  1109.4 99.4 %all-to-all-start.1 = ((bf16[4,256,1024]{2,1,0:T(8,128)(2,1)}), bf16[4,256,1024]{2,1,0:T(8,128)(2,1)}, u32[]{:S(2)}, u32[]{:S(2)}) async-start(bf16[4,256,1024]{2,1,0:T(8,128)(2,1)} %bitcast.463), calls=%async_computation.4 | async-start | bytes 4194304 | tf_op jit(solution)/shard_map/all_to_all | solution.py:51
  1122.5 53.6 %collective-permute-start.50 = (bf16[256,2048]{1,0:T(8,128)(2,1)}, bf16[256,2048]{1,0:T(8,128)(2,1)}, u32[]{:S(2)}, u32[]{:S(2)}) collective-permute-start(bf16[256,2048]{1,0:T(8,128)(2,1)} %get-tuple-element.138), channel_id=1, source_target_pairs={{0,24},{8,16},{16,8},{24,0},{1,25},{9,17},{17,9},{25,1},{2,26},{10... | collective-permute-start | bytes 3145736 | tf_op jit(solution)/shard_map/ppermute | solution.py:24
  1126.3 126.6 %collective-permute-start.49 = (bf16[256,2048]{1,0:T(8,128)(2,1)}, bf16[256,2048]{1,0:T(8,128)(2,1)}, u32[]{:S(2)}, u32[]{:S(2)}) collective-permute-start(bf16[256,2048]{1,0:T(8,128)(2,1)} %get-tuple-element.137), channel_id=1, source_target_pairs={{0,16},{8,24},{16,0},{24,8},{1,17},{9,25},{17,1},{25,9},{2,18},{10... | collective-permute-start | bytes 3145736 | tf_op jit(solution)/shard_map/ppermute | solution.py:24
  1126.3 126.6 %collective-permute-start.48 = (bf16[256,2048]{1,0:T(8,128)(2,1)}, bf16[256,2048]{1,0:T(8,128)(2,1)}, u32[]{:S(2)}, u32[]{:S(2)}) collective-permute-start(bf16[256,2048]{1,0:T(8,128)(2,1)} %get-tuple-element.136), channel_id=1, source_target_pairs={{0,8},{8,0},{16,24},{24,16},{1,9},{9,1},{17,25},{25,17},{2,10},{10... | collective-permute-start | bytes 3145736 | tf_op jit(solution)/shard_map/ppermute | solution.py:24
  1152.2 134.3 %collective-permute-start.60 = (bf16[256,2048]{1,0:T(8,128)(2,1)}, bf16[256,2048]{1,0:T(8,128)(2,1)}, u32[]{:S(2)}, u32[]{:S(2)}) collective-permute-start(bf16[256,2048]{1,0:T(8,128)(2,1)} %get-tuple-element.134), channel_id=1, source_target_pairs={{0,3},{1,2},{2,1},{3,0},{4,7},{5,6},{6,5},{7,4},{8,11},{9,10},{10,... | collective-permute-start | bytes 3145736 | tf_op jit(solution)/shard_map/ppermute | solution.py:24
  1152.2 134.3 %collective-permute-start.59 = (bf16[256,2048]{1,0:T(8,128)(2,1)}, bf16[256,2048]{1,0:T(8,128)(2,1)}, u32[]{:S(2)}, u32[]{:S(2)}) collective-permute-start(bf16[256,2048]{1,0:T(8,128)(2,1)} %get-tuple-element.135), channel_id=1, source_target_pairs={{0,2},{1,3},{2,0},{3,1},{4,6},{5,7},{6,4},{7,5},{8,10},{9,11},{10,... | collective-permute-start | bytes 3145736 | tf_op jit(solution)/shard_map/ppermute | solution.py:24
  1176.1 110.4 %collective-permute-start.58 = (bf16[256,2048]{1,0:T(8,128)(2,1)}, bf16[256,2048]{1,0:T(8,128)(2,1)}, u32[]{:S(2)}, u32[]{:S(2)}) collective-permute-start(bf16[256,2048]{1,0:T(8,128)(2,1)} %get-tuple-element.133), channel_id=1, source_target_pairs={{0,1},{1,0},{2,3},{3,2},{4,5},{5,4},{6,7},{7,6},{8,9},{9,8},{10,11... | collective-permute-start | bytes 3145736 | tf_op jit(solution)/shard_map/ppermute | solution.py:24
  1301.6 76.4 %all-to-all-start.2 = ((bf16[4,256,1024]{2,1,0:T(8,128)(2,1)}), bf16[4,256,1024]{2,1,0:T(8,128)(2,1)}, u32[]{:S(2)}, u32[]{:S(2)}) async-start(bf16[4,256,1024]{2,1,0:T(8,128)(2,1)} %bitcast.440), calls=%async_computation.5 | async-start | bytes 4194304 | tf_op jit(solution)/shard_map/all_to_all | solution.py:51
  (131 other events, 1843.2 us)
Sparse Core Ops, SparseCore 0:
  101.4 92.9 all-gather.4
  196.8 89.8 all-gather.6
  384.9 106.0 all-gather.8
  492.7 87.5 all-gather.10
  797.9 134.9 reduce-scatter.5
  936.3 157.1 reduce-scatter.7
  1097.0 160.8 reduce-scatter.3

commit v14 on v12

--- a/solution.py
+++ b/solution.py
@@ -537,14 +537,14 @@
         for message in messages
     ]
     mine = in_order(columns, "s").reshape(part, 4 * cols + PAD)
-    seq_tokens = in_order([message[:own] for message in messages], "s")
-    seq_tokens = seq_tokens.reshape(seq, width).astype(f32)
     inputs = inputs.astype(f32)
-    gate_ready = in_order(gate_blocks, "z", token(mine))
+    gate_ready = in_order(gate_blocks, "z", token(*messages))
     w_gate = gather_plane(gate_ready)
-    up_ready = in_order(up_blocks, "z", token(seq_tokens, place, gate_of))
+    up_ready = in_order(up_blocks, "z", token(gate_ready, mine))
     w_up = gather_plane(up_ready)
     in_blocks = gather_near(after(mine, up_ready), "z")
+    seq_tokens = in_order([message[:own] for message in messages], "s", token(up_ready))
+    seq_tokens = seq_tokens.reshape(seq, width).astype(f32)
     seq_factor = rms_factor(seq_tokens)
     w_in = stack_rows(in_blocks, token(seq_factor))
     w_in_other = send(w_in, "c", 1)

time: 1410 us -> 1410 us (level)
    dynamic_update_slice x31 -> x30, local copies, waits for them, and re-layouts: 41.9 us -> 36.5 us  [in_order(): lax.dynamic_update_index_in_dim(stacked, block, (rank ^ k) + start, 0)]
    unnamed x182 -> x194, local copies, waits for them, and re-layouts: 62.2 us -> 66.5 us
    slice x38 -> x40, local copies, waits for them, and re-layouts: 32 us -> 34.5 us  [token(): value[(slice(0, 1),) * value.ndim].reshape(()).astype(f32)]
  transfers between devices with their start and end apart: 81 -> 81, of which waited for: 31 -> 34; matrix products, arithmetic and copies ran while one was open for 28% -> 28% of each run, Pallas kernels for 12% -> 12%
where the time goes in v14:
time: 1410 us; the launch traced here: 1400 us
  waiting for transfers between devices  516 us (37%)
  local copies, waits for them, and re-layouts  230 us (16%)
  starting transfers between devices  178 us (13%)
  Pallas kernels  172 us (12%)
  other arithmetic  124 us (9%)
  matrix products  109 us (8%)
  between operations  66.7 us (5%)
    ppermute x71, waiting for transfers between devices, send(): return lax.ppermute(block, axis, [(i, i ^ step) for i in range(size)])  470 us
    ppermute x71, starting transfers between devices, send(): return lax.ppermute(block, axis, [(i, i ^ step) for i in range(size)])  164 us
    pallas_call x6, Pallas kernels, run(): pl.pallas_call(functools.partial(kernel, self.count, self.slots), grid=(s...  135 us
    dot_general x10, matrix products, dot(): return jnp.einsum(spec, left, right, preferred_element_type=f32)  96.6 us
    unnamed x194, local copies, waits for them, and re-layouts  66.5 us
    all_to_all x3, waiting for transfers between devices, swap(): return lax.all_to_all(pieces, axis, split_axis=0, concat_axis=0, tiled=True)  45 us
    add x21, other arithmetic, after(): return value + token(*others).astype(value.dtype)  40.8 us
    dynamic_update_slice x30, local copies, waits for them, and re-layouts, in_order(): lax.dynamic_update_index_in_dim(stacked, block, (rank ^ k) + start, 0)  36.5 us
  transfers between devices with their start and end apart: 81, of which 34 were waited for; matrix products, arithmetic and copies ran while one was open for 28% of the time, Pallas kernels for 12%

profile of v14, /device:TPU:0, one launch (start us, length us, event | category | flops | bytes accessed | tf_op | source)
XLA Modules:
  0.0 1396.0 jit_solution(15279009158355498965)
XLA Ops:
  41.8 19.6 %collective-permute-done = bf16[256,1024]{1,0:T(8,128)(2,1)S(1)} collective-permute-done((bf16[256,1024]{1,0:T(8,128)(2,1)S(1)}, bf16[256,1024]{1,0:T(8,128)(2,1)S(1)}, u32[]{:S(2)}, u32[]{:S(2)}) %collective-permute-start) | collective-permute-done | bytes 524320 | tf_op jit(solution)/shard_map/ppermute | solution.py:24
  126.9 14.1 %collective-permute-done.7 = bf16[256,1024]{1,0:T(8,128)(2,1)} collective-permute-done((bf16[256,1024]{1,0:T(8,128)(2,1)}, bf16[256,1024]{1,0:T(8,128)(2,1)}, u32[]{:S(2)}, u32[]{:S(2)}) %collective-permute-start.7) | collective-permute-done | bytes 524320 | tf_op jit(solution)/shard_map/ppermute | solution.py:24
  172.5 39.8 %collective-permute-done.9 = bf16[256,2176]{1,0:T(8,128)(2,1)S(1)} collective-permute-done((bf16[256,2176]{1,0:T(8,128)(2,1)S(1)}, bf16[256,2176]{1,0:T(8,128)(2,1)S(1)}, u32[]{:S(2)}, u32[]{:S(2)}) %collective-permute-start.9) | collective-permute-done | bytes 1114144 | tf_op jit(solution)/shard_map/ppermute | solution.py:24
  213.4 29.2 %collective-permute-done.10 = bf16[256,2176]{1,0:T(8,128)(2,1)} collective-permute-done((bf16[256,2176]{1,0:T(8,128)(2,1)S(1)}, bf16[256,2176]{1,0:T(8,128)(2,1)}, u32[]{:S(2)}, u32[]{:S(2)}) %collective-permute-start.10) | collective-permute-done | bytes 1114144 | tf_op jit(solution)/shard_map/ppermute | solution.py:24
  286.8 17.6 %shard_map.145 = (bf16[1024,512]{1,0:T(8,128)(2,1)S(1)}, bf16[1024,512]{1,0:T(8,128)(2,1)S(1)}, bf16[1024,512]{1,0:T(8,128)(2,1)S(1)}, bf16[1024,512]{1,0:T(8,128)(2,1)}, f32[4,1024,1]{2,1,0:T(8,128)}) custom-call(f32[1024,1536]{1,0:T(8,128)} %copy-done.15, f32[1024,1536]{1,0:T(8,128)} %copy-done.15, f32[1024,1536]{1,0:T(8,128)} %copy-done.15, ...), custom_call_target="tpu_custom_call" | custom-call | flops 1000000 | bytes 100000 | tf_op jit(solution)/shard_map/pallas_call | solution.py:233
  317.8 19.5 %collective-permute-start.19 = (bf16[256,1024]{1,0:T(8,128)(2,1)}, bf16[256,1024]{1,0:T(8,128)(2,1)}, u32[]{:S(2)}, u32[]{:S(2)}) collective-permute-start(bf16[256,1024]{1,0:T(8,128)(2,1)} %get-tuple-element.122), channel_id=1, source_target_pairs={{0,8},{8,0},{16,24},{24,16},{1,9},{9,1},{17,25},{25,17},{2,10},{10... | collective-permute-start | bytes 1572872 | tf_op jit(solution)/shard_map/ppermute | solution.py:24
  339.6 18.3 %collective-permute-done.17 = bf16[256,2048]{1,0:T(8,128)(2,1)} collective-permute-done((bf16[256,2048]{1,0:T(8,128)(2,1)}, bf16[256,2048]{1,0:T(8,128)(2,1)}, u32[]{:S(2)}, u32[]{:S(2)}) %collective-permute-start.17) | collective-permute-done | bytes 1048608 | tf_op jit(solution)/shard_map/ppermute | solution.py:24
  379.0 15.7 %collective-permute-start.23 = (f32[256,16]{0,1:T(8,128)S(1)}, f32[256,16]{0,1:T(8,128)S(1)}, u32[]{:S(2)}, u32[]{:S(2)}) collective-permute-start(f32[256,16]{0,1:T(8,128)S(1)} %get-tuple-element.183), channel_id=1, source_target_pairs={{0,16},{8,24},{16,0},{24,8},{1,17},{9,25},{17,1},{25,9},{2,18},{10... | collective-permute-start | bytes 49160 | tf_op jit(solution)/shard_map/ppermute | solution.py:24
  412.8 39.1 %collective-permute-done.25.refs_1_ = bf16[256,2048]{1,0:T(8,128)(2,1)} collective-permute-done((bf16[256,2048]{1,0:T(8,128)(2,1)}, bf16[256,2048]{1,0:T(8,128)(2,1)}, u32[]{:S(2)}, u32[]{:S(2)}) %collective-permute-start.25) | collective-permute-done | bytes 1048608 | tf_op jit(solution)/shard_map/ppermute | solution.py:24
  458.7 20.7 %shard_map.146 = (bf16[4,2,288,2048]{3,2,1,0:T(8,128)(2,1)}, bf16[4,2,288,1024]{3,2,1,0:T(8,128)(2,1)}, bf16[4,288,1024]{2,1,0:T(8,128)(2,1)}, bf16[4,288,1024]{2,1,0:T(8,128)(2,1)}) custom-call(s32[4,4,1,256]{3,2,1,0:T(1,128)} %pad_add_fusion.place, bf16[256,2048]{1,0:T(8,128)(2,1)} %multiply_convert_fusion.2.refs_0_, ...), custom_call_target="tpu_custom_call" | custom-call | flops 9663676416 | bytes 50331648 | tf_op jit(solution)/shard_map/pallas_call | solution.py:368
  480.1 14.8 %shard_map.147 = (bf16[256,2048]{1,0:T(8,128)(2,1)}, bf16[256,2048]{1,0:T(8,128)(2,1)}) custom-call(s32[4,4,1,256]{3,2,1,0:T(1,128)} %pad_add_fusion.place, f32[4,4,1,256]{3,2,1,0:T(1,128)} %pad_maximum_fusion.9.gate, bf16[4,2,288,1024]{3,2,1,0:T(8,128)(2,1)} %get-tuple-element.41.activated.refs_5_, bf16[4,2048,1024]{2,1,0:T(8,128)(2,1)} %bitcast.419), custom_call_target="tpu_custom_call" | custom-call | flops 9663676416 | bytes 50331648 | tf_op jit(solution)/shard_map/pallas_call | solution.py:368
  507.0 21.4 %shard_map.148 = (bf16[4,2,288,2048]{3,2,1,0:T(8,128)(2,1)}, bf16[4,2,288,1024]{3,2,1,0:T(8,128)(2,1)}, bf16[4,288,1024]{2,1,0:T(8,128)(2,1)}, bf16[4,288,1024]{2,1,0:T(8,128)(2,1)}) custom-call(s32[4,4,1,256]{3,2,1,0:T(1,128)} %pad_add_fusion.place, bf16[256,2048]{1,0:T(8,128)(2,1)} %broadcast_add_fusion.15.refs_0_, ...), custom_call_target="tpu_custom_call", output_to_operand_aliasing={{0}: (5, {}), {1}: (6, {})} | custom-call | flops 9663676416 | bytes 50331648 | tf_op jit(solution)/shard_map/pallas_call | solution.py:368
  528.3 14.4 %shard_map.149 = (bf16[256,2048]{1,0:T(8,128)(2,1)}, bf16[256,2048]{1,0:T(8,128)(2,1)}) custom-call(s32[4,4,1,256]{3,2,1,0:T(1,128)} %pad_add_fusion.place, f32[4,4,1,256]{3,2,1,0:T(1,128)} %pad_maximum_fusion.9.gate, bf16[4,2,288,1024]{3,2,1,0:T(8,128)(2,1)} %get-tuple-element.45.activated, bf16[4,2048,1024]{2,1,0:T(8,128)(2,1)} %bitcast.420), custom_call_target="tpu_custom_call" | custom-call | flops 9663676416 | bytes 50331648 | tf_op jit(solution)/shard_map/pallas_call | solution.py:368
  557.3 15.8 %collective-permute-start.29 = (bf16[256,2048]{1,0:T(8,128)(2,1)}, bf16[256,2048]{1,0:T(8,128)(2,1)}, u32[]{:S(2)}, u32[]{:S(2)}) collective-permute-start(bf16[256,2048]{1,0:T(8,128)(2,1)} %broadcast_add_fusion.14), channel_id=1, source_target_pairs={{0,8},{8,0},{16,24},{24,16},{1,9},{9,1},{17,25},{25,17},{2,10},{10... | collective-permute-start | bytes 3145736 | tf_op jit(solution)/shard_map/ppermute | solution.py:24
  613.6 47.0 %collective-permute-done.31.refs_1_ = bf16[256,2048]{1,0:T(8,128)(2,1)S(1)} collective-permute-done((bf16[256,2048]{1,0:T(8,128)(2,1)S(1)}, bf16[256,2048]{1,0:T(8,128)(2,1)S(1)}, u32[]{:S(2)}, u32[]{:S(2)}) %collective-permute-start.31) | collective-permute-done | bytes 1048608 | tf_op jit(solution)/shard_map/ppermute | solution.py:24
  665.9 32.0 %shard_map.150 = (bf16[4,2,288,2048]{3,2,1,0:T(8,128)(2,1)}, bf16[4,2,288,1024]{3,2,1,0:T(8,128)(2,1)}, bf16[4,2,288,1024]{3,2,1,0:T(8,128)(2,1)}, bf16[256,2048]{1,0:T(8,128)(2,1)}, bf16[256,2048]{1,0:T(8,128)(2,1)}) custom-call(s32[4,4,1,256]{3,2,1,0:T(1,128)} %pad_add_fusion.place, f32[4,4,1,256]{3,2,1,0:T(1,128)} %pad_maximum_fusion.9.gate, ...), custom_call_target="tpu_custom_call" | custom-call | flops 9663676416 | bytes 50331648 | tf_op jit(solution)/shard_map/pallas_call | solution.py:368
  713.6 32.2 %shard_map.151 = (bf16[4,2,288,2048]{3,2,1,0:T(8,128)(2,1)}, bf16[4,2,288,1024]{3,2,1,0:T(8,128)(2,1)}, bf16[4,2,288,1024]{3,2,1,0:T(8,128)(2,1)}, bf16[256,2048]{1,0:T(8,128)(2,1)}, bf16[256,2048]{1,0:T(8,128)(2,1)}) custom-call(s32[4,4,1,256]{3,2,1,0:T(1,128)} %pad_add_fusion.place, ...), custom_call_target="tpu_custom_call", output_to_operand_aliasing={{0}: (9, {}), {1}: (10, {}), {2}: (11, {})} | custom-call | flops 9663676416 | bytes 50331648 | tf_op jit(solution)/shard_map/pallas_call | solution.py:368
  770.0 20.7 %convolution_convert_fusion.2 = bf16[4,2048,1024]{2,1,0:T(8,128)(2,1)} fusion(bf16[4,576,2048]{2,1,0:T(8,128)(2,1)} %bitcast.435, bf16[4,576,1024]{2,1,0:T(8,128)(2,1)} %bitcast.448), kind=kOutput, calls=%fused_computation.2 | convolution fusion | flops 9672065024 | bytes 30932992 | tf_op jit(solution)/shard_map/krd,krf->kdf/dot_general | solution.py:405
  794.7 14.1 %collective-permute-start.35 = (bf16[256,2048]{1,0:T(8,128)(2,1)}, bf16[256,2048]{1,0:T(8,128)(2,1)S(1)}, u32[]{:S(2)}, u32[]{:S(2)}) collective-permute-start(bf16[256,2048]{1,0:T(8,128)(2,1)} %copy-done.64), channel_id=1, source_target_pairs={{0,8},{8,0},{16,24},{24,16},{1,9},{9,1},{17,25},{25,17},{2,10},{10... | collective-permute-start | bytes 3145736 | tf_op jit(solution)/shard_map/ppermute | solution.py:24
  820.2 21.3 %collective-permute-done.35 = bf16[256,2048]{1,0:T(8,128)(2,1)S(1)} collective-permute-done((bf16[256,2048]{1,0:T(8,128)(2,1)}, bf16[256,2048]{1,0:T(8,128)(2,1)S(1)}, u32[]{:S(2)}, u32[]{:S(2)}) %collective-permute-start.35) | collective-permute-done | bytes 1048608 | tf_op jit(solution)/shard_map/ppermute | solution.py:24
  852.1 20.9 %convolution_convert_fusion.1 = bf16[4,2048,1024]{2,1,0:T(8,128)(2,1)} fusion(bf16[4,576,2048]{2,1,0:T(8,128)(2,1)} %bitcast.440, bf16[4,576,1024]{2,1,0:T(8,128)(2,1)} %bitcast.449), kind=kOutput, calls=%fused_computation.1 | convolution fusion | flops 9672065024 | bytes 30932992 | tf_op jit(solution)/shard_map/krd,krf->kdf/dot_general | solution.py:405
  896.6 10.2 collective-permute-done.38
  917.7 22.1 %convolution_convert_fusion = bf16[4,2048,1024]{2,1,0:T(8,128)(2,1)} fusion(bf16[4,576,2048]{2,1,0:T(8,128)(2,1)} %bitcast.441, bf16[4,576,1024]{2,1,0:T(8,128)(2,1)} %bitcast.450), kind=kOutput, calls=%fused_computation | convolution fusion | flops 9672065024 | bytes 30932992 | tf_op jit(solution)/shard_map/krd,krf->kdf/dot_general | solution.py:405
  949.7 18.9 %shard_map.152 = (f32[1024,512]{1,0:T(8,128)}, f32[1024,512]{1,0:T(8,128)}, bf16[1024,512]{1,0:T(8,128)(2,1)S(1)}, f32[1024,1]{1,0:T(8,128)S(1)}, f32[1024,1]{1,...) custom-call(f32[1024,1536]{1,0:T(8,128)} %copy-done.15, f32[1024,1536]{1,0:T(8,128)} %copy-done.15, ...), custom_call_target="tpu_custom_call" | custom-call | flops 1000000 | bytes 100000 | tf_op jit(solution)/shard_map/pallas_call | solution.py:251
  981.4 45.1 %collective-permute-done.40 = bf16[256,2048]{1,0:T(8,128)(2,1)} collective-permute-done((bf16[256,2048]{1,0:T(8,128)(2,1)}, bf16[256,2048]{1,0:T(8,128)(2,1)}, u32[]{:S(2)}, u32[]{:S(2)}) %collective-permute-start.40) | collective-permute-done | bytes 1048608 | tf_op jit(solution)/shard_map/ppermute | solution.py:24
  1029.8 28.2 %collective-permute-done.42 = bf16[256,2048]{1,0:T(8,128)(2,1)S(1)} collective-permute-done((bf16[256,2048]{1,0:T(8,128)(2,1)}, bf16[256,2048]{1,0:T(8,128)(2,1)S(1)}, u32[]{:S(2)}, u32[]{:S(2)}) %collective-permute-start.42) | collective-permute-done | bytes 1048608 | tf_op jit(solution)/shard_map/ppermute | solution.py:24
  1145.6 23.8 %collective-permute-done.50 = bf16[256,2048]{1,0:T(8,128)(2,1)} collective-permute-done((bf16[256,2048]{1,0:T(8,128)(2,1)}, bf16[256,2048]{1,0:T(8,128)(2,1)}, u32[]{:S(2)}, u32[]{:S(2)}) %collective-permute-start.50) | collective-permute-done | bytes 1048608 | tf_op jit(solution)/shard_map/ppermute | solution.py:24
  1181.1 21.0 %all-to-all-done.1 = bf16[4,256,1024]{2,1,0:T(8,128)(2,1)} async-done(((bf16[4,256,1024]{2,1,0:T(8,128)(2,1)}), bf16[4,256,1024]{2,1,0:T(8,128)(2,1)}, u32[]{:S(2)}, u32[]{:S(2)}) %all-to-all-start.1) | async-done | bytes 2097184 | tf_op jit(solution)/shard_map/all_to_all | solution.py:51
  1204.5 41.6 %collective-permute-done.49 = bf16[256,2048]{1,0:T(8,128)(2,1)} collective-permute-done((bf16[256,2048]{1,0:T(8,128)(2,1)}, bf16[256,2048]{1,0:T(8,128)(2,1)}, u32[]{:S(2)}, u32[]{:S(2)}) %collective-permute-start.49) | collective-permute-done | bytes 1048608 | tf_op jit(solution)/shard_map/ppermute | solution.py:24
  1269.9 14.0 %collective-permute-start.65 = (f32[4,2048]{1,0:T(4,128)S(1)}, f32[4,2048]{1,0:T(4,128)S(1)}, u32[]{:S(2)}, u32[]{:S(2)}) collective-permute-start(f32[4,2048]{1,0:T(4,128)S(1)} %maximum_add_fusion.1), channel_id=1, source_target_pairs={{0,16},{8,24},{16,0},{24,8},{1,17},{9,25},{17,1},{25,9},{2,18},{10... | collective-permute-start | bytes 98312 | tf_op jit(solution)/shard_map/ppermute | solution.py:24
  1340.7 24.0 %all-to-all-done.2 = bf16[4,256,1024]{2,1,0:T(8,128)(2,1)} async-done(((bf16[4,256,1024]{2,1,0:T(8,128)(2,1)}), bf16[4,256,1024]{2,1,0:T(8,128)(2,1)}, u32[]{:S(2)}, u32[]{:S(2)}) %all-to-all-start.2) | async-done | bytes 2097184 | tf_op jit(solution)/shard_map/all_to_all | solution.py:51
  1368.3 19.3 %copy.156 = f32[256,4,3072]{2,1,0:T(4,128)} copy(f32[256,4,3072]{2,0,1:T(8,128)S(1)} %convert_bitcast_fusion) | data formatting | bytes 25165824
  (598 shorter events, 573.1 us)
Async XLA Ops:
  7.2 276.0 %all-gather.5.cloned.1.call-start = ((), (), s32[]{:S(2)}) async-start(), calls=%async_computation.6 | async-start | bytes 18874368 | tf_op jit(solution)/shard_map/all_gather | solution.py:478
  23.5 54.0 %collective-permute-start.3 = (bf16[328,2048]{1,0:T(8,128)(2,1)}, bf16[328,2048]{1,0:T(8,128)(2,1)}, u32[]{:S(2)}, u32[]{:S(2)}) collective-permute-start(bf16[328,2048]{1,0:T(8,128)(2,1)} %get-tuple-element.147), channel_id=1, source_target_pairs={{0,1},{1,0},{2,3},{3,2},{4,5},{5,4},{6,7},{7,6},{8,9},{9,8},{10,11... | collective-permute-start | bytes 4030472 | tf_op jit(solution)/shard_map/ppermute | solution.py:24
  26.4 60.0 %collective-permute-start.4 = (bf16[328,2048]{1,0:T(8,128)(2,1)}, bf16[328,2048]{1,0:T(8,128)(2,1)}, u32[]{:S(2)}, u32[]{:S(2)}) collective-permute-start(bf16[328,2048]{1,0:T(8,128)(2,1)} %get-tuple-element.148), channel_id=1, source_target_pairs={{0,2},{1,3},{2,0},{3,1},{4,6},{5,7},{6,4},{7,5},{8,10},{9,11},{10,... | collective-permute-start | bytes 4030472 | tf_op jit(solution)/shard_map/ppermute | solution.py:24
  28.0 60.3 %collective-permute-start.5 = (bf16[328,2048]{1,0:T(8,128)(2,1)}, bf16[328,2048]{1,0:T(8,128)(2,1)}, u32[]{:S(2)}, u32[]{:S(2)}) collective-permute-start(bf16[328,2048]{1,0:T(8,128)(2,1)} %get-tuple-element.146), channel_id=1, source_target_pairs={{0,3},{1,2},{2,1},{3,0},{4,7},{5,6},{6,5},{7,4},{8,11},{9,10},{10,... | collective-permute-start | bytes 4030472 | tf_op jit(solution)/shard_map/ppermute | solution.py:24
  95.7 311.4 %all-gather.7.cloned.1.call-start = ((), (), s32[]{:S(2)}) async-start(), calls=%async_computation.7 | async-start | bytes 18874368 | tf_op jit(solution)/shard_map/all_gather | solution.py:478
  143.9 336.2 %all-gather.9.cloned.1.call-start = ((), (), s32[]{:S(2)}) async-start(), calls=%async_computation.8 | async-start | bytes 18874368 | tf_op jit(solution)/shard_map/all_gather | solution.py:478
  157.6 54.7 %collective-permute-start.9 = (bf16[256,2176]{1,0:T(8,128)(2,1)S(1)}, bf16[256,2176]{1,0:T(8,128)(2,1)S(1)}, u32[]{:S(2)}, u32[]{:S(2)}) collective-permute-start(bf16[256,2176]{1,0:T(8,128)(2,1)S(1)} %broadcast_add_fusion.5), channel_id=1, source_target_pairs={{0,8},{8,0},{16,24},{24,16},{1,9},{9,1},{17,25},{25,17},{2,10},{10... | collective-permute-start | bytes 3342344 | tf_op jit(solution)/shard_map/ppermute | solution.py:24
  166.3 76.3 %collective-permute-start.10 = (bf16[256,2176]{1,0:T(8,128)(2,1)S(1)}, bf16[256,2176]{1,0:T(8,128)(2,1)}, u32[]{:S(2)}, u32[]{:S(2)}) collective-permute-start(bf16[256,2176]{1,0:T(8,128)(2,1)S(1)} %broadcast_add_fusion.5), channel_id=1, source_target_pairs={{0,16},{8,24},{16,0},{24,8},{1,17},{9,25},{17,1},{25,9},{2,18},{10... | collective-permute-start | bytes 3342344 | tf_op jit(solution)/shard_map/ppermute | solution.py:24
  166.3 78.6 %collective-permute-start.11 = (bf16[256,2176]{1,0:T(8,128)(2,1)S(1)}, bf16[256,2176]{1,0:T(8,128)(2,1)}, u32[]{:S(2)}, u32[]{:S(2)}) collective-permute-start(bf16[256,2176]{1,0:T(8,128)(2,1)S(1)} %broadcast_add_fusion.5), channel_id=1, source_target_pairs={{0,24},{8,16},{16,8},{24,0},{1,25},{9,17},{17,9},{25,1},{2,26},{10... | collective-permute-start | bytes 3342344 | tf_op jit(solution)/shard_map/ppermute | solution.py:24
  317.8 50.0 %collective-permute-start.19 = (bf16[256,1024]{1,0:T(8,128)(2,1)}, bf16[256,1024]{1,0:T(8,128)(2,1)}, u32[]{:S(2)}, u32[]{:S(2)}) collective-permute-start(bf16[256,1024]{1,0:T(8,128)(2,1)} %get-tuple-element.122), channel_id=1, source_target_pairs={{0,8},{8,0},{16,24},{24,16},{1,9},{9,1},{17,25},{25,17},{2,10},{10... | collective-permute-start | bytes 1572872 | tf_op jit(solution)/shard_map/ppermute | solution.py:24
  378.8 499.3 %all-gather.11.cloned.1.call-start = ((), (), s32[]{:S(2)}) async-start(), calls=%async_computation.9 | async-start | bytes 10485760 | tf_op jit(solution)/shard_map/all_gather | solution.py:640
  412.8 529.6 %reduce-scatter.4.cloned.1.call-start = ((), (), s32[]{:S(2)}) async-start(), calls=%async_computation.10 | async-start | bytes 18874368 | tf_op jit(solution)/shard_map/reduce_scatter | solution.py:650
  457.3 47.4 %collective-permute-start.27 = (bf16[256,2048]{1,0:T(8,128)(2,1)}, bf16[256,2048]{1,0:T(8,128)(2,1)}, u32[]{:S(2)}, u32[]{:S(2)}) collective-permute-start(bf16[256,2048]{1,0:T(8,128)(2,1)} %broadcast_add_fusion.16), channel_id=1, source_target_pairs={{0,8},{8,0},{16,24},{24,16},{1,9},{9,1},{17,25},{25,17},{2,10},{10... | collective-permute-start | bytes 3145736 | tf_op jit(solution)/shard_map/ppermute | solution.py:24
  457.3 49.7 %collective-permute-start.28 = (bf16[256,2048]{1,0:T(8,128)(2,1)}, bf16[256,2048]{1,0:T(8,128)(2,1)}, u32[]{:S(2)}, u32[]{:S(2)}) collective-permute-start(bf16[256,2048]{1,0:T(8,128)(2,1)} %broadcast_add_fusion.16), channel_id=1, source_target_pairs={{0,24},{8,16},{16,8},{24,0},{1,25},{9,17},{17,9},{25,1},{2,26},{10... | collective-permute-start | bytes 3145736 | tf_op jit(solution)/shard_map/ppermute | solution.py:24
  497.4 53.8 %collective-permute-start.26 = (bf16[256,2048]{1,0:T(8,128)(2,1)}, bf16[256,2048]{1,0:T(8,128)(2,1)S(1)}, u32[]{:S(2)}, u32[]{:S(2)}) collective-permute-start(bf16[256,2048]{1,0:T(8,128)(2,1)} %get-tuple-element.43), channel_id=1, source_target_pairs={{0,16},{8,24},{16,0},{24,8},{1,17},{9,25},{17,1},{25,9},{2,18},{10... | collective-permute-start | bytes 3145736 | tf_op jit(solution)/shard_map/ppermute | solution.py:24
  612.2 48.4 %collective-permute-start.31 = (bf16[256,2048]{1,0:T(8,128)(2,1)S(1)}, bf16[256,2048]{1,0:T(8,128)(2,1)S(1)}, u32[]{:S(2)}, u32[]{:S(2)}) collective-permute-start(bf16[256,2048]{1,0:T(8,128)(2,1)S(1)} %get-tuple-element.111.refs_0_), channel_id=1, source_target_pairs={{0,16},{8,24},{16,0},{24,8},{1,17},{9,25},{17,1},{25,9},{2,18},{10... | collective-permute-start | bytes 3145736 | tf_op jit(solution)/shard_map/ppermute | solution.py:24
  663.5 49.1 %collective-permute-start.34 = (bf16[256,2048]{1,0:T(8,128)(2,1)}, bf16[256,2048]{1,0:T(8,128)(2,1)S(1)}, u32[]{:S(2)}, u32[]{:S(2)}) collective-permute-start(bf16[256,2048]{1,0:T(8,128)(2,1)} %broadcast_add_fusion.12), channel_id=1, source_target_pairs={{0,24},{8,16},{16,8},{24,0},{1,25},{9,17},{17,9},{25,1},{2,26},{10... | collective-permute-start | bytes 3145736 | tf_op jit(solution)/shard_map/ppermute | solution.py:24
  700.4 57.0 %collective-permute-start.32 = (bf16[256,2048]{1,0:T(8,128)(2,1)}, bf16[256,2048]{1,0:T(8,128)(2,1)}, u32[]{:S(2)}, u32[]{:S(2)}) collective-permute-start(bf16[256,2048]{1,0:T(8,128)(2,1)} %get-tuple-element.54), channel_id=1, source_target_pairs={{0,16},{8,24},{16,0},{24,8},{1,17},{9,25},{17,1},{25,9},{2,18},{10... | collective-permute-start | bytes 3145736 | tf_op jit(solution)/shard_map/ppermute | solution.py:24
  790.7 311.9 %reduce-scatter.6.cloned.1.call-start = ((), (), s32[]{:S(2)}) async-start(), calls=%async_computation.11 | async-start | bytes 18874368 | tf_op jit(solution)/shard_map/reduce_scatter | solution.py:650
  873.1 434.9 %reduce-scatter.8.cloned.1.call-start = ((), (), s32[]{:S(2)}) async-start(), calls=%async_computation.12 | async-start | bytes 18874368 | tf_op jit(solution)/shard_map/reduce_scatter | solution.py:650
  942.4 117.9 %all-to-all-start = ((bf16[4,256,1024]{2,1,0:T(8,128)(2,1)}), bf16[4,256,1024]{2,1,0:T(8,128)(2,1)}, u32[]{:S(2)}, u32[]{:S(2)}) async-start(bf16[4,256,1024]{2,1,0:T(8,128)(2,1)} %bitcast.465), calls=%async_computation.1 | async-start | bytes 4194304 | tf_op jit(solution)/shard_map/all_to_all | solution.py:51
  977.7 48.8 %collective-permute-start.40 = (bf16[256,2048]{1,0:T(8,128)(2,1)}, bf16[256,2048]{1,0:T(8,128)(2,1)}, u32[]{:S(2)}, u32[]{:S(2)}) collective-permute-start(bf16[256,2048]{1,0:T(8,128)(2,1)} %get-tuple-element.109), channel_id=1, source_target_pairs={{0,1},{1,0},{2,3},{3,2},{4,5},{5,4},{6,7},{7,6},{8,9},{9,8},{10,11... | collective-permute-start | bytes 3145736 | tf_op jit(solution)/shard_map/ppermute | solution.py:24
  978.1 50.7 %collective-permute-start.41 = (bf16[256,2048]{1,0:T(8,128)(2,1)}, bf16[256,2048]{1,0:T(8,128)(2,1)S(1)}, u32[]{:S(2)}, u32[]{:S(2)}) collective-permute-start(bf16[256,2048]{1,0:T(8,128)(2,1)} %get-tuple-element.109), channel_id=1, source_target_pairs={{0,2},{1,3},{2,0},{3,1},{4,6},{5,7},{6,4},{7,5},{8,10},{9,11},{10,... | collective-permute-start | bytes 3145736 | tf_op jit(solution)/shard_map/ppermute | solution.py:24
  979.6 78.4 %collective-permute-start.42 = (bf16[256,2048]{1,0:T(8,128)(2,1)}, bf16[256,2048]{1,0:T(8,128)(2,1)S(1)}, u32[]{:S(2)}, u32[]{:S(2)}) collective-permute-start(bf16[256,2048]{1,0:T(8,128)(2,1)} %get-tuple-element.109), channel_id=1, source_target_pairs={{0,3},{1,2},{2,1},{3,0},{4,7},{5,6},{6,5},{7,4},{8,11},{9,10},{10,... | collective-permute-start | bytes 3145736 | tf_op jit(solution)/shard_map/ppermute | solution.py:24
  1102.6 99.4 %all-to-all-start.1 = ((bf16[4,256,1024]{2,1,0:T(8,128)(2,1)}), bf16[4,256,1024]{2,1,0:T(8,128)(2,1)}, u32[]{:S(2)}, u32[]{:S(2)}) async-start(bf16[4,256,1024]{2,1,0:T(8,128)(2,1)} %bitcast.464), calls=%async_computation.3 | async-start | bytes 4194304 | tf_op jit(solution)/shard_map/all_to_all | solution.py:51
  1115.7 53.7 %collective-permute-start.50 = (bf16[256,2048]{1,0:T(8,128)(2,1)}, bf16[256,2048]{1,0:T(8,128)(2,1)}, u32[]{:S(2)}, u32[]{:S(2)}) collective-permute-start(bf16[256,2048]{1,0:T(8,128)(2,1)} %get-tuple-element.138), channel_id=1, source_target_pairs={{0,24},{8,16},{16,8},{24,0},{1,25},{9,17},{17,9},{25,1},{2,26},{10... | collective-permute-start | bytes 3145736 | tf_op jit(solution)/shard_map/ppermute | solution.py:24
  1119.4 126.6 %collective-permute-start.49 = (bf16[256,2048]{1,0:T(8,128)(2,1)}, bf16[256,2048]{1,0:T(8,128)(2,1)}, u32[]{:S(2)}, u32[]{:S(2)}) collective-permute-start(bf16[256,2048]{1,0:T(8,128)(2,1)} %get-tuple-element.137), channel_id=1, source_target_pairs={{0,16},{8,24},{16,0},{24,8},{1,17},{9,25},{17,1},{25,9},{2,18},{10... | collective-permute-start | bytes 3145736 | tf_op jit(solution)/shard_map/ppermute | solution.py:24
  1119.4 126.6 %collective-permute-start.48 = (bf16[256,2048]{1,0:T(8,128)(2,1)}, bf16[256,2048]{1,0:T(8,128)(2,1)}, u32[]{:S(2)}, u32[]{:S(2)}) collective-permute-start(bf16[256,2048]{1,0:T(8,128)(2,1)} %get-tuple-element.136), channel_id=1, source_target_pairs={{0,8},{8,0},{16,24},{24,16},{1,9},{9,1},{17,25},{25,17},{2,10},{10... | collective-permute-start | bytes 3145736 | tf_op jit(solution)/shard_map/ppermute | solution.py:24
  1145.6 108.2 %collective-permute-start.60 = (bf16[256,2048]{1,0:T(8,128)(2,1)}, bf16[256,2048]{1,0:T(8,128)(2,1)}, u32[]{:S(2)}, u32[]{:S(2)}) collective-permute-start(bf16[256,2048]{1,0:T(8,128)(2,1)} %get-tuple-element.134), channel_id=1, source_target_pairs={{0,3},{1,2},{2,1},{3,0},{4,7},{5,6},{6,5},{7,4},{8,11},{9,10},{10,... | collective-permute-start | bytes 3145736 | tf_op jit(solution)/shard_map/ppermute | solution.py:24
  1145.6 111.2 %collective-permute-start.59 = (bf16[256,2048]{1,0:T(8,128)(2,1)}, bf16[256,2048]{1,0:T(8,128)(2,1)}, u32[]{:S(2)}, u32[]{:S(2)}) collective-permute-start(bf16[256,2048]{1,0:T(8,128)(2,1)} %get-tuple-element.135), channel_id=1, source_target_pairs={{0,2},{1,3},{2,0},{3,1},{4,6},{5,7},{6,4},{7,5},{8,10},{9,11},{10,... | collective-permute-start | bytes 3145736 | tf_op jit(solution)/shard_map/ppermute | solution.py:24
  1169.4 87.4 %collective-permute-start.58 = (bf16[256,2048]{1,0:T(8,128)(2,1)}, bf16[256,2048]{1,0:T(8,128)(2,1)}, u32[]{:S(2)}, u32[]{:S(2)}) collective-permute-start(bf16[256,2048]{1,0:T(8,128)(2,1)} %get-tuple-element.133), channel_id=1, source_target_pairs={{0,1},{1,0},{2,3},{3,2},{4,5},{5,4},{6,7},{7,6},{8,9},{9,8},{10,11... | collective-permute-start | bytes 3145736 | tf_op jit(solution)/shard_map/ppermute | solution.py:24
  1311.1 53.6 %all-to-all-start.2 = ((bf16[4,256,1024]{2,1,0:T(8,128)(2,1)}), bf16[4,256,1024]{2,1,0:T(8,128)(2,1)}, u32[]{:S(2)}, u32[]{:S(2)}) async-start(bf16[4,256,1024]{2,1,0:T(8,128)(2,1)} %bitcast.190), calls=%async_computation.5 | async-start | bytes 4194304 | tf_op jit(solution)/shard_map/all_to_all | solution.py:51
  (135 other events, 1950.8 us)
Sparse Core Ops, SparseCore 0:
  95.8 93.4 all-gather.4
  191.7 89.8 all-gather.6
  379.0 101.0 all-gather.8
  481.8 87.6 all-gather.10
  790.8 136.2 reduce-scatter.3
  930.6 156.9 reduce-scatter.5
  1091.2 160.7 reduce-scatter.7

commit v15 on v14

--- a/solution.py
+++ b/solution.py
@@ -735,7 +735,7 @@
         [got[s, :, i * cols : (i + 1) * cols] for i in range(4) for s in range(seqs)], axis=1
     )
     grad_expert = jnp.concatenate([gate_ready, up_ready, down_ready], axis=2)
-    grad_expert = grad_expert.astype(f32).transpose(1, 0, 2)
+    grad_expert = lax.optimization_barrier(grad_expert.transpose(1, 0, 2)).astype(f32)
     return (
         to_outer(final_out).astype(bf16),
         loss_value,

time: 1410 us -> 1400 us (level)
  transfers between devices with their start and end apart: 81 -> 81, of which waited for: 34 -> 33; matrix products, arithmetic and copies ran while one was open for 28% -> 28% of each run, Pallas kernels for 12% -> 12%
where the time goes in v15:
time: 1400 us; the launch traced here: 1390 us
  waiting for transfers between devices  516 us (37%)
  local copies, waits for them, and re-layouts  223 us (16%)
  starting transfers between devices  179 us (13%)
  Pallas kernels  172 us (12%)
  other arithmetic  126 us (9%)
  matrix products  109 us (8%)
  between operations  66.5 us (5%)
    ppermute x71, waiting for transfers between devices, send(): return lax.ppermute(block, axis, [(i, i ^ step) for i in range(size)])  470 us
    ppermute x71, starting transfers between devices, send(): return lax.ppermute(block, axis, [(i, i ^ step) for i in range(size)])  164 us
    pallas_call x6, Pallas kernels, run(): pl.pallas_call(functools.partial(kernel, self.count, self.slots), grid=(s...  135 us
    dot_general x10, matrix products, dot(): return jnp.einsum(spec, left, right, preferred_element_type=f32)  96.9 us
    unnamed x194, local copies, waits for them, and re-layouts  59.6 us
    all_to_all x3, waiting for transfers between devices, swap(): return lax.all_to_all(pieces, axis, split_axis=0, concat_axis=0, tiled=True)  45 us
    add x21, other arithmetic, after(): return value + token(*others).astype(value.dtype)  40.9 us
    dynamic_update_slice x30, local copies, waits for them, and re-layouts, in_order(): lax.dynamic_update_index_in_dim(stacked, block, (rank ^ k) + start, 0)  36.4 us
  transfers between devices with their start and end apart: 81, of which 33 were waited for; matrix products, arithmetic and copies ran while one was open for 28% of the time, Pallas kernels for 12%

profile of v15, /device:TPU:0, one launch (start us, length us, event | category | flops | bytes accessed | tf_op | source)
XLA Modules:
  0.0 1391.2 jit_solution(11235897628676253717)
XLA Ops:
  41.8 19.6 %collective-permute-done = bf16[256,1024]{1,0:T(8,128)(2,1)S(1)} collective-permute-done((bf16[256,1024]{1,0:T(8,128)(2,1)S(1)}, bf16[256,1024]{1,0:T(8,128)(2,1)S(1)}, u32[]{:S(2)}, u32[]{:S(2)}) %collective-permute-start) | collective-permute-done | bytes 524320 | tf_op jit(solution)/shard_map/ppermute | solution.py:24
  126.9 14.1 %collective-permute-done.7 = bf16[256,1024]{1,0:T(8,128)(2,1)} collective-permute-done((bf16[256,1024]{1,0:T(8,128)(2,1)}, bf16[256,1024]{1,0:T(8,128)(2,1)}, u32[]{:S(2)}, u32[]{:S(2)}) %collective-permute-start.7) | collective-permute-done | bytes 524320 | tf_op jit(solution)/shard_map/ppermute | solution.py:24
  172.7 39.8 %collective-permute-done.9 = bf16[256,2176]{1,0:T(8,128)(2,1)S(1)} collective-permute-done((bf16[256,2176]{1,0:T(8,128)(2,1)S(1)}, bf16[256,2176]{1,0:T(8,128)(2,1)S(1)}, u32[]{:S(2)}, u32[]{:S(2)}) %collective-permute-start.9) | collective-permute-done | bytes 1114144 | tf_op jit(solution)/shard_map/ppermute | solution.py:24
  213.7 29.1 %collective-permute-done.10 = bf16[256,2176]{1,0:T(8,128)(2,1)} collective-permute-done((bf16[256,2176]{1,0:T(8,128)(2,1)S(1)}, bf16[256,2176]{1,0:T(8,128)(2,1)}, u32[]{:S(2)}, u32[]{:S(2)}) %collective-permute-start.10) | collective-permute-done | bytes 1114144 | tf_op jit(solution)/shard_map/ppermute | solution.py:24
  286.7 17.6 %shard_map.145 = (bf16[1024,512]{1,0:T(8,128)(2,1)S(1)}, bf16[1024,512]{1,0:T(8,128)(2,1)S(1)}, bf16[1024,512]{1,0:T(8,128)(2,1)S(1)}, bf16[1024,512]{1,0:T(8,128)(2,1)}, f32[4,1024,1]{2,1,0:T(8,128)}) custom-call(f32[1024,1536]{1,0:T(8,128)} %copy-done.15, f32[1024,1536]{1,0:T(8,128)} %copy-done.15, f32[1024,1536]{1,0:T(8,128)} %copy-done.15, ...), custom_call_target="tpu_custom_call" | custom-call | flops 1000000 | bytes 100000 | tf_op jit(solution)/shard_map/pallas_call | solution.py:233
  317.8 19.6 %collective-permute-start.19 = (bf16[256,1024]{1,0:T(8,128)(2,1)}, bf16[256,1024]{1,0:T(8,128)(2,1)}, u32[]{:S(2)}, u32[]{:S(2)}) collective-permute-start(bf16[256,1024]{1,0:T(8,128)(2,1)} %get-tuple-element.122), channel_id=1, source_target_pairs={{0,8},{8,0},{16,24},{24,16},{1,9},{9,1},{17,25},{25,17},{2,10},{10... | collective-permute-start | bytes 1572872 | tf_op jit(solution)/shard_map/ppermute | solution.py:24
  339.7 18.1 %collective-permute-done.17 = bf16[256,2048]{1,0:T(8,128)(2,1)} collective-permute-done((bf16[256,2048]{1,0:T(8,128)(2,1)}, bf16[256,2048]{1,0:T(8,128)(2,1)}, u32[]{:S(2)}, u32[]{:S(2)}) %collective-permute-start.17) | collective-permute-done | bytes 1048608 | tf_op jit(solution)/shard_map/ppermute | solution.py:24
  379.0 15.8 %collective-permute-start.23 = (f32[256,16]{0,1:T(8,128)S(1)}, f32[256,16]{0,1:T(8,128)S(1)}, u32[]{:S(2)}, u32[]{:S(2)}) collective-permute-start(f32[256,16]{0,1:T(8,128)S(1)} %get-tuple-element.183), channel_id=1, source_target_pairs={{0,16},{8,24},{16,0},{24,8},{1,17},{9,25},{17,1},{25,9},{2,18},{10... | collective-permute-start | bytes 49160 | tf_op jit(solution)/shard_map/ppermute | solution.py:24
  412.9 39.1 %collective-permute-done.25.refs_1_ = bf16[256,2048]{1,0:T(8,128)(2,1)} collective-permute-done((bf16[256,2048]{1,0:T(8,128)(2,1)}, bf16[256,2048]{1,0:T(8,128)(2,1)}, u32[]{:S(2)}, u32[]{:S(2)}) %collective-permute-start.25) | collective-permute-done | bytes 1048608 | tf_op jit(solution)/shard_map/ppermute | solution.py:24
  458.7 20.7 %shard_map.146 = (bf16[4,2,288,2048]{3,2,1,0:T(8,128)(2,1)}, bf16[4,2,288,1024]{3,2,1,0:T(8,128)(2,1)}, bf16[4,288,1024]{2,1,0:T(8,128)(2,1)}, bf16[4,288,1024]{2,1,0:T(8,128)(2,1)}) custom-call(s32[4,4,1,256]{3,2,1,0:T(1,128)} %pad_add_fusion.place, bf16[256,2048]{1,0:T(8,128)(2,1)} %multiply_convert_fusion.2.refs_0_, ...), custom_call_target="tpu_custom_call" | custom-call | flops 9663676416 | bytes 50331648 | tf_op jit(solution)/shard_map/pallas_call | solution.py:368
  480.1 14.8 %shard_map.147 = (bf16[256,2048]{1,0:T(8,128)(2,1)}, bf16[256,2048]{1,0:T(8,128)(2,1)}) custom-call(s32[4,4,1,256]{3,2,1,0:T(1,128)} %pad_add_fusion.place, f32[4,4,1,256]{3,2,1,0:T(1,128)} %pad_maximum_fusion.9.gate, bf16[4,2,288,1024]{3,2,1,0:T(8,128)(2,1)} %get-tuple-element.41.activated.refs_5_, bf16[4,2048,1024]{2,1,0:T(8,128)(2,1)} %bitcast.419), custom_call_target="tpu_custom_call" | custom-call | flops 9663676416 | bytes 50331648 | tf_op jit(solution)/shard_map/pallas_call | solution.py:368
  507.0 21.4 %shard_map.148 = (bf16[4,2,288,2048]{3,2,1,0:T(8,128)(2,1)}, bf16[4,2,288,1024]{3,2,1,0:T(8,128)(2,1)}, bf16[4,288,1024]{2,1,0:T(8,128)(2,1)}, bf16[4,288,1024]{2,1,0:T(8,128)(2,1)}) custom-call(s32[4,4,1,256]{3,2,1,0:T(1,128)} %pad_add_fusion.place, bf16[256,2048]{1,0:T(8,128)(2,1)} %broadcast_add_fusion.15.refs_0_, ...), custom_call_target="tpu_custom_call", output_to_operand_aliasing={{0}: (5, {}), {1}: (6, {})} | custom-call | flops 9663676416 | bytes 50331648 | tf_op jit(solution)/shard_map/pallas_call | solution.py:368
  528.4 14.4 %shard_map.149 = (bf16[256,2048]{1,0:T(8,128)(2,1)}, bf16[256,2048]{1,0:T(8,128)(2,1)}) custom-call(s32[4,4,1,256]{3,2,1,0:T(1,128)} %pad_add_fusion.place, f32[4,4,1,256]{3,2,1,0:T(1,128)} %pad_maximum_fusion.9.gate, bf16[4,2,288,1024]{3,2,1,0:T(8,128)(2,1)} %get-tuple-element.45.activated, bf16[4,2048,1024]{2,1,0:T(8,128)(2,1)} %bitcast.420), custom_call_target="tpu_custom_call" | custom-call | flops 9663676416 | bytes 50331648 | tf_op jit(solution)/shard_map/pallas_call | solution.py:368
  557.4 15.8 %collective-permute-start.29 = (bf16[256,2048]{1,0:T(8,128)(2,1)}, bf16[256,2048]{1,0:T(8,128)(2,1)}, u32[]{:S(2)}, u32[]{:S(2)}) collective-permute-start(bf16[256,2048]{1,0:T(8,128)(2,1)} %broadcast_add_fusion.14), channel_id=1, source_target_pairs={{0,8},{8,0},{16,24},{24,16},{1,9},{9,1},{17,25},{25,17},{2,10},{10... | collective-permute-start | bytes 3145736 | tf_op jit(solution)/shard_map/ppermute | solution.py:24
  613.7 47.0 %collective-permute-done.31.refs_1_ = bf16[256,2048]{1,0:T(8,128)(2,1)S(1)} collective-permute-done((bf16[256,2048]{1,0:T(8,128)(2,1)S(1)}, bf16[256,2048]{1,0:T(8,128)(2,1)S(1)}, u32[]{:S(2)}, u32[]{:S(2)}) %collective-permute-start.31) | collective-permute-done | bytes 1048608 | tf_op jit(solution)/shard_map/ppermute | solution.py:24
  665.9 32.0 %shard_map.150 = (bf16[4,2,288,2048]{3,2,1,0:T(8,128)(2,1)}, bf16[4,2,288,1024]{3,2,1,0:T(8,128)(2,1)}, bf16[4,2,288,1024]{3,2,1,0:T(8,128)(2,1)}, bf16[256,2048]{1,0:T(8,128)(2,1)}, bf16[256,2048]{1,0:T(8,128)(2,1)}) custom-call(s32[4,4,1,256]{3,2,1,0:T(1,128)} %pad_add_fusion.place, f32[4,4,1,256]{3,2,1,0:T(1,128)} %pad_maximum_fusion.9.gate, ...), custom_call_target="tpu_custom_call" | custom-call | flops 9663676416 | bytes 50331648 | tf_op jit(solution)/shard_map/pallas_call | solution.py:368
  713.6 32.0 %shard_map.151 = (bf16[4,2,288,2048]{3,2,1,0:T(8,128)(2,1)}, bf16[4,2,288,1024]{3,2,1,0:T(8,128)(2,1)}, bf16[4,2,288,1024]{3,2,1,0:T(8,128)(2,1)}, bf16[256,2048]{1,0:T(8,128)(2,1)}, bf16[256,2048]{1,0:T(8,128)(2,1)}) custom-call(s32[4,4,1,256]{3,2,1,0:T(1,128)} %pad_add_fusion.place, ...), custom_call_target="tpu_custom_call", output_to_operand_aliasing={{0}: (9, {}), {1}: (10, {}), {2}: (11, {})} | custom-call | flops 9663676416 | bytes 50331648 | tf_op jit(solution)/shard_map/pallas_call | solution.py:368
  770.1 20.7 %convolution_convert_fusion.2 = bf16[4,2048,1024]{2,1,0:T(8,128)(2,1)} fusion(bf16[4,576,2048]{2,1,0:T(8,128)(2,1)} %bitcast.435, bf16[4,576,1024]{2,1,0:T(8,128)(2,1)} %bitcast.448), kind=kOutput, calls=%fused_computation.2 | convolution fusion | flops 9672065024 | bytes 30932992 | tf_op jit(solution)/shard_map/krd,krf->kdf/dot_general | solution.py:405
  794.8 13.8 collective-permute-start.35
  820.3 21.3 %collective-permute-done.35 = bf16[256,2048]{1,0:T(8,128)(2,1)S(1)} collective-permute-done((bf16[256,2048]{1,0:T(8,128)(2,1)}, bf16[256,2048]{1,0:T(8,128)(2,1)S(1)}, u32[]{:S(2)}, u32[]{:S(2)}) %collective-permute-start.35) | collective-permute-done | bytes 1048608 | tf_op jit(solution)/shard_map/ppermute | solution.py:24
  852.3 21.0 %convolution_convert_fusion.1 = bf16[4,2048,1024]{2,1,0:T(8,128)(2,1)} fusion(bf16[4,576,2048]{2,1,0:T(8,128)(2,1)} %bitcast.440, bf16[4,576,1024]{2,1,0:T(8,128)(2,1)} %bitcast.449), kind=kOutput, calls=%fused_computation.1 | convolution fusion | flops 9672065024 | bytes 30932992 | tf_op jit(solution)/shard_map/krd,krf->kdf/dot_general | solution.py:405
  896.6 10.7 collective-permute-done.38
  918.1 22.3 %convolution_convert_fusion = bf16[4,2048,1024]{2,1,0:T(8,128)(2,1)} fusion(bf16[4,576,2048]{2,1,0:T(8,128)(2,1)} %bitcast.441, bf16[4,576,1024]{2,1,0:T(8,128)(2,1)} %bitcast.450), kind=kOutput, calls=%fused_computation | convolution fusion | flops 9672065024 | bytes 30932992 | tf_op jit(solution)/shard_map/krd,krf->kdf/dot_general | solution.py:405
  950.3 18.9 %shard_map.152 = (f32[1024,512]{1,0:T(8,128)}, f32[1024,512]{1,0:T(8,128)}, bf16[1024,512]{1,0:T(8,128)(2,1)S(1)}, f32[1024,1]{1,0:T(8,128)S(1)}, f32[1024,1]{1,...) custom-call(f32[1024,1536]{1,0:T(8,128)} %copy-done.15, f32[1024,1536]{1,0:T(8,128)} %copy-done.15, ...), custom_call_target="tpu_custom_call" | custom-call | flops 1000000 | bytes 100000 | tf_op jit(solution)/shard_map/pallas_call | solution.py:251
  982.1 45.1 %collective-permute-done.40 = bf16[256,2048]{1,0:T(8,128)(2,1)} collective-permute-done((bf16[256,2048]{1,0:T(8,128)(2,1)}, bf16[256,2048]{1,0:T(8,128)(2,1)}, u32[]{:S(2)}, u32[]{:S(2)}) %collective-permute-start.40) | collective-permute-done | bytes 1048608 | tf_op jit(solution)/shard_map/ppermute | solution.py:24
  1030.5 27.6 %collective-permute-done.42 = bf16[256,2048]{1,0:T(8,128)(2,1)S(1)} collective-permute-done((bf16[256,2048]{1,0:T(8,128)(2,1)}, bf16[256,2048]{1,0:T(8,128)(2,1)S(1)}, u32[]{:S(2)}, u32[]{:S(2)}) %collective-permute-start.42) | collective-permute-done | bytes 1048608 | tf_op jit(solution)/shard_map/ppermute | solution.py:24
  1145.7 23.8 %collective-permute-done.50 = bf16[256,2048]{1,0:T(8,128)(2,1)} collective-permute-done((bf16[256,2048]{1,0:T(8,128)(2,1)}, bf16[256,2048]{1,0:T(8,128)(2,1)}, u32[]{:S(2)}, u32[]{:S(2)}) %collective-permute-start.50) | collective-permute-done | bytes 1048608 | tf_op jit(solution)/shard_map/ppermute | solution.py:24
  1181.1 21.0 %all-to-all-done.1 = bf16[4,256,1024]{2,1,0:T(8,128)(2,1)} async-done(((bf16[4,256,1024]{2,1,0:T(8,128)(2,1)}), bf16[4,256,1024]{2,1,0:T(8,128)(2,1)}, u32[]{:S(2)}, u32[]{:S(2)}) %all-to-all-start.1) | async-done | bytes 2097184 | tf_op jit(solution)/shard_map/all_to_all | solution.py:51
  1204.5 41.6 %collective-permute-done.49 = bf16[256,2048]{1,0:T(8,128)(2,1)} collective-permute-done((bf16[256,2048]{1,0:T(8,128)(2,1)}, bf16[256,2048]{1,0:T(8,128)(2,1)}, u32[]{:S(2)}, u32[]{:S(2)}) %collective-permute-start.49) | collective-permute-done | bytes 1048608 | tf_op jit(solution)/shard_map/ppermute | solution.py:24
  1270.2 14.1 %collective-permute-start.65 = (f32[4,2048]{1,0:T(4,128)S(1)}, f32[4,2048]{1,0:T(4,128)S(1)}, u32[]{:S(2)}, u32[]{:S(2)}) collective-permute-start(f32[4,2048]{1,0:T(4,128)S(1)} %maximum_add_fusion.1), channel_id=1, source_target_pairs={{0,16},{8,24},{16,0},{24,8},{1,17},{9,25},{17,1},{25,9},{2,18},{10... | collective-permute-start | bytes 98312 | tf_op jit(solution)/shard_map/ppermute | solution.py:24
  1341.2 24.0 %all-to-all-done.2 = bf16[4,256,1024]{2,1,0:T(8,128)(2,1)} async-done(((bf16[4,256,1024]{2,1,0:T(8,128)(2,1)}), bf16[4,256,1024]{2,1,0:T(8,128)(2,1)}, u32[]{:S(2)}, u32[]{:S(2)}) %all-to-all-start.2) | async-done | bytes 2097184 | tf_op jit(solution)/shard_map/all_to_all | solution.py:51
  1370.7 12.4 copy.156
  (598 shorter events, 575.6 us)
Async XLA Ops:
  7.2 276.0 %all-gather.5.cloned.1.call-start = ((), (), s32[]{:S(2)}) async-start(), calls=%async_computation.6 | async-start | bytes 18874368 | tf_op jit(solution)/shard_map/all_gather | solution.py:478
  23.5 54.0 %collective-permute-start.3 = (bf16[328,2048]{1,0:T(8,128)(2,1)}, bf16[328,2048]{1,0:T(8,128)(2,1)}, u32[]{:S(2)}, u32[]{:S(2)}) collective-permute-start(bf16[328,2048]{1,0:T(8,128)(2,1)} %get-tuple-element.147), channel_id=1, source_target_pairs={{0,1},{1,0},{2,3},{3,2},{4,5},{5,4},{6,7},{7,6},{8,9},{9,8},{10,11... | collective-permute-start | bytes 4030472 | tf_op jit(solution)/shard_map/ppermute | solution.py:24
  26.4 60.0 %collective-permute-start.4 = (bf16[328,2048]{1,0:T(8,128)(2,1)}, bf16[328,2048]{1,0:T(8,128)(2,1)}, u32[]{:S(2)}, u32[]{:S(2)}) collective-permute-start(bf16[328,2048]{1,0:T(8,128)(2,1)} %get-tuple-element.148), channel_id=1, source_target_pairs={{0,2},{1,3},{2,0},{3,1},{4,6},{5,7},{6,4},{7,5},{8,10},{9,11},{10,... | collective-permute-start | bytes 4030472 | tf_op jit(solution)/shard_map/ppermute | solution.py:24
  28.0 60.3 %collective-permute-start.5 = (bf16[328,2048]{1,0:T(8,128)(2,1)}, bf16[328,2048]{1,0:T(8,128)(2,1)}, u32[]{:S(2)}, u32[]{:S(2)}) collective-permute-start(bf16[328,2048]{1,0:T(8,128)(2,1)} %get-tuple-element.146), channel_id=1, source_target_pairs={{0,3},{1,2},{2,1},{3,0},{4,7},{5,6},{6,5},{7,4},{8,11},{9,10},{10,... | collective-permute-start | bytes 4030472 | tf_op jit(solution)/shard_map/ppermute | solution.py:24
  95.7 311.4 %all-gather.7.cloned.1.call-start = ((), (), s32[]{:S(2)}) async-start(), calls=%async_computation.7 | async-start | bytes 18874368 | tf_op jit(solution)/shard_map/all_gather | solution.py:478
  143.9 336.3 %all-gather.9.cloned.1.call-start = ((), (), s32[]{:S(2)}) async-start(), calls=%async_computation.8 | async-start | bytes 18874368 | tf_op jit(solution)/shard_map/all_gather | solution.py:478
  157.8 54.7 %collective-permute-start.9 = (bf16[256,2176]{1,0:T(8,128)(2,1)S(1)}, bf16[256,2176]{1,0:T(8,128)(2,1)S(1)}, u32[]{:S(2)}, u32[]{:S(2)}) collective-permute-start(bf16[256,2176]{1,0:T(8,128)(2,1)S(1)} %broadcast_add_fusion.5), channel_id=1, source_target_pairs={{0,8},{8,0},{16,24},{24,16},{1,9},{9,1},{17,25},{25,17},{2,10},{10... | collective-permute-start | bytes 3342344 | tf_op jit(solution)/shard_map/ppermute | solution.py:24
  166.5 76.3 %collective-permute-start.10 = (bf16[256,2176]{1,0:T(8,128)(2,1)S(1)}, bf16[256,2176]{1,0:T(8,128)(2,1)}, u32[]{:S(2)}, u32[]{:S(2)}) collective-permute-start(bf16[256,2176]{1,0:T(8,128)(2,1)S(1)} %broadcast_add_fusion.5), channel_id=1, source_target_pairs={{0,16},{8,24},{16,0},{24,8},{1,17},{9,25},{17,1},{25,9},{2,18},{10... | collective-permute-start | bytes 3342344 | tf_op jit(solution)/shard_map/ppermute | solution.py:24
  166.5 78.6 %collective-permute-start.11 = (bf16[256,2176]{1,0:T(8,128)(2,1)S(1)}, bf16[256,2176]{1,0:T(8,128)(2,1)}, u32[]{:S(2)}, u32[]{:S(2)}) collective-permute-start(bf16[256,2176]{1,0:T(8,128)(2,1)S(1)} %broadcast_add_fusion.5), channel_id=1, source_target_pairs={{0,24},{8,16},{16,8},{24,0},{1,25},{9,17},{17,9},{25,1},{2,26},{10... | collective-permute-start | bytes 3342344 | tf_op jit(solution)/shard_map/ppermute | solution.py:24
  317.8 50.0 %collective-permute-start.19 = (bf16[256,1024]{1,0:T(8,128)(2,1)}, bf16[256,1024]{1,0:T(8,128)(2,1)}, u32[]{:S(2)}, u32[]{:S(2)}) collective-permute-start(bf16[256,1024]{1,0:T(8,128)(2,1)} %get-tuple-element.122), channel_id=1, source_target_pairs={{0,8},{8,0},{16,24},{24,16},{1,9},{9,1},{17,25},{25,17},{2,10},{10... | collective-permute-start | bytes 1572872 | tf_op jit(solution)/shard_map/ppermute | solution.py:24
  378.8 499.6 %all-gather.11.cloned.1.call-start = ((), (), s32[]{:S(2)}) async-start(), calls=%async_computation.9 | async-start | bytes 10485760 | tf_op jit(solution)/shard_map/all_gather | solution.py:640
  412.8 530.1 %reduce-scatter.4.cloned.1.call-start = ((), (), s32[]{:S(2)}) async-start(), calls=%async_computation.10 | async-start | bytes 18874368 | tf_op jit(solution)/shard_map/reduce_scatter | solution.py:650
  457.3 47.4 %collective-permute-start.27 = (bf16[256,2048]{1,0:T(8,128)(2,1)}, bf16[256,2048]{1,0:T(8,128)(2,1)}, u32[]{:S(2)}, u32[]{:S(2)}) collective-permute-start(bf16[256,2048]{1,0:T(8,128)(2,1)} %broadcast_add_fusion.16), channel_id=1, source_target_pairs={{0,8},{8,0},{16,24},{24,16},{1,9},{9,1},{17,25},{25,17},{2,10},{10... | collective-permute-start | bytes 3145736 | tf_op jit(solution)/shard_map/ppermute | solution.py:24
  457.3 49.7 %collective-permute-start.28 = (bf16[256,2048]{1,0:T(8,128)(2,1)}, bf16[256,2048]{1,0:T(8,128)(2,1)}, u32[]{:S(2)}, u32[]{:S(2)}) collective-permute-start(bf16[256,2048]{1,0:T(8,128)(2,1)} %broadcast_add_fusion.16), channel_id=1, source_target_pairs={{0,24},{8,16},{16,8},{24,0},{1,25},{9,17},{17,9},{25,1},{2,26},{10... | collective-permute-start | bytes 3145736 | tf_op jit(solution)/shard_map/ppermute | solution.py:24
  497.5 53.7 %collective-permute-start.26 = (bf16[256,2048]{1,0:T(8,128)(2,1)}, bf16[256,2048]{1,0:T(8,128)(2,1)S(1)}, u32[]{:S(2)}, u32[]{:S(2)}) collective-permute-start(bf16[256,2048]{1,0:T(8,128)(2,1)} %get-tuple-element.43), channel_id=1, source_target_pairs={{0,16},{8,24},{16,0},{24,8},{1,17},{9,25},{17,1},{25,9},{2,18},{10... | collective-permute-start | bytes 3145736 | tf_op jit(solution)/shard_map/ppermute | solution.py:24
  612.2 48.4 %collective-permute-start.31 = (bf16[256,2048]{1,0:T(8,128)(2,1)S(1)}, bf16[256,2048]{1,0:T(8,128)(2,1)S(1)}, u32[]{:S(2)}, u32[]{:S(2)}) collective-permute-start(bf16[256,2048]{1,0:T(8,128)(2,1)S(1)} %get-tuple-element.111.refs_0_), channel_id=1, source_target_pairs={{0,16},{8,24},{16,0},{24,8},{1,17},{9,25},{17,1},{25,9},{2,18},{10... | collective-permute-start | bytes 3145736 | tf_op jit(solution)/shard_map/ppermute | solution.py:24
  663.5 49.1 %collective-permute-start.34 = (bf16[256,2048]{1,0:T(8,128)(2,1)}, bf16[256,2048]{1,0:T(8,128)(2,1)S(1)}, u32[]{:S(2)}, u32[]{:S(2)}) collective-permute-start(bf16[256,2048]{1,0:T(8,128)(2,1)} %broadcast_add_fusion.12), channel_id=1, source_target_pairs={{0,24},{8,16},{16,8},{24,0},{1,25},{9,17},{17,9},{25,1},{2,26},{10... | collective-permute-start | bytes 3145736 | tf_op jit(solution)/shard_map/ppermute | solution.py:24
  700.4 57.0 %collective-permute-start.32 = (bf16[256,2048]{1,0:T(8,128)(2,1)}, bf16[256,2048]{1,0:T(8,128)(2,1)}, u32[]{:S(2)}, u32[]{:S(2)}) collective-permute-start(bf16[256,2048]{1,0:T(8,128)(2,1)} %get-tuple-element.54), channel_id=1, source_target_pairs={{0,16},{8,24},{16,0},{24,8},{1,17},{9,25},{17,1},{25,9},{2,18},{10... | collective-permute-start | bytes 3145736 | tf_op jit(solution)/shard_map/ppermute | solution.py:24
  790.8 311.9 %reduce-scatter.6.cloned.1.call-start = ((), (), s32[]{:S(2)}) async-start(), calls=%async_computation.11 | async-start | bytes 18874368 | tf_op jit(solution)/shard_map/reduce_scatter | solution.py:650
  873.3 435.1 %reduce-scatter.8.cloned.1.call-start = ((), (), s32[]{:S(2)}) async-start(), calls=%async_computation.12 | async-start | bytes 18874368 | tf_op jit(solution)/shard_map/reduce_scatter | solution.py:650
  942.9 117.4 %all-to-all-start = ((bf16[4,256,1024]{2,1,0:T(8,128)(2,1)}), bf16[4,256,1024]{2,1,0:T(8,128)(2,1)}, u32[]{:S(2)}, u32[]{:S(2)}) async-start(bf16[4,256,1024]{2,1,0:T(8,128)(2,1)} %bitcast.465), calls=%async_computation.1 | async-start | bytes 4194304 | tf_op jit(solution)/shard_map/all_to_all | solution.py:51
  978.3 48.8 %collective-permute-start.40 = (bf16[256,2048]{1,0:T(8,128)(2,1)}, bf16[256,2048]{1,0:T(8,128)(2,1)}, u32[]{:S(2)}, u32[]{:S(2)}) collective-permute-start(bf16[256,2048]{1,0:T(8,128)(2,1)} %get-tuple-element.109), channel_id=1, source_target_pairs={{0,1},{1,0},{2,3},{3,2},{4,5},{5,4},{6,7},{7,6},{8,9},{9,8},{10,11... | collective-permute-start | bytes 3145736 | tf_op jit(solution)/shard_map/ppermute | solution.py:24
  978.3 51.1 %collective-permute-start.41 = (bf16[256,2048]{1,0:T(8,128)(2,1)}, bf16[256,2048]{1,0:T(8,128)(2,1)S(1)}, u32[]{:S(2)}, u32[]{:S(2)}) collective-permute-start(bf16[256,2048]{1,0:T(8,128)(2,1)} %get-tuple-element.109), channel_id=1, source_target_pairs={{0,2},{1,3},{2,0},{3,1},{4,6},{5,7},{6,4},{7,5},{8,10},{9,11},{10,... | collective-permute-start | bytes 3145736 | tf_op jit(solution)/shard_map/ppermute | solution.py:24
  979.9 78.2 %collective-permute-start.42 = (bf16[256,2048]{1,0:T(8,128)(2,1)}, bf16[256,2048]{1,0:T(8,128)(2,1)S(1)}, u32[]{:S(2)}, u32[]{:S(2)}) collective-permute-start(bf16[256,2048]{1,0:T(8,128)(2,1)} %get-tuple-element.109), channel_id=1, source_target_pairs={{0,3},{1,2},{2,1},{3,0},{4,7},{5,6},{6,5},{7,4},{8,11},{9,10},{10,... | collective-permute-start | bytes 3145736 | tf_op jit(solution)/shard_map/ppermute | solution.py:24
  1102.7 99.4 %all-to-all-start.1 = ((bf16[4,256,1024]{2,1,0:T(8,128)(2,1)}), bf16[4,256,1024]{2,1,0:T(8,128)(2,1)}, u32[]{:S(2)}, u32[]{:S(2)}) async-start(bf16[4,256,1024]{2,1,0:T(8,128)(2,1)} %bitcast.464), calls=%async_computation.3 | async-start | bytes 4194304 | tf_op jit(solution)/shard_map/all_to_all | solution.py:51
  1115.7 53.7 %collective-permute-start.50 = (bf16[256,2048]{1,0:T(8,128)(2,1)}, bf16[256,2048]{1,0:T(8,128)(2,1)}, u32[]{:S(2)}, u32[]{:S(2)}) collective-permute-start(bf16[256,2048]{1,0:T(8,128)(2,1)} %get-tuple-element.138), channel_id=1, source_target_pairs={{0,24},{8,16},{16,8},{24,0},{1,25},{9,17},{17,9},{25,1},{2,26},{10... | collective-permute-start | bytes 3145736 | tf_op jit(solution)/shard_map/ppermute | solution.py:24
  1119.5 126.6 %collective-permute-start.49 = (bf16[256,2048]{1,0:T(8,128)(2,1)}, bf16[256,2048]{1,0:T(8,128)(2,1)}, u32[]{:S(2)}, u32[]{:S(2)}) collective-permute-start(bf16[256,2048]{1,0:T(8,128)(2,1)} %get-tuple-element.137), channel_id=1, source_target_pairs={{0,16},{8,24},{16,0},{24,8},{1,17},{9,25},{17,1},{25,9},{2,18},{10... | collective-permute-start | bytes 3145736 | tf_op jit(solution)/shard_map/ppermute | solution.py:24
  1119.5 126.6 %collective-permute-start.48 = (bf16[256,2048]{1,0:T(8,128)(2,1)}, bf16[256,2048]{1,0:T(8,128)(2,1)}, u32[]{:S(2)}, u32[]{:S(2)}) collective-permute-start(bf16[256,2048]{1,0:T(8,128)(2,1)} %get-tuple-element.136), channel_id=1, source_target_pairs={{0,8},{8,0},{16,24},{24,16},{1,9},{9,1},{17,25},{25,17},{2,10},{10... | collective-permute-start | bytes 3145736 | tf_op jit(solution)/shard_map/ppermute | solution.py:24
  1145.7 108.2 %collective-permute-start.60 = (bf16[256,2048]{1,0:T(8,128)(2,1)}, bf16[256,2048]{1,0:T(8,128)(2,1)}, u32[]{:S(2)}, u32[]{:S(2)}) collective-permute-start(bf16[256,2048]{1,0:T(8,128)(2,1)} %get-tuple-element.134), channel_id=1, source_target_pairs={{0,3},{1,2},{2,1},{3,0},{4,7},{5,6},{6,5},{7,4},{8,11},{9,10},{10,... | collective-permute-start | bytes 3145736 | tf_op jit(solution)/shard_map/ppermute | solution.py:24
  1145.7 111.2 %collective-permute-start.59 = (bf16[256,2048]{1,0:T(8,128)(2,1)}, bf16[256,2048]{1,0:T(8,128)(2,1)}, u32[]{:S(2)}, u32[]{:S(2)}) collective-permute-start(bf16[256,2048]{1,0:T(8,128)(2,1)} %get-tuple-element.135), channel_id=1, source_target_pairs={{0,2},{1,3},{2,0},{3,1},{4,6},{5,7},{6,4},{7,5},{8,10},{9,11},{10,... | collective-permute-start | bytes 3145736 | tf_op jit(solution)/shard_map/ppermute | solution.py:24
  1169.4 87.4 %collective-permute-start.58 = (bf16[256,2048]{1,0:T(8,128)(2,1)}, bf16[256,2048]{1,0:T(8,128)(2,1)}, u32[]{:S(2)}, u32[]{:S(2)}) collective-permute-start(bf16[256,2048]{1,0:T(8,128)(2,1)} %get-tuple-element.133), channel_id=1, source_target_pairs={{0,1},{1,0},{2,3},{3,2},{4,5},{5,4},{6,7},{7,6},{8,9},{9,8},{10,11... | collective-permute-start | bytes 3145736 | tf_op jit(solution)/shard_map/ppermute | solution.py:24
  1311.4 53.8 %all-to-all-start.2 = ((bf16[4,256,1024]{2,1,0:T(8,128)(2,1)}), bf16[4,256,1024]{2,1,0:T(8,128)(2,1)}, u32[]{:S(2)}, u32[]{:S(2)}) async-start(bf16[4,256,1024]{2,1,0:T(8,128)(2,1)} %bitcast.190), calls=%async_computation.5 | async-start | bytes 4194304 | tf_op jit(solution)/shard_map/all_to_all | solution.py:51
  (135 other events, 1953.7 us)
Sparse Core Ops, SparseCore 0:
  95.8 93.4 all-gather.4
  191.7 89.8 all-gather.6
  378.9 101.1 all-gather.8
  481.8 87.6 all-gather.10
  790.9 136.2 reduce-scatter.3
  930.7 156.8 reduce-scatter.5
  1091.2 160.7 reduce-scatter.7
